TPU v7x, 128 devices: a whole 4x4x4 slice. The times are simulated.
128 devices in a mesh: row: 4 (over x_hi, core), col: 4 (over y), depth: 8 (over z, x_lo).
Axes of the slice: x: 4 (x_hi: 2, x_lo: 2; x = x_hi * 2 + x_lo), y: 4, z: 4, core: 2. Of those that a mesh axis runs over, the one named last changes fastest.
Arguments:
- tokens: bfloat16 [8192, 6144], P(('depth', 'col'), 'row'), may hold values from -6 to 6
- weight: bfloat16 [6144, 12288], P('row', 'col'), may hold values from -0.078125 to 0.078125
- cotangent: bfloat16 [8192, 12288], P(('depth', 'row'), 'col'), may hold values from -6 to 6
Outputs:
- activation: bfloat16 [8192, 12288], P(('depth', 'row'), 'col')
- input_grad: bfloat16 [8192, 6144], P(('depth', 'col'), 'row')
- weight_grad: bfloat16 [6144, 12288], P('row', ('col', 'depth'))
All inputs are finite; a program needn't handle non-finite values.
Results may differ from a plain program's by a relative error of at most 0.02.
Values may be sent and summed in bfloat16 or wider, within the bound.
No kernel may reach another device: no remote copies, remote signals or barrier semaphores. Data moves between devices by JAX's collectives and lax.ppermute only.
A program may use at most 128 MiB of HBM per device.

v0:
```python
import jax
import jax.numpy as jnp
from jax import lax
from jax.sharding import PartitionSpec as P

gelu_coef = 0.7978845608028654


def gelu_pair(pre, cotangent):
    inner = gelu_coef * (pre + 0.044715 * pre * pre * pre)
    tangent = jnp.tanh(inner)
    activation = (0.5 * pre * (1.0 + tangent)).astype(jnp.bfloat16)
    slope = 0.5 * (1.0 + tangent) + 0.5 * pre * (1.0 - tangent * tangent) * gelu_coef * (
        1.0 + 3.0 * 0.044715 * pre * pre
    )
    pre_grad = (cotangent.astype(jnp.float32) * slope).astype(jnp.bfloat16)
    return (activation, pre_grad)


def input_part(pre_grad, weight):
    term = lax.dot_general(
        pre_grad, weight, (((1,), (1,)), ((), ())), preferred_element_type=jnp.float32
    )
    return lax.psum_scatter(term.astype(jnp.bfloat16), "col", scatter_dimension=0, tiled=True)


def weight_part(gathered, pre_grad):
    term = lax.dot_general(
        gathered, pre_grad, (((0,), (0,)), ((), ())), preferred_element_type=jnp.float32
    )
    return lax.psum_scatter(term.astype(jnp.bfloat16), "depth", scatter_dimension=1, tiled=True)


def shards(tokens, weight, cotangent):
    gathered = lax.all_gather(tokens, "col", axis=0, tiled=True)
    partial_value = jnp.dot(gathered, weight, preferred_element_type=jnp.float32).astype(
        jnp.bfloat16
    )
    own_rows = cotangent.shape[0]
    pre_whole = lax.psum(partial_value, "row").astype(jnp.float32)
    cot_whole = lax.all_gather(cotangent, "row", axis=0, tiled=True)
    act_whole, pre_grad = gelu_pair(pre_whole, cot_whole)
    start = lax.axis_index("row") * own_rows
    activation = lax.dynamic_slice_in_dim(act_whole, start, own_rows, 0)
    input_grad = input_part(pre_grad, weight)
    weight_grad = weight_part(gathered, pre_grad)
    return (activation, input_grad, weight_grad)


def solution(mesh):
    in_specs = (P(("depth", "col"), "row"), P("row", "col"), P(("depth", "row"), "col"))
    out_specs = (P(("depth", "row"), "col"), P(("depth", "col"), "row"), P("row", ("col", "depth")))
    return jax.shard_map(shards, mesh=mesh, in_specs=in_specs, out_specs=out_specs, check_vma=False)
```

profile of v0, /device:TPU:1, one launch (start us, length us, event | category | flops | bytes accessed | tf_op | source)
XLA Modules:
  0.0 502.4 jit_solution(5226435542829770670)
XLA Ops:
  7.2 0.0 all-gather.3.cloned.1.call-start
  7.2 0.7 all-gather.3.cloned.1.call-update
  7.9 0.0 all-gather.5.cloned.1.call-start
  7.9 0.7 all-gather.5.cloned.1.call-update
  8.6 0.0 all-reduce.2.cloned.1.call-start
  8.7 43.8 %all-gather.3.cloned.1.call-done = bf16[1024,1536]{1,0:T(8,128)(2,1)} async-done(((bf16[256,1536]{1,0:T(8,128)(2,1)}), bf16[1024,1536]{1,0:T(8,128)(2,1)}) %all-gather.3.cloned.1.call-update) | async-done | bytes 3145744 | tf_op jit(solution)/shard_map/all_gather | solution.py:35
  52.5 15.2 %convolution_convert_fusion.1 = bf16[1024,3072]{1,0:T(8,128)(2,1)} fusion(bf16[1024,1536]{1,0:T(8,128)(2,1)} %all-gather.3.cloned.1.call-done, bf16[1536,3072]{1,0:T(8,128)(2,1)} %param.4), kind=kOutput, calls=%fused_computation.17 | convolution fusion | flops 9666822144 | bytes 18874368 | tf_op jit(solution)/shard_map/dot_general | solution.py:36
  67.7 0.0 all-reduce.2.cloned.1.call-update
  67.7 0.0 copy-start.1
  67.7 0.0 reduce-scatter.5.cloned.1.call-start
  67.8 37.4 %all-gather.5.cloned.1.call-done = bf16[1024,3072]{1,0:T(8,128)(2,1)} async-done(((bf16[256,3072]{1,0:T(8,128)(2,1)}), bf16[1024,3072]{1,0:T(8,128)(2,1)}) %all-gather.5.cloned.1.call-update) | async-done | bytes 6291472 | tf_op jit(solution)/shard_map/all_gather | solution.py:41
  105.2 129.0 %all-reduce.2.cloned.1.call-done = bf16[1024,3072]{1,0:T(8,128)(2,1)} async-done(((bf16[1024,3072]{1,0:T(8,128)(2,1)}), bf16[1024,3072]{1,0:T(8,128)(2,1)}) %all-reduce.2.cloned.1.call-update) | async-done | bytes 6291472 | tf_op jit(solution)/shard_map/psum | solution.py:40
  234.2 16.8 %fusion.6 = (bf16[1024,3072]{1,0:T(8,128)(2,1)S(1)}, f32[1024,3072]{1,0:T(8,128)}, f32[1024,3072]{1,0:T(8,128)}) fusion(bf16[1024,3072]{1,0:T(8,128)(2,1)} %all-reduce.2.cloned.1.call-done, bf16[1024,3072]{1,0:T(8,128)(2,1)} %all-gather.5.cloned.1.call-done), kind=kLoop, calls=%fused_computation.13 | loop fusion | flops 66060288 | bytes 44040192 | tf_op jit(solution)/shard_map/convert_element_type | solution.py:16
  250.9 0.0 copy-start
  250.9 2.6 copy-done
  253.5 0.0 copy-done.1
  253.5 12.1 %fusion.8 = bf16[1536,3072]{0,1:T(8,128)(2,1)} fusion(bf16[1024,3072]{1,0:T(8,128)(2,1)S(1)} %get-tuple-element.6, bf16[1024,1536]{1,0:T(8,128)(2,1)S(1)} %copy-done.1), kind=kOutput, calls=%fused_computation.16 | convolution fusion | flops 9668395008 | bytes 18874368 | tf_op jit(solution)/shard_map/dot_general | solution.py:28
  265.6 0.0 reduce-scatter.5.cloned.1.call-update
  265.6 0.2 reduce-scatter.3.cloned.1.call-start
  265.9 15.6 %convolution_convert_fusion.2 = bf16[1024,1536]{1,0:T(8,128)(2,1)} fusion(bf16[1024,3072]{1,0:T(8,128)(2,1)} %copy-done, bf16[1536,3072]{1,0:T(8,128)(2,1)} %param.4), kind=kOutput, calls=%fused_computation.18 | convolution fusion | flops 9665249280 | bytes 18874368 | tf_op jit(solution)/shard_map/dot_general | solution.py:21
  281.4 0.0 reduce-scatter.3.cloned.1.call-update
  281.5 4.5 fusion.9
  286.0 167.7 %reduce-scatter.5.cloned.1.call-done = bf16[1536,384]{0,1:T(8,128)(2,1)} async-done(((bf16[1536,3072]{0,1:T(8,128)(2,1)}), bf16[1536,384]{0,1:T(8,128)(2,1)}) %reduce-scatter.5.cloned.1.call-update) | async-done | bytes 1179664 | tf_op jit(solution)/shard_map/reduce_scatter | solution.py:31
  453.7 2.4 copy.6
  456.1 39.8 %reduce-scatter.3.cloned.1.call-done = bf16[256,1536]{1,0:T(8,128)(2,1)} async-done(((bf16[1024,1536]{1,0:T(8,128)(2,1)}), bf16[256,1536]{1,0:T(8,128)(2,1)}) %reduce-scatter.3.cloned.1.call-update) | async-done | bytes 786448 | tf_op jit(solution)/shard_map/reduce_scatter | solution.py:24
Async XLA Ops:
  7.2 45.3 %all-gather.3.cloned.1.call-start = ((), (), s32[]{:S(2)}) async-start(), calls=%async_computation.2 | async-start | bytes 3932160 | tf_op jit(solution)/shard_map/all_gather | solution.py:35
  7.9 97.3 %all-gather.5.cloned.1.call-start = ((), (), s32[]{:S(2)}) async-start(), calls=%async_computation.4 | async-start | bytes 7864320 | tf_op jit(solution)/shard_map/all_gather | solution.py:41
  8.6 225.5 %all-reduce.2.cloned.1.call-start = ((), (), s32[]{:S(2)}) async-start(), calls=%async_computation.3 | async-start | bytes 12582912 | tf_op jit(solution)/shard_map/psum | solution.py:40
  67.7 185.8 %copy-start.1 = (bf16[1024,1536]{1,0:T(8,128)(2,1)S(1)}, bf16[1024,1536]{1,0:T(8,128)(2,1)}, u32[]{:S(2)}) copy-start(bf16[1024,1536]{1,0:T(8,128)(2,1)} %all-gather.3.cloned.1.call-done) | copy-start | bytes 9437188
  67.7 386.0 %reduce-scatter.5.cloned.1.call-start = ((), (), s32[]{:S(2)}) async-start(), calls=%async_computation.6 | async-start | bytes 10616832 | tf_op jit(solution)/shard_map/reduce_scatter | solution.py:31
  250.9 2.6 copy-start
  265.6 230.2 %reduce-scatter.3.cloned.1.call-start = ((), (), s32[]{:S(2)}) async-start(), calls=%async_computation.5 | async-start | bytes 3932160 | tf_op jit(solution)/shard_map/reduce_scatter | solution.py:24
Sparse Core Ops, SparseCore 0:
  9.7 42.7 all-gather.2
  54.1 50.9 all-gather.4
  107.7 126.4 all-reduce.1
  265.7 187.9 reduce-scatter.4
  456.5 39.2 reduce-scatter.2
where the time goes:
time: 502 us
  waiting for transfers between devices  419 us (83%)
  matrix products  42.9 us (9%)
  other arithmetic  21.3 us (4%)
  between operations  13.8 us (3%)
    reduce_scatter x1, waiting for transfers between devices, weight_part(): lax.psum_scatter(term.astype(jnp.bfloat16), 'depth', scatter_dimension=1,...  168 us
    psum x1, waiting for transfers between devices, shards(): pre_whole = lax.psum(partial_value, 'row').astype(jnp.float32)  129 us
    all_gather x1, waiting for transfers between devices, shards(): gathered = lax.all_gather(tokens, 'col', axis=0, tiled=True)  43.8 us
    reduce_scatter x1, waiting for transfers between devices, input_part(): lax.psum_scatter(term.astype(jnp.bfloat16), 'col', scatter_dimension=0, t...  39.8 us
    all_gather x1, waiting for transfers between devices, shards(): cot_whole = lax.all_gather(cotangent, 'row', axis=0, tiled=True)  37.4 us
    convert_element_type x1, other arithmetic, gelu_pair(): pre_grad = (cotangent.astype(jnp.float32) * slope).astype(jnp.bfloat16)  16.8 us
    dot_general x1, matrix products, input_part(): lax.dot_general(pre_grad, weight, (((1,), (1,)), ((), ())), preferred_ele...  15.6 us
    dot_general x1, matrix products, shards(): jnp.dot(gathered, weight, preferred_element_type=jnp.float32)  15.2 us
  transfers between devices with their start and end apart: 5, of which 5 were waited for; matrix products, arithmetic and copies ran while one was open for 7% of the time, Pallas kernels for 0%

commit v1 on v0

v1 whole, which is shorter than its diff:
```python
import functools

import jax
import jax.numpy as jnp
from jax import lax
from jax.experimental import pallas as pl
from jax.experimental.pallas import tpu as pltpu
from jax.sharding import Mesh
from jax.sharding import PartitionSpec as P

K = 1536
F = 3072
S = 256
CHUNKS = 3
DEPTH = 8
CW = F // CHUNKS
HALF = CW // 2
LANE = 128
gelu_coef = 0.7978845608028654
bf16 = jnp.bfloat16
f32 = jnp.float32
MIB = 1 << 20


def params(mib):
    return pltpu.CompilerParams(vmem_limit_bytes=mib * MIB)


def cost(flops, bytes_accessed, transcendentals=0):
    return pl.CostEstimate(flops=flops, bytes_accessed=bytes_accessed, transcendentals=transcendentals)


def partial_kernel(q_ref, b0, b1, b2, b3, w_ref, send_ref, keep_ref, tk_ref, sems):
    @pl.when(pl.program_id(0) == 0)
    def _():
        q = q_ref[0]
        copies = []
        for m, block in enumerate((b0, b1, b2, b3)):
            slot = pl.multiple_of(jnp.bitwise_xor(q, m) * S, S)
            copies.append(pltpu.make_async_copy(block, tk_ref.at[pl.ds(slot, S)], sems.at[m]))
        for copy in copies:
            copy.start()
        for copy in copies:
            copy.wait()

    w = w_ref[...]
    for k, (ref, at) in ((1, (send_ref, 0)), (3, (send_ref, 1)), (0, (keep_ref, 0)), (2, (keep_ref, 1))):
        term = jnp.dot(tk_ref[k * S:(k + 1) * S, :], w, preferred_element_type=f32)
        ref[at * S:(at + 1) * S, :] = term.astype(bf16)


def block_partials(q, blocks, weight):
    tile = 512
    grid_spec = pltpu.PrefetchScalarGridSpec(
        num_scalar_prefetch=1,
        grid=(F // tile,),
        in_specs=[pl.BlockSpec(memory_space=pl.ANY)] * 4 + [pl.BlockSpec((K, tile), lambda i, q: (0, i))],
        out_specs=[
            pl.BlockSpec((2 * S, tile), lambda i, q: (0, i)),
            pl.BlockSpec((2 * S, tile), lambda i, q: (0, i)),
            pl.BlockSpec((4 * S, K), lambda i, q: (0, 0)),
        ],
        scratch_shapes=[pltpu.SemaphoreType.DMA((4,))],
    )
    return pl.pallas_call(
        partial_kernel,
        grid_spec=grid_spec,
        out_shape=[
            jax.ShapeDtypeStruct((2 * S, F), bf16),
            jax.ShapeDtypeStruct((2 * S, F), bf16),
            jax.ShapeDtypeStruct((4 * S, K), bf16),
        ],
        compiler_params=params(40),
        cost_estimate=cost(2 * 4 * S * K * F, 21 * MIB),
        name="block_partials",
    )(q, *blocks, weight)


def gelu_kernel(xl_ref, own_ref, core_ref, far_ref, cot_ref, act_ref, *outs):
    xl = xl_ref[0]
    pgs, halves = outs[:CHUNKS], outs[CHUNKS:]
    pieces = {}
    for d in range(DEPTH):
        for f in range(CHUNKS):
            at = slice((d * CHUNKS + f) * LANE, (d * CHUNKS + f + 1) * LANE)
            pre = own_ref[:, at].astype(f32) + core_ref[:, at].astype(f32) + far_ref[:, at].astype(f32)
            inner = gelu_coef * (pre + 0.044715 * pre * pre * pre)
            tangent = jnp.tanh(inner)
            act_ref[:, at] = (0.5 * pre * (1.0 + tangent)).astype(bf16)
            slope = 0.5 * (1.0 + tangent) + 0.5 * pre * (1.0 - tangent * tangent) * gelu_coef * (
                1.0 + 3.0 * 0.044715 * pre * pre
            )
            grad = (cot_ref[:, at].astype(f32) * slope).astype(bf16)
            pgs[f][:, d * LANE:(d + 1) * LANE] = grad
            pieces[f, d % 2] = grad
            if d % 2:
                z = d // 2
                halves[f][:, z * LANE:(z + 1) * LANE] = jnp.where(xl == 0, pieces[f, 1], pieces[f, 0])


def gelu_pair(xl, keep, core, far, cot):
    rows = 64
    grid_spec = pltpu.PrefetchScalarGridSpec(
        num_scalar_prefetch=1,
        grid=(S // rows,),
        in_specs=[pl.BlockSpec((rows, F), lambda i, x: (i, 0))] * 4,
        out_specs=[pl.BlockSpec((rows, F), lambda i, x: (i, 0))]
        + [pl.BlockSpec((rows, CW), lambda i, x: (i, 0))] * CHUNKS
        + [pl.BlockSpec((rows, HALF), lambda i, x: (i, 0))] * CHUNKS,
    )
    outs = pl.pallas_call(
        gelu_kernel,
        grid_spec=grid_spec,
        out_shape=[jax.ShapeDtypeStruct((S, F), bf16)]
        + [jax.ShapeDtypeStruct((S, CW), bf16)] * CHUNKS
        + [jax.ShapeDtypeStruct((S, HALF), bf16)] * CHUNKS,
        compiler_params=params(40),
        cost_estimate=cost(30 * S * F, 10 * MIB, S * F),
        name="gelu_pair",
    )(xl, keep, core, far, cot)
    return outs[0], outs[1:1 + CHUNKS], outs[1 + CHUNKS:]


def weight_kernel(ids_ref, tk_ref, tx_ref, *refs):
    own, other, out_ref, pg = refs[:4], refs[4:8], refs[8], refs[9]

    @pl.when(pl.program_id(0) == 0)
    def _():
        xl, r = ids_ref[0], ids_ref[1]
        for k in range(4):
            for z in range(4):
                at = pl.multiple_of((2 * z + xl) * LANE, LANE)
                pg[k * S:(k + 1) * S, z * LANE:(z + 1) * LANE] = own[k][:, pl.ds(at, LANE)]
            slot = pl.multiple_of(4 * S + jnp.bitwise_xor(r, k) * S, S)
            pg[pl.ds(slot, S), :] = other[k][...]

    total = jnp.dot(tk_ref[...], pg[:4 * S, :], preferred_element_type=f32)
    total += jnp.dot(tx_ref[...], pg[4 * S:, :], preferred_element_type=f32)
    for z in range(4):
        out_ref[z] = total[:, z * LANE:(z + 1) * LANE].astype(bf16)


def weight_part(ids, tk, tx, own, other):
    rows = 512
    grid_spec = pltpu.PrefetchScalarGridSpec(
        num_scalar_prefetch=1,
        grid=(K // rows,),
        in_specs=[pl.BlockSpec((rows, 4 * S), lambda i, x: (i, 0))] * 2
        + [pl.BlockSpec((S, CW), lambda i, x: (0, 0))] * 4
        + [pl.BlockSpec((S, HALF), lambda i, x: (0, 0))] * 4,
        out_specs=pl.BlockSpec((4, rows, LANE), lambda i, x: (0, i, 0)),
        scratch_shapes=[pltpu.VMEM((8 * S, HALF), bf16)],
    )
    return pl.pallas_call(
        weight_kernel,
        grid_spec=grid_spec,
        out_shape=jax.ShapeDtypeStruct((4, K, LANE), bf16),
        compiler_params=params(40),
        cost_estimate=cost(2 * 8 * S * K * HALF, 11 * MIB),
        name="weight_part",
    )(ids, tk, tx, *own, *other)


def input_kernel(q_ref, *refs):
    grads, w_ref, outs, lhs, sems = refs[:12], refs[12], refs[13:17], refs[17], refs[18]

    @pl.when(pl.program_id(0) == 0)
    def _():
        q = q_ref[0]
        copies = []
        for k in range(4):
            slot = pl.multiple_of(jnp.bitwise_xor(q, k) * S, S)
            for f in range(CHUNKS):
                copies.append(
                    pltpu.make_async_copy(
                        grads[k * CHUNKS + f],
                        lhs.at[pl.ds(slot, S), pl.ds(f * CW, CW)],
                        sems.at[k * CHUNKS + f],
                    )
                )
        for copy in copies:
            copy.start()
        for copy in copies:
            copy.wait()

    w = w_ref[...]
    for m in range(4):
        outs[m][...] = jnp.dot(lhs[m * S:(m + 1) * S, :], w, preferred_element_type=f32).astype(bf16)


def input_part(q, grads, weight_t):
    tile = 512
    grid_spec = pltpu.PrefetchScalarGridSpec(
        num_scalar_prefetch=1,
        grid=(K // tile,),
        in_specs=[pl.BlockSpec(memory_space=pl.ANY)] * 12 + [pl.BlockSpec((F, tile), lambda i, q: (0, i))],
        out_specs=[pl.BlockSpec((S, tile), lambda i, q: (0, i))] * 4,
        scratch_shapes=[pltpu.VMEM((4 * S, F), bf16), pltpu.SemaphoreType.DMA((12,))],
    )
    return pl.pallas_call(
        input_kernel,
        grid_spec=grid_spec,
        out_shape=[jax.ShapeDtypeStruct((S, K), bf16)] * 4,
        compiler_params=params(40),
        cost_estimate=cost(2 * 4 * S * K * F, 18 * MIB),
        name="input_part",
    )(q, *grads, weight_t)


def swap(value, axis, mask):
    n = lax.axis_size(axis)
    return lax.ppermute(value, axis, [(i, i ^ mask) for i in range(n)])


def shards(tokens, weight, cotangent):
    xh, core, y, xl = (lax.axis_index(a) for a in ("xh", "core", "y", "xl"))
    r = 2 * xh + core
    q = jnp.bitwise_xor(r, y).astype(jnp.int32).reshape(1)
    ids = jnp.stack([xl, r]).astype(jnp.int32)

    blocks = [tokens] + [swap(tokens, "y", m) for m in (1, 2, 3)]
    other_tokens = lax.all_gather(swap(tokens, "xl", 1), "y", axis=0, tiled=True)
    weight_t = weight.reshape(K, DEPTH, CHUNKS, LANE).transpose(2, 1, 3, 0).reshape(F, K)

    send, keep, tk = block_partials(q, blocks, weight)
    came = swap(send, "core", 1)
    second = (keep[S:].astype(f32) + came[S:].astype(f32)).astype(bf16)
    far = swap(second, "xh", 1)
    activation, grads, halves = gelu_pair(ids[:1], keep, came, far, cotangent)

    tk_t = tk.T
    tx_t = other_tokens.T
    own = []
    sums = []
    for f in range(CHUNKS):
        pair = swap(grads[f], "xh", 1)
        own.append([grads[f], swap(grads[f], "core", 1), pair, swap(pair, "core", 1)])
        near = swap(halves[f], "xl", 1)
        cross = lax.ppermute(halves[f], ("xh", "xl"), [(i, 3 - i) for i in range(4)])
        other = [near, swap(near, "core", 1), cross, swap(cross, "core", 1)]
        part = weight_part(ids, tk_t, tx_t, own[f], other)
        sums.append(lax.psum_scatter(part, "z", scatter_dimension=0, tiled=True)[0])
    weight_grad = jnp.concatenate(sums, axis=1)

    dx = input_part(q, [own[f][k] for k in range(4) for f in range(CHUNKS)], weight_t)
    total = dx[0].astype(f32)
    for m in (1, 2, 3):
        total += swap(dx[m], "y", m).astype(f32)
    return activation, total.astype(bf16), weight_grad


def solution(mesh):
    split = Mesh(mesh.devices.reshape(2, 2, 4, 4, 2), ("xh", "core", "y", "z", "xl"))
    hidden = P(("z", "xl", "xh", "core"), "y")
    tokens = P(("z", "xl", "y"), ("xh", "core"))
    return jax.shard_map(
        shards,
        mesh=split,
        in_specs=(tokens, P(("xh", "core"), "y"), hidden),
        out_specs=(hidden, tokens, P(("xh", "core"), ("y", "z", "xl"))),
        check_vma=False,
    )
```

time: 502 us -> 333 us (0.66)
  waiting for transfers between devices: 419 us -> 165 us
  local copies, waits for them, and re-layouts: 4.98 us -> 57.3 us
  Pallas kernels: 0 us -> 48.5 us
  matrix products: 42.9 us -> 0 us
  starting transfers between devices: 0.38 us -> 39.1 us
  other arithmetic: 21.3 us -> 6.88 us
    reduce_scatter x2 -> x3, waiting for transfers between devices: 208 us -> 0.01 us  [shards(): sums.append(lax.psum_scatter(part, 'z', scatter_dimension=0, tiled=True)[0])]
    ppermute x0 -> x30, waiting for transfers between devices: none -> 165 us  [the longest x27 154 us: swap(): return lax.ppermute(value, axis, [(i, i ^ mask) for i in range(n)])]
    psum x1 -> x0, waiting for transfers between devices: 129 us -> none  [shards(): pre_whole = lax.psum(partial_value, 'row').astype(jnp.float32)]
    all_gather x2 -> x1, waiting for transfers between devices: 81.2 us -> 0.02 us  [shards(): lax.all_gather(swap(tokens, 'xl', 1), 'y', axis=0, tiled=True)]
    pallas_call x0 -> x6, Pallas kernels: none -> 48.5 us  [the longest x3 16.2 us: weight_part(): pl.pallas_call(weight_kernel, grid_spec=grid_spec, out_shape=jax.ShapeDty...]
    dot_general x3 -> x0, matrix products: 42.9 us -> none  [the longest x1 15.6 us: input_part(): lax.dot_general(pre_grad, weight, (((1,), (1,)), ((), ())), preferred_ele...]
    unnamed x5 -> x70, local copies, waits for them, and re-layouts: 4.98 us -> 45.7 us
    ppermute x0 -> x30, starting transfers between devices: none -> 39 us  [the longest x27 34.5 us: swap(): return lax.ppermute(value, axis, [(i, i ^ mask) for i in range(n)])]
  transfers between devices with their start and end apart: 5 -> 34, of which waited for: 5 -> 16; matrix products, arithmetic and copies ran while one was open for 7% -> 9% of each run, Pallas kernels for 0% -> 9%
where the time goes in v1:
time: 333 us; the launch traced here: 331 us
  waiting for transfers between devices  165 us (50%)
  local copies, waits for them, and re-layouts  57.3 us (17%)
  Pallas kernels  48.5 us (15%)
  starting transfers between devices  39.1 us (12%)
  between operations  14 us (4%)
  other arithmetic  6.88 us (2%)
    ppermute x27, waiting for transfers between devices, swap(): return lax.ppermute(value, axis, [(i, i ^ mask) for i in range(n)])  154 us
    unnamed x70, local copies, waits for them, and re-layouts  45.7 us
    ppermute x27, starting transfers between devices, swap(): return lax.ppermute(value, axis, [(i, i ^ mask) for i in range(n)])  34.5 us
    pallas_call x3, Pallas kernels, weight_part(): pl.pallas_call(weight_kernel, grid_spec=grid_spec, out_shape=jax.ShapeDty...  16.2 us
    pallas_call x1, Pallas kernels, input_part(): pl.pallas_call(input_kernel, grid_spec=grid_spec, out_shape=[jax.ShapeDty...  14.3 us
    pallas_call x1, Pallas kernels, block_partials(): pl.pallas_call(partial_kernel, grid_spec=grid_spec, out_shape=[jax.ShapeD...  12.7 us
    ppermute x3, waiting for transfers between devices, shards(): lax.ppermute(halves[f], ('xh', 'xl'), [(i, 3 - i) for i in range(4)])  11.7 us
    transpose x1, local copies, waits for them, and re-layouts, shards(): weight.reshape(K, DEPTH, CHUNKS, LANE).transpose(2, 1, 3, 0).reshape(F, K)  8.43 us
  transfers between devices with their start and end apart: 34, of which 16 were waited for; matrix products, arithmetic and copies ran while one was open for 9% of the time, Pallas kernels for 9%

profile of v1, /device:TPU:1, one launch (start us, length us, event | category | flops | bytes accessed | tf_op | source)
XLA Modules:
  0.0 331.3 jit_solution(16105625778361023001)
XLA Ops:
  7.2 3.6 %collective-permute-start.2 = (bf16[256,1536]{1,0:T(8,128)(2,1)}, bf16[256,1536]{1,0:T(8,128)(2,1)S(1)}, u32[]{:S(2)}, u32[]{:S(2)}) collective-permute-start(bf16[256,1536]{1,0:T(8,128)(2,1)} %b0.1), channel_id=1, source_target_pairs={{0,24},{8,16},{16,8},{24,0},{1,25},{9,17},{17,9},{25,1},{2,26},{10... | collective-permute-start | bytes 2359304 | tf_op jit(solution)/shard_map/ppermute | solution.py:212
  11.5 33.5 %collective-permute-done.2.b3 = bf16[256,1536]{1,0:T(8,128)(2,1)S(1)} collective-permute-done((bf16[256,1536]{1,0:T(8,128)(2,1)}, bf16[256,1536]{1,0:T(8,128)(2,1)S(1)}, u32[]{:S(2)}, u32[]{:S(2)}) %collective-permute-start.2) | collective-permute-done | bytes 786464 | tf_op jit(solution)/shard_map/ppermute | solution.py:212
  45.0 0.9 copy-done.9
  45.9 0.9 copy-done.11
  46.8 0.9 copy-done.13
  47.7 1.1 copy-done.5
  48.8 1.1 copy-done.10
  50.0 1.1 copy-done.12
  51.1 1.1 copy-done.14
  52.2 12.7 %block_partials.1 = (bf16[512,3072]{1,0:T(8,128)(2,1)}, bf16[512,3072]{1,0:T(8,128)(2,1)S(1)}, bf16[1024,1536]{1,0:T(8,128)(2,1)S(1)}) custom-call(s32[1]{0:T(128)} %bitcast.1.q_ref, bf16[256,1536]{1,0:T(8,128)(2,1)S(1)} %copy-done.5, bf16[256,1536]{1,0:T(8,128)(2,1)S(1)} %copy-done.14, bf16[256,1536]{1,0:T(8,128)(2,1)S(1)} %copy-done.12, ...), custom_call_target="tpu_custom_call" | custom-call | flops 9663676416 | bytes 22020096 | tf_op jit(solution)/shard_map/block_partials/pallas_call | solution.py:65
  64.9 1.7 copy-done
  66.6 1.4 collective-permute-start.3
  68.0 2.3 copy.12
  70.3 1.2 collective-permute-start.17
  71.5 18.3 %collective-permute-done.17 = bf16[256,1536]{0,1:T(8,128)(2,1)} collective-permute-done((bf16[256,1536]{0,1:T(8,128)(2,1)}, bf16[256,1536]{0,1:T(8,128)(2,1)}, u32[]{:S(2)}, u32[]{:S(2)}) %collective-permute-start.17) | collective-permute-done | bytes 786464 | tf_op jit(solution)/shard_map/ppermute | solution.py:212
  89.8 3.1 add_convert_fusion
  93.0 2.7 collective-permute-start.4
  95.7 34.2 %collective-permute-done.4.far_ref = bf16[256,3072]{1,0:T(8,128)(2,1)} collective-permute-done((bf16[256,3072]{1,0:T(8,128)(2,1)}, bf16[256,3072]{1,0:T(8,128)(2,1)}, u32[]{:S(2)}, u32[]{:S(2)}) %collective-permute-start.4) | collective-permute-done | bytes 1572896 | tf_op jit(solution)/shard_map/ppermute | solution.py:212
  129.9 1.4 copy-done.1
  131.3 5.3 %gelu_pair.1 = (bf16[256,3072]{1,0:T(8,128)(2,1)}, bf16[256,1024]{1,0:T(8,128)(2,1)}, bf16[256,1024]{1,0:T(8,128)(2,1)S(1)}, bf16[256,1024]{1,0:T(8,128)(2,1)S(1...) custom-call(s32[1]{0:T(128)} %bitcast.xl_ref, ...), custom_call_target="tpu_custom_call" | custom-call | flops 23592960 | bytes 10485760 | tf_op jit(solution)/shard_map/gelu_pair/pallas_call | solution.py:111
  139.0 2.7 collective-permute-start.8
  141.7 0.9 collective-permute-start.20
  142.6 2.2 collective-permute-start.5
  144.8 7.8 %collective-permute-done.8.refs_6_.refs_2_ = bf16[256,1024]{1,0:T(8,128)(2,1)} collective-permute-done((bf16[256,1024]{1,0:T(8,128)(2,1)}, bf16[256,1024]{1,0:T(8,128)(2,1)}, u32[]{:S(2)}, u32[]{:S(2)}) %collective-permute-start.8) | collective-permute-done | bytes 524320 | tf_op jit(solution)/shard_map/ppermute | solution.py:212
  152.6 4.8 %collective-permute-start.11 = (bf16[256,1024]{1,0:T(8,128)(2,1)}, bf16[256,1024]{1,0:T(8,128)(2,1)}, u32[]{:S(2)}, u32[]{:S(2)}) collective-permute-start(bf16[256,1024]{1,0:T(8,128)(2,1)} %collective-permute-done.8.refs_6_.refs_2_), channel_id=1, source_target_pairs={{0,32},{32,0},{1,33},{33,1},{2,34},{34,2},{3,35},{35,3},{4,36},{36... | collective-permute-start | bytes 1572872 | tf_op jit(solution)/shard_map/ppermute | solution.py:212
  157.4 2.9 collective-permute-done.20.refs_6_
  160.9 3.2 copy.11
  164.2 1.9 copy-done.6
  166.1 6.7 %weight_part.3 = bf16[4,1536,128]{2,1,0:T(8,128)(2,1)S(1)} custom-call(s32[2]{0:T(128)S(1)} %pad_add_fusion.ids_ref, bf16[1536,1024]{1,0:T(8,128)(2,1)S(1)} %bitcast.12, bf16[1536,1024]{1,0:T(8,128)(2,1)S(1)} %bitcast.15, bf16[256,1024]{1,0:T(8,128)(2,1)} %get-tuple-element.20.refs_0_, bf16[256,1024]{1,0:T(8,128)(2,1)} %collective-permute-done.5.refs_3_.refs_1_, ...), custom_call_target="tpu_custom_call" | custom-call | flops 3221225472 | bytes 11534336 | tf_op jit(solution)/shard_map/weight_part/pallas_call | solution.py:154
  172.8 1.1 copy-done.2
  174.0 1.8 collective-permute-start.9
  175.8 1.8 collective-permute-start.24
  177.6 1.0 collective-permute-start.6
  178.6 10.3 %collective-permute-done.9.refs_7_.refs_2_ = bf16[256,1024]{1,0:T(8,128)(2,1)S(1)} collective-permute-done((bf16[256,1024]{1,0:T(8,128)(2,1)}, bf16[256,1024]{1,0:T(8,128)(2,1)S(1)}, u32[]{:S(2)}, u32[]{:S(2)}) %collective-permute-start.9) | collective-permute-done | bytes 524320 | tf_op jit(solution)/shard_map/ppermute | solution.py:212
  188.9 2.0 collective-permute-start.12
  191.0 4.4 %collective-permute-done.24.refs_6_ = bf16[256,512]{1,0:T(8,128)(2,1)S(1)} collective-permute-done((bf16[256,512]{1,0:T(8,128)(2,1)}, bf16[256,512]{1,0:T(8,128)(2,1)S(1)}, u32[]{:S(2)}, u32[]{:S(2)}) %collective-permute-start.24) | collective-permute-done | bytes 262176 | tf_op jit(solution)/shard_map/ppermute | solution.py:239
  195.9 1.0 collective-permute-done.25.refs_7_
  197.3 1.9 copy-done.7
  199.2 1.1 copy-done.16
  200.3 4.8 %weight_part.4 = bf16[4,1536,128]{2,1,0:T(8,128)(2,1)S(1)} custom-call(s32[2]{0:T(128)S(1)} %pad_add_fusion.ids_ref, bf16[1536,1024]{1,0:T(8,128)(2,1)S(1)} %bitcast.13, bf16[1536,1024]{1,0:T(8,128)(2,1)S(1)} %bitcast.16, bf16[256,1024]{1,0:T(8,128)(2,1)S(1)} %copy-done.16, bf16[256,1024]{1,0:T(8,128)(2,1)S(1)} %collective-permute-done.6.refs_4_.refs_1_, ...), custom_call_target="tpu_custom_call" | custom-call | flops 3221225472 | bytes 11534336 | tf_op jit(solution)/shard_map/weight_part/pallas_call | solution.py:154
  205.1 1.1 copy-done.3
  206.2 0.8 copy-done.21
  208.7 1.8 collective-permute-start.10
  210.5 1.8 collective-permute-start.28
  212.3 0.9 collective-permute-start.7
  213.2 10.5 %collective-permute-done.10.refs_8_.refs_2_ = bf16[256,1024]{1,0:T(8,128)(2,1)S(1)} collective-permute-done((bf16[256,1024]{1,0:T(8,128)(2,1)}, bf16[256,1024]{1,0:T(8,128)(2,1)S(1)}, u32[]{:S(2)}, u32[]{:S(2)}) %collective-permute-start.10) | collective-permute-done | bytes 524320 | tf_op jit(solution)/shard_map/ppermute | solution.py:212
  223.7 1.9 collective-permute-start.13
  225.6 4.4 %collective-permute-done.28.refs_6_ = bf16[256,512]{1,0:T(8,128)(2,1)S(1)} collective-permute-done((bf16[256,512]{1,0:T(8,128)(2,1)S(1)}, bf16[256,512]{1,0:T(8,128)(2,1)S(1)}, u32[]{:S(2)}, u32[]{:S(2)}) %collective-permute-start.28) | collective-permute-done | bytes 262176 | tf_op jit(solution)/shard_map/ppermute | solution.py:239
  230.6 1.0 collective-permute-done.29.refs_7_
  232.0 1.9 copy-done.8
  233.9 1.1 copy-done.19
  235.0 4.8 %weight_part.5 = bf16[4,1536,128]{2,1,0:T(8,128)(2,1)S(1)} custom-call(s32[2]{0:T(128)S(1)} %pad_add_fusion.ids_ref, bf16[1536,1024]{1,0:T(8,128)(2,1)S(1)} %bitcast.14, bf16[1536,1024]{1,0:T(8,128)(2,1)S(1)} %bitcast.17, bf16[256,1024]{1,0:T(8,128)(2,1)S(1)} %copy-done.19, bf16[256,1024]{1,0:T(8,128)(2,1)S(1)} %collective-permute-done.7.refs_5_.refs_1_, ...), custom_call_target="tpu_custom_call" | custom-call | flops 3221225472 | bytes 11534336 | tf_op jit(solution)/shard_map/weight_part/pallas_call | solution.py:154
  239.8 1.1 copy-done.4
  243.3 12.7 %copy.9 = bf16[1536,3072]{0,1:T(8,128)(2,1)} copy(bf16[1536,3072]{1,0:T(8,128)(2,1)} %w_ref.1) | data formatting | bytes 18874368 | tf_op args[1]
  256.1 8.4 %copy.10 = bf16[3,8,128,1536]{3,2,1,0:T(8,128)(2,1)} copy(bf16[3,8,128,1536]{3,2,0,1:T(8,128)(2,1)} %bitcast.18) | data formatting | bytes 18874368 | tf_op jit(solution)/shard_map/transpose | solution.py:223
  264.5 1.0 copy-done.30
  265.6 1.0 copy-done.32
  266.6 14.3 %input_part.1 = (bf16[256,1536]{1,0:T(8,128)(2,1)S(1)}, bf16[256,1536]{1,0:T(8,128)(2,1)S(1)}, bf16[256,1536]{1,0:T(8,128)(2,1)S(1)}, bf16[256,1536]{1,0:T(8,128)(2,1)S(1)}) custom-call(s32[1]{0:T(128)} %bitcast.1.q_ref, bf16[256,1024]{1,0:T(8,128)(2,1)} %get-tuple-element.20.refs_0_, bf16[256,1024]{1,0:T(8,128)(2,1)S(1)} %copy-done.17, ...), custom_call_target="tpu_custom_call" | custom-call | flops 9663676416 | bytes 18874368 | tf_op jit(solution)/shard_map/input_part/pallas_call | solution.py:200
  281.0 3.9 %collective-permute-start.15 = (bf16[256,1536]{1,0:T(8,128)(2,1)S(1)}, bf16[256,1536]{1,0:T(8,128)(2,1)S(1)}, u32[]{:S(2)}, u32[]{:S(2)}) collective-permute-start(bf16[256,1536]{1,0:T(8,128)(2,1)S(1)} %get-tuple-element.25), channel_id=1, source_target_pairs={{0,16},{8,24},{16,0},{24,8},{1,17},{9,25},{17,1},{25,9},{2,18},{10... | collective-permute-start | bytes 2359304 | tf_op jit(solution)/shard_map/ppermute | solution.py:212
  284.9 14.9 %collective-permute-done.14 = bf16[256,1536]{1,0:T(8,128)(2,1)S(1)} collective-permute-done((bf16[256,1536]{1,0:T(8,128)(2,1)S(1)}, bf16[256,1536]{1,0:T(8,128)(2,1)S(1)}, u32[]{:S(2)}, u32[]{:S(2)}) %collective-permute-start.14) | collective-permute-done | bytes 786464 | tf_op jit(solution)/shard_map/ppermute | solution.py:212
  299.8 19.3 %collective-permute-done.15 = bf16[256,1536]{1,0:T(8,128)(2,1)S(1)} collective-permute-done((bf16[256,1536]{1,0:T(8,128)(2,1)S(1)}, bf16[256,1536]{1,0:T(8,128)(2,1)S(1)}, u32[]{:S(2)}, u32[]{:S(2)}) %collective-permute-start.15) | collective-permute-done | bytes 786464 | tf_op jit(solution)/shard_map/ppermute | solution.py:212
  319.1 2.0 collective-permute-done.16
  321.1 1.3 add_convert_fusion.1
  322.4 2.4 pad_maximum_fusion
  (90 shorter events, 9.9 us)
Async XLA Ops:
  7.2 157.0 %all-gather.2.cloned.1.call-start = ((), (), s32[]{:S(2)}) async-start(), calls=%async_computation.3 | async-start | bytes 3932160 | tf_op jit(solution)/shard_map/all_gather | solution.py:222
  7.2 37.8 %collective-permute-start.2 = (bf16[256,1536]{1,0:T(8,128)(2,1)}, bf16[256,1536]{1,0:T(8,128)(2,1)S(1)}, u32[]{:S(2)}, u32[]{:S(2)}) collective-permute-start(bf16[256,1536]{1,0:T(8,128)(2,1)} %b0.1), channel_id=1, source_target_pairs={{0,24},{8,16},{16,8},{24,0},{1,25},{9,17},{17,9},{25,1},{2,26},{10... | collective-permute-start | bytes 2359304 | tf_op jit(solution)/shard_map/ppermute | solution.py:212
  10.9 35.1 %collective-permute-start.1 = (bf16[256,1536]{1,0:T(8,128)(2,1)}, bf16[256,1536]{1,0:T(8,128)(2,1)S(1)}, u32[]{:S(2)}, u32[]{:S(2)}) collective-permute-start(bf16[256,1536]{1,0:T(8,128)(2,1)} %b0.1), channel_id=1, source_target_pairs={{0,16},{8,24},{16,0},{24,8},{1,17},{9,25},{17,1},{25,9},{2,18},{10... | collective-permute-start | bytes 2359304 | tf_op jit(solution)/shard_map/ppermute | solution.py:212
  11.2 35.6 %collective-permute-start = (bf16[256,1536]{1,0:T(8,128)(2,1)}, bf16[256,1536]{1,0:T(8,128)(2,1)S(1)}, u32[]{:S(2)}, u32[]{:S(2)}) collective-permute-start(bf16[256,1536]{1,0:T(8,128)(2,1)} %b0.1), channel_id=1, source_target_pairs={{0,8},{8,0},{16,24},{24,16},{1,9},{9,1},{17,25},{25,17},{2,10},{10... | collective-permute-start | bytes 2359304 | tf_op jit(solution)/shard_map/ppermute | solution.py:212
  45.0 0.9 copy-start.9
  45.9 0.9 copy-start.11
  46.8 0.9 copy-start.13
  47.7 1.1 copy-start.5
  48.8 1.1 copy-start.10
  50.0 1.1 copy-start.12
  51.1 1.1 copy-start.14
  64.9 1.7 copy-start
  66.6 23.2 %collective-permute-start.3 = (bf16[512,3072]{1,0:T(8,128)(2,1)}, bf16[512,3072]{1,0:T(8,128)(2,1)}, u32[]{:S(2)}, u32[]{:S(2)}) collective-permute-start(bf16[512,3072]{1,0:T(8,128)(2,1)} %get-tuple-element.18), channel_id=1, source_target_pairs={{0,32},{32,0},{1,33},{33,1},{2,34},{34,2},{3,35},{35,3},{4,36},{36... | collective-permute-start | bytes 9437192 | tf_op jit(solution)/shard_map/ppermute | solution.py:212
  70.3 19.5 %collective-permute-start.17 = (bf16[256,1536]{0,1:T(8,128)(2,1)}, bf16[256,1536]{0,1:T(8,128)(2,1)}, u32[]{:S(2)}, u32[]{:S(2)}) collective-permute-start(bf16[256,1536]{0,1:T(8,128)(2,1)} %copy.12), channel_id=1, source_target_pairs={{0,1},{1,0},{2,3},{3,2},{4,5},{5,4},{6,7},{7,6},{8,9},{9,8},{10,11... | collective-permute-start | bytes 2359304 | tf_op jit(solution)/shard_map/ppermute | solution.py:212
  89.8 232.6 %reduce-scatter.4.cloned.1.call-start = ((), (), s32[]{:S(2)}) async-start(), calls=%async_computation.4 | async-start | bytes 1966080 | tf_op jit(solution)/shard_map/reduce_scatter | solution.py:242
  93.0 37.0 %collective-permute-start.4 = (bf16[256,3072]{1,0:T(8,128)(2,1)}, bf16[256,3072]{1,0:T(8,128)(2,1)}, u32[]{:S(2)}, u32[]{:S(2)}) collective-permute-start(bf16[256,3072]{1,0:T(8,128)(2,1)} %add_convert_fusion), channel_id=1, source_target_pairs={{0,64},{64,0},{1,65},{65,1},{2,66},{66,2},{3,67},{67,3},{4,68},{68... | collective-permute-start | bytes 4718600 | tf_op jit(solution)/shard_map/ppermute | solution.py:212
  129.9 1.4 copy-start.1
  136.6 0.8 copy-start.15
  137.4 0.8 copy-start.18
  139.0 13.6 %collective-permute-start.8 = (bf16[256,1024]{1,0:T(8,128)(2,1)}, bf16[256,1024]{1,0:T(8,128)(2,1)}, u32[]{:S(2)}, u32[]{:S(2)}) collective-permute-start(bf16[256,1024]{1,0:T(8,128)(2,1)} %get-tuple-element.20.refs_0_), channel_id=1, source_target_pairs={{0,64},{64,0},{1,65},{65,1},{2,66},{66,2},{3,67},{67,3},{4,68},{68... | collective-permute-start | bytes 1572872 | tf_op jit(solution)/shard_map/ppermute | solution.py:212
  141.7 18.5 %collective-permute-start.20 = (bf16[256,512]{1,0:T(8,128)(2,1)S(1)}, bf16[256,512]{1,0:T(8,128)(2,1)}, u32[]{:S(2)}, u32[]{:S(2)}) collective-permute-start(bf16[256,512]{1,0:T(8,128)(2,1)S(1)} %get-tuple-element.28), channel_id=1, source_target_pairs={{0,65},{1,64},{64,1},{65,0},{2,67},{3,66},{66,3},{67,2},{4,69},{5,... | collective-permute-start | bytes 786440 | tf_op jit(solution)/shard_map/ppermute | solution.py:239
  142.6 21.6 %collective-permute-start.5 = (bf16[256,1024]{1,0:T(8,128)(2,1)}, bf16[256,1024]{1,0:T(8,128)(2,1)}, u32[]{:S(2)}, u32[]{:S(2)}) collective-permute-start(bf16[256,1024]{1,0:T(8,128)(2,1)} %get-tuple-element.20.refs_0_), channel_id=1, source_target_pairs={{0,32},{32,0},{1,33},{33,1},{2,34},{34,2},{3,35},{35,3},{4,36},{36... | collective-permute-start | bytes 1572872 | tf_op jit(solution)/shard_map/ppermute | solution.py:212
  144.8 15.9 %collective-permute-start.18 = (bf16[256,512]{1,0:T(8,128)(2,1)S(1)}, bf16[256,512]{1,0:T(8,128)(2,1)}, u32[]{:S(2)}, u32[]{:S(2)}) collective-permute-start(bf16[256,512]{1,0:T(8,128)(2,1)S(1)} %get-tuple-element.28), channel_id=1, source_target_pairs={{0,1},{1,0},{2,3},{3,2},{4,5},{5,4},{6,7},{7,6},{8,9},{9,8},{10,11... | collective-permute-start | bytes 786440 | tf_op jit(solution)/shard_map/ppermute | solution.py:212
  152.6 11.6 %collective-permute-start.11 = (bf16[256,1024]{1,0:T(8,128)(2,1)}, bf16[256,1024]{1,0:T(8,128)(2,1)}, u32[]{:S(2)}, u32[]{:S(2)}) collective-permute-start(bf16[256,1024]{1,0:T(8,128)(2,1)} %collective-permute-done.8.refs_6_.refs_2_), channel_id=1, source_target_pairs={{0,32},{32,0},{1,33},{33,1},{2,34},{34,2},{3,35},{35,3},{4,36},{36... | collective-permute-start | bytes 1572872 | tf_op jit(solution)/shard_map/ppermute | solution.py:212
  160.2 3.9 %collective-permute-start.21 = (bf16[256,512]{1,0:T(8,128)(2,1)}, bf16[256,512]{1,0:T(8,128)(2,1)}, u32[]{:S(2)}, u32[]{:S(2)}) collective-permute-start(bf16[256,512]{1,0:T(8,128)(2,1)} %collective-permute-done.20.refs_6_), channel_id=1, source_target_pairs={{0,32},{32,0},{1,33},{33,1},{2,34},{34,2},{3,35},{35,3},{4,36},{36... | collective-permute-start | bytes 786440 | tf_op jit(solution)/shard_map/ppermute | solution.py:212
  160.7 3.4 %collective-permute-start.19 = (bf16[256,512]{1,0:T(8,128)(2,1)}, bf16[256,512]{1,0:T(8,128)(2,1)}, u32[]{:S(2)}, u32[]{:S(2)}) collective-permute-start(bf16[256,512]{1,0:T(8,128)(2,1)} %collective-permute-done.18.refs_4_), channel_id=1, source_target_pairs={{0,32},{32,0},{1,33},{33,1},{2,34},{34,2},{3,35},{35,3},{4,36},{36... | collective-permute-start | bytes 786440 | tf_op jit(solution)/shard_map/ppermute | solution.py:212
  164.2 1.9 copy-start.6
  172.7 1.2 copy-start.2
  173.9 148.5 %reduce-scatter.6.cloned.1.call-start = ((), (), s32[]{:S(2)}) async-start(), calls=%async_computation.5 | async-start | bytes 1966080 | tf_op jit(solution)/shard_map/reduce_scatter | solution.py:242
  174.0 15.0 %collective-permute-start.9 = (bf16[256,1024]{1,0:T(8,128)(2,1)}, bf16[256,1024]{1,0:T(8,128)(2,1)S(1)}, u32[]{:S(2)}, u32[]{:S(2)}) collective-permute-start(bf16[256,1024]{1,0:T(8,128)(2,1)} %copy-done.15), channel_id=1, source_target_pairs={{0,64},{64,0},{1,65},{65,1},{2,66},{66,2},{3,67},{67,3},{4,68},{68... | collective-permute-start | bytes 1572872 | tf_op jit(solution)/shard_map/ppermute | solution.py:212
  175.8 19.6 %collective-permute-start.24 = (bf16[256,512]{1,0:T(8,128)(2,1)}, bf16[256,512]{1,0:T(8,128)(2,1)S(1)}, u32[]{:S(2)}, u32[]{:S(2)}) collective-permute-start(bf16[256,512]{1,0:T(8,128)(2,1)} %copy-done.33), channel_id=1, source_target_pairs={{0,65},{1,64},{64,1},{65,0},{2,67},{3,66},{66,3},{67,2},{4,69},{5,... | collective-permute-start | bytes 786440 | tf_op jit(solution)/shard_map/ppermute | solution.py:239
  177.6 18.2 %collective-permute-start.6 = (bf16[256,1024]{1,0:T(8,128)(2,1)}, bf16[256,1024]{1,0:T(8,128)(2,1)S(1)}, u32[]{:S(2)}, u32[]{:S(2)}) collective-permute-start(bf16[256,1024]{1,0:T(8,128)(2,1)} %copy-done.15), channel_id=1, source_target_pairs={{0,32},{32,0},{1,33},{33,1},{2,34},{34,2},{3,35},{35,3},{4,36},{36... | collective-permute-start | bytes 1572872 | tf_op jit(solution)/shard_map/ppermute | solution.py:212
  178.6 17.1 %collective-permute-start.22 = (bf16[256,512]{1,0:T(8,128)(2,1)}, bf16[256,512]{1,0:T(8,128)(2,1)S(1)}, u32[]{:S(2)}, u32[]{:S(2)}) collective-permute-start(bf16[256,512]{1,0:T(8,128)(2,1)} %copy-done.33), channel_id=1, source_target_pairs={{0,1},{1,0},{2,3},{3,2},{4,5},{5,4},{6,7},{7,6},{8,9},{9,8},{10,11... | collective-permute-start | bytes 786440 | tf_op jit(solution)/shard_map/ppermute | solution.py:212
  188.9 8.3 %collective-permute-start.12 = (bf16[256,1024]{1,0:T(8,128)(2,1)S(1)}, bf16[256,1024]{1,0:T(8,128)(2,1)S(1)}, u32[]{:S(2)}, u32[]{:S(2)}) collective-permute-start(bf16[256,1024]{1,0:T(8,128)(2,1)S(1)} %collective-permute-done.9.refs_7_.refs_2_), channel_id=1, source_target_pairs={{0,32},{32,0},{1,33},{33,1},{2,34},{34,2},{3,35},{35,3},{4,36},{36... | collective-permute-start | bytes 1572872 | tf_op jit(solution)/shard_map/ppermute | solution.py:212
  195.3 1.6 collective-permute-start.25
  195.7 1.5 collective-permute-start.23
  197.3 1.9 copy-start.7
  199.2 1.1 copy-start.16
  205.1 1.2 copy-start.3
  206.2 0.8 copy-start.21
  208.6 113.7 %reduce-scatter.8.cloned.1.call-start = ((), (), s32[]{:S(2)}) async-start(), calls=%async_computation.6 | async-start | bytes 1966080 | tf_op jit(solution)/shard_map/reduce_scatter | solution.py:242
  208.7 15.0 %collective-permute-start.10 = (bf16[256,1024]{1,0:T(8,128)(2,1)}, bf16[256,1024]{1,0:T(8,128)(2,1)S(1)}, u32[]{:S(2)}, u32[]{:S(2)}) collective-permute-start(bf16[256,1024]{1,0:T(8,128)(2,1)} %copy-done.18), channel_id=1, source_target_pairs={{0,64},{64,0},{1,65},{65,1},{2,66},{66,2},{3,67},{67,3},{4,68},{68... | collective-permute-start | bytes 1572872 | tf_op jit(solution)/shard_map/ppermute | solution.py:212
  210.5 19.6 %collective-permute-start.28 = (bf16[256,512]{1,0:T(8,128)(2,1)S(1)}, bf16[256,512]{1,0:T(8,128)(2,1)S(1)}, u32[]{:S(2)}, u32[]{:S(2)}) collective-permute-start(bf16[256,512]{1,0:T(8,128)(2,1)S(1)} %get-tuple-element.30), channel_id=1, source_target_pairs={{0,65},{1,64},{64,1},{65,0},{2,67},{3,66},{66,3},{67,2},{4,69},{5,... | collective-permute-start | bytes 786440 | tf_op jit(solution)/shard_map/ppermute | solution.py:239
  212.3 18.2 %collective-permute-start.7 = (bf16[256,1024]{1,0:T(8,128)(2,1)}, bf16[256,1024]{1,0:T(8,128)(2,1)S(1)}, u32[]{:S(2)}, u32[]{:S(2)}) collective-permute-start(bf16[256,1024]{1,0:T(8,128)(2,1)} %copy-done.18), channel_id=1, source_target_pairs={{0,32},{32,0},{1,33},{33,1},{2,34},{34,2},{3,35},{35,3},{4,36},{36... | collective-permute-start | bytes 1572872 | tf_op jit(solution)/shard_map/ppermute | solution.py:212
  213.2 17.2 %collective-permute-start.26 = (bf16[256,512]{1,0:T(8,128)(2,1)S(1)}, bf16[256,512]{1,0:T(8,128)(2,1)S(1)}, u32[]{:S(2)}, u32[]{:S(2)}) collective-permute-start(bf16[256,512]{1,0:T(8,128)(2,1)S(1)} %get-tuple-element.30), channel_id=1, source_target_pairs={{0,1},{1,0},{2,3},{3,2},{4,5},{5,4},{6,7},{7,6},{8,9},{9,8},{10,11... | collective-permute-start | bytes 786440 | tf_op jit(solution)/shard_map/ppermute | solution.py:212
  223.7 8.3 %collective-permute-start.13 = (bf16[256,1024]{1,0:T(8,128)(2,1)S(1)}, bf16[256,1024]{1,0:T(8,128)(2,1)S(1)}, u32[]{:S(2)}, u32[]{:S(2)}) collective-permute-start(bf16[256,1024]{1,0:T(8,128)(2,1)S(1)} %collective-permute-done.10.refs_8_.refs_2_), channel_id=1, source_target_pairs={{0,32},{32,0},{1,33},{33,1},{2,34},{34,2},{3,35},{35,3},{4,36},{36... | collective-permute-start | bytes 1572872 | tf_op jit(solution)/shard_map/ppermute | solution.py:212
  230.1 1.6 collective-permute-start.29
  230.4 1.5 collective-permute-start.27
  232.0 1.9 copy-start.8
  233.9 1.1 copy-start.19
  239.8 1.1 copy-start.4
  240.9 0.8 copy-start.27
  242.5 0.8 copy-start.31
  256.0 8.5 %copy-start.17 = (bf16[256,1024]{1,0:T(8,128)(2,1)S(1)}, bf16[256,1024]{1,0:T(8,128)(2,1)}, u32[]{:S(2)}) copy-start(bf16[256,1024]{1,0:T(8,128)(2,1)} %copy-done.15) | copy-start | bytes 1572868
  256.0 8.5 %copy-start.20 = (bf16[256,1024]{1,0:T(8,128)(2,1)S(1)}, bf16[256,1024]{1,0:T(8,128)(2,1)}, u32[]{:S(2)}) copy-start(bf16[256,1024]{1,0:T(8,128)(2,1)} %copy-done.18) | copy-start | bytes 1572868
  256.0 8.5 %copy-start.22 = (bf16[256,1024]{1,0:T(8,128)(2,1)S(1)}, bf16[256,1024]{1,0:T(8,128)(2,1)}, u32[]{:S(2)}) copy-start(bf16[256,1024]{1,0:T(8,128)(2,1)} %copy-done.21) | copy-start | bytes 1572868
  256.0 8.5 %copy-start.24 = (bf16[256,1024]{1,0:T(8,128)(2,1)S(1)}, bf16[256,1024]{1,0:T(8,128)(2,1)}, u32[]{:S(2)}) copy-start(bf16[256,1024]{1,0:T(8,128)(2,1)} %copy-done.23) | copy-start | bytes 1572868
  256.0 8.5 %copy-start.26 = (bf16[256,1024]{1,0:T(8,128)(2,1)S(1)}, bf16[256,1024]{1,0:T(8,128)(2,1)}, u32[]{:S(2)}) copy-start(bf16[256,1024]{1,0:T(8,128)(2,1)} %copy-done.25) | copy-start | bytes 1572868
  256.0 8.5 %copy-start.28 = (bf16[256,1024]{1,0:T(8,128)(2,1)S(1)}, bf16[256,1024]{1,0:T(8,128)(2,1)}, u32[]{:S(2)}) copy-start(bf16[256,1024]{1,0:T(8,128)(2,1)} %copy-done.27) | copy-start | bytes 1572868
  264.5 1.0 copy-start.30
  265.6 1.0 copy-start.32
  280.9 18.9 %collective-permute-start.14 = (bf16[256,1536]{1,0:T(8,128)(2,1)S(1)}, bf16[256,1536]{1,0:T(8,128)(2,1)S(1)}, u32[]{:S(2)}, u32[]{:S(2)}) collective-permute-start(bf16[256,1536]{1,0:T(8,128)(2,1)S(1)} %get-tuple-element.24), channel_id=1, source_target_pairs={{0,8},{8,0},{16,24},{24,16},{1,9},{9,1},{17,25},{25,17},{2,10},{10... | collective-permute-start | bytes 2359304 | tf_op jit(solution)/shard_map/ppermute | solution.py:212
  281.0 38.1 %collective-permute-start.15 = (bf16[256,1536]{1,0:T(8,128)(2,1)S(1)}, bf16[256,1536]{1,0:T(8,128)(2,1)S(1)}, u32[]{:S(2)}, u32[]{:S(2)}) collective-permute-start(bf16[256,1536]{1,0:T(8,128)(2,1)S(1)} %get-tuple-element.25), channel_id=1, source_target_pairs={{0,16},{8,24},{16,0},{24,8},{1,17},{9,25},{17,1},{25,9},{2,18},{10... | collective-permute-start | bytes 2359304 | tf_op jit(solution)/shard_map/ppermute | solution.py:212
  284.9 36.2 %collective-permute-start.16 = (bf16[256,1536]{1,0:T(8,128)(2,1)S(1)}, bf16[256,1536]{1,0:T(8,128)(2,1)S(1)}, u32[]{:S(2)}, u32[]{:S(2)}) collective-permute-start(bf16[256,1536]{1,0:T(8,128)(2,1)S(1)} %get-tuple-element.26), channel_id=1, source_target_pairs={{0,24},{8,16},{16,8},{24,0},{1,25},{9,17},{17,9},{25,1},{2,26},{10... | collective-permute-start | bytes 2359304 | tf_op jit(solution)/shard_map/ppermute | solution.py:212
  (4 other events, 3.1 us)
Sparse Core Ops, SparseCore 0:
  89.9 44.5 all-gather.1
  174.0 26.7 reduce-scatter.3
  208.8 26.5 reduce-scatter.5
  243.5 26.5 reduce-scatter.7

commit v2 on v1

v2 whole, which is shorter than its diff:
```python
import jax
import jax.numpy as jnp
from jax import lax
from jax.experimental import pallas as pl
from jax.experimental.pallas import tpu as pltpu
from jax.sharding import Mesh
from jax.sharding import PartitionSpec as P

K = 1536
F = 3072
S = 256
H = 128
CHUNKS = 3
DEPTH = 8
CW = F // CHUNKS
HALF = CW // 2
LANE = 128
gelu_coef = 0.7978845608028654
bf16 = jnp.bfloat16
f32 = jnp.float32
MIB = 1 << 20
ANY = pl.BlockSpec(memory_space=pl.ANY)


def params():
    return pltpu.CompilerParams(vmem_limit_bytes=60 * MIB)


def cost(flops, bytes_accessed, transcendentals=0):
    return pl.CostEstimate(flops=flops, bytes_accessed=bytes_accessed, transcendentals=transcendentals)


def after_kernel(*refs):
    pass


def after(value, *others):
    return pl.pallas_call(
        after_kernel,
        in_specs=[ANY] * (1 + len(others)),
        out_specs=ANY,
        out_shape=jax.ShapeDtypeStruct(value.shape, value.dtype),
        input_output_aliases={0: 0},
        cost_estimate=cost(0, 0),
        name="after",
    )(value, *others)


def partial_kernel(q_ref, b0, b1, b2, b3, w_ref, p0_ref, p1_ref, p2_ref, p3_ref, tk_ref, sems):
    @pl.when(pl.program_id(0) == 0)
    def _():
        q = q_ref[0]
        copies = []
        for m, block in enumerate((b0, b1, b2, b3)):
            slot = pl.multiple_of(jnp.bitwise_xor(q, m) * H, H)
            copies.append(pltpu.make_async_copy(block, tk_ref.at[pl.ds(slot, H)], sems.at[m]))
        for copy in copies:
            copy.start()
        for copy in copies:
            copy.wait()

    term = jnp.dot(tk_ref[...], w_ref[...], preferred_element_type=f32).astype(bf16)
    for k, ref in enumerate((p0_ref, p1_ref, p2_ref, p3_ref)):
        ref[...] = term[k * H:(k + 1) * H, :]


def block_partials(q, blocks, weight):
    tile = 512
    grid_spec = pltpu.PrefetchScalarGridSpec(
        num_scalar_prefetch=1,
        grid=(F // tile,),
        in_specs=[ANY] * 4 + [pl.BlockSpec((K, tile), lambda i, q: (0, i))],
        out_specs=[pl.BlockSpec((H, tile), lambda i, q: (0, i))] * 4 + [pl.BlockSpec((4 * H, K), lambda i, q: (0, 0))],
        scratch_shapes=[pltpu.SemaphoreType.DMA((4,))],
    )
    return pl.pallas_call(
        partial_kernel,
        grid_spec=grid_spec,
        out_shape=[jax.ShapeDtypeStruct((H, F), bf16)] * 4 + [jax.ShapeDtypeStruct((4 * H, K), bf16)],
        compiler_params=params(),
        cost_estimate=cost(2 * 4 * H * K * F, 16 * MIB),
        name="block_partials",
    )(q, *blocks, weight)


def gelu_kernel(xl_ref, own_ref, core_ref, far_ref, cot_ref, *refs):
    outs = refs[-(1 + 2 * CHUNKS):]
    xl = xl_ref[0]
    act_ref, pgs, halves = outs[0], outs[1:1 + CHUNKS], outs[1 + CHUNKS:]
    pieces = {}
    for d in range(DEPTH):
        for f in range(CHUNKS):
            at = slice((d * CHUNKS + f) * LANE, (d * CHUNKS + f + 1) * LANE)
            pre = own_ref[:, at].astype(f32) + core_ref[:, at].astype(f32) + far_ref[:, at].astype(f32)
            inner = gelu_coef * (pre + 0.044715 * pre * pre * pre)
            tangent = jnp.tanh(inner)
            act_ref[:, at] = (0.5 * pre * (1.0 + tangent)).astype(bf16)
            slope = 0.5 * (1.0 + tangent) + 0.5 * pre * (1.0 - tangent * tangent) * gelu_coef * (
                1.0 + 3.0 * 0.044715 * pre * pre
            )
            grad = (cot_ref[:, at].astype(f32) * slope).astype(bf16)
            pgs[f][:, d * LANE:(d + 1) * LANE] = grad
            pieces[f, d % 2] = grad
            if d % 2:
                z = d // 2
                halves[f][:, z * LANE:(z + 1) * LANE] = jnp.where(xl == 0, pieces[f, 1], pieces[f, 0])


def gelu_pair(xl, own, core, far, cot, part, earlier=()):
    rows = 64
    steps = H // rows
    grid_spec = pltpu.PrefetchScalarGridSpec(
        num_scalar_prefetch=1,
        grid=(steps,),
        in_specs=[pl.BlockSpec((rows, F), lambda i, x: (i, 0))] * 3
        + [pl.BlockSpec((rows, F), lambda i, x: (i + part * steps, 0))]
        + [ANY] * len(earlier),
        out_specs=[pl.BlockSpec((rows, F), lambda i, x: (i + part * steps, 0))]
        + [pl.BlockSpec((rows, CW), lambda i, x: (i + part * steps, 0))] * CHUNKS
        + [pl.BlockSpec((rows, HALF), lambda i, x: (i + part * steps, 0))] * CHUNKS,
    )
    return pl.pallas_call(
        gelu_kernel,
        grid_spec=grid_spec,
        out_shape=[jax.ShapeDtypeStruct((S, F), bf16)]
        + [jax.ShapeDtypeStruct((S, CW), bf16)] * CHUNKS
        + [jax.ShapeDtypeStruct((S, HALF), bf16)] * CHUNKS,
        input_output_aliases={5 + i: i for i in range(len(earlier))},
        compiler_params=params(),
        cost_estimate=cost(30 * H * F, 5 * MIB, H * F),
        name="gelu_pair",
    )(xl, own, core, far, cot, *earlier)


def weight_kernel(ids_ref, ta_ref, tb_ref, tx_ref, *refs):
    own, other, out_ref, pg = refs[:4], refs[4:8], refs[8], refs[9]

    @pl.when(pl.program_id(0) == 0)
    def _():
        xl, r = ids_ref[0], ids_ref[1]
        for k in range(4):
            for z in range(4):
                at = pl.multiple_of((2 * z + xl) * LANE, LANE)
                for part in range(2):
                    row = (4 * part + k) * H
                    pg[row:row + H, z * LANE:(z + 1) * LANE] = own[k][part * H:(part + 1) * H, pl.ds(at, LANE)]
            slot = pl.multiple_of(4 * S + jnp.bitwise_xor(r, k) * S, S)
            pg[pl.ds(slot, S), :] = other[k][...]

    total = jnp.dot(ta_ref[...], pg[:4 * H, :], preferred_element_type=f32)
    total += jnp.dot(tb_ref[...], pg[4 * H:8 * H, :], preferred_element_type=f32)
    total += jnp.dot(tx_ref[...], pg[8 * H:, :], preferred_element_type=f32)
    for z in range(4):
        out_ref[z] = total[:, z * LANE:(z + 1) * LANE].astype(bf16)


def weight_part(ids, ta, tb, tx, own, other):
    rows = 512
    grid_spec = pltpu.PrefetchScalarGridSpec(
        num_scalar_prefetch=1,
        grid=(K // rows,),
        in_specs=[pl.BlockSpec((rows, 4 * H), lambda i, x: (i, 0))] * 2
        + [pl.BlockSpec((rows, 4 * S), lambda i, x: (i, 0))]
        + [pl.BlockSpec((S, CW), lambda i, x: (0, 0))] * 4
        + [pl.BlockSpec((S, HALF), lambda i, x: (0, 0))] * 4,
        out_specs=pl.BlockSpec((4, rows, LANE), lambda i, x: (0, i, 0)),
        scratch_shapes=[pltpu.VMEM((8 * S, HALF), bf16)],
    )
    return pl.pallas_call(
        weight_kernel,
        grid_spec=grid_spec,
        out_shape=jax.ShapeDtypeStruct((4, K, LANE), bf16),
        compiler_params=params(),
        cost_estimate=cost(2 * 8 * S * K * HALF, 11 * MIB),
        name="weight_part",
    )(ids, ta, tb, tx, *own, *other)


def input_kernel(q_ref, *refs):
    grads, w_ref, outs, lhs, sems = refs[:12], refs[12], refs[13:17], refs[17], refs[18]

    @pl.when(pl.program_id(0) == 0)
    def _():
        q = q_ref[0]
        copies = []
        for k in range(4):
            slot = pl.multiple_of(jnp.bitwise_xor(q, k) * S, S)
            for f in range(CHUNKS):
                copies.append(
                    pltpu.make_async_copy(
                        grads[k * CHUNKS + f],
                        lhs.at[pl.ds(slot, S), pl.ds(f * CW, CW)],
                        sems.at[k * CHUNKS + f],
                    )
                )
        for copy in copies:
            copy.start()
        for copy in copies:
            copy.wait()

    w = jnp.concatenate(
        [
            w_ref[:, (d * CHUNKS + f) * LANE:(d * CHUNKS + f + 1) * LANE]
            for f in range(CHUNKS)
            for d in range(DEPTH)
        ],
        axis=1,
    )
    total = lax.dot_general(lhs[...], w, (((1,), (1,)), ((), ())), preferred_element_type=f32).astype(bf16)
    for m in range(4):
        outs[m][...] = total[m * S:(m + 1) * S, :]


def input_part(q, grads, weight):
    tile = 256
    grid_spec = pltpu.PrefetchScalarGridSpec(
        num_scalar_prefetch=1,
        grid=(K // tile,),
        in_specs=[ANY] * 12 + [pl.BlockSpec((tile, F), lambda i, q: (i, 0))],
        out_specs=[pl.BlockSpec((S, tile), lambda i, q: (0, i))] * 4,
        scratch_shapes=[pltpu.VMEM((4 * S, F), bf16), pltpu.SemaphoreType.DMA((12,))],
    )
    return pl.pallas_call(
        input_kernel,
        grid_spec=grid_spec,
        out_shape=[jax.ShapeDtypeStruct((S, K), bf16)] * 4,
        compiler_params=params(),
        cost_estimate=cost(2 * 4 * S * K * F, 18 * MIB),
        name="input_part",
    )(q, *grads, weight)


def swap(value, axis, mask):
    n = lax.axis_size(axis)
    return lax.ppermute(value, axis, [(i, i ^ mask) for i in range(n)])


def shards(tokens, weight, cotangent):
    xh, core, y, xl, z = (lax.axis_index(a) for a in ("xh", "core", "y", "xl", "z"))
    r = 2 * xh + core
    q = jnp.bitwise_xor(r, y).astype(jnp.int32).reshape(1)
    ids = jnp.stack([xl, r]).astype(jnp.int32)

    parts = [tokens[:H], tokens[H:]]
    others = lax.all_gather(swap(tokens, "xl", 1), "y", axis=0, tiled=True)
    tx = others.T
    out = ()
    turned = []
    gathered = None
    for part in range(2):
        mine = parts[part] if part == 0 else after(parts[part], gathered[2])
        gathered = [swap(mine, "y", 2), swap(mine, "y", 1), swap(mine, "y", 3)]
        p0, p1, p2, p3, tk = block_partials(q, [mine, gathered[1], gathered[0], gathered[2]], weight)
        second = (p2.astype(f32) + swap(p3, "core", 1).astype(f32)).astype(bf16)
        far = swap(second, "xh", 1)
        turned.append(tk.T)
        out = gelu_pair(ids[:1], p0, swap(p1, "core", 1), far, cotangent, part, out)
    activation, grads, halves = out[0], out[1:1 + CHUNKS], out[1 + CHUNKS:]

    own = []
    sums = []
    for f in range(CHUNKS):
        pair = swap(grads[f], "xh", 1)
        own.append([grads[f], swap(grads[f], "core", 1), pair, swap(pair, "core", 1)])
        near = swap(halves[f], "xl", 1)
        cross = lax.ppermute(halves[f], ("xh", "xl"), [(i, 3 - i) for i in range(4)])
        other = [near, swap(near, "core", 1), cross, swap(cross, "core", 1)]
        part = weight_part(ids, turned[0], turned[1], tx, own[f], other)
        if f == 0:
            sums.append(lax.psum_scatter(part, "z", scatter_dimension=0, tiled=True)[0].astype(f32))
        else:
            total = lax.dynamic_index_in_dim(part, z, 0, False).astype(f32)
            for m in (2, 1, 3):
                piece = lax.dynamic_index_in_dim(part, jnp.bitwise_xor(z, m), 0, False)
                total += swap(piece, "z", m).astype(f32)
            sums.append(total)
    weight_grad = jnp.concatenate(sums, axis=1).astype(bf16)

    dx = input_part(q, [own[f][k] for k in range(4) for f in range(CHUNKS)], weight)
    total = dx[0].astype(f32)
    for m in (2, 1, 3):
        total += swap(dx[m], "y", m).astype(f32)
    return activation, total.astype(bf16), weight_grad


def solution(mesh):
    split = Mesh(mesh.devices.reshape(2, 2, 4, 4, 2), ("xh", "core", "y", "z", "xl"))
    hidden = P(("z", "xl", "xh", "core"), "y")
    tokens = P(("z", "xl", "y"), ("xh", "core"))
    return jax.shard_map(
        shards,
        mesh=split,
        in_specs=(tokens, P(("xh", "core"), "y"), hidden),
        out_specs=(hidden, tokens, P(("xh", "core"), ("y", "z", "xl"))),
        check_vma=False,
    )
```

time: 333 us -> 280 us (0.84)
  waiting for transfers between devices: 165 us -> 114 us
  local copies, waits for them, and re-layouts: 57.3 us -> 17.6 us
  Pallas kernels: 48.5 us -> 73 us
  starting transfers between devices: 39.1 us -> 51.6 us
    ppermute x27 -> x40, waiting for transfers between devices: 154 us -> 73.6 us  [swap(): return lax.ppermute(value, axis, [(i, i ^ mask) for i in range(n)])]
    unnamed x70 -> x69, local copies, waits for them, and re-layouts: 45.7 us -> 9.77 us
    ppermute x3, waiting for transfers between devices: 11.7 us -> 40.4 us  [shards(): lax.ppermute(halves[f], ('xh', 'xl'), [(i, 3 - i) for i in range(4)])]
    ppermute x27 -> x40, starting transfers between devices: 34.5 us -> 47.1 us  [swap(): return lax.ppermute(value, axis, [(i, i ^ mask) for i in range(n)])]
    pallas_call x1 -> x2, Pallas kernels: 12.7 us -> 22.8 us  [block_partials(): pl.pallas_call(partial_kernel, grid_spec=grid_spec, out_shape=[jax.ShapeD...]
    pallas_call x3, Pallas kernels: 16.2 us -> 26.1 us  [weight_part(): pl.pallas_call(weight_kernel, grid_spec=grid_spec, out_shape=jax.ShapeDty...]
    transpose x1 -> x0, local copies, waits for them, and re-layouts: 8.43 us -> none  [shards(): weight.reshape(K, DEPTH, CHUNKS, LANE).transpose(2, 1, 3, 0).reshape(F, K)]
    pallas_call x1 -> x2, Pallas kernels: 5.29 us -> 7.79 us  [gelu_pair(): pl.pallas_call(gelu_kernel, grid_spec=grid_spec, out_shape=[jax.ShapeDtyp...]
  transfers between devices with their start and end apart: 34 -> 45, of which waited for: 16 -> 14; matrix products, arithmetic and copies ran while one was open for 9% -> 4% of each run, Pallas kernels for 9% -> 26%
where the time goes in v2:
time: 280 us; the launch traced here: 279 us
  waiting for transfers between devices  114 us (41%)
  Pallas kernels  73 us (26%)
  starting transfers between devices  51.6 us (18%)
  local copies, waits for them, and re-layouts  17.6 us (6%)
  between operations  14.3 us (5%)
  other arithmetic  8.46 us (3%)
    ppermute x40, waiting for transfers between devices, swap(): return lax.ppermute(value, axis, [(i, i ^ mask) for i in range(n)])  73.6 us
    ppermute x40, starting transfers between devices, swap(): return lax.ppermute(value, axis, [(i, i ^ mask) for i in range(n)])  47.1 us
    ppermute x3, waiting for transfers between devices, shards(): lax.ppermute(halves[f], ('xh', 'xl'), [(i, 3 - i) for i in range(4)])  40.4 us
    pallas_call x3, Pallas kernels, weight_part(): pl.pallas_call(weight_kernel, grid_spec=grid_spec, out_shape=jax.ShapeDty...  26.1 us
    pallas_call x2, Pallas kernels, block_partials(): pl.pallas_call(partial_kernel, grid_spec=grid_spec, out_shape=[jax.ShapeD...  22.8 us
    pallas_call x1, Pallas kernels, input_part(): pl.pallas_call(input_kernel, grid_spec=grid_spec, out_shape=[jax.ShapeDty...  16.3 us
    unnamed x69, local copies, waits for them, and re-layouts  9.77 us
    pallas_call x2, Pallas kernels, gelu_pair(): pl.pallas_call(gelu_kernel, grid_spec=grid_spec, out_shape=[jax.ShapeDtyp...  7.79 us
  transfers between devices with their start and end apart: 45, of which 14 were waited for; matrix products, arithmetic and copies ran while one was open for 4% of the time, Pallas kernels for 26%

profile of v2, /device:TPU:1, one launch (start us, length us, event | category | flops | bytes accessed | tf_op | source)
XLA Modules:
  0.0 279.1 jit_solution(9793224592394968072)
XLA Ops:
  7.2 2.0 fusion.6
  9.2 3.6 %collective-permute-start = (bf16[128,1536]{1,0:T(8,128)(2,1)S(1)}, bf16[128,1536]{1,0:T(8,128)(2,1)S(1)}, u32[]{:S(2)}, u32[]{:S(2)}) collective-permute-start(bf16[128,1536]{1,0:T(8,128)(2,1)S(1)} %get-tuple-element.65.b0), channel_id=1, source_target_pairs={{0,24},{8,16},{16,8},{24,0},{1,25},{9,17},{17,9},{25,1},{2,26},{10... | collective-permute-start | bytes 1179656 | tf_op jit(solution)/shard_map/ppermute | solution.py:235
  12.8 1.2 collective-permute-start.8
  14.2 1.3 collective-permute-start.24
  15.5 5.9 %collective-permute-done.refs_1_.b3 = bf16[128,1536]{1,0:T(8,128)(2,1)S(1)} collective-permute-done((bf16[128,1536]{1,0:T(8,128)(2,1)S(1)}, bf16[128,1536]{1,0:T(8,128)(2,1)S(1)}, u32[]{:S(2)}, u32[]{:S(2)}) %collective-permute-start) | collective-permute-done | bytes 393248 | tf_op jit(solution)/shard_map/ppermute | solution.py:235
  21.4 0.7 copy-done.10
  22.2 3.7 %collective-permute-start.2 = (bf16[128,1536]{1,0:T(8,128)(2,1)}, bf16[128,1536]{1,0:T(8,128)(2,1)}, u32[]{:S(2)}, u32[]{:S(2)}) collective-permute-start(bf16[128,1536]{1,0:T(8,128)(2,1)} %after.1.b0), channel_id=1, source_target_pairs={{0,16},{8,24},{16,0},{24,8},{1,17},{9,25},{17,1},{25,9},{2,18},{10... | collective-permute-start | bytes 1179656 | tf_op jit(solution)/shard_map/ppermute | solution.py:235
  26.1 4.7 %collective-permute-done.8.b2 = bf16[128,1536]{1,0:T(8,128)(2,1)S(1)} collective-permute-done((bf16[128,1536]{1,0:T(8,128)(2,1)S(1)}, bf16[128,1536]{1,0:T(8,128)(2,1)S(1)}, u32[]{:S(2)}, u32[]{:S(2)}) %collective-permute-start.8) | collective-permute-done | bytes 393248 | tf_op jit(solution)/shard_map/ppermute | solution.py:235
  30.7 0.8 copy-done.23
  31.5 11.4 %block_partials.3 = (bf16[128,3072]{1,0:T(8,128)(2,1)}, bf16[128,3072]{1,0:T(8,128)(2,1)}, bf16[128,3072]{1,0:T(8,128)(2,1)}, bf16[128,3072]{1,0:T(8,128)(2,1)}, bf16[512,1536]{1,0:T(8,128)(2,1)}) custom-call(s32[1]{0:T(128)} %bitcast.1.q_ref, bf16[128,1536]{1,0:T(8,128)(2,1)} %copy-done.9, bf16[128,1536]{1,0:T(8,128)(2,1)} %copy-done.22, ...), custom_call_target="tpu_custom_call" | custom-call | flops 4831838208 | bytes 16777216 | tf_op jit(solution)/shard_map/block_partials/pallas_call | solution.py:76
  42.9 3.1 %collective-permute-start.10 = (bf16[128,3072]{1,0:T(8,128)(2,1)}, bf16[128,3072]{1,0:T(8,128)(2,1)S(1)}, u32[]{:S(2)}, u32[]{:S(2)}) collective-permute-start(bf16[128,3072]{1,0:T(8,128)(2,1)} %get-tuple-element.38), channel_id=1, source_target_pairs={{0,32},{32,0},{1,33},{33,1},{2,34},{34,2},{3,35},{35,3},{4,36},{36... | collective-permute-start | bytes 2359304 | tf_op jit(solution)/shard_map/ppermute | solution.py:235
  46.0 0.9 copy-done.3
  47.8 11.4 %block_partials.2 = (bf16[128,3072]{1,0:T(8,128)(2,1)}, bf16[128,3072]{1,0:T(8,128)(2,1)}, bf16[128,3072]{1,0:T(8,128)(2,1)}, bf16[128,3072]{1,0:T(8,128)(2,1)}, bf16[512,1536]{1,0:T(8,128)(2,1)}) custom-call(s32[1]{0:T(128)} %bitcast.1.q_ref, bf16[128,1536]{1,0:T(8,128)(2,1)} %after.1.b0, bf16[128,1536]{1,0:T(8,128)(2,1)} %copy-done.24, ...), custom_call_target="tpu_custom_call" | custom-call | flops 4831838208 | bytes 16777216 | tf_op jit(solution)/shard_map/block_partials/pallas_call | solution.py:76
  59.2 1.8 collective-permute-start.5
  61.7 2.8 %collective-permute-start.11 = (bf16[128,3072]{1,0:T(8,128)(2,1)S(1)}, bf16[128,3072]{1,0:T(8,128)(2,1)S(1)}, u32[]{:S(2)}, u32[]{:S(2)}) collective-permute-start(bf16[128,3072]{1,0:T(8,128)(2,1)S(1)} %add_convert_fusion.1), channel_id=1, source_target_pairs={{0,64},{64,0},{1,65},{65,1},{2,66},{66,2},{3,67},{67,3},{4,68},{68... | collective-permute-start | bytes 2359304 | tf_op jit(solution)/shard_map/ppermute | solution.py:235
  64.7 1.4 collective-permute-start.6
  66.1 16.3 %collective-permute-done.11.far_ref = bf16[128,3072]{1,0:T(8,128)(2,1)S(1)} collective-permute-done((bf16[128,3072]{1,0:T(8,128)(2,1)S(1)}, bf16[128,3072]{1,0:T(8,128)(2,1)S(1)}, u32[]{:S(2)}, u32[]{:S(2)}) %collective-permute-start.11) | collective-permute-done | bytes 786464 | tf_op jit(solution)/shard_map/ppermute | solution.py:235
  82.4 0.9 copy-done.7
  83.3 3.9 %gelu_pair.2 = (bf16[256,3072]{1,0:T(8,128)(2,1)}, bf16[256,1024]{1,0:T(8,128)(2,1)}, bf16[256,1024]{1,0:T(8,128)(2,1)}, bf16[256,1024]{1,0:T(8,128)(2,1)}, bf16...) custom-call(s32[1]{0:T(128)} %bitcast.xl_ref, ...), custom_call_target="tpu_custom_call" | custom-call | flops 11796480 | bytes 5242880 | tf_op jit(solution)/shard_map/gelu_pair/pallas_call | solution.py:122
  87.2 12.1 %collective-permute-done.6.far_ref = bf16[128,3072]{1,0:T(8,128)(2,1)} collective-permute-done((bf16[128,3072]{1,0:T(8,128)(2,1)S(1)}, bf16[128,3072]{1,0:T(8,128)(2,1)}, u32[]{:S(2)}, u32[]{:S(2)}) %collective-permute-start.6) | collective-permute-done | bytes 786464 | tf_op jit(solution)/shard_map/ppermute | solution.py:235
  99.3 3.9 %gelu_pair.3 = (bf16[256,3072]{1,0:T(8,128)(2,1)}, bf16[256,1024]{1,0:T(8,128)(2,1)}, bf16[256,1024]{1,0:T(8,128)(2,1)}, bf16[256,1024]{1,0:T(8,128)(2,1)}, bf16...) custom-call(s32[1]{0:T(128)} %bitcast.xl_ref, ...), custom_call_target="tpu_custom_call", output_to_operand_aliasing={{0}: (5, {}), {1}: (6, {}), {2}: (7, {}), {3}: (8, {}), {4}... | custom-call | flops 11796480 | bytes 5242880 | tf_op jit(solution)/shard_map/gelu_pair/pallas_call | solution.py:122
  103.2 1.3 collective-permute-start.25
  104.5 2.5 collective-permute-start.15
  107.0 1.4 collective-permute-start.12
  108.9 2.5 collective-permute-start.17
  111.4 1.6 collective-permute-start.27
  112.9 40.4 %collective-permute-done.27.refs_6_ = bf16[256,512]{1,0:T(8,128)(2,1)} collective-permute-done((bf16[256,512]{1,0:T(8,128)(2,1)}, bf16[256,512]{1,0:T(8,128)(2,1)}, u32[]{:S(2)}, u32[]{:S(2)}) %collective-permute-start.27) | collective-permute-done | bytes 262176 | tf_op jit(solution)/shard_map/ppermute | solution.py:266
  156.0 1.1 collective-permute-done.14.refs_5_.refs_1_
  158.3 0.8 copy-done.18
  159.1 0.8 copy-done.16
  159.9 16.3 %input_part.1 = (bf16[256,1536]{1,0:T(8,128)(2,1)}, bf16[256,1536]{1,0:T(8,128)(2,1)}, bf16[256,1536]{1,0:T(8,128)(2,1)}, bf16[256,1536]{1,0:T(8,128)(2,1)}) custom-call(s32[1]{0:T(128)} %bitcast.1.q_ref, bf16[256,1024]{1,0:T(8,128)(2,1)} %get-tuple-element.47.refs_0_, bf16[256,1024]{1,0:T(8,128)(2,1)} %get-tuple-element.48.refs_1_.refs_0_, ...), custom_call_target="tpu_custom_call" | custom-call | flops 9663676416 | bytes 18874368 | tf_op jit(solution)/shard_map/input_part/pallas_call | solution.py:223
  176.2 1.8 collective-permute-start.21
  178.0 1.6 collective-permute-start.22
  180.2 1.6 copy.14
  181.9 1.6 copy.15
  183.5 0.8 collective-permute-start.31
  184.3 8.7 %weight_part.3 = bf16[4,1536,128]{2,1,0:T(8,128)(2,1)} custom-call(s32[2]{0:T(128)} %pad_add_fusion.ids_ref, bf16[1536,512]{1,0:T(8,128)(2,1)} %bitcast.25, bf16[1536,512]{1,0:T(8,128)(2,1)} %bitcast.28, bf16[1536,1024]{1,0:T(8,128)(2,1)} %bitcast.32, bf16[256,1024]{1,0:T(8,128)(2,1)} %get-tuple-element.47.refs_0_, bf16[256,1024]{1,0:T(8,128)(2,1)} %copy-done.20, ...), custom_call_target="tpu_custom_call" | custom-call | flops 3221225472 | bytes 11534336 | tf_op jit(solution)/shard_map/weight_part/pallas_call | solution.py:169
  193.0 0.9 copy-done.12
  194.0 0.7 collective-permute-start.36
  194.6 2.1 collective-permute-start.38
  196.7 3.6 %collective-permute-done.36.refs_4_ = bf16[256,512]{1,0:T(8,128)(2,1)S(1)} collective-permute-done((bf16[256,512]{1,0:T(8,128)(2,1)S(1)}, bf16[256,512]{1,0:T(8,128)(2,1)S(1)}, u32[]{:S(2)}, u32[]{:S(2)}) %collective-permute-start.36) | collective-permute-done | bytes 262176 | tf_op jit(solution)/shard_map/ppermute | solution.py:235
  200.3 2.3 collective-permute-start.30
  202.7 1.9 collective-permute-start.32
  204.7 9.6 %collective-permute-done.22 = bf16[256,1536]{1,0:T(8,128)(2,1)} collective-permute-done((bf16[256,1536]{1,0:T(8,128)(2,1)}, bf16[256,1536]{1,0:T(8,128)(2,1)}, u32[]{:S(2)}, u32[]{:S(2)}) %collective-permute-start.22) | collective-permute-done | bytes 786464 | tf_op jit(solution)/shard_map/ppermute | solution.py:235
  214.3 1.0 collective-permute-start.39
  215.3 2.9 %add_convert_fusion = bf16[256,1536]{1,0:T(8,128)(2,1)} fusion(bf16[256,1536]{1,0:T(8,128)(2,1)} %collective-permute-done.23, bf16[256,1536]{1,0:T(8,128)(2,1)} %collective-permute-done.22, bf16[256,1536]{1,0:T(8,128)(2,1)} %collective-permute-done.21, bf16[256,1536]{1,0:T(8,128)(2,1)S(1)} %copy-done.8), kind=kLoop, calls=%fused_computation | loop fusion | flops 3145728 | bytes 3932160 | tf_op jit(solution)/shard_map/convert_element_type | solution.py:283
  218.3 0.7 copy-done.32
  219.0 0.7 copy-done.33
  219.7 8.8 %weight_part.4 = bf16[4,1536,128]{2,1,0:T(8,128)(2,1)} custom-call(s32[2]{0:T(128)} %pad_add_fusion.ids_ref, bf16[1536,512]{1,0:T(8,128)(2,1)} %bitcast.26, bf16[1536,512]{1,0:T(8,128)(2,1)} %bitcast.29, bf16[1536,1024]{1,0:T(8,128)(2,1)} %bitcast.33, bf16[256,1024]{1,0:T(8,128)(2,1)} %get-tuple-element.48.refs_1_.refs_0_, bf16[256,1024]{1,0:T(8,128)(2,1)} %copy-done.17, ...), custom_call_target="tpu_custom_call" | custom-call | flops 3221225472 | bytes 11534336 | tf_op jit(solution)/shard_map/weight_part/pallas_call | solution.py:169
  228.4 1.3 dynamic-slice_bitcast_fusion.5
  229.7 3.7 %collective-permute-start.33 = (bf16[1536,128]{1,0:T(8,128)(2,1)S(1)}, bf16[1536,128]{1,0:T(8,128)(2,1)S(1)}, u32[]{:S(2)}, u32[]{:S(2)}) collective-permute-start(bf16[1536,128]{1,0:T(8,128)(2,1)S(1)} %get-tuple-element.59), channel_id=1, source_target_pairs={{0,4},{2,6},{4,0},{6,2},{1,5},{3,7},{5,1},{7,3},{8,12},{10,14},{12... | collective-permute-start | bytes 1179656 | tf_op jit(solution)/shard_map/ppermute | solution.py:235
  233.4 0.8 collective-permute-start.34
  234.2 0.7 copy-done.30
  234.9 0.7 copy-done.31
  235.6 8.7 %weight_part.5 = bf16[4,1536,128]{2,1,0:T(8,128)(2,1)} custom-call(s32[2]{0:T(128)} %pad_add_fusion.ids_ref, bf16[1536,512]{1,0:T(8,128)(2,1)} %bitcast.27, bf16[1536,512]{1,0:T(8,128)(2,1)} %bitcast.30, bf16[1536,1024]{1,0:T(8,128)(2,1)} %bitcast.34, bf16[256,1024]{1,0:T(8,128)(2,1)} %get-tuple-element.49.refs_2_.refs_0_, bf16[256,1024]{1,0:T(8,128)(2,1)} %copy-done.14, ...), custom_call_target="tpu_custom_call" | custom-call | flops 3221225472 | bytes 11534336 | tf_op jit(solution)/shard_map/weight_part/pallas_call | solution.py:169
  244.3 1.3 dynamic-slice_bitcast_fusion.2
  245.6 2.6 collective-permute-start.40
  248.2 0.8 collective-permute-start.41
  248.9 3.0 %collective-permute-done.34 = bf16[1536,128]{1,0:T(8,128)(2,1)S(1)} collective-permute-done((bf16[1536,128]{1,0:T(8,128)(2,1)S(1)}, bf16[1536,128]{1,0:T(8,128)(2,1)S(1)}, u32[]{:S(2)}, u32[]{:S(2)}) %collective-permute-start.34) | collective-permute-done | bytes 393248 | tf_op jit(solution)/shard_map/ppermute | solution.py:235
  252.0 1.2 fusion.5
  253.2 6.7 %collective-permute-done.40 = bf16[1536,128]{1,0:T(8,128)(2,1)S(1)} collective-permute-done((bf16[1536,128]{1,0:T(8,128)(2,1)S(1)}, bf16[1536,128]{1,0:T(8,128)(2,1)S(1)}, u32[]{:S(2)}, u32[]{:S(2)}) %collective-permute-start.40) | collective-permute-done | bytes 393248 | tf_op jit(solution)/shard_map/ppermute | solution.py:235
  259.9 9.0 %collective-permute-done.41 = bf16[1536,128]{1,0:T(8,128)(2,1)S(1)} collective-permute-done((bf16[1536,128]{1,0:T(8,128)(2,1)S(1)}, bf16[1536,128]{1,0:T(8,128)(2,1)S(1)}, u32[]{:S(2)}, u32[]{:S(2)}) %collective-permute-start.41) | collective-permute-done | bytes 393248 | tf_op jit(solution)/shard_map/ppermute | solution.py:235
  268.9 1.2 fusion.2
  270.1 2.2 pad_maximum_fusion
  (118 shorter events, 7.4 us)
Async XLA Ops:
  7.2 6.8 %copy-start = (bf16[256,1536]{1,0:T(8,128)(2,1)S(1)}, bf16[256,1536]{1,0:T(8,128)(2,1)}, u32[]{:S(2)}) copy-start(bf16[256,1536]{1,0:T(8,128)(2,1)} %param.3) | copy-start | bytes 2359300
  7.2 177.1 %all-gather.2.cloned.1.call-start = ((), (), s32[]{:S(2)}) async-start(), calls=%async_computation.1 | async-start | bytes 3932160 | tf_op jit(solution)/shard_map/all_gather | solution.py:245
  9.2 21.5 %copy-start.9 = (bf16[128,1536]{1,0:T(8,128)(2,1)}, bf16[128,1536]{1,0:T(8,128)(2,1)S(1)}, u32[]{:S(2)}) copy-start(bf16[128,1536]{1,0:T(8,128)(2,1)S(1)} %get-tuple-element.65.b0) | copy-start | bytes 1179652
  9.2 12.2 %collective-permute-start = (bf16[128,1536]{1,0:T(8,128)(2,1)S(1)}, bf16[128,1536]{1,0:T(8,128)(2,1)S(1)}, u32[]{:S(2)}, u32[]{:S(2)}) collective-permute-start(bf16[128,1536]{1,0:T(8,128)(2,1)S(1)} %get-tuple-element.65.b0), channel_id=1, source_target_pairs={{0,24},{8,16},{16,8},{24,0},{1,25},{9,17},{17,9},{25,1},{2,26},{10... | collective-permute-start | bytes 1179656 | tf_op jit(solution)/shard_map/ppermute | solution.py:235
  12.8 13.1 %collective-permute-start.7 = (bf16[128,1536]{1,0:T(8,128)(2,1)S(1)}, bf16[128,1536]{1,0:T(8,128)(2,1)S(1)}, u32[]{:S(2)}, u32[]{:S(2)}) collective-permute-start(bf16[128,1536]{1,0:T(8,128)(2,1)S(1)} %get-tuple-element.65.b0), channel_id=1, source_target_pairs={{0,8},{8,0},{16,24},{24,16},{1,9},{9,1},{17,25},{25,17},{2,10},{10... | collective-permute-start | bytes 1179656 | tf_op jit(solution)/shard_map/ppermute | solution.py:235
  12.8 18.0 %collective-permute-start.8 = (bf16[128,1536]{1,0:T(8,128)(2,1)S(1)}, bf16[128,1536]{1,0:T(8,128)(2,1)S(1)}, u32[]{:S(2)}, u32[]{:S(2)}) collective-permute-start(bf16[128,1536]{1,0:T(8,128)(2,1)S(1)} %get-tuple-element.65.b0), channel_id=1, source_target_pairs={{0,16},{8,24},{16,0},{24,8},{1,17},{9,25},{17,1},{25,9},{2,18},{10... | collective-permute-start | bytes 1179656 | tf_op jit(solution)/shard_map/ppermute | solution.py:235
  14.2 31.8 %collective-permute-start.24 = (bf16[256,1536]{0,1:T(8,128)(2,1)S(1)}, bf16[256,1536]{0,1:T(8,128)(2,1)S(1)}, u32[]{:S(2)}, u32[]{:S(2)}) collective-permute-start(bf16[256,1536]{0,1:T(8,128)(2,1)S(1)} %copy.16), channel_id=1, source_target_pairs={{0,1},{1,0},{2,3},{3,2},{4,5},{5,4},{6,7},{7,6},{8,9},{9,8},{10,11... | collective-permute-start | bytes 2359304 | tf_op jit(solution)/shard_map/ppermute | solution.py:235
  22.2 24.8 %collective-permute-start.1 = (bf16[128,1536]{1,0:T(8,128)(2,1)}, bf16[128,1536]{1,0:T(8,128)(2,1)S(1)}, u32[]{:S(2)}, u32[]{:S(2)}) collective-permute-start(bf16[128,1536]{1,0:T(8,128)(2,1)} %after.1.b0), channel_id=1, source_target_pairs={{0,8},{8,0},{16,24},{24,16},{1,9},{9,1},{17,25},{25,17},{2,10},{10... | collective-permute-start | bytes 1179656 | tf_op jit(solution)/shard_map/ppermute | solution.py:235
  22.2 25.5 %collective-permute-start.2 = (bf16[128,1536]{1,0:T(8,128)(2,1)}, bf16[128,1536]{1,0:T(8,128)(2,1)}, u32[]{:S(2)}, u32[]{:S(2)}) collective-permute-start(bf16[128,1536]{1,0:T(8,128)(2,1)} %after.1.b0), channel_id=1, source_target_pairs={{0,16},{8,24},{16,0},{24,8},{1,17},{9,25},{17,1},{25,9},{2,18},{10... | collective-permute-start | bytes 1179656 | tf_op jit(solution)/shard_map/ppermute | solution.py:235
  25.9 4.8 %copy-start.22 = (bf16[128,1536]{1,0:T(8,128)(2,1)}, bf16[128,1536]{1,0:T(8,128)(2,1)S(1)}, u32[]{:S(2)}) copy-start(bf16[128,1536]{1,0:T(8,128)(2,1)S(1)} %collective-permute-done.7.b1) | copy-start | bytes 1179652
  25.9 21.8 %collective-permute-start.3 = (bf16[128,1536]{1,0:T(8,128)(2,1)}, bf16[128,1536]{1,0:T(8,128)(2,1)}, u32[]{:S(2)}, u32[]{:S(2)}) collective-permute-start(bf16[128,1536]{1,0:T(8,128)(2,1)} %after.1.b0), channel_id=1, source_target_pairs={{0,24},{8,16},{16,8},{24,0},{1,25},{9,17},{17,9},{25,1},{2,26},{10... | collective-permute-start | bytes 1179656 | tf_op jit(solution)/shard_map/ppermute | solution.py:235
  42.9 18.6 %collective-permute-start.10 = (bf16[128,3072]{1,0:T(8,128)(2,1)}, bf16[128,3072]{1,0:T(8,128)(2,1)S(1)}, u32[]{:S(2)}, u32[]{:S(2)}) collective-permute-start(bf16[128,3072]{1,0:T(8,128)(2,1)} %get-tuple-element.38), channel_id=1, source_target_pairs={{0,32},{32,0},{1,33},{33,1},{2,34},{34,2},{3,35},{35,3},{4,36},{36... | collective-permute-start | bytes 2359304 | tf_op jit(solution)/shard_map/ppermute | solution.py:235
  46.9 14.6 %copy-start.4 = (bf16[128,3072]{1,0:T(8,128)(2,1)S(1)}, bf16[128,3072]{1,0:T(8,128)(2,1)}, u32[]{:S(2)}) copy-start(bf16[128,3072]{1,0:T(8,128)(2,1)} %get-tuple-element.37) | copy-start | bytes 2359300
  46.9 223.2 %reduce-scatter.2.cloned.1.call-start = ((), (), s32[]{:S(2)}) async-start(), calls=%async_computation.2 | async-start | bytes 1966080 | tf_op jit(solution)/shard_map/reduce_scatter | solution.py:270
  59.2 5.4 %copy-start.6 = (bf16[128,3072]{1,0:T(8,128)(2,1)S(1)}, bf16[128,3072]{1,0:T(8,128)(2,1)}, u32[]{:S(2)}) copy-start(bf16[128,3072]{1,0:T(8,128)(2,1)} %get-tuple-element.33) | copy-start | bytes 2359300
  59.2 5.4 %collective-permute-start.5 = (bf16[128,3072]{1,0:T(8,128)(2,1)}, bf16[128,3072]{1,0:T(8,128)(2,1)S(1)}, u32[]{:S(2)}, u32[]{:S(2)}) collective-permute-start(bf16[128,3072]{1,0:T(8,128)(2,1)} %get-tuple-element.34), channel_id=1, source_target_pairs={{0,32},{32,0},{1,33},{33,1},{2,34},{34,2},{3,35},{35,3},{4,36},{36... | collective-permute-start | bytes 2359304 | tf_op jit(solution)/shard_map/ppermute | solution.py:235
  61.0 5.1 %collective-permute-start.9 = (bf16[128,3072]{1,0:T(8,128)(2,1)}, bf16[128,3072]{1,0:T(8,128)(2,1)S(1)}, u32[]{:S(2)}, u32[]{:S(2)}) collective-permute-start(bf16[128,3072]{1,0:T(8,128)(2,1)} %get-tuple-element.36), channel_id=1, source_target_pairs={{0,32},{32,0},{1,33},{33,1},{2,34},{34,2},{3,35},{35,3},{4,36},{36... | collective-permute-start | bytes 2359304 | tf_op jit(solution)/shard_map/ppermute | solution.py:235
  61.1 26.1 %collective-permute-start.4 = (bf16[128,3072]{1,0:T(8,128)(2,1)}, bf16[128,3072]{1,0:T(8,128)(2,1)}, u32[]{:S(2)}, u32[]{:S(2)}) collective-permute-start(bf16[128,3072]{1,0:T(8,128)(2,1)} %get-tuple-element.32), channel_id=1, source_target_pairs={{0,32},{32,0},{1,33},{33,1},{2,34},{34,2},{3,35},{35,3},{4,36},{36... | collective-permute-start | bytes 2359304 | tf_op jit(solution)/shard_map/ppermute | solution.py:235
  61.7 20.7 %collective-permute-start.11 = (bf16[128,3072]{1,0:T(8,128)(2,1)S(1)}, bf16[128,3072]{1,0:T(8,128)(2,1)S(1)}, u32[]{:S(2)}, u32[]{:S(2)}) collective-permute-start(bf16[128,3072]{1,0:T(8,128)(2,1)S(1)} %add_convert_fusion.1), channel_id=1, source_target_pairs={{0,64},{64,0},{1,65},{65,1},{2,66},{66,2},{3,67},{67,3},{4,68},{68... | collective-permute-start | bytes 2359304 | tf_op jit(solution)/shard_map/ppermute | solution.py:235
  64.7 34.6 %collective-permute-start.6 = (bf16[128,3072]{1,0:T(8,128)(2,1)S(1)}, bf16[128,3072]{1,0:T(8,128)(2,1)}, u32[]{:S(2)}, u32[]{:S(2)}) collective-permute-start(bf16[128,3072]{1,0:T(8,128)(2,1)S(1)} %add_convert_fusion.2), channel_id=1, source_target_pairs={{0,64},{64,0},{1,65},{65,1},{2,66},{66,2},{3,67},{67,3},{4,68},{68... | collective-permute-start | bytes 2359304 | tf_op jit(solution)/shard_map/ppermute | solution.py:235
  66.1 16.3 %copy-start.5 = (bf16[128,3072]{1,0:T(8,128)(2,1)}, bf16[128,3072]{1,0:T(8,128)(2,1)S(1)}, u32[]{:S(2)}) copy-start(bf16[128,3072]{1,0:T(8,128)(2,1)S(1)} %collective-permute-done.9.core_ref) | copy-start | bytes 2359300
  103.2 8.1 %collective-permute-start.25 = (bf16[256,512]{1,0:T(8,128)(2,1)}, bf16[256,512]{1,0:T(8,128)(2,1)S(1)}, u32[]{:S(2)}, u32[]{:S(2)}) collective-permute-start(bf16[256,512]{1,0:T(8,128)(2,1)} %get-tuple-element.56), channel_id=1, source_target_pairs={{0,1},{1,0},{2,3},{3,2},{4,5},{5,4},{6,7},{7,6},{8,9},{9,8},{10,11... | collective-permute-start | bytes 786440 | tf_op jit(solution)/shard_map/ppermute | solution.py:235
  104.5 49.4 %collective-permute-start.15 = (bf16[256,1024]{1,0:T(8,128)(2,1)}, bf16[256,1024]{1,0:T(8,128)(2,1)S(1)}, u32[]{:S(2)}, u32[]{:S(2)}) collective-permute-start(bf16[256,1024]{1,0:T(8,128)(2,1)} %get-tuple-element.47.refs_0_), channel_id=1, source_target_pairs={{0,64},{64,0},{1,65},{65,1},{2,66},{66,2},{3,67},{67,3},{4,68},{68... | collective-permute-start | bytes 1572872 | tf_op jit(solution)/shard_map/ppermute | solution.py:235
  107.0 47.0 %collective-permute-start.12 = (bf16[256,1024]{1,0:T(8,128)(2,1)}, bf16[256,1024]{1,0:T(8,128)(2,1)S(1)}, u32[]{:S(2)}, u32[]{:S(2)}) collective-permute-start(bf16[256,1024]{1,0:T(8,128)(2,1)} %get-tuple-element.47.refs_0_), channel_id=1, source_target_pairs={{0,32},{32,0},{1,33},{33,1},{2,34},{34,2},{3,35},{35,3},{4,36},{36... | collective-permute-start | bytes 1572872 | tf_op jit(solution)/shard_map/ppermute | solution.py:235
  108.4 46.5 %collective-permute-start.16 = (bf16[256,1024]{1,0:T(8,128)(2,1)}, bf16[256,1024]{1,0:T(8,128)(2,1)S(1)}, u32[]{:S(2)}, u32[]{:S(2)}) collective-permute-start(bf16[256,1024]{1,0:T(8,128)(2,1)} %get-tuple-element.48.refs_1_.refs_0_), channel_id=1, source_target_pairs={{0,64},{64,0},{1,65},{65,1},{2,66},{66,2},{3,67},{67,3},{4,68},{68... | collective-permute-start | bytes 1572872 | tf_op jit(solution)/shard_map/ppermute | solution.py:235
  108.9 71.3 %copy-start.1 = (bf16[512,1536]{1,0:T(8,128)(2,1)S(1)}, bf16[512,1536]{1,0:T(8,128)(2,1)}, u32[]{:S(2)}) copy-start(bf16[512,1536]{1,0:T(8,128)(2,1)} %get-tuple-element.54) | copy-start | bytes 4718596
  108.9 46.3 %collective-permute-start.17 = (bf16[256,1024]{1,0:T(8,128)(2,1)}, bf16[256,1024]{1,0:T(8,128)(2,1)S(1)}, u32[]{:S(2)}, u32[]{:S(2)}) collective-permute-start(bf16[256,1024]{1,0:T(8,128)(2,1)} %get-tuple-element.49.refs_2_.refs_0_), channel_id=1, source_target_pairs={{0,64},{64,0},{1,65},{65,1},{2,66},{66,2},{3,67},{67,3},{4,68},{68... | collective-permute-start | bytes 1572872 | tf_op jit(solution)/shard_map/ppermute | solution.py:235
  111.4 64.9 %copy-start.27 = (bf16[256,512]{1,0:T(8,128)(2,1)}, bf16[256,512]{1,0:T(8,128)(2,1)S(1)}, u32[]{:S(2)}) copy-start(bf16[256,512]{1,0:T(8,128)(2,1)S(1)} %collective-permute-done.25.refs_4_) | copy-start | bytes 786436
  111.4 42.0 %collective-permute-start.27 = (bf16[256,512]{1,0:T(8,128)(2,1)}, bf16[256,512]{1,0:T(8,128)(2,1)}, u32[]{:S(2)}, u32[]{:S(2)}) collective-permute-start(bf16[256,512]{1,0:T(8,128)(2,1)} %get-tuple-element.56), channel_id=1, source_target_pairs={{0,65},{1,64},{64,1},{65,0},{2,67},{3,66},{66,3},{67,2},{4,69},{5,... | collective-permute-start | bytes 786440 | tf_op jit(solution)/shard_map/ppermute | solution.py:266
  153.4 2.2 collective-permute-start.13
  153.9 4.2 %copy-start.19 = (bf16[256,1024]{1,0:T(8,128)(2,1)}, bf16[256,1024]{1,0:T(8,128)(2,1)S(1)}, u32[]{:S(2)}) copy-start(bf16[256,1024]{1,0:T(8,128)(2,1)S(1)} %collective-permute-done.15.refs_6_.refs_2_) | copy-start | bytes 1572868
  153.9 3.2 %collective-permute-start.14 = (bf16[256,1024]{1,0:T(8,128)(2,1)}, bf16[256,1024]{1,0:T(8,128)(2,1)S(1)}, u32[]{:S(2)}, u32[]{:S(2)}) collective-permute-start(bf16[256,1024]{1,0:T(8,128)(2,1)} %get-tuple-element.49.refs_2_.refs_0_), channel_id=1, source_target_pairs={{0,32},{32,0},{1,33},{33,1},{2,34},{34,2},{3,35},{35,3},{4,36},{36... | collective-permute-start | bytes 1572872 | tf_op jit(solution)/shard_map/ppermute | solution.py:235
  153.9 3.5 %collective-permute-start.18 = (bf16[256,1024]{1,0:T(8,128)(2,1)S(1)}, bf16[256,1024]{1,0:T(8,128)(2,1)S(1)}, u32[]{:S(2)}, u32[]{:S(2)}) collective-permute-start(bf16[256,1024]{1,0:T(8,128)(2,1)S(1)} %collective-permute-done.15.refs_6_.refs_2_), channel_id=1, source_target_pairs={{0,32},{32,0},{1,33},{33,1},{2,34},{34,2},{3,35},{35,3},{4,36},{36... | collective-permute-start | bytes 1572872 | tf_op jit(solution)/shard_map/ppermute | solution.py:235
  154.9 4.2 %copy-start.15 = (bf16[256,1024]{1,0:T(8,128)(2,1)}, bf16[256,1024]{1,0:T(8,128)(2,1)S(1)}, u32[]{:S(2)}) copy-start(bf16[256,1024]{1,0:T(8,128)(2,1)S(1)} %collective-permute-done.16.refs_7_.refs_2_) | copy-start | bytes 1572868
  154.9 3.1 %collective-permute-start.19 = (bf16[256,1024]{1,0:T(8,128)(2,1)S(1)}, bf16[256,1024]{1,0:T(8,128)(2,1)S(1)}, u32[]{:S(2)}, u32[]{:S(2)}) collective-permute-start(bf16[256,1024]{1,0:T(8,128)(2,1)S(1)} %collective-permute-done.16.refs_7_.refs_2_), channel_id=1, source_target_pairs={{0,32},{32,0},{1,33},{33,1},{2,34},{34,2},{3,35},{35,3},{4,36},{36... | collective-permute-start | bytes 1572872 | tf_op jit(solution)/shard_map/ppermute | solution.py:235
  155.2 3.9 %copy-start.13 = (bf16[256,1024]{1,0:T(8,128)(2,1)}, bf16[256,1024]{1,0:T(8,128)(2,1)S(1)}, u32[]{:S(2)}) copy-start(bf16[256,1024]{1,0:T(8,128)(2,1)S(1)} %collective-permute-done.17.refs_8_.refs_2_) | copy-start | bytes 1572868
  155.2 3.9 %collective-permute-start.20 = (bf16[256,1024]{1,0:T(8,128)(2,1)S(1)}, bf16[256,1024]{1,0:T(8,128)(2,1)S(1)}, u32[]{:S(2)}, u32[]{:S(2)}) collective-permute-start(bf16[256,1024]{1,0:T(8,128)(2,1)S(1)} %collective-permute-done.17.refs_8_.refs_2_), channel_id=1, source_target_pairs={{0,32},{32,0},{1,33},{33,1},{2,34},{34,2},{3,35},{35,3},{4,36},{36... | collective-permute-start | bytes 1572872 | tf_op jit(solution)/shard_map/ppermute | solution.py:235
  155.6 2.4 copy-start.17
  155.6 27.9 %collective-permute-start.26 = (bf16[256,512]{1,0:T(8,128)(2,1)S(1)}, bf16[256,512]{1,0:T(8,128)(2,1)}, u32[]{:S(2)}, u32[]{:S(2)}) collective-permute-start(bf16[256,512]{1,0:T(8,128)(2,1)S(1)} %collective-permute-done.25.refs_4_), channel_id=1, source_target_pairs={{0,32},{32,0},{1,33},{33,1},{2,34},{34,2},{3,35},{35,3},{4,36},{36... | collective-permute-start | bytes 786440 | tf_op jit(solution)/shard_map/ppermute | solution.py:235
  157.1 2.0 copy-start.14
  157.1 26.4 %collective-permute-start.28 = (bf16[256,512]{1,0:T(8,128)(2,1)}, bf16[256,512]{1,0:T(8,128)(2,1)}, u32[]{:S(2)}, u32[]{:S(2)}) collective-permute-start(bf16[256,512]{1,0:T(8,128)(2,1)} %collective-permute-done.27.refs_6_), channel_id=1, source_target_pairs={{0,32},{32,0},{1,33},{33,1},{2,34},{34,2},{3,35},{35,3},{4,36},{36... | collective-permute-start | bytes 786440 | tf_op jit(solution)/shard_map/ppermute | solution.py:235
  176.2 28.4 %collective-permute-start.21 = (bf16[256,1536]{1,0:T(8,128)(2,1)}, bf16[256,1536]{1,0:T(8,128)(2,1)}, u32[]{:S(2)}, u32[]{:S(2)}) collective-permute-start(bf16[256,1536]{1,0:T(8,128)(2,1)} %get-tuple-element.51), channel_id=1, source_target_pairs={{0,16},{8,24},{16,0},{24,8},{1,17},{9,25},{17,1},{25,9},{2,18},{10... | collective-permute-start | bytes 2359304 | tf_op jit(solution)/shard_map/ppermute | solution.py:235
  178.0 36.3 %collective-permute-start.22 = (bf16[256,1536]{1,0:T(8,128)(2,1)}, bf16[256,1536]{1,0:T(8,128)(2,1)}, u32[]{:S(2)}, u32[]{:S(2)}) collective-permute-start(bf16[256,1536]{1,0:T(8,128)(2,1)} %get-tuple-element.52), channel_id=1, source_target_pairs={{0,8},{8,0},{16,24},{24,16},{1,9},{9,1},{17,25},{25,17},{2,10},{10... | collective-permute-start | bytes 2359304 | tf_op jit(solution)/shard_map/ppermute | solution.py:235
  179.6 35.7 %collective-permute-start.23 = (bf16[256,1536]{1,0:T(8,128)(2,1)}, bf16[256,1536]{1,0:T(8,128)(2,1)}, u32[]{:S(2)}, u32[]{:S(2)}) collective-permute-start(bf16[256,1536]{1,0:T(8,128)(2,1)} %get-tuple-element.53), channel_id=1, source_target_pairs={{0,24},{8,16},{16,8},{24,0},{1,25},{9,17},{17,9},{25,1},{2,26},{10... | collective-permute-start | bytes 2359304 | tf_op jit(solution)/shard_map/ppermute | solution.py:235
  180.2 1.6 copy-start.2
  183.5 9.5 %collective-permute-start.29 = (bf16[256,512]{1,0:T(8,128)(2,1)S(1)}, bf16[256,512]{1,0:T(8,128)(2,1)S(1)}, u32[]{:S(2)}, u32[]{:S(2)}) collective-permute-start(bf16[256,512]{1,0:T(8,128)(2,1)S(1)} %copy-done.11), channel_id=1, source_target_pairs={{0,1},{1,0},{2,3},{3,2},{4,5},{5,4},{6,7},{7,6},{8,9},{9,8},{10,11... | collective-permute-start | bytes 786440 | tf_op jit(solution)/shard_map/ppermute | solution.py:235
  183.5 11.2 %collective-permute-start.31 = (bf16[256,512]{1,0:T(8,128)(2,1)S(1)}, bf16[256,512]{1,0:T(8,128)(2,1)S(1)}, u32[]{:S(2)}, u32[]{:S(2)}) collective-permute-start(bf16[256,512]{1,0:T(8,128)(2,1)S(1)} %copy-done.11), channel_id=1, source_target_pairs={{0,65},{1,64},{64,1},{65,0},{2,67},{3,66},{66,3},{67,2},{4,69},{5,... | collective-permute-start | bytes 786440 | tf_op jit(solution)/shard_map/ppermute | solution.py:266
  193.0 22.4 %copy-start.8 = (bf16[256,1536]{1,0:T(8,128)(2,1)S(1)}, bf16[256,1536]{1,0:T(8,128)(2,1)}, u32[]{:S(2)}) copy-start(bf16[256,1536]{1,0:T(8,128)(2,1)} %get-tuple-element.50) | copy-start | bytes 2359300
  193.0 25.2 %copy-start.26 = (bf16[256,512]{1,0:T(8,128)(2,1)}, bf16[256,512]{1,0:T(8,128)(2,1)S(1)}, u32[]{:S(2)}) copy-start(bf16[256,512]{1,0:T(8,128)(2,1)S(1)} %collective-permute-done.29.refs_4_) | copy-start | bytes 786436
  194.0 6.4 %collective-permute-start.36 = (bf16[256,512]{1,0:T(8,128)(2,1)S(1)}, bf16[256,512]{1,0:T(8,128)(2,1)S(1)}, u32[]{:S(2)}, u32[]{:S(2)}) collective-permute-start(bf16[256,512]{1,0:T(8,128)(2,1)S(1)} %copy-done.12), channel_id=1, source_target_pairs={{0,1},{1,0},{2,3},{3,2},{4,5},{5,4},{6,7},{7,6},{8,9},{9,8},{10,11... | collective-permute-start | bytes 786440 | tf_op jit(solution)/shard_map/ppermute | solution.py:235
  194.6 23.6 %copy-start.28 = (bf16[256,512]{1,0:T(8,128)(2,1)}, bf16[256,512]{1,0:T(8,128)(2,1)S(1)}, u32[]{:S(2)}) copy-start(bf16[256,512]{1,0:T(8,128)(2,1)S(1)} %collective-permute-done.31.refs_6_) | copy-start | bytes 786436
  194.6 8.0 %collective-permute-start.38 = (bf16[256,512]{1,0:T(8,128)(2,1)S(1)}, bf16[256,512]{1,0:T(8,128)(2,1)S(1)}, u32[]{:S(2)}, u32[]{:S(2)}) collective-permute-start(bf16[256,512]{1,0:T(8,128)(2,1)S(1)} %copy-done.12), channel_id=1, source_target_pairs={{0,65},{1,64},{64,1},{65,0},{2,67},{3,66},{66,3},{67,2},{4,69},{5,... | collective-permute-start | bytes 786440 | tf_op jit(solution)/shard_map/ppermute | solution.py:266
  200.3 17.9 %copy-start.25 = (bf16[256,512]{1,0:T(8,128)(2,1)}, bf16[256,512]{1,0:T(8,128)(2,1)S(1)}, u32[]{:S(2)}) copy-start(bf16[256,512]{1,0:T(8,128)(2,1)S(1)} %collective-permute-done.36.refs_4_) | copy-start | bytes 786436
  200.3 17.9 %collective-permute-start.30 = (bf16[256,512]{1,0:T(8,128)(2,1)S(1)}, bf16[256,512]{1,0:T(8,128)(2,1)S(1)}, u32[]{:S(2)}, u32[]{:S(2)}) collective-permute-start(bf16[256,512]{1,0:T(8,128)(2,1)S(1)} %collective-permute-done.29.refs_4_), channel_id=1, source_target_pairs={{0,32},{32,0},{1,33},{33,1},{2,34},{34,2},{3,35},{35,3},{4,36},{36... | collective-permute-start | bytes 786440 | tf_op jit(solution)/shard_map/ppermute | solution.py:235
  202.7 15.6 %copy-start.29 = (bf16[256,512]{1,0:T(8,128)(2,1)}, bf16[256,512]{1,0:T(8,128)(2,1)S(1)}, u32[]{:S(2)}) copy-start(bf16[256,512]{1,0:T(8,128)(2,1)S(1)} %collective-permute-done.38.refs_6_) | copy-start | bytes 786436
  202.7 15.6 %collective-permute-start.32 = (bf16[256,512]{1,0:T(8,128)(2,1)S(1)}, bf16[256,512]{1,0:T(8,128)(2,1)S(1)}, u32[]{:S(2)}, u32[]{:S(2)}) collective-permute-start(bf16[256,512]{1,0:T(8,128)(2,1)S(1)} %collective-permute-done.31.refs_6_), channel_id=1, source_target_pairs={{0,32},{32,0},{1,33},{33,1},{2,34},{34,2},{3,35},{35,3},{4,36},{36... | collective-permute-start | bytes 786440 | tf_op jit(solution)/shard_map/ppermute | solution.py:235
  204.6 29.6 %collective-permute-start.37 = (bf16[256,512]{1,0:T(8,128)(2,1)S(1)}, bf16[256,512]{1,0:T(8,128)(2,1)S(1)}, u32[]{:S(2)}, u32[]{:S(2)}) collective-permute-start(bf16[256,512]{1,0:T(8,128)(2,1)S(1)} %collective-permute-done.36.refs_4_), channel_id=1, source_target_pairs={{0,32},{32,0},{1,33},{33,1},{2,34},{34,2},{3,35},{35,3},{4,36},{36... | collective-permute-start | bytes 786440 | tf_op jit(solution)/shard_map/ppermute | solution.py:235
  214.3 19.9 %collective-permute-start.39 = (bf16[256,512]{1,0:T(8,128)(2,1)S(1)}, bf16[256,512]{1,0:T(8,128)(2,1)S(1)}, u32[]{:S(2)}, u32[]{:S(2)}) collective-permute-start(bf16[256,512]{1,0:T(8,128)(2,1)S(1)} %collective-permute-done.38.refs_6_), channel_id=1, source_target_pairs={{0,32},{32,0},{1,33},{33,1},{2,34},{34,2},{3,35},{35,3},{4,36},{36... | collective-permute-start | bytes 786440 | tf_op jit(solution)/shard_map/ppermute | solution.py:235
  229.7 19.2 %collective-permute-start.33 = (bf16[1536,128]{1,0:T(8,128)(2,1)S(1)}, bf16[1536,128]{1,0:T(8,128)(2,1)S(1)}, u32[]{:S(2)}, u32[]{:S(2)}) collective-permute-start(bf16[1536,128]{1,0:T(8,128)(2,1)S(1)} %get-tuple-element.59), channel_id=1, source_target_pairs={{0,4},{2,6},{4,0},{6,2},{1,5},{3,7},{5,1},{7,3},{8,12},{10,14},{12... | collective-permute-start | bytes 1179656 | tf_op jit(solution)/shard_map/ppermute | solution.py:235
  233.4 18.5 %collective-permute-start.34 = (bf16[1536,128]{1,0:T(8,128)(2,1)S(1)}, bf16[1536,128]{1,0:T(8,128)(2,1)S(1)}, u32[]{:S(2)}, u32[]{:S(2)}) collective-permute-start(bf16[1536,128]{1,0:T(8,128)(2,1)S(1)} %get-tuple-element.61), channel_id=1, source_target_pairs={{0,2},{2,0},{4,6},{6,4},{1,3},{3,1},{5,7},{7,5},{8,10},{10,8},{12,... | collective-permute-start | bytes 1179656 | tf_op jit(solution)/shard_map/ppermute | solution.py:235
  234.2 17.8 %collective-permute-start.35 = (bf16[1536,128]{1,0:T(8,128)(2,1)S(1)}, bf16[1536,128]{1,0:T(8,128)(2,1)S(1)}, u32[]{:S(2)}, u32[]{:S(2)}) collective-permute-start(bf16[1536,128]{1,0:T(8,128)(2,1)S(1)} %get-tuple-element.60), channel_id=1, source_target_pairs={{0,6},{2,4},{4,2},{6,0},{1,7},{3,5},{5,3},{7,1},{8,14},{10,12},{12... | collective-permute-start | bytes 1179656 | tf_op jit(solution)/shard_map/ppermute | solution.py:235
  245.6 14.3 %collective-permute-start.40 = (bf16[1536,128]{1,0:T(8,128)(2,1)S(1)}, bf16[1536,128]{1,0:T(8,128)(2,1)S(1)}, u32[]{:S(2)}, u32[]{:S(2)}) collective-permute-start(bf16[1536,128]{1,0:T(8,128)(2,1)S(1)} %get-tuple-element.62), channel_id=1, source_target_pairs={{0,4},{2,6},{4,0},{6,2},{1,5},{3,7},{5,1},{7,3},{8,12},{10,14},{12... | collective-permute-start | bytes 1179656 | tf_op jit(solution)/shard_map/ppermute | solution.py:235
  248.2 20.7 %collective-permute-start.41 = (bf16[1536,128]{1,0:T(8,128)(2,1)S(1)}, bf16[1536,128]{1,0:T(8,128)(2,1)S(1)}, u32[]{:S(2)}, u32[]{:S(2)}) collective-permute-start(bf16[1536,128]{1,0:T(8,128)(2,1)S(1)} %get-tuple-element.64), channel_id=1, source_target_pairs={{0,2},{2,0},{4,6},{6,4},{1,3},{3,1},{5,7},{7,5},{8,10},{10,8},{12,... | collective-permute-start | bytes 1179656 | tf_op jit(solution)/shard_map/ppermute | solution.py:235
  248.9 19.9 %collective-permute-start.42 = (bf16[1536,128]{1,0:T(8,128)(2,1)S(1)}, bf16[1536,128]{1,0:T(8,128)(2,1)S(1)}, u32[]{:S(2)}, u32[]{:S(2)}) collective-permute-start(bf16[1536,128]{1,0:T(8,128)(2,1)S(1)} %get-tuple-element.63), channel_id=1, source_target_pairs={{0,6},{2,4},{4,2},{6,0},{1,7},{3,5},{5,3},{7,1},{8,14},{10,12},{12... | collective-permute-start | bytes 1179656 | tf_op jit(solution)/shard_map/ppermute | solution.py:235
  (15 other events, 12.8 us)
Sparse Core Ops, SparseCore 0:
  47.1 44.1 all-gather.1
  193.1 27.9 reduce-scatter.1

commit v3 on v0

v3 whole, which is shorter than its diff:
```python
import jax
import jax.numpy as jnp
from jax import lax
from jax.experimental import pallas as pl
from jax.experimental.pallas import tpu as pltpu
from jax.sharding import Mesh
from jax.sharding import PartitionSpec as P

K = 1536
F = 3072
S = 256
H = 128
DEPTH = 8
LANE = 128
UNITS = F // (DEPTH * LANE)
CHUNKS = ((0, 2), (2, 1))
N = len(CHUNKS)
gelu_coef = 0.7978845608028654
bf16 = jnp.bfloat16
f32 = jnp.float32
MIB = 1 << 20
TF, TG, TK, TE = 0.01, 30, 3, 300
LATE = True
ANY = pl.BlockSpec(memory_space=pl.ANY)
PARAMS = pltpu.CompilerParams(vmem_limit_bytes=63 * MIB)


def cost(micros):
    return pl.CostEstimate(flops=int(micros * 1.15e9), bytes_accessed=int(micros * 3.6e6), transcendentals=0)


def width(chunk):
    return DEPTH * CHUNKS[chunk][1] * LANE


def after_kernel(*refs):
    pass


def after(values, other, micros=300):
    return pl.pallas_call(
        after_kernel,
        in_specs=[ANY] * (len(values) + 1),
        out_specs=[ANY] * len(values),
        out_shape=[jax.ShapeDtypeStruct(value.shape, value.dtype) for value in values],
        input_output_aliases={n: n for n in range(len(values))},
        cost_estimate=cost(micros),
        name="after",
    )(*values, other)


def partial_kernel(q_ref, b0, b1, b2, b3, w_ref, *refs):
    p0_ref, p1_ref, p2_ref, p3_ref, tk_ref = refs[-5:]

    @pl.when(pl.program_id(0) == 0)
    def _():
        q = q_ref[0]
        for m, block in enumerate((b0, b1, b2, b3)):
            slot = pl.multiple_of(jnp.bitwise_xor(q, m) * H, H)
            tk_ref[pl.ds(slot, H), :] = block[...]

    term = jnp.dot(tk_ref[...], w_ref[...], preferred_element_type=f32).astype(bf16)
    for k, ref in enumerate((p0_ref, p1_ref, p2_ref, p3_ref)):
        ref[...] = term[k * H:(k + 1) * H, :]


def block_partials(q, blocks, weight, part, earlier, wait):
    tile = 1024
    rows = [pl.BlockSpec((H, K), lambda i, q, at=part if block.shape[0] == S else 0: (at, 0)) for block in blocks]
    grid_spec = pltpu.PrefetchScalarGridSpec(
        num_scalar_prefetch=1,
        grid=(F // tile,),
        in_specs=rows + [pl.BlockSpec((K, tile), lambda i, q: (0, i))] + [ANY] * (len(earlier) + len(wait)),
        out_specs=[pl.BlockSpec((H, tile), lambda i, q: (0, i))] * 4
        + [pl.BlockSpec((4 * H, K), lambda i, q: (part, 0))],
    )
    return pl.pallas_call(
        partial_kernel,
        grid_spec=grid_spec,
        out_shape=[jax.ShapeDtypeStruct((H, F), bf16)] * 4 + [jax.ShapeDtypeStruct((4 * S, K), bf16)],
        input_output_aliases={6: 4} if earlier else {},
        compiler_params=PARAMS,
        cost_estimate=cost(TF),
        name="block_partials",
    )(q, *blocks, weight, *earlier, *wait)


def gelu_kernel(n_pg, xl_ref, own_ref, core_ref, far_ref, cot_ref, *refs):
    outs = refs[-(1 + n_pg + N):]
    xl = xl_ref[0]
    act_ref, pgs, halves = outs[0], outs[1 + N:], outs[1:1 + N]
    base = 0
    for chunk, (start, units) in enumerate(CHUNKS):
        size = units * LANE
        pieces = []
        for d in range(DEPTH):
            at = slice(d * UNITS * LANE + start * LANE, d * UNITS * LANE + start * LANE + size)
            pre = own_ref[:, at].astype(f32) + core_ref[:, at].astype(f32) + far_ref[:, at].astype(f32)
            inner = gelu_coef * (pre + 0.044715 * pre * pre * pre)
            tangent = jnp.tanh(inner)
            act_ref[:, at] = (0.5 * pre * (1.0 + tangent)).astype(bf16)
            slope = 0.5 * (1.0 + tangent) + 0.5 * pre * (1.0 - tangent * tangent) * gelu_coef * (
                1.0 + 3.0 * 0.044715 * pre * pre
            )
            grad = (cot_ref[:, at].astype(f32) * slope).astype(bf16)
            if n_pg == 1:
                pgs[0][:, base + d * size:base + (d + 1) * size] = grad
            else:
                pgs[chunk][:, d * size:(d + 1) * size] = grad
            pieces.append(grad)
            if d % 2:
                z = d // 2
                halves[chunk][:, z * size:(z + 1) * size] = jnp.where(xl == 0, pieces[d], pieces[d - 1])
        base += DEPTH * size


def gelu_pair(xl, own, core, far, cot, part, earlier, wait):
    rows = 64
    steps = H // rows
    widths = [width(chunk) for chunk in range(N)] if part else [F]
    whole = lambda w: pl.BlockSpec((rows, w), lambda i, x: (i + part * steps, 0))
    local = lambda w: pl.BlockSpec((rows, w), lambda i, x: (i, 0))
    grid_spec = pltpu.PrefetchScalarGridSpec(
        num_scalar_prefetch=1,
        grid=(steps,),
        in_specs=[local(F)] * 3 + [whole(F)] + [ANY] * (len(earlier) + len(wait)),
        out_specs=[whole(F)] + [whole(width(chunk) // 2) for chunk in range(N)] + [local(w) for w in widths],
    )
    outs = pl.pallas_call(
        lambda *refs: gelu_kernel(len(widths), *refs),
        grid_spec=grid_spec,
        out_shape=[jax.ShapeDtypeStruct((S, F), bf16)]
        + [jax.ShapeDtypeStruct((S, width(chunk) // 2), bf16) for chunk in range(N)]
        + [jax.ShapeDtypeStruct((H, w), bf16) for w in widths],
        input_output_aliases={5 + i: i for i in range(len(earlier))},
        compiler_params=PARAMS,
        cost_estimate=cost(TG),
        name="gelu_pair",
    )(xl, own, core, far, cot, *earlier, *wait)
    return outs[:1 + N], outs[1 + N:]


def weight_kernel(size, ids_ref, tk_ref, tx_ref, *refs):
    first, second, other = refs[:4], refs[4:8], refs[8:12]
    out_ref, pg = refs[-2:]

    @pl.when(pl.program_id(0) == 0)
    def _():
        xl, r = ids_ref[0], ids_ref[1]
        for k in range(4):
            for z in range(4):
                at = pl.multiple_of((2 * z + xl) * size, size)
                for part, grads in enumerate((first, second)):
                    row = (4 * part + k) * H
                    pg[row:row + H, z * size:(z + 1) * size] = grads[k][:, pl.ds(at, size)]
            slot = pl.multiple_of(4 * S + jnp.bitwise_xor(r, k) * S, S)
            pg[pl.ds(slot, S), :] = other[k][...]

    tokens = jnp.concatenate([tk_ref[...], tx_ref[...]], axis=0)
    total = lax.dot_general(tokens, pg[...], (((0,), (0,)), ((), ())), preferred_element_type=f32).astype(bf16)
    for z in range(4):
        out_ref[z] = total[:, z * size:(z + 1) * size]


def weight_part(ids, tk, tx, first, second, other, chunk, wait):
    rows = 512
    w = width(chunk)
    size = CHUNKS[chunk][1] * LANE
    before = sum(width(c) for c in range(chunk))
    assert before % w == 0
    grid_spec = pltpu.PrefetchScalarGridSpec(
        num_scalar_prefetch=1,
        grid=(K // rows,),
        in_specs=[pl.BlockSpec((4 * S, rows), lambda i, x: (0, i))] * 2
        + [pl.BlockSpec((H, w), lambda i, x: (0, before // w))] * 4
        + [pl.BlockSpec((H, w), lambda i, x: (0, 0))] * 4
        + [pl.BlockSpec((S, w // 2), lambda i, x: (0, 0))] * 4
        + [ANY] * len(wait),
        out_specs=pl.BlockSpec((4, rows, size), lambda i, x: (0, i, 0)),
        scratch_shapes=[pltpu.VMEM((8 * S, w // 2), bf16)],
    )
    return pl.pallas_call(
        lambda *refs: weight_kernel(size, *refs),
        grid_spec=grid_spec,
        out_shape=jax.ShapeDtypeStruct((4, K, size), bf16),
        compiler_params=PARAMS,
        cost_estimate=cost(TK),
        name="weight_part",
    )(ids, tk, tx, *first, *second, *other, *wait)


def input_kernel(pieces, r_ref, *refs):
    grads, w_ref, out_ref = refs[:4 * pieces], refs[4 * pieces], refs[-1]
    rows = [jnp.concatenate([grads[k * pieces + f][...] for f in range(pieces)], axis=1) for k in range(4)]
    w = jnp.concatenate(
        [
            w_ref[:, (d * UNITS + start) * LANE:(d * UNITS + start + units) * LANE]
            for start, units in CHUNKS
            for d in range(DEPTH)
        ],
        axis=1,
    )
    lhs = jnp.concatenate(rows, axis=0)
    total = lax.dot_general(lhs, w, (((1,), (1,)), ((), ())), preferred_element_type=f32).astype(bf16)
    for k in range(4):
        slot = pl.multiple_of(jnp.bitwise_xor(r_ref[1], k) * H, H)
        out_ref[pl.ds(slot, H), :] = total[k * H:(k + 1) * H, :]


def input_part(ids, grads, weight, wait):
    tile = 512
    grid_spec = pltpu.PrefetchScalarGridSpec(
        num_scalar_prefetch=1,
        grid=(K // tile,),
        in_specs=[pl.BlockSpec(grad.shape, lambda i, q: (0, 0)) for grad in grads]
        + [pl.BlockSpec((tile, F), lambda i, q: (i, 0))]
        + [ANY] * len(wait),
        out_specs=pl.BlockSpec((4 * H, tile), lambda i, q: (0, i)),
    )
    return pl.pallas_call(
        lambda *refs: input_kernel(len(grads) // 4, *refs),
        grid_spec=grid_spec,
        out_shape=jax.ShapeDtypeStruct((4 * H, K), bf16),
        compiler_params=PARAMS,
        cost_estimate=cost(TK),
        name="input_part",
    )(ids, *grads, weight, *wait)


def add_kernel(a_ref, b_ref, wait_ref, out_ref):
    out_ref[...] = (a_ref[...].astype(f32) + b_ref[...].astype(f32)).astype(bf16)


def add(a, b, wait):
    block = pl.BlockSpec((H, F // 2), lambda i: (0, i))
    return pl.pallas_call(
        add_kernel,
        grid=(2,),
        in_specs=[block, block, ANY],
        out_specs=block,
        out_shape=jax.ShapeDtypeStruct(a.shape, bf16),
        compiler_params=PARAMS,
        cost_estimate=cost(1),
        name="add",
    )(a, b, wait)


def fold_kernel(in_ref, *refs):
    total = in_ref[0].astype(f32)
    for n in range(1, in_ref.shape[0]):
        total += in_ref[n].astype(f32)
    refs[-1][...] = total.astype(bf16)


def fold(pieces, shape, at, earlier=()):
    block = pieces.shape[1:]
    return pl.pallas_call(
        fold_kernel,
        grid=(1,),
        in_specs=[pl.BlockSpec(pieces.shape, lambda i: (0, 0, 0))] + [ANY] * len(earlier),
        out_specs=pl.BlockSpec(block, lambda i: at),
        out_shape=jax.ShapeDtypeStruct(shape, bf16),
        input_output_aliases={1: 0} if earlier else {},
        compiler_params=PARAMS,
        cost_estimate=cost(TK),
        name="fold",
    )(pieces, *earlier)


def swap(value, axis, mask):
    n = lax.axis_size(axis)
    return lax.ppermute(value, axis, [(i, i ^ mask) for i in range(n)])


def shards(tokens, weight, cotangent):
    xh, core, y, xl, z = (lax.axis_index(a) for a in ("xh", "core", "y", "xl", "z"))
    r = 2 * xh + core
    q = jnp.bitwise_xor(r, y).astype(jnp.int32).reshape(1)
    ids = jnp.stack([xl, r]).astype(jnp.int32)

    partner = swap(tokens, "xl", 1)
    tx = lax.all_gather(partner, "y", axis=0, tiled=True)
    opposite = [swap(tokens[:H], "y", 2)]
    y1, y3 = swap(tokens, "y", 1), swap(tokens, "y", 3)
    opposite += after([swap(tokens[H:], "y", 2)], partner, TE)
    tk = ()
    wait = partner
    terms = []
    for part in range(2):
        p0, p1, p2, p3, *tk = block_partials(q, [tokens, y1, opposite[part], y3], weight, part, tk, (wait,))
        terms.append((p0, swap(p1, "core", 1)))
        if part == 0:
            wait = total = add(p2, swap(p3, "core", 1), opposite[1])
        else:
            shared, (first,) = gelu_pair(ids, *terms[0], swap(total, "xh", 1), cotangent, 0, (), ())
            total = add(p2, swap(p3, "core", 1), first if LATE else wait)
            terms[1] += (swap(total, "xh", 1),)
    first_far = swap(first, "xh", 1)
    (activation, *halves), second = gelu_pair(ids, *terms[1], cotangent, 1, shared, (tx,))
    far = [swap(value, "xh", 1) for value in second]
    near = [swap(half, "xl", 1) for half in halves]
    cross = [lax.ppermute(half, ("xh", "xl"), [(i, 3 - i) for i in range(4)]) for half in halves]

    def both(values, other):
        values = after(values, other)
        return [(value, swap(value, "core", 1)) for value in values]

    first, first_far = both([first, first_far], halves[0])
    first = [*first, *first_far]
    dxa = input_part(ids, first, weight, ())
    mine, theirs, n, c = both([second[0], far[0], near[0], cross[0]], dxa)
    grads = [[*mine, *theirs]]
    dw0 = weight_part(ids, tk[0], tx, first, grads[0], [*n, *c], 0, ())
    mine, theirs = both([second[1], far[1]], dw0)
    grads.append([*mine, *theirs])
    dxb = input_part(ids, [grads[g][k] for k in range(4) for g in range(N)], weight, ())

    dxb_own = dxb
    dxa, dxb = (lax.all_to_all(v.reshape(4, H, K), "y", 0, 0, tiled=True) for v in (dxa, dxb))
    input_grad = fold(dxa, (S, K), (0, 0))
    n, c = both([near[1], cross[1]], dxb_own)
    dw1 = weight_part(ids, tk[0], tx, first, grads[1], [*n, *c], 1, (input_grad,))

    dw0 = lax.psum_scatter(dw0, "z", scatter_dimension=0, tiled=True)[0]
    total = lax.dynamic_index_in_dim(dw1, z, 0, False).astype(f32)
    for m in (2, 1, 3):
        piece = lax.dynamic_index_in_dim(dw1, jnp.bitwise_xor(z, m), 0, False)
        total += swap(piece, "z", m).astype(f32)
    input_grad = fold(dxb, (S, K), (1, 0), (input_grad,))
    weight_grad = jnp.concatenate([dw0, total.astype(bf16)], axis=1)
    return activation, input_grad, weight_grad


def solution(mesh):
    split = Mesh(mesh.devices.reshape(2, 2, 4, 4, 2), ("xh", "core", "y", "z", "xl"))
    hidden = P(("z", "xl", "xh", "core"), "y")
    tokens = P(("z", "xl", "y"), ("xh", "core"))
    return jax.shard_map(
        shards,
        mesh=split,
        in_specs=(tokens, P(("xh", "core"), "y"), hidden),
        out_specs=(hidden, tokens, P(("xh", "core"), ("y", "z", "xl"))),
        check_vma=False,
    )
```

time: 502 us -> 250 us (0.50)
  waiting for transfers between devices: 419 us -> 99.9 us
  Pallas kernels: 0 us -> 79 us
  matrix products: 42.9 us -> 0 us
  starting transfers between devices: 0.38 us -> 41.3 us
  other arithmetic: 21.3 us -> 4.1 us
  local copies, waits for them, and re-layouts: 4.98 us -> 10.8 us
    reduce_scatter x2 -> x1, waiting for transfers between devices: 208 us -> 0.01 us  [shards(): dw0 = lax.psum_scatter(dw0, 'z', scatter_dimension=0, tiled=True)[0]]
    psum x1 -> x0, waiting for transfers between devices: 129 us -> none  [shards(): pre_whole = lax.psum(partial_value, 'row').astype(jnp.float32)]
    ppermute x0 -> x31, waiting for transfers between devices: none -> 92.5 us  [the longest x29 80.5 us: swap(): return lax.ppermute(value, axis, [(i, i ^ mask) for i in range(n)])]
    all_gather x2 -> x1, waiting for transfers between devices: 81.2 us -> 0.01 us  [shards(): tx = lax.all_gather(partner, 'y', axis=0, tiled=True)]
    pallas_call x0 -> x17, Pallas kernels: none -> 79 us  [the longest x2 21.6 us: weight_part(): pl.pallas_call(lambda *refs: weight_kernel(size, *refs), grid_spec=grid_s...]
    dot_general x3 -> x0, matrix products: 42.9 us -> none  [the longest x1 15.6 us: input_part(): lax.dot_general(pre_grad, weight, (((1,), (1,)), ((), ())), preferred_ele...]
    ppermute x0 -> x31, starting transfers between devices: none -> 32.5 us  [the longest x29 30.6 us: swap(): return lax.ppermute(value, axis, [(i, i ^ mask) for i in range(n)])]
    convert_element_type x2 -> x1, other arithmetic: 21.3 us -> 1.2 us  [shards(): weight_grad = jnp.concatenate([dw0, total.astype(bf16)], axis=1)]
  transfers between devices with their start and end apart: 5 -> 35, of which waited for: 5 -> 14; matrix products, arithmetic and copies ran while one was open for 7% -> 2% of each run, Pallas kernels for 0% -> 32%
where the time goes in v3:
time: 250 us; the launch traced here: 249 us
  waiting for transfers between devices  99.9 us (40%)
  Pallas kernels  79 us (32%)
  starting transfers between devices  41.3 us (17%)
  between operations  14.2 us (6%)
  local copies, waits for them, and re-layouts  10.8 us (4%)
  other arithmetic  4.1 us (2%)
    ppermute x29, waiting for transfers between devices, swap(): return lax.ppermute(value, axis, [(i, i ^ mask) for i in range(n)])  80.5 us
    ppermute x29, starting transfers between devices, swap(): return lax.ppermute(value, axis, [(i, i ^ mask) for i in range(n)])  30.6 us
    pallas_call x2, Pallas kernels, weight_part(): pl.pallas_call(lambda *refs: weight_kernel(size, *refs), grid_spec=grid_s...  21.6 us
    pallas_call x2, Pallas kernels, input_part(): pl.pallas_call(lambda *refs: input_kernel(len(grads) // 4, *refs), grid_s...  20 us
    pallas_call x2, Pallas kernels, block_partials(): pl.pallas_call(partial_kernel, grid_spec=grid_spec, out_shape=[jax.ShapeD...  19.2 us
    ppermute x2, waiting for transfers between devices, shards(): lax.ppermute(half, ('xh', 'xl'), [(i, 3 - i) for i in range(4)])  12.1 us
    pallas_call x2, Pallas kernels, gelu_pair(): pl.pallas_call(lambda *refs: gelu_kernel(len(widths), *refs), grid_spec=g...  8.94 us
    all_to_all x2, starting transfers between devices, shards(): lax.all_to_all(v.reshape(4, H, K), 'y', 0, 0, tiled=True)  8.73 us
  transfers between devices with their start and end apart: 35, of which 14 were waited for; matrix products, arithmetic and copies ran while one was open for 2% of the time, Pallas kernels for 32%

profile of v3, /device:TPU:1, one launch (start us, length us, event | category | flops | bytes accessed | tf_op | source)
XLA Modules:
  0.0 249.3 jit_solution(2289480091447712959)
XLA Ops:
  7.2 3.6 %collective-permute-start.3 = (bf16[256,1536]{1,0:T(8,128)(2,1)}, bf16[256,1536]{1,0:T(8,128)(2,1)S(1)}, u32[]{:S(2)}, u32[]{:S(2)}) collective-permute-start(bf16[256,1536]{1,0:T(8,128)(2,1)} %b0.3), channel_id=1, source_target_pairs={{0,24},{8,16},{16,8},{24,0},{1,25},{9,17},{17,9},{25,1},{2,26},{10... | collective-permute-start | bytes 2359304 | tf_op jit(solution)/shard_map/ppermute | solution.py:272
  10.9 1.2 collective-permute-start.2
  12.1 1.9 fusion.3
  14.0 1.3 collective-permute-start.4
  15.3 1.7 collective-permute-start.1
  17.0 21.5 %collective-permute-done.4.b2 = bf16[128,1536]{1,0:T(8,128)(2,1)S(1)} collective-permute-done((bf16[128,1536]{1,0:T(8,128)(2,1)S(1)}, bf16[128,1536]{1,0:T(8,128)(2,1)S(1)}, u32[]{:S(2)}, u32[]{:S(2)}) %collective-permute-start.4) | collective-permute-done | bytes 393248 | tf_op jit(solution)/shard_map/ppermute | solution.py:272
  38.5 0.7 copy-done.9
  39.2 0.9 copy-done.2
  40.1 9.6 %block_partials.2 = (bf16[128,3072]{1,0:T(8,128)(2,1)}, bf16[128,3072]{1,0:T(8,128)(2,1)}, bf16[128,3072]{1,0:T(8,128)(2,1)}, bf16[128,3072]{1,0:T(8,128)(2,1)}, bf16[1024,1536]{1,0:T(8,128)(2,1)}) custom-call(s32[1]{0:T(128)} %bitcast.2.q_ref, bf16[256,1536]{1,0:T(8,128)(2,1)} %b0.3, bf16[256,1536]{1,0:T(8,128)(2,1)} %collective-permute-done.b1, ...), custom_call_target="tpu_custom_call" | custom-call | flops 11500000 | bytes 36000 | tf_op jit(solution)/shard_map/block_partials/pallas_call | solution.py:77
  49.7 3.6 %collective-permute-start.5 = (bf16[128,3072]{1,0:T(8,128)(2,1)}, bf16[128,3072]{1,0:T(8,128)(2,1)}, u32[]{:S(2)}, u32[]{:S(2)}) collective-permute-start(bf16[128,3072]{1,0:T(8,128)(2,1)} %get-tuple-element.34), channel_id=1, source_target_pairs={{0,32},{32,0},{1,33},{33,1},{2,34},{34,2},{3,35},{35,3},{4,36},{36... | collective-permute-start | bytes 2359304 | tf_op jit(solution)/shard_map/ppermute | solution.py:272
  53.4 2.2 collective-permute-done.5.b_ref
  55.5 2.2 add.55.refs_1_
  57.8 2.5 collective-permute-start.9
  60.2 0.6 pad_add_fusion.refs_0_
  60.9 9.6 %block_partials.3 = (bf16[128,3072]{1,0:T(8,128)(2,1)}, bf16[128,3072]{1,0:T(8,128)(2,1)}, bf16[128,3072]{1,0:T(8,128)(2,1)}, bf16[128,3072]{1,0:T(8,128)(2,1)}, bf16[1024,1536]{1,0:T(8,128)(2,1)}) custom-call(s32[1]{0:T(128)} %bitcast.2.q_ref, bf16[256,1536]{1,0:T(8,128)(2,1)} %b0.3, ...), custom_call_target="tpu_custom_call", output_to_operand_aliasing={{4}: (6, {})} | custom-call | flops 11500000 | bytes 36000 | tf_op jit(solution)/shard_map/block_partials/pallas_call | solution.py:77
  70.5 0.7 collective-permute-start.6
  71.2 7.0 %collective-permute-done.9.refs_3_ = bf16[128,3072]{1,0:T(8,128)(2,1)S(1)} collective-permute-done((bf16[128,3072]{1,0:T(8,128)(2,1)}, bf16[128,3072]{1,0:T(8,128)(2,1)S(1)}, u32[]{:S(2)}, u32[]{:S(2)}) %collective-permute-start.9) | collective-permute-done | bytes 786464 | tf_op jit(solution)/shard_map/ppermute | solution.py:272
  78.2 0.9 copy-done.13
  79.1 4.5 %gelu_pair.2 = (bf16[256,3072]{1,0:T(8,128)(2,1)}, bf16[256,1024]{1,0:T(8,128)(2,1)}, bf16[256,512]{1,0:T(8,128)(2,1)}, bf16[128,3072]{1,0:T(8,128)(2,1)}) custom-call(s32[2]{0:T(128)} %pad_add_fusion.refs_0_, bf16[128,3072]{1,0:T(8,128)(2,1)} %get-tuple-element.39.refs_1_, bf16[128,3072]{1,0:T(8,128)(2,1)} %collective-permute-done.8.refs_2_, ...), custom_call_target="tpu_custom_call" | custom-call | flops 34500001792 | bytes 108000000 | tf_op jit(solution)/shard_map/gelu_pair/pallas_call | solution.py:129
  83.7 2.3 add.56
  86.0 2.6 %collective-permute-start.10 = (bf16[128,3072]{1,0:T(8,128)(2,1)}, bf16[128,3072]{1,0:T(8,128)(2,1)}, u32[]{:S(2)}, u32[]{:S(2)}) collective-permute-start(bf16[128,3072]{1,0:T(8,128)(2,1)} %add.56), channel_id=1, source_target_pairs={{0,64},{64,0},{1,65},{65,1},{2,66},{66,2},{3,67},{67,3},{4,68},{68... | collective-permute-start | bytes 2359304 | tf_op jit(solution)/shard_map/ppermute | solution.py:272
  88.5 0.4 collective-permute-start.14
  88.9 16.7 %collective-permute-done.10.refs_3_ = bf16[128,3072]{1,0:T(8,128)(2,1)} collective-permute-done((bf16[128,3072]{1,0:T(8,128)(2,1)}, bf16[128,3072]{1,0:T(8,128)(2,1)}, u32[]{:S(2)}, u32[]{:S(2)}) %collective-permute-start.10) | collective-permute-done | bytes 786464 | tf_op jit(solution)/shard_map/ppermute | solution.py:272
  105.6 4.4 %gelu_pair.3 = (bf16[256,3072]{1,0:T(8,128)(2,1)}, bf16[256,1024]{1,0:T(8,128)(2,1)}, bf16[256,512]{1,0:T(8,128)(2,1)}, bf16[128,2048]{1,0:T(8,128)(2,1)}, bf16[128,1024]{1,0:T(8,128)(2,1)}) custom-call(s32[2]{0:T(128)} %pad_add_fusion.refs_0_, ...), custom_call_target="tpu_custom_call", output_to_operand_aliasing={{0}: (5, {}), {1}: (6, {}), {2}: (7, {})} | custom-call | flops 34500001792 | bytes 108000000 | tf_op jit(solution)/shard_map/gelu_pair/pallas_call | solution.py:129
  110.1 12.4 %collective-permute-done.14.refs_1_ = bf16[128,3072]{1,0:T(8,128)(2,1)} collective-permute-done((bf16[128,3072]{1,0:T(8,128)(2,1)S(1)}, bf16[128,3072]{1,0:T(8,128)(2,1)}, u32[]{:S(2)}, u32[]{:S(2)}) %collective-permute-start.14) | collective-permute-done | bytes 786464 | tf_op jit(solution)/shard_map/ppermute | solution.py:272
  122.5 2.1 collective-permute-start.15
  124.6 2.6 %collective-permute-start.11 = (bf16[128,2048]{1,0:T(8,128)(2,1)}, bf16[128,2048]{1,0:T(8,128)(2,1)}, u32[]{:S(2)}, u32[]{:S(2)}) collective-permute-start(bf16[128,2048]{1,0:T(8,128)(2,1)} %get-tuple-element.46.refs_0_), channel_id=1, source_target_pairs={{0,64},{64,0},{1,65},{65,1},{2,66},{66,2},{3,67},{67,3},{4,68},{68... | collective-permute-start | bytes 1572872 | tf_op jit(solution)/shard_map/ppermute | solution.py:272
  127.3 0.5 collective-permute-done.15.refs_2_.refs_4_
  127.8 0.2 collective-permute-done.16.refs_4_.refs_6_
  128.0 0.7 copy-done
  128.7 10.0 %input_part.2.refs_4_ = bf16[512,1536]{1,0:T(8,128)(2,1)} custom-call(s32[2]{0:T(128)} %pad_add_fusion.refs_0_, bf16[128,3072]{1,0:T(8,128)(2,1)} %get-tuple-element.48.refs_1_.refs_3_, bf16[128,3072]{1,0:T(8,128)(2,1)} %copy-done, bf16[128,3072]{1,0:T(8,128)(2,1)} %get-tuple-element.49.refs_3_.refs_5_, ...), custom_call_target="tpu_custom_call" | custom-call | flops 3449999872 | bytes 10800000 | tf_op jit(solution)/shard_map/input_part/pallas_call | solution.py:220
  138.7 0.7 collective-permute-done.11.refs_1_
  139.4 12.1 %collective-permute-done.13.refs_3_ = bf16[256,1024]{1,0:T(8,128)(2,1)} collective-permute-done((bf16[256,1024]{1,0:T(8,128)(2,1)}, bf16[256,1024]{1,0:T(8,128)(2,1)}, u32[]{:S(2)}, u32[]{:S(2)}) %collective-permute-start.13) | collective-permute-done | bytes 524320 | tf_op jit(solution)/shard_map/ppermute | solution.py:302
  151.5 0.5 collective-permute-start.20
  152.1 0.4 collective-permute-start.18
  152.6 1.5 collective-permute-start.17
  154.1 1.2 collective-permute-done.21.refs_14_
  155.3 0.7 collective-permute-done.18.refs_8_.refs_3_
  156.1 0.7 copy-done.3
  156.8 12.9 %weight_part.2.refs_2_ = bf16[4,1536,256]{2,1,0:T(8,128)(2,1)} custom-call(s32[2]{0:T(128)} %pad_add_fusion.refs_0_, bf16[1024,1536]{1,0:T(8,128)(2,1)} %get-tuple-element.52.refs_1_, bf16[1024,1536]{1,0:T(8,128)(2,1)} %all-gather.2.cloned.1.call-done.refs_8_.refs_2_, bf16[128,3072]{1,0:T(8,128)(2,1)} %get-tuple-element.48.refs_1_.refs_3_, ...), custom_call_target="tpu_custom_call" | custom-call | flops 3449999872 | bytes 10800000 | tf_op jit(solution)/shard_map/weight_part/pallas_call | solution.py:182
  169.7 0.4 collective-permute-start.22
  170.3 1.8 collective-permute-start.25
  172.2 4.3 %all-to-all-start.1 = ((bf16[4,128,1536]{2,1,0:T(8,128)(2,1)}), bf16[4,128,1536]{2,1,0:T(8,128)(2,1)}, u32[]{:S(2)}, u32[]{:S(2)}) async-start(bf16[4,128,1536]{2,1,0:T(8,128)(2,1)} %bitcast.4), calls=%async_computation.1 | async-start | bytes 3145728 | tf_op jit(solution)/shard_map/all_to_all | solution.py:319
  176.6 0.7 reduce-scatter.2.cloned.1.call-update
  177.3 0.7 copy-done.4
  178.0 0.7 copy-done.5
  178.7 10.0 %input_part.3.refs_2_ = bf16[512,1536]{1,0:T(8,128)(2,1)} custom-call(s32[2]{0:T(128)} %pad_add_fusion.refs_0_, bf16[128,2048]{1,0:T(8,128)(2,1)} %get-tuple-element.50.refs_7_.refs_1_, bf16[128,1024]{1,0:T(8,128)(2,1)} %get-tuple-element.56.refs_2_.refs_7_, bf16[128,2048]{1,0:T(8,128)(2,1)} %copy-done.3, bf16[128,1024]{1,0:T(8,128)(2,1)} %copy-done.4, ...), custom_call_target="tpu_custom_call" | custom-call | flops 3449999872 | bytes 10800000 | tf_op jit(solution)/shard_map/input_part/pallas_call | solution.py:220
  188.7 0.7 copy-done.10
  189.4 0.7 collective-permute-start.26
  190.1 6.6 %all-to-all-done.1.in_ref = bf16[4,128,1536]{2,1,0:T(8,128)(2,1)} async-done(((bf16[4,128,1536]{2,1,0:T(8,128)(2,1)}), bf16[4,128,1536]{2,1,0:T(8,128)(2,1)}, u32[]{:S(2)}, u32[]{:S(2)}) %all-to-all-start.1) | async-done | bytes 1572896 | tf_op jit(solution)/shard_map/all_to_all | solution.py:319
  196.7 4.4 %all-to-all-start = ((bf16[4,128,1536]{2,1,0:T(8,128)(2,1)}), bf16[4,128,1536]{2,1,0:T(8,128)(2,1)}, u32[]{:S(2)}, u32[]{:S(2)}) async-start(bf16[4,128,1536]{2,1,0:T(8,128)(2,1)} %bitcast.3), calls=%async_computation | async-start | bytes 3145728 | tf_op jit(solution)/shard_map/all_to_all | solution.py:319
  201.1 2.4 fold.2.refs_0_.refs_15_
  203.5 0.7 copy-done.11
  204.2 0.7 copy-done.12
  204.9 8.7 %weight_part.3 = bf16[4,1536,128]{2,1,0:T(8,128)(2,1)} custom-call(s32[2]{0:T(128)} %pad_add_fusion.refs_0_, bf16[1024,1536]{1,0:T(8,128)(2,1)} %get-tuple-element.52.refs_1_, bf16[1024,1536]{1,0:T(8,128)(2,1)} %all-gather.2.cloned.1.call-done.refs_8_.refs_2_, bf16[128,3072]{1,0:T(8,128)(2,1)} %get-tuple-element.48.refs_1_.refs_3_, ...), custom_call_target="tpu_custom_call" | custom-call | flops 3449999872 | bytes 10800000 | tf_op jit(solution)/shard_map/weight_part/pallas_call | solution.py:182
  213.6 1.3 dynamic-slice_bitcast_fusion.2
  215.0 3.6 %collective-permute-start.28 = (bf16[1536,128]{1,0:T(8,128)(2,1)S(1)}, bf16[1536,128]{1,0:T(8,128)(2,1)S(1)}, u32[]{:S(2)}, u32[]{:S(2)}) collective-permute-start(bf16[1536,128]{1,0:T(8,128)(2,1)S(1)} %get-tuple-element.61), channel_id=1, source_target_pairs={{0,4},{2,6},{4,0},{6,2},{1,5},{3,7},{5,1},{7,3},{8,12},{10,14},{12... | collective-permute-start | bytes 1179656 | tf_op jit(solution)/shard_map/ppermute | solution.py:272
  218.6 0.5 collective-permute-start.30
  219.1 0.3 collective-permute-start.29
  219.4 7.2 %collective-permute-done.28 = bf16[1536,128]{1,0:T(8,128)(2,1)S(1)} collective-permute-done((bf16[1536,128]{1,0:T(8,128)(2,1)S(1)}, bf16[1536,128]{1,0:T(8,128)(2,1)S(1)}, u32[]{:S(2)}, u32[]{:S(2)}) %collective-permute-start.28) | collective-permute-done | bytes 393248 | tf_op jit(solution)/shard_map/ppermute | solution.py:272
  226.5 10.1 %collective-permute-done.30 = bf16[1536,128]{1,0:T(8,128)(2,1)S(1)} collective-permute-done((bf16[1536,128]{1,0:T(8,128)(2,1)S(1)}, bf16[1536,128]{1,0:T(8,128)(2,1)S(1)}, u32[]{:S(2)}, u32[]{:S(2)}) %collective-permute-start.30) | collective-permute-done | bytes 393248 | tf_op jit(solution)/shard_map/ppermute | solution.py:272
  236.6 1.2 fusion.2
  237.8 2.4 fold.3
  240.2 2.3 pad_maximum_fusion
  (58 shorter events, 0.9 us)
Async XLA Ops:
  7.2 98.5 %all-gather.2.cloned.1.call-start = ((), (), s32[]{:S(2)}) async-start(), calls=%async_computation.3 | async-start | bytes 3932160 | tf_op jit(solution)/shard_map/all_gather | solution.py:282
  7.2 31.3 %collective-permute-start.3 = (bf16[256,1536]{1,0:T(8,128)(2,1)}, bf16[256,1536]{1,0:T(8,128)(2,1)S(1)}, u32[]{:S(2)}, u32[]{:S(2)}) collective-permute-start(bf16[256,1536]{1,0:T(8,128)(2,1)} %b0.3), channel_id=1, source_target_pairs={{0,24},{8,16},{16,8},{24,0},{1,25},{9,17},{17,9},{25,1},{2,26},{10... | collective-permute-start | bytes 2359304 | tf_op jit(solution)/shard_map/ppermute | solution.py:272
  10.9 28.4 %collective-permute-start.2 = (bf16[256,1536]{1,0:T(8,128)(2,1)}, bf16[256,1536]{1,0:T(8,128)(2,1)}, u32[]{:S(2)}, u32[]{:S(2)}) collective-permute-start(bf16[256,1536]{1,0:T(8,128)(2,1)} %b0.3), channel_id=1, source_target_pairs={{0,1},{1,0},{2,3},{3,2},{4,5},{5,4},{6,7},{7,6},{8,9},{9,8},{10,11... | collective-permute-start | bytes 2359304 | tf_op jit(solution)/shard_map/ppermute | solution.py:272
  12.1 27.2 %collective-permute-start = (bf16[256,1536]{1,0:T(8,128)(2,1)}, bf16[256,1536]{1,0:T(8,128)(2,1)}, u32[]{:S(2)}, u32[]{:S(2)}) collective-permute-start(bf16[256,1536]{1,0:T(8,128)(2,1)} %b0.3), channel_id=1, source_target_pairs={{0,8},{8,0},{16,24},{24,16},{1,9},{9,1},{17,25},{25,17},{2,10},{10... | collective-permute-start | bytes 2359304 | tf_op jit(solution)/shard_map/ppermute | solution.py:272
  14.0 24.5 %collective-permute-start.4 = (bf16[128,1536]{1,0:T(8,128)(2,1)S(1)}, bf16[128,1536]{1,0:T(8,128)(2,1)S(1)}, u32[]{:S(2)}, u32[]{:S(2)}) collective-permute-start(bf16[128,1536]{1,0:T(8,128)(2,1)S(1)} %get-tuple-element.64), channel_id=1, source_target_pairs={{0,16},{8,24},{16,0},{24,8},{1,17},{9,25},{17,1},{25,9},{2,18},{10... | collective-permute-start | bytes 1179656 | tf_op jit(solution)/shard_map/ppermute | solution.py:272
  15.3 38.1 %collective-permute-start.1 = (bf16[128,1536]{1,0:T(8,128)(2,1)}, bf16[128,1536]{1,0:T(8,128)(2,1)}, u32[]{:S(2)}, u32[]{:S(2)}) collective-permute-start(bf16[128,1536]{1,0:T(8,128)(2,1)} %get-tuple-element.65), channel_id=1, source_target_pairs={{0,16},{8,24},{16,0},{24,8},{1,17},{9,25},{17,1},{25,9},{2,18},{10... | collective-permute-start | bytes 1179656 | tf_op jit(solution)/shard_map/ppermute | solution.py:272
  38.5 0.7 copy-start.9
  39.2 0.9 copy-start.2
  49.7 5.9 %collective-permute-start.5 = (bf16[128,3072]{1,0:T(8,128)(2,1)}, bf16[128,3072]{1,0:T(8,128)(2,1)}, u32[]{:S(2)}, u32[]{:S(2)}) collective-permute-start(bf16[128,3072]{1,0:T(8,128)(2,1)} %get-tuple-element.34), channel_id=1, source_target_pairs={{0,32},{32,0},{1,33},{33,1},{2,34},{34,2},{3,35},{35,3},{4,36},{36... | collective-permute-start | bytes 2359304 | tf_op jit(solution)/shard_map/ppermute | solution.py:272
  53.3 17.9 %collective-permute-start.8 = (bf16[128,3072]{1,0:T(8,128)(2,1)}, bf16[128,3072]{1,0:T(8,128)(2,1)}, u32[]{:S(2)}, u32[]{:S(2)}) collective-permute-start(bf16[128,3072]{1,0:T(8,128)(2,1)} %get-tuple-element.40), channel_id=1, source_target_pairs={{0,32},{32,0},{1,33},{33,1},{2,34},{34,2},{3,35},{35,3},{4,36},{36... | collective-permute-start | bytes 2359304 | tf_op jit(solution)/shard_map/ppermute | solution.py:272
  57.8 20.5 %collective-permute-start.9 = (bf16[128,3072]{1,0:T(8,128)(2,1)}, bf16[128,3072]{1,0:T(8,128)(2,1)S(1)}, u32[]{:S(2)}, u32[]{:S(2)}) collective-permute-start(bf16[128,3072]{1,0:T(8,128)(2,1)} %add.55.refs_1_), channel_id=1, source_target_pairs={{0,64},{64,0},{1,65},{65,1},{2,66},{66,2},{3,67},{67,3},{4,68},{68... | collective-permute-start | bytes 2359304 | tf_op jit(solution)/shard_map/ppermute | solution.py:272
  70.5 18.5 %collective-permute-start.6 = (bf16[128,3072]{1,0:T(8,128)(2,1)}, bf16[128,3072]{1,0:T(8,128)(2,1)}, u32[]{:S(2)}, u32[]{:S(2)}) collective-permute-start(bf16[128,3072]{1,0:T(8,128)(2,1)} %get-tuple-element.36), channel_id=1, source_target_pairs={{0,32},{32,0},{1,33},{33,1},{2,34},{34,2},{3,35},{35,3},{4,36},{36... | collective-permute-start | bytes 2359304 | tf_op jit(solution)/shard_map/ppermute | solution.py:272
  71.1 12.5 %collective-permute-start.7 = (bf16[128,3072]{1,0:T(8,128)(2,1)}, bf16[128,3072]{1,0:T(8,128)(2,1)}, u32[]{:S(2)}, u32[]{:S(2)}) collective-permute-start(bf16[128,3072]{1,0:T(8,128)(2,1)} %get-tuple-element.38), channel_id=1, source_target_pairs={{0,32},{32,0},{1,33},{33,1},{2,34},{34,2},{3,35},{35,3},{4,36},{36... | collective-permute-start | bytes 2359304 | tf_op jit(solution)/shard_map/ppermute | solution.py:272
  78.2 0.9 copy-start.13
  83.7 4.9 %copy-start.1 = (bf16[128,3072]{1,0:T(8,128)(2,1)S(1)}, bf16[128,3072]{1,0:T(8,128)(2,1)}, u32[]{:S(2)}) copy-start(bf16[128,3072]{1,0:T(8,128)(2,1)} %get-tuple-element.41.wait_ref.refs_0_) | copy-start | bytes 2359300
  86.0 19.7 %collective-permute-start.10 = (bf16[128,3072]{1,0:T(8,128)(2,1)}, bf16[128,3072]{1,0:T(8,128)(2,1)}, u32[]{:S(2)}, u32[]{:S(2)}) collective-permute-start(bf16[128,3072]{1,0:T(8,128)(2,1)} %add.56), channel_id=1, source_target_pairs={{0,64},{64,0},{1,65},{65,1},{2,66},{66,2},{3,67},{67,3},{4,68},{68... | collective-permute-start | bytes 2359304 | tf_op jit(solution)/shard_map/ppermute | solution.py:272
  88.5 34.0 %collective-permute-start.14 = (bf16[128,3072]{1,0:T(8,128)(2,1)S(1)}, bf16[128,3072]{1,0:T(8,128)(2,1)}, u32[]{:S(2)}, u32[]{:S(2)}) collective-permute-start(bf16[128,3072]{1,0:T(8,128)(2,1)S(1)} %copy-done.1), channel_id=1, source_target_pairs={{0,64},{64,0},{1,65},{65,1},{2,66},{66,2},{3,67},{67,3},{4,68},{68... | collective-permute-start | bytes 2359304 | tf_op jit(solution)/shard_map/ppermute | solution.py:272
  122.5 5.3 %collective-permute-start.15 = (bf16[128,3072]{1,0:T(8,128)(2,1)}, bf16[128,3072]{1,0:T(8,128)(2,1)S(1)}, u32[]{:S(2)}, u32[]{:S(2)}) collective-permute-start(bf16[128,3072]{1,0:T(8,128)(2,1)} %get-tuple-element.48.refs_1_.refs_3_), channel_id=1, source_target_pairs={{0,32},{32,0},{1,33},{33,1},{2,34},{34,2},{3,35},{35,3},{4,36},{36... | collective-permute-start | bytes 2359304 | tf_op jit(solution)/shard_map/ppermute | solution.py:272
  124.6 3.4 %collective-permute-start.16 = (bf16[128,3072]{1,0:T(8,128)(2,1)}, bf16[128,3072]{1,0:T(8,128)(2,1)}, u32[]{:S(2)}, u32[]{:S(2)}) collective-permute-start(bf16[128,3072]{1,0:T(8,128)(2,1)} %get-tuple-element.49.refs_3_.refs_5_), channel_id=1, source_target_pairs={{0,32},{32,0},{1,33},{33,1},{2,34},{34,2},{3,35},{35,3},{4,36},{36... | collective-permute-start | bytes 2359304 | tf_op jit(solution)/shard_map/ppermute | solution.py:272
  124.6 14.8 %collective-permute-start.11 = (bf16[128,2048]{1,0:T(8,128)(2,1)}, bf16[128,2048]{1,0:T(8,128)(2,1)}, u32[]{:S(2)}, u32[]{:S(2)}) collective-permute-start(bf16[128,2048]{1,0:T(8,128)(2,1)} %get-tuple-element.46.refs_0_), channel_id=1, source_target_pairs={{0,64},{64,0},{1,65},{65,1},{2,66},{66,2},{3,67},{67,3},{4,68},{68... | collective-permute-start | bytes 1572872 | tf_op jit(solution)/shard_map/ppermute | solution.py:272
  127.2 24.3 %collective-permute-start.13 = (bf16[256,1024]{1,0:T(8,128)(2,1)}, bf16[256,1024]{1,0:T(8,128)(2,1)}, u32[]{:S(2)}, u32[]{:S(2)}) collective-permute-start(bf16[256,1024]{1,0:T(8,128)(2,1)} %get-tuple-element.47.refs_2_), channel_id=1, source_target_pairs={{0,65},{1,64},{64,1},{65,0},{2,67},{3,66},{66,3},{67,2},{4,69},{5,... | collective-permute-start | bytes 1572872 | tf_op jit(solution)/shard_map/ppermute | solution.py:302
  127.3 24.2 %collective-permute-start.12 = (bf16[256,1024]{1,0:T(8,128)(2,1)}, bf16[256,1024]{1,0:T(8,128)(2,1)}, u32[]{:S(2)}, u32[]{:S(2)}) collective-permute-start(bf16[256,1024]{1,0:T(8,128)(2,1)} %get-tuple-element.47.refs_2_), channel_id=1, source_target_pairs={{0,1},{1,0},{2,3},{3,2},{4,5},{5,4},{6,7},{7,6},{8,9},{9,8},{10,11... | collective-permute-start | bytes 1572872 | tf_op jit(solution)/shard_map/ppermute | solution.py:272
  127.8 0.9 copy-start
  151.5 1.1 copy-start.6
  151.5 2.6 %collective-permute-start.20 = (bf16[256,1024]{1,0:T(8,128)(2,1)}, bf16[256,1024]{1,0:T(8,128)(2,1)S(1)}, u32[]{:S(2)}, u32[]{:S(2)}) collective-permute-start(bf16[256,1024]{1,0:T(8,128)(2,1)} %get-tuple-element.54.refs_11_), channel_id=1, source_target_pairs={{0,32},{32,0},{1,33},{33,1},{2,34},{34,2},{3,35},{35,3},{4,36},{36... | collective-permute-start | bytes 1572872 | tf_op jit(solution)/shard_map/ppermute | solution.py:272
  152.0 3.2 %collective-permute-start.21 = (bf16[256,1024]{1,0:T(8,128)(2,1)}, bf16[256,1024]{1,0:T(8,128)(2,1)S(1)}, u32[]{:S(2)}, u32[]{:S(2)}) collective-permute-start(bf16[256,1024]{1,0:T(8,128)(2,1)} %get-tuple-element.55.refs_13_), channel_id=1, source_target_pairs={{0,32},{32,0},{1,33},{33,1},{2,34},{34,2},{3,35},{35,3},{4,36},{36... | collective-permute-start | bytes 1572872 | tf_op jit(solution)/shard_map/ppermute | solution.py:272
  152.1 3.9 %collective-permute-start.18 = (bf16[128,2048]{1,0:T(8,128)(2,1)}, bf16[128,2048]{1,0:T(8,128)(2,1)S(1)}, u32[]{:S(2)}, u32[]{:S(2)}) collective-permute-start(bf16[128,2048]{1,0:T(8,128)(2,1)} %get-tuple-element.50.refs_7_.refs_1_), channel_id=1, source_target_pairs={{0,32},{32,0},{1,33},{33,1},{2,34},{34,2},{3,35},{35,3},{4,36},{36... | collective-permute-start | bytes 1572872 | tf_op jit(solution)/shard_map/ppermute | solution.py:272
  152.5 3.5 %collective-permute-start.19 = (bf16[128,2048]{1,0:T(8,128)(2,1)}, bf16[128,2048]{1,0:T(8,128)(2,1)}, u32[]{:S(2)}, u32[]{:S(2)}) collective-permute-start(bf16[128,2048]{1,0:T(8,128)(2,1)} %get-tuple-element.53.refs_9_.refs_5_), channel_id=1, source_target_pairs={{0,32},{32,0},{1,33},{33,1},{2,34},{34,2},{3,35},{35,3},{4,36},{36... | collective-permute-start | bytes 1572872 | tf_op jit(solution)/shard_map/ppermute | solution.py:272
  152.6 17.1 %collective-permute-start.17 = (bf16[128,1024]{1,0:T(8,128)(2,1)S(1)}, bf16[128,1024]{1,0:T(8,128)(2,1)}, u32[]{:S(2)}, u32[]{:S(2)}) collective-permute-start(bf16[128,1024]{1,0:T(8,128)(2,1)S(1)} %copy-done.6), channel_id=1, source_target_pairs={{0,64},{64,0},{1,65},{65,1},{2,66},{66,2},{3,67},{67,3},{4,68},{68... | collective-permute-start | bytes 786440 | tf_op jit(solution)/shard_map/ppermute | solution.py:272
  154.1 1.9 copy-start.7
  155.2 0.9 copy-start.8
  156.0 0.8 copy-start.3
  169.7 7.5 %collective-permute-start.22 = (bf16[128,1024]{1,0:T(8,128)(2,1)}, bf16[128,1024]{1,0:T(8,128)(2,1)S(1)}, u32[]{:S(2)}, u32[]{:S(2)}) collective-permute-start(bf16[128,1024]{1,0:T(8,128)(2,1)} %get-tuple-element.56.refs_2_.refs_7_), channel_id=1, source_target_pairs={{0,32},{32,0},{1,33},{33,1},{2,34},{34,2},{3,35},{35,3},{4,36},{36... | collective-permute-start | bytes 786440 | tf_op jit(solution)/shard_map/ppermute | solution.py:272
  170.2 7.1 %collective-permute-start.23 = (bf16[128,1024]{1,0:T(8,128)(2,1)}, bf16[128,1024]{1,0:T(8,128)(2,1)S(1)}, u32[]{:S(2)}, u32[]{:S(2)}) collective-permute-start(bf16[128,1024]{1,0:T(8,128)(2,1)} %get-tuple-element.57.refs_6_.refs_9_), channel_id=1, source_target_pairs={{0,32},{32,0},{1,33},{33,1},{2,34},{34,2},{3,35},{35,3},{4,36},{36... | collective-permute-start | bytes 786440 | tf_op jit(solution)/shard_map/ppermute | solution.py:272
  170.3 18.4 %collective-permute-start.25 = (bf16[256,512]{1,0:T(8,128)(2,1)}, bf16[256,512]{1,0:T(8,128)(2,1)S(1)}, u32[]{:S(2)}, u32[]{:S(2)}) collective-permute-start(bf16[256,512]{1,0:T(8,128)(2,1)} %get-tuple-element.58), channel_id=1, source_target_pairs={{0,65},{1,64},{64,1},{65,0},{2,67},{3,66},{66,3},{67,2},{4,69},{5,... | collective-permute-start | bytes 786440 | tf_op jit(solution)/shard_map/ppermute | solution.py:302
  172.2 16.5 %collective-permute-start.24 = (bf16[256,512]{1,0:T(8,128)(2,1)}, bf16[256,512]{1,0:T(8,128)(2,1)}, u32[]{:S(2)}, u32[]{:S(2)}) collective-permute-start(bf16[256,512]{1,0:T(8,128)(2,1)} %get-tuple-element.58), channel_id=1, source_target_pairs={{0,1},{1,0},{2,3},{3,2},{4,5},{5,4},{6,7},{7,6},{8,9},{9,8},{10,11... | collective-permute-start | bytes 786440 | tf_op jit(solution)/shard_map/ppermute | solution.py:272
  172.2 24.5 %all-to-all-start.1 = ((bf16[4,128,1536]{2,1,0:T(8,128)(2,1)}), bf16[4,128,1536]{2,1,0:T(8,128)(2,1)}, u32[]{:S(2)}, u32[]{:S(2)}) async-start(bf16[4,128,1536]{2,1,0:T(8,128)(2,1)} %bitcast.4), calls=%async_computation.1 | async-start | bytes 3145728 | tf_op jit(solution)/shard_map/all_to_all | solution.py:319
  176.5 63.7 %reduce-scatter.2.cloned.1.call-start = ((), (), s32[]{:S(2)}) async-start(), calls=%async_computation.4 | async-start | bytes 3932160 | tf_op jit(solution)/shard_map/reduce_scatter | solution.py:324
  177.3 0.7 copy-start.4
  178.0 0.7 copy-start.5
  188.7 0.7 copy-start.10
  189.4 14.1 %collective-permute-start.26 = (bf16[256,512]{1,0:T(8,128)(2,1)}, bf16[256,512]{1,0:T(8,128)(2,1)S(1)}, u32[]{:S(2)}, u32[]{:S(2)}) collective-permute-start(bf16[256,512]{1,0:T(8,128)(2,1)} %get-tuple-element.59.refs_11_), channel_id=1, source_target_pairs={{0,32},{32,0},{1,33},{33,1},{2,34},{34,2},{3,35},{35,3},{4,36},{36... | collective-permute-start | bytes 786440 | tf_op jit(solution)/shard_map/ppermute | solution.py:272
  190.1 13.4 %collective-permute-start.27 = (bf16[256,512]{1,0:T(8,128)(2,1)}, bf16[256,512]{1,0:T(8,128)(2,1)S(1)}, u32[]{:S(2)}, u32[]{:S(2)}) collective-permute-start(bf16[256,512]{1,0:T(8,128)(2,1)} %get-tuple-element.60.refs_13_), channel_id=1, source_target_pairs={{0,32},{32,0},{1,33},{33,1},{2,34},{34,2},{3,35},{35,3},{4,36},{36... | collective-permute-start | bytes 786440 | tf_op jit(solution)/shard_map/ppermute | solution.py:272
  196.7 41.1 %all-to-all-start = ((bf16[4,128,1536]{2,1,0:T(8,128)(2,1)}), bf16[4,128,1536]{2,1,0:T(8,128)(2,1)}, u32[]{:S(2)}, u32[]{:S(2)}) async-start(bf16[4,128,1536]{2,1,0:T(8,128)(2,1)} %bitcast.3), calls=%async_computation | async-start | bytes 3145728 | tf_op jit(solution)/shard_map/all_to_all | solution.py:319
  203.5 0.7 copy-start.11
  204.2 0.7 copy-start.12
  215.0 11.5 %collective-permute-start.28 = (bf16[1536,128]{1,0:T(8,128)(2,1)S(1)}, bf16[1536,128]{1,0:T(8,128)(2,1)S(1)}, u32[]{:S(2)}, u32[]{:S(2)}) collective-permute-start(bf16[1536,128]{1,0:T(8,128)(2,1)S(1)} %get-tuple-element.61), channel_id=1, source_target_pairs={{0,4},{2,6},{4,0},{6,2},{1,5},{3,7},{5,1},{7,3},{8,12},{10,14},{12... | collective-permute-start | bytes 1179656 | tf_op jit(solution)/shard_map/ppermute | solution.py:272
  218.6 18.0 %collective-permute-start.30 = (bf16[1536,128]{1,0:T(8,128)(2,1)S(1)}, bf16[1536,128]{1,0:T(8,128)(2,1)S(1)}, u32[]{:S(2)}, u32[]{:S(2)}) collective-permute-start(bf16[1536,128]{1,0:T(8,128)(2,1)S(1)} %get-tuple-element.62), channel_id=1, source_target_pairs={{0,6},{2,4},{4,2},{6,0},{1,7},{3,5},{5,3},{7,1},{8,14},{10,12},{12... | collective-permute-start | bytes 1179656 | tf_op jit(solution)/shard_map/ppermute | solution.py:272
  219.1 17.5 %collective-permute-start.29 = (bf16[1536,128]{1,0:T(8,128)(2,1)S(1)}, bf16[1536,128]{1,0:T(8,128)(2,1)S(1)}, u32[]{:S(2)}, u32[]{:S(2)}) collective-permute-start(bf16[1536,128]{1,0:T(8,128)(2,1)S(1)} %get-tuple-element.63), channel_id=1, source_target_pairs={{0,2},{2,0},{4,6},{6,4},{1,3},{3,1},{5,7},{7,5},{8,10},{10,8},{12,... | collective-permute-start | bytes 1179656 | tf_op jit(solution)/shard_map/ppermute | solution.py:272
Sparse Core Ops, SparseCore 0:
  60.4 39.5 all-gather.1
  179.8 40.6 reduce-scatter.1

commit v4 on v3

v4 whole, which is shorter than its diff:
```python
import jax
import jax.numpy as jnp
from jax import lax
from jax.experimental import pallas as pl
from jax.experimental.pallas import tpu as pltpu
from jax.sharding import Mesh
from jax.sharding import PartitionSpec as P

K = 1536
F = 3072
S = 256
H = 128
DEPTH = 8
LANE = 128
UNITS = F // (DEPTH * LANE)
CHUNKS = ((0, 1), (1, 2))
N = len(CHUNKS)
LAID = (1, 0)
gelu_coef = 0.7978845608028654
bf16 = jnp.bfloat16
f32 = jnp.float32
MIB = 1 << 20
TF, TG, TK, TE, T4, T5 = 0.01, 30, 0.5, 300, 300, 300
ANY = pl.BlockSpec(memory_space=pl.ANY)
PARAMS = pltpu.CompilerParams(vmem_limit_bytes=63 * MIB)


def cost(micros):
    return pl.CostEstimate(flops=int(micros * 1.15e9), bytes_accessed=int(micros * 3.6e6), transcendentals=0)


def width(chunk):
    return DEPTH * CHUNKS[chunk][1] * LANE


def place(chunk):
    return sum(width(other) for other in LAID[:LAID.index(chunk)])


def after_kernel(*refs):
    pass


def after(values, other, micros=300):
    return pl.pallas_call(
        after_kernel,
        in_specs=[ANY] * (len(values) + 1),
        out_specs=[ANY] * len(values),
        out_shape=[jax.ShapeDtypeStruct(value.shape, value.dtype) for value in values],
        input_output_aliases={n: n for n in range(len(values))},
        cost_estimate=cost(micros),
        name="after",
    )(*values, other)


def partial_kernel(q_ref, b0, b1, b2, b3, w_ref, *refs):
    p0_ref, p1_ref, p2_ref, p3_ref, tk_ref = refs[-5:]

    @pl.when(pl.program_id(0) == 0)
    def _():
        q = q_ref[0]
        for m, block in enumerate((b0, b1, b2, b3)):
            slot = pl.multiple_of(jnp.bitwise_xor(q, m) * H, H)
            tk_ref[pl.ds(slot, H), :] = block[...]

    term = jnp.dot(tk_ref[...], w_ref[...], preferred_element_type=f32).astype(bf16)
    for k, ref in enumerate((p0_ref, p1_ref, p2_ref, p3_ref)):
        ref[...] = term[k * H:(k + 1) * H, :]


def block_partials(q, blocks, weight, part, earlier, wait):
    tile = 1024
    rows = [pl.BlockSpec((H, K), lambda i, q, at=part if block.shape[0] == S else 0: (at, 0)) for block in blocks]
    grid_spec = pltpu.PrefetchScalarGridSpec(
        num_scalar_prefetch=1,
        grid=(F // tile,),
        in_specs=rows + [pl.BlockSpec((K, tile), lambda i, q: (0, i))] + [ANY] * (len(earlier) + len(wait)),
        out_specs=[pl.BlockSpec((H, tile), lambda i, q: (0, i))] * 4
        + [pl.BlockSpec((4 * H, K), lambda i, q: (part, 0))],
    )
    return pl.pallas_call(
        partial_kernel,
        grid_spec=grid_spec,
        out_shape=[jax.ShapeDtypeStruct((H, F), bf16)] * 4 + [jax.ShapeDtypeStruct((4 * S, K), bf16)],
        input_output_aliases={6: 4} if earlier else {},
        compiler_params=PARAMS,
        cost_estimate=cost(TF),
        name="block_partials",
    )(q, *blocks, weight, *earlier, *wait)


def gelu_kernel(part, xl_ref, own_ref, core_ref, far_ref, cot_ref, *refs):
    act_ref, *outs = refs[-(2 + N + part * N):]
    halves, grad_ref, pieces = outs[:N], outs[N], outs[N + 1:]
    xl = xl_ref[0]
    for chunk, (start, units) in enumerate(CHUNKS):
        size = units * LANE
        base = place(chunk)
        for d in range(DEPTH):
            at = slice(d * UNITS * LANE + start * LANE, d * UNITS * LANE + start * LANE + size)
            pre = own_ref[:, at].astype(f32) + core_ref[:, at].astype(f32) + far_ref[:, at].astype(f32)
            inner = gelu_coef * (pre + 0.044715 * pre * pre * pre)
            tangent = jnp.tanh(inner)
            act_ref[:, at] = (0.5 * pre * (1.0 + tangent)).astype(bf16)
            slope = 0.5 * (1.0 + tangent) + 0.5 * pre * (1.0 - tangent * tangent) * gelu_coef * (
                1.0 + 3.0 * 0.044715 * pre * pre
            )
            grad = (cot_ref[:, at].astype(f32) * slope).astype(bf16)
            grad_ref[:, base + d * size:base + (d + 1) * size] = grad
            if part:
                pieces[chunk][:, d * size:(d + 1) * size] = grad
            if d % 2:
                to = d // 2 * size
                halves[chunk][:, to:to + size] = jnp.where(xl == 0, grad, even)
            else:
                even = grad


def gelu_pair(xl, own, core, far, cot, part, earlier, wait):
    rows = 64
    steps = H // rows
    whole = lambda w: pl.BlockSpec((rows, w), lambda i, x: (i + part * steps, 0))
    local = lambda w: pl.BlockSpec((rows, w), lambda i, x: (i, 0))
    widths = [width(chunk) for chunk in range(N)]
    extra = widths if part else []
    grid_spec = pltpu.PrefetchScalarGridSpec(
        num_scalar_prefetch=1,
        grid=(steps,),
        in_specs=[local(F)] * 3 + [whole(F)] + [ANY] * (len(earlier) + len(wait)),
        out_specs=[whole(F)] + [whole(w // 2) for w in widths] + [local(w) for w in [F] + extra],
    )
    return pl.pallas_call(
        lambda *refs: gelu_kernel(part, *refs),
        grid_spec=grid_spec,
        out_shape=[jax.ShapeDtypeStruct((S, F), bf16)]
        + [jax.ShapeDtypeStruct((S, w // 2), bf16) for w in widths]
        + [jax.ShapeDtypeStruct((H, w), bf16) for w in [F] + extra],
        input_output_aliases={5 + i: i for i in range(len(earlier))},
        compiler_params=PARAMS,
        cost_estimate=cost(TG),
        name="gelu_pair",
    )(xl, own, core, far, cot, *earlier, *wait)


def weight_kernel(size, apart, ids_ref, tk_ref, tx_ref, *refs):
    first, second, other = refs[:4], refs[4:8], refs[8:12]
    outs, pg = refs[-5 if apart else -2:-1], refs[-1]

    @pl.when(pl.program_id(0) == 0)
    def _():
        xl, r = ids_ref[0], ids_ref[1]
        for k in range(4):
            for z in range(4):
                at = pl.multiple_of((2 * z + xl) * size, size)
                for part, grads in enumerate((first, second)):
                    row = (4 * part + k) * H
                    pg[row:row + H, z * size:(z + 1) * size] = grads[k][:, pl.ds(at, size)]
            slot = pl.multiple_of(4 * S + jnp.bitwise_xor(r, k) * S, S)
            pg[pl.ds(slot, S), :] = other[k][...]

    tokens = jnp.concatenate([tk_ref[...], tx_ref[...]], axis=0)
    total = lax.dot_general(tokens, pg[...], (((0,), (0,)), ((), ())), preferred_element_type=f32).astype(bf16)
    pieces = [total[:, z * size:(z + 1) * size] for z in range(4)]
    if apart:
        z = ids_ref[2]
        low = [jnp.where(z % 2 == 0, pieces[m], pieces[m ^ 1]) for m in range(4)]
        for m, ref in enumerate(outs):
            ref[...] = jnp.where(z // 2 == 0, low[m], low[m ^ 2])
    else:
        for m, piece in enumerate(pieces):
            outs[0][m] = piece


def weight_part(ids, tk, tx, first, second, other, chunk, apart, wait):
    rows = 512
    w = width(chunk)
    size = CHUNKS[chunk][1] * LANE
    at = lambda array: place(chunk) // w if array.shape[1] == F else 0
    if apart:
        out_specs = [pl.BlockSpec((rows, size), lambda i, x: (i, 0))] * 4
        out_shape = [jax.ShapeDtypeStruct((K, size), bf16)] * 4
    else:
        out_specs = pl.BlockSpec((4, rows, size), lambda i, x: (0, i, 0))
        out_shape = jax.ShapeDtypeStruct((4, K, size), bf16)
    grid_spec = pltpu.PrefetchScalarGridSpec(
        num_scalar_prefetch=1,
        grid=(K // rows,),
        in_specs=[pl.BlockSpec((4 * S, rows), lambda i, x: (0, i))] * 2
        + [pl.BlockSpec((H, w), lambda i, x, at=at(array): (0, at)) for array in (*first, *second)]
        + [pl.BlockSpec((S, w // 2), lambda i, x: (0, 0))] * 4
        + [ANY] * len(wait),
        out_specs=out_specs,
        scratch_shapes=[pltpu.VMEM((8 * S, w // 2), bf16)],
    )
    return pl.pallas_call(
        lambda *refs: weight_kernel(size, apart, *refs),
        grid_spec=grid_spec,
        out_shape=out_shape,
        compiler_params=PARAMS,
        cost_estimate=cost(TK),
        name="weight_part",
    )(ids, tk, tx, *first, *second, *other, *wait)


def input_kernel(counts, r_ref, *refs):
    total = sum(counts)
    w_ref, out_ref = refs[total], refs[-1]
    w = jnp.concatenate(
        [
            w_ref[:, (d * UNITS + start) * LANE:(d * UNITS + start + units) * LANE]
            for start, units in (CHUNKS[chunk] for chunk in LAID)
            for d in range(DEPTH)
        ],
        axis=1,
    )
    rows = []
    for count in counts:
        rows.append(jnp.concatenate([ref[...] for ref in refs[:count]], axis=1))
        refs = refs[count:]
    lhs = jnp.concatenate(rows, axis=0)
    total = lax.dot_general(lhs, w, (((1,), (1,)), ((), ())), preferred_element_type=f32).astype(bf16)
    for k in range(4):
        out_ref[jnp.bitwise_xor(r_ref[1], k)] = total[k * H:(k + 1) * H, :]


def input_part(ids, grads, weight, part, earlier, wait):
    tile = 512
    arrays = [array for block in grads for array in block]
    counts = [len(block) for block in grads]
    grid_spec = pltpu.PrefetchScalarGridSpec(
        num_scalar_prefetch=1,
        grid=(K // tile,),
        in_specs=[pl.BlockSpec(array.shape, lambda i, q: (0, 0)) for array in arrays]
        + [pl.BlockSpec((tile, F), lambda i, q: (i, 0))]
        + [ANY] * (len(earlier) + len(wait)),
        out_specs=pl.BlockSpec((4, H, tile), lambda i, q: (0, part, i)),
    )
    return pl.pallas_call(
        lambda *refs: input_kernel(counts, *refs),
        grid_spec=grid_spec,
        out_shape=jax.ShapeDtypeStruct((4, S, K), bf16),
        input_output_aliases={len(arrays) + 2: 0} if earlier else {},
        compiler_params=PARAMS,
        cost_estimate=cost(TK),
        name="input_part",
    )(ids, *arrays, weight, *earlier, *wait)


def join_kernel(first_ref, second_ref, wait_ref, out_ref):
    size = first_ref.shape[1]
    out_ref[:, :size] = first_ref[...]
    out_ref[:, size:] = second_ref[...]


def join(first, second, wait):
    rows = 768
    block = lambda size: pl.BlockSpec((rows, size), lambda i: (i, 0))
    sizes = [first.shape[1], second.shape[1]]
    return pl.pallas_call(
        join_kernel,
        grid=(K // rows,),
        in_specs=[block(size) for size in sizes] + [ANY],
        out_specs=block(sum(sizes)),
        out_shape=jax.ShapeDtypeStruct((K, sum(sizes)), bf16),
        compiler_params=PARAMS,
        cost_estimate=cost(TK),
        name="join",
    )(first, second, wait)


def add_kernel(a_ref, b_ref, wait_ref, out_ref):
    out_ref[...] = (a_ref[...].astype(f32) + b_ref[...].astype(f32)).astype(bf16)


def add(a, b, wait):
    block = pl.BlockSpec((H, F // 2), lambda i: (0, i))
    return pl.pallas_call(
        add_kernel,
        grid=(2,),
        in_specs=[block, block, ANY],
        out_specs=block,
        out_shape=jax.ShapeDtypeStruct(a.shape, bf16),
        compiler_params=PARAMS,
        cost_estimate=cost(1),
        name="add",
    )(a, b, wait)


def fold_kernel(in_ref, out_ref):
    total = in_ref[0].astype(f32)
    for n in range(1, in_ref.shape[0]):
        total += in_ref[n].astype(f32)
    out_ref[...] = total.astype(bf16)


def fold(pieces):
    count, rows, columns = pieces.shape
    tile = rows // 2
    return pl.pallas_call(
        fold_kernel,
        grid=(2,),
        in_specs=[pl.BlockSpec((count, tile, columns), lambda i: (0, i, 0))],
        out_specs=pl.BlockSpec((tile, columns), lambda i: (i, 0)),
        out_shape=jax.ShapeDtypeStruct((rows, columns), bf16),
        compiler_params=PARAMS,
        cost_estimate=cost(TK),
        name="fold",
    )(pieces)


def swap(value, axis, mask):
    n = lax.axis_size(axis)
    return lax.ppermute(value, axis, [(i, i ^ mask) for i in range(n)])


def shards(tokens, weight, cotangent):
    xh, core, y, xl, z = (lax.axis_index(a) for a in ("xh", "core", "y", "xl", "z"))
    r = 2 * xh + core
    q = jnp.bitwise_xor(r, y).astype(jnp.int32).reshape(1)
    ids = jnp.stack([xl, r, z]).astype(jnp.int32)

    partner = swap(tokens, "xl", 1)
    tx = lax.all_gather(partner, "y", axis=0, tiled=True)
    mine = [tokens[:H], tokens[H:]]
    around = [[swap(half, "y", m) for m in (1, 2, 3)] for half in mine]
    around[1] = after(around[1], tokens, TE)

    p0, p1, p2, p3, tk = block_partials(q, [mine[0], *around[0]], weight, 0, (), ())
    total = add(p2, swap(p3, "core", 1), around[1][0])
    (far,) = after([swap(total, "xh", 1)], total)
    terms = [p0, swap(p1, "core", 1), far]
    p0, p1, p2, p3, tk = block_partials(q, [mine[1], *around[1]], weight, 1, (tk,), (total, partner))
    total = add(p2, swap(p3, "core", 1), far)
    *shared, first = gelu_pair(ids, *terms, cotangent, 0, (), ())
    terms = [p0, swap(p1, "core", 1), swap(total, "xh", 1)]
    first_far = swap(first, "xh", 1)
    activation, *halves, second, second_a, second_b = gelu_pair(ids, *terms, cotangent, 1, shared, (tx,))
    far = [swap(value, "xh", 1) for value in (second_a, second_b)]
    near = [swap(half, "xl", 1) for half in halves]
    cross = [lax.ppermute(half, ("xh", "xl"), [(i, 3 - i) for i in range(4)]) for half in halves]

    def pairs(values, wait, micros=300):
        return [(value, swap(value, "core", 1)) for value in after(values, wait, micros)]

    (first, first_core), first_far, (second, second_core) = pairs([first, first_far, second], halves[0])
    first = [first, first_core, *first_far]
    dx = input_part(ids, [[value] for value in first], weight, 0, (), (second_core,))
    far[0], near[0], cross[0] = pairs([far[0], near[0], cross[0]], dx)
    own = [second, second_core]
    dw0 = weight_part(ids, tk, tx, first, [*own, *far[0]], [*near[0], *cross[0]], 0, False, ())
    (far[1],) = pairs([far[1]], dw0)
    blocks = [[value] for value in own] + [[far[chunk][c] for chunk in LAID] for c in range(2)]
    dx = input_part(ids, blocks, weight, 1, (dx,), ())
    near[1], cross[1] = pairs([near[1], cross[1]], dx, T4)
    dw1 = weight_part(ids, tk, tx, first, [*own, *far[1]], [*near[1], *cross[1]], 1, False, ())

    (dx,) = after([lax.all_to_all(dx, "y", 0, 0, tiled=True)], total, T5)
    input_grad = fold(dx)
    dw0, dw1 = (lax.psum_scatter(v, "z", scatter_dimension=0, tiled=True)[0] for v in (dw0, dw1))
    weight_grad = join(dw0, dw1, input_grad)
    return activation, input_grad, weight_grad


def solution(mesh):
    split = Mesh(mesh.devices.reshape(2, 2, 4, 4, 2), ("xh", "core", "y", "z", "xl"))
    hidden = P(("z", "xl", "xh", "core"), "y")
    tokens = P(("z", "xl", "y"), ("xh", "core"))
    return jax.shard_map(
        shards,
        mesh=split,
        in_specs=(tokens, P(("xh", "core"), "y"), hidden),
        out_specs=(hidden, tokens, P(("xh", "core"), ("y", "z", "xl"))),
        check_vma=False,
    )
```

time: 250 us -> 227 us (0.908)
  waiting for transfers between devices: 99.9 us -> 84.9 us
  local copies, waits for them, and re-layouts: 10.8 us -> 5.98 us
  other arithmetic: 4.1 us -> 0.61 us
    ppermute x29 -> x27, waiting for transfers between devices: 80.5 us -> 44.1 us  [swap(): return lax.ppermute(value, axis, [(i, i ^ mask) for i in range(n)])]
    reduce_scatter x1 -> x2, waiting for transfers between devices: 0.01 us -> 16.2 us  [shards(): lax.psum_scatter(v, 'z', scatter_dimension=0, tiled=True)[0]]
    all_to_all x2 -> x1, waiting for transfers between devices: 6.64 us -> 21 us  [shards(): dx, = after([lax.all_to_all(dx, 'y', 0, 0, tiled=True)], total, T5)]
    ppermute x2, waiting for transfers between devices: 12.1 us -> 0.01 us  [shards(): lax.ppermute(half, ('xh', 'xl'), [(i, 3 - i) for i in range(4)])]
    all_gather x1, waiting for transfers between devices: 0.01 us -> 3.57 us  [shards(): tx = lax.all_gather(partner, 'y', axis=0, tiled=True)]
    unnamed x28 -> x26, local copies, waits for them, and re-layouts: 7.5 us -> 4.81 us
    all_to_all x2 -> x1, starting transfers between devices: 8.73 us -> 7.05 us  [shards(): dx, = after([lax.all_to_all(dx, 'y', 0, 0, tiled=True)], total, T5)]
    ppermute x29 -> x27, starting transfers between devices: 30.6 us -> 30.4 us  [swap(): return lax.ppermute(value, axis, [(i, i ^ mask) for i in range(n)])]
  transfers between devices with their start and end apart: 35 -> 33, of which waited for: 14 -> 16; matrix products, arithmetic and copies ran while one was open for 2% -> 0% of each run, Pallas kernels for 32% -> 34%
where the time goes in v4:
time: 227 us; the launch traced here: 226 us
  waiting for transfers between devices  84.9 us (37%)
  Pallas kernels  79.5 us (35%)
  starting transfers between devices  41.1 us (18%)
  between operations  13.9 us (6%)
  local copies, waits for them, and re-layouts  5.98 us (3%)
    ppermute x27, waiting for transfers between devices, swap(): return lax.ppermute(value, axis, [(i, i ^ mask) for i in range(n)])  44.1 us
    ppermute x27, starting transfers between devices, swap(): return lax.ppermute(value, axis, [(i, i ^ mask) for i in range(n)])  30.4 us
    pallas_call x2, Pallas kernels, weight_part(): pl.pallas_call(lambda *refs: weight_kernel(size, apart, *refs), grid_spec...  21.7 us
    all_to_all x1, waiting for transfers between devices, shards(): dx, = after([lax.all_to_all(dx, 'y', 0, 0, tiled=True)], total, T5)  21 us
    pallas_call x2, Pallas kernels, input_part(): pl.pallas_call(lambda *refs: input_kernel(counts, *refs), grid_spec=grid_...  20.1 us
    pallas_call x2, Pallas kernels, block_partials(): pl.pallas_call(partial_kernel, grid_spec=grid_spec, out_shape=[jax.ShapeD...  19.2 us
    reduce_scatter x2, waiting for transfers between devices, shards(): lax.psum_scatter(v, 'z', scatter_dimension=0, tiled=True)[0]  16.2 us
    pallas_call x2, Pallas kernels, gelu_pair(): pl.pallas_call(lambda *refs: gelu_kernel(part, *refs), grid_spec=grid_spe...  9.17 us
  transfers between devices with their start and end apart: 33, of which 16 were waited for; matrix products, arithmetic and copies ran while one was open for 0% of the time, Pallas kernels for 34%

profile of v4, /device:TPU:1, one launch (start us, length us, event | category | flops | bytes accessed | tf_op | source)
XLA Modules:
  0.0 226.0 jit_solution(5364362134497129367)
XLA Ops:
  7.2 0.0 all-gather.2.cloned.1.call-start
  7.2 1.2 fusion
  8.4 3.6 %collective-permute-start.5 = (bf16[128,1536]{1,0:T(8,128)(2,1)S(1)}, bf16[128,1536]{1,0:T(8,128)(2,1)S(1)}, u32[]{:S(2)}, u32[]{:S(2)}) collective-permute-start(bf16[128,1536]{1,0:T(8,128)(2,1)S(1)} %get-tuple-element.65.b0), channel_id=1, source_target_pairs={{0,24},{8,16},{16,8},{24,0},{1,25},{9,17},{17,9},{25,1},{2,26},{10... | collective-permute-start | bytes 1179656 | tf_op jit(solution)/shard_map/ppermute | solution.py:313
  12.0 0.3 collective-permute-start.4
  12.4 0.3 collective-permute-start.3
  12.7 2.6 %collective-permute-start.2 = (bf16[128,1536]{1,0:T(8,128)(2,1)S(1)}, bf16[128,1536]{1,0:T(8,128)(2,1)}, u32[]{:S(2)}, u32[]{:S(2)}) collective-permute-start(bf16[128,1536]{1,0:T(8,128)(2,1)S(1)} %get-tuple-element.66.b0), channel_id=1, source_target_pairs={{0,24},{8,16},{16,8},{24,0},{1,25},{9,17},{17,9},{25,1},{2,26},{10... | collective-permute-start | bytes 1179656 | tf_op jit(solution)/shard_map/ppermute | solution.py:313
  15.3 0.3 collective-permute-start.1
  15.6 13.5 %collective-permute-done.5.b3 = bf16[128,1536]{1,0:T(8,128)(2,1)S(1)} collective-permute-done((bf16[128,1536]{1,0:T(8,128)(2,1)S(1)}, bf16[128,1536]{1,0:T(8,128)(2,1)S(1)}, u32[]{:S(2)}, u32[]{:S(2)}) %collective-permute-start.5) | collective-permute-done | bytes 393248 | tf_op jit(solution)/shard_map/ppermute | solution.py:313
  29.2 0.7 copy-done.7
  29.9 1.2 collective-permute-start.7
  31.1 0.8 copy-done.9
  31.9 9.6 %block_partials.2 = (bf16[128,3072]{1,0:T(8,128)(2,1)}, bf16[128,3072]{1,0:T(8,128)(2,1)}, bf16[128,3072]{1,0:T(8,128)(2,1)}, bf16[128,3072]{1,0:T(8,128)(2,1)}, bf16[1024,1536]{1,0:T(8,128)(2,1)}) custom-call(s32[1]{0:T(128)} %bitcast.3.q_ref, bf16[128,1536]{1,0:T(8,128)(2,1)} %copy-done.3, bf16[128,1536]{1,0:T(8,128)(2,1)} %copy-done.9, ...), custom_call_target="tpu_custom_call" | custom-call | flops 11500000 | bytes 36000 | tf_op jit(solution)/shard_map/block_partials/pallas_call | solution.py:81
  41.5 3.2 %collective-permute-start.6 = (bf16[128,3072]{1,0:T(8,128)(2,1)}, bf16[128,3072]{1,0:T(8,128)(2,1)}, u32[]{:S(2)}, u32[]{:S(2)}) collective-permute-start(bf16[128,3072]{1,0:T(8,128)(2,1)} %get-tuple-element.39), channel_id=1, source_target_pairs={{0,32},{32,0},{1,33},{33,1},{2,34},{34,2},{3,35},{35,3},{4,36},{36... | collective-permute-start | bytes 2359304 | tf_op jit(solution)/shard_map/ppermute | solution.py:313
  44.7 1.4 collective-permute-done.2.refs_2_
  46.1 0.6 collective-permute-done.refs_0_
  46.7 0.2 collective-permute-done.6.b_ref
  46.9 2.2 add.16.refs_1_
  49.2 2.5 %collective-permute-start.10 = (bf16[128,3072]{1,0:T(8,128)(2,1)}, bf16[128,3072]{1,0:T(8,128)(2,1)S(1)}, u32[]{:S(2)}, u32[]{:S(2)}) collective-permute-start(bf16[128,3072]{1,0:T(8,128)(2,1)} %add.16.refs_1_), channel_id=1, source_target_pairs={{0,64},{64,0},{1,65},{65,1},{2,66},{66,2},{3,67},{67,3},{4,68},{68... | collective-permute-start | bytes 2359304 | tf_op jit(solution)/shard_map/ppermute | solution.py:313
  51.6 0.6 pad_add_fusion.refs_0_
  52.2 1.9 collective-permute-start.12
  54.2 0.0 reduce-scatter.3.cloned.1.call-start
  54.2 9.6 %block_partials.3 = (bf16[128,3072]{1,0:T(8,128)(2,1)}, bf16[128,3072]{1,0:T(8,128)(2,1)}, bf16[128,3072]{1,0:T(8,128)(2,1)}, bf16[128,3072]{1,0:T(8,128)(2,1)}, bf16[1024,1536]{1,0:T(8,128)(2,1)}) custom-call(s32[1]{0:T(128)} %bitcast.3.q_ref, bf16[128,1536]{1,0:T(8,128)(2,1)} %copy-done.4, ...), custom_call_target="tpu_custom_call", output_to_operand_aliasing={{4}: (6, {})} | custom-call | flops 11500000 | bytes 36000 | tf_op jit(solution)/shard_map/block_partials/pallas_call | solution.py:81
  63.8 0.5 collective-permute-start.9
  64.3 4.2 %collective-permute-done.10.refs_0_ = bf16[128,3072]{1,0:T(8,128)(2,1)S(1)} collective-permute-done((bf16[128,3072]{1,0:T(8,128)(2,1)}, bf16[128,3072]{1,0:T(8,128)(2,1)S(1)}, u32[]{:S(2)}, u32[]{:S(2)}) %collective-permute-start.10) | collective-permute-done | bytes 786464 | tf_op jit(solution)/shard_map/ppermute | solution.py:313
  68.6 0.9 copy-done.12
  69.5 2.2 add.17.refs_1_
  71.7 2.2 collective-permute-start.11
  73.8 4.5 %gelu_pair.2 = (bf16[256,3072]{1,0:T(8,128)(2,1)}, bf16[256,512]{1,0:T(8,128)(2,1)}, bf16[256,1024]{1,0:T(8,128)(2,1)}, bf16[128,3072]{1,0:T(8,128)(2,1)}) custom-call(s32[3]{0:T(128)} %pad_add_fusion.refs_0_, bf16[128,3072]{1,0:T(8,128)(2,1)} %get-tuple-element.44.refs_1_, bf16[128,3072]{1,0:T(8,128)(2,1)} %collective-permute-done.12.refs_2_, ...), custom_call_target="tpu_custom_call" | custom-call | flops 34500001792 | bytes 108000000 | tf_op jit(solution)/shard_map/gelu_pair/pallas_call | solution.py:132
  78.4 0.8 collective-permute-start.13
  79.2 11.1 %collective-permute-done.11.refs_3_ = bf16[128,3072]{1,0:T(8,128)(2,1)} collective-permute-done((bf16[128,3072]{1,0:T(8,128)(2,1)}, bf16[128,3072]{1,0:T(8,128)(2,1)}, u32[]{:S(2)}, u32[]{:S(2)}) %collective-permute-start.11) | collective-permute-done | bytes 786464 | tf_op jit(solution)/shard_map/ppermute | solution.py:313
  90.2 3.6 %all-gather.2.cloned.1.call-done.refs_8_.refs_2_ = bf16[1024,1536]{1,0:T(8,128)(2,1)} async-done(((bf16[256,1536]{1,0:T(8,128)(2,1)}), bf16[1024,1536]{1,0:T(8,128)(2,1)}) %all-gather.2.cloned.1.call-update) | async-done | bytes 3145744 | tf_op jit(solution)/shard_map/all_gather | solution.py:323
  93.8 4.6 %gelu_pair.3 = (bf16[256,3072]{1,0:T(8,128)(2,1)}, bf16[256,512]{1,0:T(8,128)(2,1)}, bf16[256,1024]{1,0:T(8,128)(2,1)}, bf16[128,3072]{1,0:T(8,128)(2,1)}, bf16[...) custom-call(s32[3]{0:T(128)} %pad_add_fusion.refs_0_, ...), custom_call_target="tpu_custom_call", output_to_operand_aliasing={{0}: (5, {}), {1}: (6, {}), {2}: (7, {})} | custom-call | flops 34500001792 | bytes 108000000 | tf_op jit(solution)/shard_map/gelu_pair/pallas_call | solution.py:132
  98.5 8.5 %collective-permute-done.13.refs_1_ = bf16[128,3072]{1,0:T(8,128)(2,1)S(1)} collective-permute-done((bf16[128,3072]{1,0:T(8,128)(2,1)}, bf16[128,3072]{1,0:T(8,128)(2,1)S(1)}, u32[]{:S(2)}, u32[]{:S(2)}) %collective-permute-start.13) | collective-permute-done | bytes 786464 | tf_op jit(solution)/shard_map/ppermute | solution.py:313
  107.0 0.9 copy-done.1
  107.9 3.2 %collective-permute-start.14 = (bf16[128,3072]{1,0:T(8,128)(2,1)}, bf16[128,3072]{1,0:T(8,128)(2,1)S(1)}, u32[]{:S(2)}, u32[]{:S(2)}) collective-permute-start(bf16[128,3072]{1,0:T(8,128)(2,1)} %get-tuple-element.53.refs_7_.refs_1_), channel_id=1, source_target_pairs={{0,32},{32,0},{1,33},{33,1},{2,34},{34,2},{3,35},{35,3},{4,36},{36... | collective-permute-start | bytes 2359304 | tf_op jit(solution)/shard_map/ppermute | solution.py:313
  111.1 0.5 collective-permute-start.17
  111.6 1.9 collective-permute-start.20
  113.4 0.5 collective-permute-start.18
  114.0 0.3 collective-permute-done.14.refs_6_.refs_8_.refs_2_
  114.3 0.6 collective-permute-start.19
  114.9 2.5 %collective-permute-start.15 = (bf16[128,2048]{1,0:T(8,128)(2,1)}, bf16[128,2048]{1,0:T(8,128)(2,1)}, u32[]{:S(2)}, u32[]{:S(2)}) collective-permute-start(bf16[128,2048]{1,0:T(8,128)(2,1)} %get-tuple-element.54), channel_id=1, source_target_pairs={{0,64},{64,0},{1,65},{65,1},{2,66},{66,2},{3,67},{67,3},{4,68},{68... | collective-permute-start | bytes 1572872 | tf_op jit(solution)/shard_map/ppermute | solution.py:313
  117.3 10.0 %input_part.2.refs_3_.refs_8_ = bf16[4,256,1536]{2,1,0:T(8,128)(2,1)} custom-call(s32[3]{0:T(128)} %pad_add_fusion.refs_0_, bf16[128,3072]{1,0:T(8,128)(2,1)} %get-tuple-element.56.refs_1_.refs_3_, bf16[128,3072]{1,0:T(8,128)(2,1)} %collective-permute-done.16.refs_2_.refs_4_, bf16[128,3072]{1,0:T(8,128)(2,1)} %get-tuple-element.57.refs_3_.refs_5_, ...), custom_call_target="tpu_custom_call" | custom-call | flops 575000000 | bytes 1800000 | tf_op jit(solution)/shard_map/input_part/pallas_call | solution.py:238
  127.4 1.4 collective-permute-start.22
  128.8 0.5 collective-permute-start.21
  129.3 0.9 collective-permute-done.22.refs_12_
  130.2 0.4 collective-permute-done.23.refs_14_
  130.5 0.4 collective-permute-done.21.refs_10_.refs_6_
  130.9 0.3 copy-done.11
  131.3 0.4 copy-done.5
  131.6 8.7 %weight_part.2.refs_1_ = bf16[4,1536,128]{2,1,0:T(8,128)(2,1)} custom-call(s32[3]{0:T(128)} %pad_add_fusion.refs_0_, bf16[1024,1536]{1,0:T(8,128)(2,1)} %get-tuple-element.55.refs_1_, bf16[1024,1536]{1,0:T(8,128)(2,1)} %all-gather.2.cloned.1.call-done.refs_8_.refs_2_, bf16[128,3072]{1,0:T(8,128)(2,1)} %get-tuple-element.56.refs_1_.refs_3_, ...), custom_call_target="tpu_custom_call" | custom-call | flops 575000000 | bytes 1800000 | tf_op jit(solution)/shard_map/weight_part/pallas_call | solution.py:195
  140.4 0.5 collective-permute-start.24
  140.9 1.8 collective-permute-start.26
  142.7 0.8 copy-done.2
  143.5 10.0 %input_part.3.refs_2_ = bf16[4,256,1536]{2,1,0:T(8,128)(2,1)} custom-call(s32[3]{0:T(128)} %pad_add_fusion.refs_0_, bf16[128,3072]{1,0:T(8,128)(2,1)} %get-tuple-element.53.refs_7_.refs_1_, bf16[128,3072]{1,0:T(8,128)(2,1)} %copy-done, bf16[128,2048]{1,0:T(8,128)(2,1)} %after.11.refs_3_.refs_9_, ...), custom_call_target="tpu_custom_call", output_to_operand_aliasing={{}: (8, {})} | custom-call | flops 575000000 | bytes 1800000 | tf_op jit(solution)/shard_map/input_part/pallas_call | solution.py:238
  153.5 7.0 %all-to-all-start = ((bf16[4,256,1536]{2,1,0:T(8,128)(2,1)}), bf16[4,256,1536]{2,1,0:T(8,128)(2,1)}, u32[]{:S(2)}, u32[]{:S(2)}) async-start(bf16[4,256,1536]{2,1,0:T(8,128)(2,1)} %input_part.3.refs_2_), calls=%async_computation | async-start | bytes 6291456 | tf_op jit(solution)/shard_map/all_to_all | solution.py:357
  160.6 1.1 collective-permute-start.27
  161.7 0.1 collective-permute-start.28
  161.8 1.7 collective-permute-done.27.refs_12_
  163.4 0.9 collective-permute-done.28.refs_14_
  164.3 12.9 %weight_part.3 = bf16[4,1536,256]{2,1,0:T(8,128)(2,1)} custom-call(s32[3]{0:T(128)} %pad_add_fusion.refs_0_, bf16[1024,1536]{1,0:T(8,128)(2,1)} %get-tuple-element.55.refs_1_, bf16[1024,1536]{1,0:T(8,128)(2,1)} %all-gather.2.cloned.1.call-done.refs_8_.refs_2_, bf16[128,3072]{1,0:T(8,128)(2,1)} %get-tuple-element.56.refs_1_.refs_3_, ...), custom_call_target="tpu_custom_call" | custom-call | flops 575000000 | bytes 1800000 | tf_op jit(solution)/shard_map/weight_part/pallas_call | solution.py:195
  177.3 21.0 %all-to-all-done.refs_0_ = bf16[4,256,1536]{2,1,0:T(8,128)(2,1)} async-done(((bf16[4,256,1536]{2,1,0:T(8,128)(2,1)}), bf16[4,256,1536]{2,1,0:T(8,128)(2,1)}, u32[]{:S(2)}, u32[]{:S(2)}) %all-to-all-start) | async-done | bytes 3145760 | tf_op jit(solution)/shard_map/all_to_all | solution.py:357
  198.3 2.8 %fold.1.wait_ref = bf16[256,1536]{1,0:T(8,128)(2,1)} custom-call(bf16[4,256,1536]{2,1,0:T(8,128)(2,1)} %after.12.in_ref), custom_call_target="tpu_custom_call" | custom-call | flops 575000000 | bytes 1800000 | tf_op jit(solution)/shard_map/fold/pallas_call | solution.py:299
  201.1 16.2 %reduce-scatter.5.cloned.1.call-done = bf16[1,1536,256]{2,1,0:T(8,128)(2,1)} async-done(((bf16[4,1536,256]{2,1,0:T(8,128)(2,1)}), bf16[1,1536,256]{2,1,0:T(8,128)(2,1)}) %reduce-scatter.5.cloned.1.call-update) | async-done | bytes 786448 | tf_op jit(solution)/shard_map/reduce_scatter | solution.py:359
  217.3 2.2 join.1
  (52 shorter events, 0.2 us)
Async XLA Ops:
  7.2 86.7 %all-gather.2.cloned.1.call-start = ((), (), s32[]{:S(2)}) async-start(), calls=%async_computation.3 | async-start | bytes 3932160 | tf_op jit(solution)/shard_map/all_gather | solution.py:323
  8.4 23.5 %copy-start.3 = (bf16[128,1536]{1,0:T(8,128)(2,1)}, bf16[128,1536]{1,0:T(8,128)(2,1)S(1)}, u32[]{:S(2)}) copy-start(bf16[128,1536]{1,0:T(8,128)(2,1)S(1)} %get-tuple-element.65.b0) | copy-start | bytes 1179652
  8.4 33.1 %copy-start.4 = (bf16[128,1536]{1,0:T(8,128)(2,1)}, bf16[128,1536]{1,0:T(8,128)(2,1)S(1)}, u32[]{:S(2)}) copy-start(bf16[128,1536]{1,0:T(8,128)(2,1)S(1)} %get-tuple-element.66.b0) | copy-start | bytes 1179652
  8.4 20.8 %collective-permute-start.5 = (bf16[128,1536]{1,0:T(8,128)(2,1)S(1)}, bf16[128,1536]{1,0:T(8,128)(2,1)S(1)}, u32[]{:S(2)}, u32[]{:S(2)}) collective-permute-start(bf16[128,1536]{1,0:T(8,128)(2,1)S(1)} %get-tuple-element.65.b0), channel_id=1, source_target_pairs={{0,24},{8,16},{16,8},{24,0},{1,25},{9,17},{17,9},{25,1},{2,26},{10... | collective-permute-start | bytes 1179656 | tf_op jit(solution)/shard_map/ppermute | solution.py:313
  12.0 17.9 %collective-permute-start.4 = (bf16[128,1536]{1,0:T(8,128)(2,1)S(1)}, bf16[128,1536]{1,0:T(8,128)(2,1)S(1)}, u32[]{:S(2)}, u32[]{:S(2)}) collective-permute-start(bf16[128,1536]{1,0:T(8,128)(2,1)S(1)} %get-tuple-element.65.b0), channel_id=1, source_target_pairs={{0,16},{8,24},{16,0},{24,8},{1,17},{9,25},{17,1},{25,9},{2,18},{10... | collective-permute-start | bytes 1179656 | tf_op jit(solution)/shard_map/ppermute | solution.py:313
  12.4 18.7 %collective-permute-start.3 = (bf16[128,1536]{1,0:T(8,128)(2,1)S(1)}, bf16[128,1536]{1,0:T(8,128)(2,1)S(1)}, u32[]{:S(2)}, u32[]{:S(2)}) collective-permute-start(bf16[128,1536]{1,0:T(8,128)(2,1)S(1)} %get-tuple-element.65.b0), channel_id=1, source_target_pairs={{0,8},{8,0},{16,24},{24,16},{1,9},{9,1},{17,25},{25,17},{2,10},{10... | collective-permute-start | bytes 1179656 | tf_op jit(solution)/shard_map/ppermute | solution.py:313
  12.7 33.4 %collective-permute-start.2 = (bf16[128,1536]{1,0:T(8,128)(2,1)S(1)}, bf16[128,1536]{1,0:T(8,128)(2,1)}, u32[]{:S(2)}, u32[]{:S(2)}) collective-permute-start(bf16[128,1536]{1,0:T(8,128)(2,1)S(1)} %get-tuple-element.66.b0), channel_id=1, source_target_pairs={{0,24},{8,16},{16,8},{24,0},{1,25},{9,17},{17,9},{25,1},{2,26},{10... | collective-permute-start | bytes 1179656 | tf_op jit(solution)/shard_map/ppermute | solution.py:313
  15.3 30.8 %collective-permute-start.1 = (bf16[128,1536]{1,0:T(8,128)(2,1)S(1)}, bf16[128,1536]{1,0:T(8,128)(2,1)}, u32[]{:S(2)}, u32[]{:S(2)}) collective-permute-start(bf16[128,1536]{1,0:T(8,128)(2,1)S(1)} %get-tuple-element.66.b0), channel_id=1, source_target_pairs={{0,16},{8,24},{16,0},{24,8},{1,17},{9,25},{17,1},{25,9},{2,18},{10... | collective-permute-start | bytes 1179656 | tf_op jit(solution)/shard_map/ppermute | solution.py:313
  29.2 0.7 copy-start.7
  29.9 16.8 %collective-permute-start = (bf16[128,1536]{1,0:T(8,128)(2,1)S(1)}, bf16[128,1536]{1,0:T(8,128)(2,1)}, u32[]{:S(2)}, u32[]{:S(2)}) collective-permute-start(bf16[128,1536]{1,0:T(8,128)(2,1)S(1)} %get-tuple-element.66.b0), channel_id=1, source_target_pairs={{0,8},{8,0},{16,24},{24,16},{1,9},{9,1},{17,25},{25,17},{2,10},{10... | collective-permute-start | bytes 1179656 | tf_op jit(solution)/shard_map/ppermute | solution.py:313
  29.9 1.2 copy-start.8
  29.9 24.2 %collective-permute-start.7 = (bf16[256,1536]{1,0:T(8,128)(2,1)}, bf16[256,1536]{1,0:T(8,128)(2,1)}, u32[]{:S(2)}, u32[]{:S(2)}) collective-permute-start(bf16[256,1536]{1,0:T(8,128)(2,1)} %refs_3_.1), channel_id=1, source_target_pairs={{0,1},{1,0},{2,3},{3,2},{4,5},{5,4},{6,7},{7,6},{8,9},{9,8},{10,11... | collective-permute-start | bytes 2359304 | tf_op jit(solution)/shard_map/ppermute | solution.py:313
  31.1 0.8 copy-start.9
  41.5 5.5 %collective-permute-start.6 = (bf16[128,3072]{1,0:T(8,128)(2,1)}, bf16[128,3072]{1,0:T(8,128)(2,1)}, u32[]{:S(2)}, u32[]{:S(2)}) collective-permute-start(bf16[128,3072]{1,0:T(8,128)(2,1)} %get-tuple-element.39), channel_id=1, source_target_pairs={{0,32},{32,0},{1,33},{33,1},{2,34},{34,2},{3,35},{35,3},{4,36},{36... | collective-permute-start | bytes 2359304 | tf_op jit(solution)/shard_map/ppermute | solution.py:313
  49.2 19.4 %collective-permute-start.10 = (bf16[128,3072]{1,0:T(8,128)(2,1)}, bf16[128,3072]{1,0:T(8,128)(2,1)S(1)}, u32[]{:S(2)}, u32[]{:S(2)}) collective-permute-start(bf16[128,3072]{1,0:T(8,128)(2,1)} %add.16.refs_1_), channel_id=1, source_target_pairs={{0,64},{64,0},{1,65},{65,1},{2,66},{66,2},{3,67},{67,3},{4,68},{68... | collective-permute-start | bytes 2359304 | tf_op jit(solution)/shard_map/ppermute | solution.py:313
  52.2 21.6 %collective-permute-start.12 = (bf16[128,3072]{1,0:T(8,128)(2,1)}, bf16[128,3072]{1,0:T(8,128)(2,1)}, u32[]{:S(2)}, u32[]{:S(2)}) collective-permute-start(bf16[128,3072]{1,0:T(8,128)(2,1)} %get-tuple-element.45), channel_id=1, source_target_pairs={{0,32},{32,0},{1,33},{33,1},{2,34},{34,2},{3,35},{35,3},{4,36},{36... | collective-permute-start | bytes 2359304 | tf_op jit(solution)/shard_map/ppermute | solution.py:313
  54.2 146.9 %reduce-scatter.3.cloned.1.call-start = ((), (), s32[]{:S(2)}) async-start(), calls=%async_computation.4 | async-start | bytes 1966080 | tf_op jit(solution)/shard_map/reduce_scatter | solution.py:359
  63.8 15.4 %collective-permute-start.8 = (bf16[128,3072]{1,0:T(8,128)(2,1)}, bf16[128,3072]{1,0:T(8,128)(2,1)}, u32[]{:S(2)}, u32[]{:S(2)}) collective-permute-start(bf16[128,3072]{1,0:T(8,128)(2,1)} %get-tuple-element.41), channel_id=1, source_target_pairs={{0,32},{32,0},{1,33},{33,1},{2,34},{34,2},{3,35},{35,3},{4,36},{36... | collective-permute-start | bytes 2359304 | tf_op jit(solution)/shard_map/ppermute | solution.py:313
  63.8 5.6 %collective-permute-start.9 = (bf16[128,3072]{1,0:T(8,128)(2,1)}, bf16[128,3072]{1,0:T(8,128)(2,1)}, u32[]{:S(2)}, u32[]{:S(2)}) collective-permute-start(bf16[128,3072]{1,0:T(8,128)(2,1)} %get-tuple-element.43), channel_id=1, source_target_pairs={{0,32},{32,0},{1,33},{33,1},{2,34},{34,2},{3,35},{35,3},{4,36},{36... | collective-permute-start | bytes 2359304 | tf_op jit(solution)/shard_map/ppermute | solution.py:313
  68.6 0.9 copy-start.12
  71.7 18.6 %collective-permute-start.11 = (bf16[128,3072]{1,0:T(8,128)(2,1)}, bf16[128,3072]{1,0:T(8,128)(2,1)}, u32[]{:S(2)}, u32[]{:S(2)}) collective-permute-start(bf16[128,3072]{1,0:T(8,128)(2,1)} %add.17.refs_1_), channel_id=1, source_target_pairs={{0,64},{64,0},{1,65},{65,1},{2,66},{66,2},{3,67},{67,3},{4,68},{68... | collective-permute-start | bytes 2359304 | tf_op jit(solution)/shard_map/ppermute | solution.py:313
  78.4 28.6 %collective-permute-start.13 = (bf16[128,3072]{1,0:T(8,128)(2,1)}, bf16[128,3072]{1,0:T(8,128)(2,1)S(1)}, u32[]{:S(2)}, u32[]{:S(2)}) collective-permute-start(bf16[128,3072]{1,0:T(8,128)(2,1)} %get-tuple-element.50.refs_0_), channel_id=1, source_target_pairs={{0,64},{64,0},{1,65},{65,1},{2,66},{66,2},{3,67},{67,3},{4,68},{68... | collective-permute-start | bytes 2359304 | tf_op jit(solution)/shard_map/ppermute | solution.py:313
  107.0 0.9 copy-start.1
  107.9 6.4 %collective-permute-start.14 = (bf16[128,3072]{1,0:T(8,128)(2,1)}, bf16[128,3072]{1,0:T(8,128)(2,1)S(1)}, u32[]{:S(2)}, u32[]{:S(2)}) collective-permute-start(bf16[128,3072]{1,0:T(8,128)(2,1)} %get-tuple-element.53.refs_7_.refs_1_), channel_id=1, source_target_pairs={{0,32},{32,0},{1,33},{33,1},{2,34},{34,2},{3,35},{35,3},{4,36},{36... | collective-permute-start | bytes 2359304 | tf_op jit(solution)/shard_map/ppermute | solution.py:313
  111.1 3.8 %collective-permute-start.16 = (bf16[128,3072]{1,0:T(8,128)(2,1)}, bf16[128,3072]{1,0:T(8,128)(2,1)}, u32[]{:S(2)}, u32[]{:S(2)}) collective-permute-start(bf16[128,3072]{1,0:T(8,128)(2,1)} %get-tuple-element.56.refs_1_.refs_3_), channel_id=1, source_target_pairs={{0,32},{32,0},{1,33},{33,1},{2,34},{34,2},{3,35},{35,3},{4,36},{36... | collective-permute-start | bytes 2359304 | tf_op jit(solution)/shard_map/ppermute | solution.py:313
  111.1 6.3 %collective-permute-start.17 = (bf16[128,3072]{1,0:T(8,128)(2,1)}, bf16[128,3072]{1,0:T(8,128)(2,1)}, u32[]{:S(2)}, u32[]{:S(2)}) collective-permute-start(bf16[128,3072]{1,0:T(8,128)(2,1)} %get-tuple-element.57.refs_3_.refs_5_), channel_id=1, source_target_pairs={{0,32},{32,0},{1,33},{33,1},{2,34},{34,2},{3,35},{35,3},{4,36},{36... | collective-permute-start | bytes 2359304 | tf_op jit(solution)/shard_map/ppermute | solution.py:313
  111.6 15.8 %collective-permute-start.20 = (bf16[256,512]{1,0:T(8,128)(2,1)}, bf16[256,512]{1,0:T(8,128)(2,1)}, u32[]{:S(2)}, u32[]{:S(2)}) collective-permute-start(bf16[256,512]{1,0:T(8,128)(2,1)} %get-tuple-element.52.refs_3_), channel_id=1, source_target_pairs={{0,65},{1,64},{64,1},{65,0},{2,67},{3,66},{66,3},{67,2},{4,69},{5,... | collective-permute-start | bytes 786440 | tf_op jit(solution)/shard_map/ppermute | solution.py:340
  113.4 13.9 %collective-permute-start.18 = (bf16[128,1024]{1,0:T(8,128)(2,1)}, bf16[128,1024]{1,0:T(8,128)(2,1)}, u32[]{:S(2)}, u32[]{:S(2)}) collective-permute-start(bf16[128,1024]{1,0:T(8,128)(2,1)} %get-tuple-element.58), channel_id=1, source_target_pairs={{0,64},{64,0},{1,65},{65,1},{2,66},{66,2},{3,67},{67,3},{4,68},{68... | collective-permute-start | bytes 786440 | tf_op jit(solution)/shard_map/ppermute | solution.py:313
  114.3 3.0 %copy-start = (bf16[128,3072]{1,0:T(8,128)(2,1)}, bf16[128,3072]{1,0:T(8,128)(2,1)S(1)}, u32[]{:S(2)}) copy-start(bf16[128,3072]{1,0:T(8,128)(2,1)S(1)} %collective-permute-done.14.refs_6_.refs_8_.refs_2_) | copy-start | bytes 2359300
  114.3 13.1 %collective-permute-start.19 = (bf16[256,512]{1,0:T(8,128)(2,1)}, bf16[256,512]{1,0:T(8,128)(2,1)}, u32[]{:S(2)}, u32[]{:S(2)}) collective-permute-start(bf16[256,512]{1,0:T(8,128)(2,1)} %get-tuple-element.52.refs_3_), channel_id=1, source_target_pairs={{0,1},{1,0},{2,3},{3,2},{4,5},{5,4},{6,7},{7,6},{8,9},{9,8},{10,11... | collective-permute-start | bytes 786440 | tf_op jit(solution)/shard_map/ppermute | solution.py:313
  114.9 25.5 %collective-permute-start.15 = (bf16[128,2048]{1,0:T(8,128)(2,1)}, bf16[128,2048]{1,0:T(8,128)(2,1)}, u32[]{:S(2)}, u32[]{:S(2)}) collective-permute-start(bf16[128,2048]{1,0:T(8,128)(2,1)} %get-tuple-element.54), channel_id=1, source_target_pairs={{0,64},{64,0},{1,65},{65,1},{2,66},{66,2},{3,67},{67,3},{4,68},{68... | collective-permute-start | bytes 1572872 | tf_op jit(solution)/shard_map/ppermute | solution.py:313
  127.4 2.7 %collective-permute-start.22 = (bf16[256,512]{1,0:T(8,128)(2,1)}, bf16[256,512]{1,0:T(8,128)(2,1)S(1)}, u32[]{:S(2)}, u32[]{:S(2)}) collective-permute-start(bf16[256,512]{1,0:T(8,128)(2,1)} %get-tuple-element.60.refs_11_), channel_id=1, source_target_pairs={{0,32},{32,0},{1,33},{33,1},{2,34},{34,2},{3,35},{35,3},{4,36},{36... | collective-permute-start | bytes 786440 | tf_op jit(solution)/shard_map/ppermute | solution.py:313
  128.8 1.7 collective-permute-start.23
  128.8 2.1 collective-permute-start.21
  130.2 0.8 copy-start.10
  130.5 0.7 copy-start.11
  130.9 0.7 copy-start.5
  140.4 2.3 %collective-permute-start.24 = (bf16[128,2048]{1,0:T(8,128)(2,1)}, bf16[128,2048]{1,0:T(8,128)(2,1)S(1)}, u32[]{:S(2)}, u32[]{:S(2)}) collective-permute-start(bf16[128,2048]{1,0:T(8,128)(2,1)} %after.11.refs_3_.refs_9_), channel_id=1, source_target_pairs={{0,32},{32,0},{1,33},{33,1},{2,34},{34,2},{3,35},{35,3},{4,36},{36... | collective-permute-start | bytes 1572872 | tf_op jit(solution)/shard_map/ppermute | solution.py:313
  140.9 19.7 %collective-permute-start.26 = (bf16[256,1024]{1,0:T(8,128)(2,1)}, bf16[256,1024]{1,0:T(8,128)(2,1)}, u32[]{:S(2)}, u32[]{:S(2)}) collective-permute-start(bf16[256,1024]{1,0:T(8,128)(2,1)} %get-tuple-element.62), channel_id=1, source_target_pairs={{0,65},{1,64},{64,1},{65,0},{2,67},{3,66},{66,3},{67,2},{4,69},{5,... | collective-permute-start | bytes 1572872 | tf_op jit(solution)/shard_map/ppermute | solution.py:340
  142.7 17.9 %collective-permute-start.25 = (bf16[256,1024]{1,0:T(8,128)(2,1)}, bf16[256,1024]{1,0:T(8,128)(2,1)}, u32[]{:S(2)}, u32[]{:S(2)}) collective-permute-start(bf16[256,1024]{1,0:T(8,128)(2,1)} %get-tuple-element.62), channel_id=1, source_target_pairs={{0,1},{1,0},{2,3},{3,2},{4,5},{5,4},{6,7},{7,6},{8,9},{9,8},{10,11... | collective-permute-start | bytes 1572872 | tf_op jit(solution)/shard_map/ppermute | solution.py:313
  142.7 0.8 copy-start.2
  153.5 44.7 %all-to-all-start = ((bf16[4,256,1536]{2,1,0:T(8,128)(2,1)}), bf16[4,256,1536]{2,1,0:T(8,128)(2,1)}, u32[]{:S(2)}, u32[]{:S(2)}) async-start(bf16[4,256,1536]{2,1,0:T(8,128)(2,1)} %input_part.3.refs_2_), calls=%async_computation | async-start | bytes 6291456 | tf_op jit(solution)/shard_map/all_to_all | solution.py:357
  160.6 56.7 %reduce-scatter.5.cloned.1.call-start = ((), (), s32[]{:S(2)}) async-start(), calls=%async_computation.5 | async-start | bytes 3932160 | tf_op jit(solution)/shard_map/reduce_scatter | solution.py:359
  160.6 2.8 %collective-permute-start.27 = (bf16[256,1024]{1,0:T(8,128)(2,1)}, bf16[256,1024]{1,0:T(8,128)(2,1)S(1)}, u32[]{:S(2)}, u32[]{:S(2)}) collective-permute-start(bf16[256,1024]{1,0:T(8,128)(2,1)} %get-tuple-element.63.refs_11_), channel_id=1, source_target_pairs={{0,32},{32,0},{1,33},{33,1},{2,34},{34,2},{3,35},{35,3},{4,36},{36... | collective-permute-start | bytes 1572872 | tf_op jit(solution)/shard_map/ppermute | solution.py:313
  161.7 2.6 %collective-permute-start.28 = (bf16[256,1024]{1,0:T(8,128)(2,1)}, bf16[256,1024]{1,0:T(8,128)(2,1)}, u32[]{:S(2)}, u32[]{:S(2)}) collective-permute-start(bf16[256,1024]{1,0:T(8,128)(2,1)} %get-tuple-element.64.refs_13_), channel_id=1, source_target_pairs={{0,32},{32,0},{1,33},{33,1},{2,34},{34,2},{3,35},{35,3},{4,36},{36... | collective-permute-start | bytes 1572872 | tf_op jit(solution)/shard_map/ppermute | solution.py:313
  163.4 0.9 copy-start.6
Sparse Core Ops, SparseCore 0:
  54.3 39.4 all-gather.1
  142.8 29.3 reduce-scatter.2
  177.4 39.8 reduce-scatter.4

commit v5 on v4

--- a/solution.py
+++ b/solution.py
@@ -10,6 +10,7 @@
 F = 3072
 S = 256
 H = 128
+TILE = 1024
 DEPTH = 8
 LANE = 128
 UNITS = F // (DEPTH * LANE)
@@ -20,7 +21,7 @@
 bf16 = jnp.bfloat16
 f32 = jnp.float32
 MIB = 1 << 20
-TF, TG, TK, TE, T4, T5 = 0.01, 30, 0.5, 300, 300, 300
+TF, TG, TK, TE, T3, T4, T5 = 0.01, 30, 0.5, 300, 2, 300, 300
 ANY = pl.BlockSpec(memory_space=pl.ANY)
 PARAMS = pltpu.CompilerParams(vmem_limit_bytes=63 * MIB)
 
@@ -54,7 +55,7 @@
 
 
 def partial_kernel(q_ref, b0, b1, b2, b3, w_ref, *refs):
-    p0_ref, p1_ref, p2_ref, p3_ref, tk_ref = refs[-5:]
+    p0_ref, p1_ref, p2_ref, *p3_refs, tk_ref = refs[-(4 + F // TILE):]
 
     @pl.when(pl.program_id(0) == 0)
     def _():
@@ -64,25 +65,33 @@
             tk_ref[pl.ds(slot, H), :] = block[...]
 
     term = jnp.dot(tk_ref[...], w_ref[...], preferred_element_type=f32).astype(bf16)
-    for k, ref in enumerate((p0_ref, p1_ref, p2_ref, p3_ref)):
+    for k, ref in enumerate((p0_ref, p1_ref, p2_ref)):
         ref[...] = term[k * H:(k + 1) * H, :]
+    for n, ref in enumerate(p3_refs):
+
+        @pl.when(pl.program_id(0) == n)
+        def _():
+            ref[...] = term[3 * H:, :]
 
 
 def block_partials(q, blocks, weight, part, earlier, wait):
-    tile = 1024
+    steps = F // TILE
     rows = [pl.BlockSpec((H, K), lambda i, q, at=part if block.shape[0] == S else 0: (at, 0)) for block in blocks]
     grid_spec = pltpu.PrefetchScalarGridSpec(
         num_scalar_prefetch=1,
-        grid=(F // tile,),
-        in_specs=rows + [pl.BlockSpec((K, tile), lambda i, q: (0, i))] + [ANY] * (len(earlier) + len(wait)),
-        out_specs=[pl.BlockSpec((H, tile), lambda i, q: (0, i))] * 4
+        grid=(steps,),
+        in_specs=rows + [pl.BlockSpec((K, TILE), lambda i, q: (0, i))] + [ANY] * (len(earlier) + len(wait)),
+        out_specs=[pl.BlockSpec((H, TILE), lambda i, q: (0, i))] * 3
+        + [pl.BlockSpec((H, TILE), lambda i, q: (0, 0))] * steps
         + [pl.BlockSpec((4 * H, K), lambda i, q: (part, 0))],
     )
     return pl.pallas_call(
         partial_kernel,
         grid_spec=grid_spec,
-        out_shape=[jax.ShapeDtypeStruct((H, F), bf16)] * 4 + [jax.ShapeDtypeStruct((4 * S, K), bf16)],
-        input_output_aliases={6: 4} if earlier else {},
+        out_shape=[jax.ShapeDtypeStruct((H, F), bf16)] * 3
+        + [jax.ShapeDtypeStruct((H, TILE), bf16)] * steps
+        + [jax.ShapeDtypeStruct((4 * S, K), bf16)],
+        input_output_aliases={6: 3 + steps} if earlier else {},
         compiler_params=PARAMS,
         cost_estimate=cost(TF),
         name="block_partials",
@@ -142,43 +151,59 @@
     )(xl, own, core, far, cot, *earlier, *wait)
 
 
-def weight_kernel(size, apart, ids_ref, tk_ref, tx_ref, *refs):
+def weight_kernel(size, masks, ids_ref, tk_ref, tx_ref, *refs):
     first, second, other = refs[:4], refs[4:8], refs[8:12]
-    outs, pg = refs[-5 if apart else -2:-1], refs[-1]
+    outs, pg = refs[-(1 + count_outs(masks)):-1], refs[-1]
+    shares = masks or range(4)
 
     @pl.when(pl.program_id(0) == 0)
     def _():
-        xl, r = ids_ref[0], ids_ref[1]
-        for k in range(4):
-            for z in range(4):
-                at = pl.multiple_of((2 * z + xl) * size, size)
+        xl, r, z = ids_ref[0], ids_ref[1], ids_ref[2]
+        for n, share in enumerate(shares):
+            to = jnp.bitwise_xor(z, share) if masks else share
+            cols = slice(n * size, (n + 1) * size)
+            own = pl.ds(pl.multiple_of((2 * to + xl) * size, size), size)
+            near = pl.ds(pl.multiple_of(to * size, size), size)
+            for k in range(4):
                 for part, grads in enumerate((first, second)):
                     row = (4 * part + k) * H
-                    pg[row:row + H, z * size:(z + 1) * size] = grads[k][:, pl.ds(at, size)]
-            slot = pl.multiple_of(4 * S + jnp.bitwise_xor(r, k) * S, S)
-            pg[pl.ds(slot, S), :] = other[k][...]
+                    pg[row:row + H, cols] = grads[k][:, own]
+                slot = pl.multiple_of(4 * S + jnp.bitwise_xor(r, k) * S, S)
+                pg[pl.ds(slot, S), cols] = other[k][:, near]
 
     tokens = jnp.concatenate([tk_ref[...], tx_ref[...]], axis=0)
     total = lax.dot_general(tokens, pg[...], (((0,), (0,)), ((), ())), preferred_element_type=f32).astype(bf16)
-    pieces = [total[:, z * size:(z + 1) * size] for z in range(4)]
-    if apart:
-        z = ids_ref[2]
-        low = [jnp.where(z % 2 == 0, pieces[m], pieces[m ^ 1]) for m in range(4)]
-        for m, ref in enumerate(outs):
-            ref[...] = jnp.where(z // 2 == 0, low[m], low[m ^ 2])
+    if len(shares) == 1:
+        for n, out_ref in enumerate(outs):
+
+            @pl.when(pl.program_id(0) == n)
+            def _():
+                out_ref[...] = total
+
     else:
-        for m, piece in enumerate(pieces):
-            outs[0][m] = piece
-
-
-def weight_part(ids, tk, tx, first, second, other, chunk, apart, wait):
-    rows = 512
+        for n in range(len(shares)):
+            piece = total[:, n * size:(n + 1) * size]
+            if masks:
+                outs[n][...] = piece
+            else:
+                outs[0][n] = piece
+
+
+def count_outs(masks):
+    return max(2, len(masks)) if masks else 1
+
+
+def weight_part(ids, tk, tx, first, second, other, chunk, masks, wait):
     w = width(chunk)
     size = CHUNKS[chunk][1] * LANE
+    rows = K // 2 if len(masks) == 1 else 512
     at = lambda array: place(chunk) // w if array.shape[1] == F else 0
-    if apart:
-        out_specs = [pl.BlockSpec((rows, size), lambda i, x: (i, 0))] * 4
-        out_shape = [jax.ShapeDtypeStruct((K, size), bf16)] * 4
+    if len(masks) == 1:
+        out_specs = [pl.BlockSpec((rows, size), lambda i, x: (0, 0))] * 2
+        out_shape = [jax.ShapeDtypeStruct((rows, size), bf16)] * 2
+    elif masks:
+        out_specs = [pl.BlockSpec((rows, size), lambda i, x: (i, 0))] * len(masks)
+        out_shape = [jax.ShapeDtypeStruct((K, size), bf16)] * len(masks)
     else:
         out_specs = pl.BlockSpec((4, rows, size), lambda i, x: (0, i, 0))
         out_shape = jax.ShapeDtypeStruct((4, K, size), bf16)
@@ -190,16 +215,38 @@
         + [pl.BlockSpec((S, w // 2), lambda i, x: (0, 0))] * 4
         + [ANY] * len(wait),
         out_specs=out_specs,
-        scratch_shapes=[pltpu.VMEM((8 * S, w // 2), bf16)],
-    )
-    return pl.pallas_call(
-        lambda *refs: weight_kernel(size, apart, *refs),
+        scratch_shapes=[pltpu.VMEM((8 * S, size * (len(masks) or 4)), bf16)],
+    )
+    return pl.pallas_call(
+        lambda *refs: weight_kernel(size, masks, *refs),
         grid_spec=grid_spec,
         out_shape=out_shape,
         compiler_params=PARAMS,
         cost_estimate=cost(TK),
         name="weight_part",
     )(ids, tk, tx, *first, *second, *other, *wait)
+
+
+def relay_kernel(a_ref, b_ref, last_ref, first_ref, a_out, b_out):
+    a_out[...] = (a_ref[...].astype(f32) + last_ref[...].astype(f32)).astype(bf16)
+    b_out[...] = (b_ref[...].astype(f32) + first_ref[...].astype(f32)).astype(bf16)
+
+
+def relay(a, b, last, first):
+    rows, columns = last.shape[0] // 2, last.shape[1]
+    top = pl.BlockSpec((rows, columns), lambda i: (i, 0))
+    bottom = pl.BlockSpec((rows, columns), lambda i: (i + 2, 0))
+    return pl.pallas_call(
+        relay_kernel,
+        grid=(2,),
+        in_specs=[bottom, top, top, top],
+        out_specs=[bottom, top],
+        out_shape=[jax.ShapeDtypeStruct(a.shape, bf16)] * 2,
+        input_output_aliases={0: 0, 1: 1},
+        compiler_params=PARAMS,
+        cost_estimate=cost(TK),
+        name="relay",
+    )(a, b, last, first)
 
 
 def input_kernel(counts, r_ref, *refs):
@@ -246,44 +293,52 @@
     )(ids, *arrays, weight, *earlier, *wait)
 
 
-def join_kernel(first_ref, second_ref, wait_ref, out_ref):
+def join_kernel(first_ref, *refs):
     size = first_ref.shape[1]
-    out_ref[:, :size] = first_ref[...]
-    out_ref[:, size:] = second_ref[...]
-
-
-def join(first, second, wait):
-    rows = 768
+    total = refs[0][...].astype(f32)
+    for ref in refs[1:-1]:
+        total += ref[...].astype(f32)
+    refs[-1][:, :size] = first_ref[...]
+    refs[-1][:, size:] = total.astype(bf16)
+
+
+def join(first, pieces, wait):
+    rows = 512
     block = lambda size: pl.BlockSpec((rows, size), lambda i: (i, 0))
-    sizes = [first.shape[1], second.shape[1]]
-    return pl.pallas_call(
-        join_kernel,
+    sizes = [first.shape[1], pieces[0].shape[1]]
+    return pl.pallas_call(
+        lambda *refs: join_kernel(*refs[:1 + len(pieces)], refs[-1]),
         grid=(K // rows,),
-        in_specs=[block(size) for size in sizes] + [ANY],
+        in_specs=[block(sizes[0])] + [block(sizes[1])] * len(pieces) + [ANY],
         out_specs=block(sum(sizes)),
         out_shape=jax.ShapeDtypeStruct((K, sum(sizes)), bf16),
         compiler_params=PARAMS,
         cost_estimate=cost(TK),
         name="join",
-    )(first, second, wait)
-
-
-def add_kernel(a_ref, b_ref, wait_ref, out_ref):
-    out_ref[...] = (a_ref[...].astype(f32) + b_ref[...].astype(f32)).astype(bf16)
-
-
-def add(a, b, wait):
-    block = pl.BlockSpec((H, F // 2), lambda i: (0, i))
+    )(first, *pieces, wait)
+
+
+def add_kernel(a_ref, *refs):
+    out_ref = refs[-1]
+    for n in range(F // TILE):
+
+        @pl.when(pl.program_id(0) == n)
+        def _():
+            out_ref[...] = (a_ref[...].astype(f32) + refs[n][...].astype(f32)).astype(bf16)
+
+
+def add(a, pieces, wait):
+    block = pl.BlockSpec((H, TILE), lambda i: (0, i))
     return pl.pallas_call(
         add_kernel,
-        grid=(2,),
-        in_specs=[block, block, ANY],
+        grid=(F // TILE,),
+        in_specs=[block] + [pl.BlockSpec((H, TILE), lambda i: (0, 0))] * len(pieces) + [ANY],
         out_specs=block,
         out_shape=jax.ShapeDtypeStruct(a.shape, bf16),
         compiler_params=PARAMS,
         cost_estimate=cost(1),
         name="add",
-    )(a, b, wait)
+    )(a, *pieces, wait)
 
 
 def fold_kernel(in_ref, out_ref):
@@ -325,16 +380,16 @@
     around = [[swap(half, "y", m) for m in (1, 2, 3)] for half in mine]
     around[1] = after(around[1], tokens, TE)
 
-    p0, p1, p2, p3, tk = block_partials(q, [mine[0], *around[0]], weight, 0, (), ())
-    total = add(p2, swap(p3, "core", 1), around[1][0])
-    (far,) = after([swap(total, "xh", 1)], total)
+    p0, p1, p2, *p3, tk = block_partials(q, [mine[0], *around[0]], weight, 0, (), ())
+    total = add(p2, [swap(v, "core", 1) for v in p3], around[1][0])
+    (far,) = after([swap(total, "xh", 1)], total, T3)
     terms = [p0, swap(p1, "core", 1), far]
-    p0, p1, p2, p3, tk = block_partials(q, [mine[1], *around[1]], weight, 1, (tk,), (total, partner))
-    total = add(p2, swap(p3, "core", 1), far)
+    p0, p1, p2, *p3, tk = block_partials(q, [mine[1], *around[1]], weight, 1, (tk,), (total, partner))
+    total = add(p2, [swap(v, "core", 1) for v in p3], total)
     *shared, first = gelu_pair(ids, *terms, cotangent, 0, (), ())
     terms = [p0, swap(p1, "core", 1), swap(total, "xh", 1)]
     first_far = swap(first, "xh", 1)
-    activation, *halves, second, second_a, second_b = gelu_pair(ids, *terms, cotangent, 1, shared, (tx,))
+    activation, *halves, second, second_a, second_b = gelu_pair(ids, *terms, cotangent, 1, shared, ())
     far = [swap(value, "xh", 1) for value in (second_a, second_b)]
     near = [swap(half, "xl", 1) for half in halves]
     cross = [lax.ppermute(half, ("xh", "xl"), [(i, 3 - i) for i in range(4)]) for half in halves]
@@ -344,20 +399,24 @@
 
     (first, first_core), first_far, (second, second_core) = pairs([first, first_far, second], halves[0])
     first = [first, first_core, *first_far]
-    dx = input_part(ids, [[value] for value in first], weight, 0, (), (second_core,))
+    dx = input_part(ids, [[value] for value in first], weight, 0, (), (second_core, tx))
     far[0], near[0], cross[0] = pairs([far[0], near[0], cross[0]], dx)
     own = [second, second_core]
-    dw0 = weight_part(ids, tk, tx, first, [*own, *far[0]], [*near[0], *cross[0]], 0, False, ())
+    dw0 = weight_part(ids, tk, tx, first, [*own, *far[0]], [*near[0], *cross[0]], 0, (), ())
     (far[1],) = pairs([far[1]], dw0)
     blocks = [[value] for value in own] + [[far[chunk][c] for chunk in LAID] for c in range(2)]
     dx = input_part(ids, blocks, weight, 1, (dx,), ())
     near[1], cross[1] = pairs([near[1], cross[1]], dx, T4)
-    dw1 = weight_part(ids, tk, tx, first, [*own, *far[1]], [*near[1], *cross[1]], 1, False, ())
+    dw0 = lax.psum_scatter(dw0, "z", scatter_dimension=0, tiled=True)[0]
+    last = [first, [*own, *far[1]], [*near[1], *cross[1]], 1]
+    top, bottom = weight_part(ids, tk, tx, *last, (2,), ())
+    to_right, to_left = swap(top, "z", 1), swap(bottom, "z", 3)
+    mine, one, three = weight_part(ids, tk, tx, *last, (0, 1, 3), (top, dw0))
+    one, three = relay(one, three, to_left, to_right)
 
     (dx,) = after([lax.all_to_all(dx, "y", 0, 0, tiled=True)], total, T5)
     input_grad = fold(dx)
-    dw0, dw1 = (lax.psum_scatter(v, "z", scatter_dimension=0, tiled=True)[0] for v in (dw0, dw1))
-    weight_grad = join(dw0, dw1, input_grad)
+    weight_grad = join(dw0, [mine, swap(one, "z", 1), swap(three, "z", 3)], input_grad)
     return activation, input_grad, weight_grad
 
 

time: 227 us -> 220 us (0.969)
  waiting for transfers between devices: 84.9 us -> 65.5 us
  Pallas kernels: 79.5 us -> 91.6 us
    reduce_scatter x2 -> x1, waiting for transfers between devices: 16.2 us -> 0.01 us  [shards(): dw0 = lax.psum_scatter(dw0, 'z', scatter_dimension=0, tiled=True)[0]]
    ppermute x27 -> x35, waiting for transfers between devices: 44.1 us -> 58 us  [swap(): return lax.ppermute(value, axis, [(i, i ^ mask) for i in range(n)])]
    all_to_all x1, waiting for transfers between devices: 21 us -> 7.27 us  [shards(): dx, = after([lax.all_to_all(dx, 'y', 0, 0, tiled=True)], total, T5)]
    pallas_call x5 -> x7, Pallas kernels: 28.3 us -> 39.5 us  [the longest x3 27.2 us: weight_part(): pl.pallas_call(lambda *refs: weight_kernel(size, masks, *refs), grid_spec...]
    all_gather x1, waiting for transfers between devices: 3.57 us -> 0.01 us  [shards(): tx = lax.all_gather(partner, 'y', axis=0, tiled=True)]
    ppermute x27 -> x35, starting transfers between devices: 30.4 us -> 33.6 us  [swap(): return lax.ppermute(value, axis, [(i, i ^ mask) for i in range(n)])]
    all_to_all x1, starting transfers between devices: 7.05 us -> 4.64 us  [shards(): dx, = after([lax.all_to_all(dx, 'y', 0, 0, tiled=True)], total, T5)]
    unnamed x26 -> x30, local copies, waits for them, and re-layouts: 4.81 us -> 4.76 us
  transfers between devices with their start and end apart: 33 -> 40, of which waited for: 16 -> 22; matrix products, arithmetic and copies ran while one was open for 0% -> 0% of each run, Pallas kernels for 34% -> 40%
where the time goes in v5:
time: 220 us; the launch traced here: 218 us
  Pallas kernels  91.6 us (42%)
  waiting for transfers between devices  65.5 us (30%)
  starting transfers between devices  40.2 us (18%)
  between operations  14.2 us (6%)
  local copies, waits for them, and re-layouts  5.93 us (3%)
    ppermute x35, waiting for transfers between devices, swap(): return lax.ppermute(value, axis, [(i, i ^ mask) for i in range(n)])  58 us
    ppermute x35, starting transfers between devices, swap(): return lax.ppermute(value, axis, [(i, i ^ mask) for i in range(n)])  33.6 us
    pallas_call x3, Pallas kernels, weight_part(): pl.pallas_call(lambda *refs: weight_kernel(size, masks, *refs), grid_spec...  27.2 us
    pallas_call x2, Pallas kernels, input_part(): pl.pallas_call(lambda *refs: input_kernel(counts, *refs), grid_spec=grid_...  20.1 us
    pallas_call x2, Pallas kernels, block_partials(): pl.pallas_call(partial_kernel, grid_spec=grid_spec, out_shape=[jax.ShapeD...  19.9 us
    pallas_call x2, Pallas kernels, gelu_pair(): pl.pallas_call(lambda *refs: gelu_kernel(part, *refs), grid_spec=grid_spe...  9.16 us
    all_to_all x1, waiting for transfers between devices, shards(): dx, = after([lax.all_to_all(dx, 'y', 0, 0, tiled=True)], total, T5)  7.27 us
    pallas_call x2, Pallas kernels, add(): pl.pallas_call(add_kernel, grid=(F // TILE,), in_specs=[block] + [pl.Bloc...  6.43 us
  transfers between devices with their start and end apart: 40, of which 22 were waited for; matrix products, arithmetic and copies ran while one was open for 0% of the time, Pallas kernels for 40%

profile of v5, /device:TPU:1, one launch (start us, length us, event | category | flops | bytes accessed | tf_op | source)
XLA Modules:
  0.0 217.9 jit_solution(7165649724078364939)
XLA Ops:
  7.2 1.2 fusion
  8.4 3.6 %collective-permute-start.5 = (bf16[128,1536]{1,0:T(8,128)(2,1)S(1)}, bf16[128,1536]{1,0:T(8,128)(2,1)S(1)}, u32[]{:S(2)}, u32[]{:S(2)}) collective-permute-start(bf16[128,1536]{1,0:T(8,128)(2,1)S(1)} %get-tuple-element.87.b0), channel_id=1, source_target_pairs={{0,24},{8,16},{16,8},{24,0},{1,25},{9,17},{17,9},{25,1},{2,26},{10... | collective-permute-start | bytes 1179656 | tf_op jit(solution)/shard_map/ppermute | solution.py:368
  12.7 2.6 %collective-permute-start.2 = (bf16[128,1536]{1,0:T(8,128)(2,1)S(1)}, bf16[128,1536]{1,0:T(8,128)(2,1)}, u32[]{:S(2)}, u32[]{:S(2)}) collective-permute-start(bf16[128,1536]{1,0:T(8,128)(2,1)S(1)} %get-tuple-element.88.b0), channel_id=1, source_target_pairs={{0,24},{8,16},{16,8},{24,0},{1,25},{9,17},{17,9},{25,1},{2,26},{10... | collective-permute-start | bytes 1179656 | tf_op jit(solution)/shard_map/ppermute | solution.py:368
  15.6 13.5 %collective-permute-done.5.b3 = bf16[128,1536]{1,0:T(8,128)(2,1)S(1)} collective-permute-done((bf16[128,1536]{1,0:T(8,128)(2,1)S(1)}, bf16[128,1536]{1,0:T(8,128)(2,1)S(1)}, u32[]{:S(2)}, u32[]{:S(2)}) %collective-permute-start.5) | collective-permute-done | bytes 393248 | tf_op jit(solution)/shard_map/ppermute | solution.py:368
  29.2 0.8 copy-done.7
  29.9 1.2 collective-permute-start.9
  31.1 0.8 copy-done.9
  31.9 10.0 %block_partials.2 = (bf16[128,3072]{1,0:T(8,128)(2,1)}, bf16[128,3072]{1,0:T(8,128)(2,1)}, bf16[128,3072]{1,0:T(8,128)(2,1)}, bf16[128,1024]{1,0:T(8,128)(2,1)},...) custom-call(s32[1]{0:T(128)} %bitcast.3.q_ref, bf16[128,1536]{1,0:T(8,128)(2,1)} %copy-done.4, ...), custom_call_target="tpu_custom_call" | custom-call | flops 11500000 | bytes 36000 | tf_op jit(solution)/shard_map/block_partials/pallas_call | solution.py:88
  41.9 3.2 %collective-permute-start.6 = (bf16[128,1024]{1,0:T(8,128)(2,1)}, bf16[128,1024]{1,0:T(8,128)(2,1)}, u32[]{:S(2)}, u32[]{:S(2)}) collective-permute-start(bf16[128,1024]{1,0:T(8,128)(2,1)} %get-tuple-element.50), channel_id=1, source_target_pairs={{0,32},{32,0},{1,33},{33,1},{2,34},{34,2},{3,35},{35,3},{4,36},{36... | collective-permute-start | bytes 786440 | tf_op jit(solution)/shard_map/ppermute | solution.py:368
  45.1 1.0 collective-permute-done.2.refs_2_
  46.1 1.4 collective-permute-start.7
  47.5 1.5 collective-permute-done.7.refs_1_
  49.0 0.4 collective-permute-done.8.refs_2_
  49.4 3.2 %add.13.refs_1_.refs_3_ = bf16[128,3072]{1,0:T(8,128)(2,1)} custom-call(bf16[128,3072]{1,0:T(8,128)(2,1)} %get-tuple-element.49.a_ref, bf16[128,1024]{1,0:T(8,128)(2,1)} %collective-permute-done.6.refs_0_, bf16[128,1024]{1,0:T(8,128)(2,1)} %collective-permute-done.7.refs_1_, bf16[128,1024]{1,0:T(8,128)(2,1)} %collective-permute-done.8.refs_2_, ...), custom_call_target="tpu_custom_call" | custom-call | flops 1150000000 | bytes 3600000 | tf_op jit(solution)/shard_map/add/pallas_call | solution.py:332
  52.6 2.7 %collective-permute-start.16 = (bf16[128,3072]{1,0:T(8,128)(2,1)}, bf16[128,3072]{1,0:T(8,128)(2,1)}, u32[]{:S(2)}, u32[]{:S(2)}) collective-permute-start(bf16[128,3072]{1,0:T(8,128)(2,1)} %add.13.refs_1_.refs_3_), channel_id=1, source_target_pairs={{0,64},{64,0},{1,65},{65,1},{2,66},{66,2},{3,67},{67,3},{4,68},{68... | collective-permute-start | bytes 2359304 | tf_op jit(solution)/shard_map/ppermute | solution.py:368
  55.3 0.7 collective-permute-start.15
  56.0 9.9 %block_partials.3 = (bf16[128,3072]{1,0:T(8,128)(2,1)}, bf16[128,3072]{1,0:T(8,128)(2,1)}, bf16[128,3072]{1,0:T(8,128)(2,1)}, bf16[128,1024]{1,0:T(8,128)(2,1)},...) custom-call(s32[1]{0:T(128)} %bitcast.3.q_ref, ...), custom_call_target="tpu_custom_call", output_to_operand_aliasing={{6}: (6, {})} | custom-call | flops 11500000 | bytes 36000 | tf_op jit(solution)/shard_map/block_partials/pallas_call | solution.py:88
  66.0 0.5 collective-permute-start.12
  66.6 0.6 pad_add_fusion.refs_0_
  67.2 0.6 collective-permute-done.11.refs_0_
  68.2 0.4 collective-permute-done.13.refs_2_
  68.6 3.2 %add.14.refs_1_ = bf16[128,3072]{1,0:T(8,128)(2,1)} custom-call(bf16[128,3072]{1,0:T(8,128)(2,1)} %get-tuple-element.55.a_ref, bf16[128,1024]{1,0:T(8,128)(2,1)} %collective-permute-done.11.refs_0_, bf16[128,1024]{1,0:T(8,128)(2,1)} %collective-permute-done.12.refs_1_, bf16[128,1024]{1,0:T(8,128)(2,1)} %collective-permute-done.13.refs_2_, ...), custom_call_target="tpu_custom_call" | custom-call | flops 1150000000 | bytes 3600000 | tf_op jit(solution)/shard_map/add/pallas_call | solution.py:332
  72.1 1.1 collective-permute-done.16.refs_0_
  73.2 4.5 %gelu_pair.2 = (bf16[256,3072]{1,0:T(8,128)(2,1)}, bf16[256,512]{1,0:T(8,128)(2,1)}, bf16[256,1024]{1,0:T(8,128)(2,1)}, bf16[128,3072]{1,0:T(8,128)(2,1)}) custom-call(s32[3]{0:T(128)} %pad_add_fusion.refs_0_, bf16[128,3072]{1,0:T(8,128)(2,1)} %get-tuple-element.59.refs_1_, bf16[128,3072]{1,0:T(8,128)(2,1)} %collective-permute-done.15.refs_2_, ...), custom_call_target="tpu_custom_call" | custom-call | flops 34500001792 | bytes 108000000 | tf_op jit(solution)/shard_map/gelu_pair/pallas_call | solution.py:141
  77.7 2.7 %collective-permute-start.17 = (bf16[128,3072]{1,0:T(8,128)(2,1)}, bf16[128,3072]{1,0:T(8,128)(2,1)S(1)}, u32[]{:S(2)}, u32[]{:S(2)}) collective-permute-start(bf16[128,3072]{1,0:T(8,128)(2,1)} %get-tuple-element.65.refs_0_), channel_id=1, source_target_pairs={{0,64},{64,0},{1,65},{65,1},{2,66},{66,2},{3,67},{67,3},{4,68},{68... | collective-permute-start | bytes 2359304 | tf_op jit(solution)/shard_map/ppermute | solution.py:368
  80.4 12.3 %collective-permute-done.14.refs_3_ = bf16[128,3072]{1,0:T(8,128)(2,1)} collective-permute-done((bf16[128,3072]{1,0:T(8,128)(2,1)}, bf16[128,3072]{1,0:T(8,128)(2,1)}, u32[]{:S(2)}, u32[]{:S(2)}) %collective-permute-start.14) | collective-permute-done | bytes 786464 | tf_op jit(solution)/shard_map/ppermute | solution.py:368
  92.7 4.7 %gelu_pair.3 = (bf16[256,3072]{1,0:T(8,128)(2,1)}, bf16[256,512]{1,0:T(8,128)(2,1)}, bf16[256,1024]{1,0:T(8,128)(2,1)}, bf16[128,3072]{1,0:T(8,128)(2,1)}, bf16[...) custom-call(s32[3]{0:T(128)} %pad_add_fusion.refs_0_, ...), custom_call_target="tpu_custom_call", output_to_operand_aliasing={{0}: (5, {}), {1}: (6, {}), {2}: (7, {})} | custom-call | flops 34500001792 | bytes 108000000 | tf_op jit(solution)/shard_map/gelu_pair/pallas_call | solution.py:141
  97.3 12.1 %collective-permute-done.17.refs_1_ = bf16[128,3072]{1,0:T(8,128)(2,1)S(1)} collective-permute-done((bf16[128,3072]{1,0:T(8,128)(2,1)}, bf16[128,3072]{1,0:T(8,128)(2,1)S(1)}, u32[]{:S(2)}, u32[]{:S(2)}) %collective-permute-start.17) | collective-permute-done | bytes 786464 | tf_op jit(solution)/shard_map/ppermute | solution.py:368
  109.4 0.9 copy-done.1
  110.3 1.0 collective-permute-start.18
  111.2 0.5 collective-permute-start.21
  111.8 0.9 collective-permute-start.24
  112.6 1.2 collective-permute-start.22
  113.9 0.6 collective-permute-done.18.refs_6_.refs_8_.refs_2_
  114.5 0.6 collective-permute-start.23
  115.0 1.5 collective-permute-start.19
  116.5 10.1 %input_part.2.refs_3_.refs_8_ = bf16[4,256,1536]{2,1,0:T(8,128)(2,1)} custom-call(s32[3]{0:T(128)} %pad_add_fusion.refs_0_, bf16[128,3072]{1,0:T(8,128)(2,1)} %get-tuple-element.71.refs_1_.refs_3_, bf16[128,3072]{1,0:T(8,128)(2,1)} %collective-permute-done.20.refs_2_.refs_4_, bf16[128,3072]{1,0:T(8,128)(2,1)} %get-tuple-element.72.refs_3_.refs_5_, ...), custom_call_target="tpu_custom_call" | custom-call | flops 575000000 | bytes 1800000 | tf_op jit(solution)/shard_map/input_part/pallas_call | solution.py:285
  127.1 1.8 collective-permute-start.26
  129.0 0.5 collective-permute-start.25
  129.5 0.9 collective-permute-done.26.refs_12_
  130.3 0.4 collective-permute-done.27.refs_14_
  130.7 0.4 collective-permute-done.25.refs_10_.refs_6_
  131.4 0.4 copy-done.6
  131.8 8.7 %weight_part.3.refs_1_ = bf16[4,1536,128]{2,1,0:T(8,128)(2,1)} custom-call(s32[3]{0:T(128)} %pad_add_fusion.refs_0_, bf16[1024,1536]{1,0:T(8,128)(2,1)} %get-tuple-element.70.refs_1_, bf16[1024,1536]{1,0:T(8,128)(2,1)} %all-gather.2.cloned.1.call-done.refs_7_.refs_2_, bf16[128,3072]{1,0:T(8,128)(2,1)} %get-tuple-element.71.refs_1_.refs_3_, ...), custom_call_target="tpu_custom_call" | custom-call | flops 575000000 | bytes 1800000 | tf_op jit(solution)/shard_map/weight_part/pallas_call | solution.py:220
  140.5 0.5 collective-permute-start.28
  140.9 1.0 collective-permute-start.30
  141.9 0.8 collective-permute-done.28.refs_5_.refs_10_
  142.7 0.8 copy-done.2
  143.5 10.0 %input_part.3.refs_2_ = bf16[4,256,1536]{2,1,0:T(8,128)(2,1)} custom-call(s32[3]{0:T(128)} %pad_add_fusion.refs_0_, bf16[128,3072]{1,0:T(8,128)(2,1)} %get-tuple-element.68.refs_7_.refs_1_, bf16[128,3072]{1,0:T(8,128)(2,1)} %copy-done, bf16[128,2048]{1,0:T(8,128)(2,1)} %after.11.refs_3_.refs_9_, ...), custom_call_target="tpu_custom_call", output_to_operand_aliasing={{}: (8, {})} | custom-call | flops 575000000 | bytes 1800000 | tf_op jit(solution)/shard_map/input_part/pallas_call | solution.py:285
  153.4 4.6 %all-to-all-start = ((bf16[4,256,1536]{2,1,0:T(8,128)(2,1)}), bf16[4,256,1536]{2,1,0:T(8,128)(2,1)}, u32[]{:S(2)}, u32[]{:S(2)}) async-start(bf16[4,256,1536]{2,1,0:T(8,128)(2,1)} %input_part.3.refs_2_), calls=%async_computation | async-start | bytes 6291456 | tf_op jit(solution)/shard_map/all_to_all | solution.py:417
  158.1 0.5 collective-permute-start.31
  158.7 1.6 collective-permute-done.31.refs_12_
  160.3 0.9 collective-permute-done.32.refs_14_
  161.2 7.7 %weight_part.4 = (bf16[768,256]{1,0:T(8,128)(2,1)}, bf16[768,256]{1,0:T(8,128)(2,1)}) custom-call(s32[3]{0:T(128)} %pad_add_fusion.refs_0_, bf16[1024,1536]{1,0:T(8,128)(2,1)} %get-tuple-element.70.refs_1_, bf16[1024,1536]{1,0:T(8,128)(2,1)} %all-gather.2.cloned.1.call-done.refs_7_.refs_2_, bf16[128,3072]{1,0:T(8,128)(2,1)} %get-tuple-element.71.refs_1_.refs_3_, ...), custom_call_target="tpu_custom_call" | custom-call | flops 575000000 | bytes 1800000 | tf_op jit(solution)/shard_map/weight_part/pallas_call | solution.py:220
  168.9 3.7 %collective-permute-start.33 = (bf16[768,256]{1,0:T(8,128)(2,1)}, bf16[768,256]{1,0:T(8,128)(2,1)S(1)}, u32[]{:S(2)}, u32[]{:S(2)}) collective-permute-start(bf16[768,256]{1,0:T(8,128)(2,1)} %get-tuple-element.84), channel_id=1, source_target_pairs={{0,6},{2,4},{4,2},{6,0},{1,7},{3,5},{5,3},{7,1},{8,14},{10,12},{12... | collective-permute-start | bytes 1179656 | tf_op jit(solution)/shard_map/ppermute | solution.py:368
  172.6 10.9 %weight_part.5 = (bf16[1536,256]{1,0:T(8,128)(2,1)}, bf16[1536,256]{1,0:T(8,128)(2,1)}, bf16[1536,256]{1,0:T(8,128)(2,1)}) custom-call(s32[3]{0:T(128)} %pad_add_fusion.refs_0_, bf16[1024,1536]{1,0:T(8,128)(2,1)} %get-tuple-element.70.refs_1_, bf16[1024,1536]{1,0:T(8,128)(2,1)} %all-gather.2.cloned.1.call-done.refs_7_.refs_2_, ...), custom_call_target="tpu_custom_call" | custom-call | flops 575000000 | bytes 1800000 | tf_op jit(solution)/shard_map/weight_part/pallas_call | solution.py:220
  183.5 0.7 copy-done.10
  184.4 2.3 %relay.1 = (bf16[1536,256]{1,0:T(8,128)(2,1)}, bf16[1536,256]{1,0:T(8,128)(2,1)}) custom-call(bf16[1536,256]{1,0:T(8,128)(2,1)} %get-tuple-element.82.a_ref, bf16[1536,256]{1,0:T(8,128)(2,1)} %get-tuple-element.83.b_ref, bf16[768,256]{1,0:T(8,128)(2,1)} %copy-done.10, bf16[768,256]{1,0:T(8,128)(2,1)} %copy-done.11), custom_call_target="tpu_custom_call", output_to_operand_aliasing={{0}: (0, {}), {1}: (1, {})} | custom-call | flops 575000000 | bytes 1800000 | tf_op jit(solution)/shard_map/relay/pallas_call | solution.py:239
  186.7 1.5 collective-permute-start.35
  188.2 7.3 %all-to-all-done.refs_0_ = bf16[4,256,1536]{2,1,0:T(8,128)(2,1)} async-done(((bf16[4,256,1536]{2,1,0:T(8,128)(2,1)}), bf16[4,256,1536]{2,1,0:T(8,128)(2,1)}, u32[]{:S(2)}, u32[]{:S(2)}) %all-to-all-start) | async-done | bytes 3145760 | tf_op jit(solution)/shard_map/all_to_all | solution.py:417
  195.5 2.8 %fold.1.refs_4_ = bf16[256,1536]{1,0:T(8,128)(2,1)} custom-call(bf16[4,256,1536]{2,1,0:T(8,128)(2,1)} %after.12.in_ref), custom_call_target="tpu_custom_call" | custom-call | flops 575000000 | bytes 1800000 | tf_op jit(solution)/shard_map/fold/pallas_call | solution.py:354
  198.3 7.0 %collective-permute-done.35.refs_2_ = bf16[1536,256]{1,0:T(8,128)(2,1)} collective-permute-done((bf16[1536,256]{1,0:T(8,128)(2,1)}, bf16[1536,256]{1,0:T(8,128)(2,1)}, u32[]{:S(2)}, u32[]{:S(2)}) %collective-permute-start.35) | collective-permute-done | bytes 786464 | tf_op jit(solution)/shard_map/ppermute | solution.py:368
  205.3 2.2 collective-permute-done.36.refs_3_
  207.5 3.6 %join.1 = bf16[1536,384]{1,0:T(8,128)(2,1)} custom-call(bf16[1536,128]{1,0:T(8,128)(2,1)} %bitcast.6, bf16[1536,256]{1,0:T(8,128)(2,1)} %get-tuple-element.81.refs_1_, bf16[1536,256]{1,0:T(8,128)(2,1)} %collective-permute-done.35.refs_2_, bf16[1536,256]{1,0:T(8,128)(2,1)} %collective-permute-done.36.refs_3_, bf16[256,1536]{1,0:T(8,128)(2,1)} %fold.1.refs_4_), custom_call_target="tpu_custom_call" | custom-call | flops 575000000 | bytes 1800000 | tf_op jit(solution)/shard_map/join/pallas_call | solution.py:309
  (71 shorter events, 3.2 us)
Async XLA Ops:
  7.2 109.4 %all-gather.2.cloned.1.call-start = ((), (), s32[]{:S(2)}) async-start(), calls=%async_computation.2 | async-start | bytes 3932160 | tf_op jit(solution)/shard_map/all_gather | solution.py:378
  8.4 23.5 %copy-start.4 = (bf16[128,1536]{1,0:T(8,128)(2,1)}, bf16[128,1536]{1,0:T(8,128)(2,1)S(1)}, u32[]{:S(2)}) copy-start(bf16[128,1536]{1,0:T(8,128)(2,1)S(1)} %get-tuple-element.87.b0) | copy-start | bytes 1179652
  8.4 33.5 %copy-start.5 = (bf16[128,1536]{1,0:T(8,128)(2,1)}, bf16[128,1536]{1,0:T(8,128)(2,1)S(1)}, u32[]{:S(2)}) copy-start(bf16[128,1536]{1,0:T(8,128)(2,1)S(1)} %get-tuple-element.88.b0) | copy-start | bytes 1179652
  8.4 20.8 %collective-permute-start.5 = (bf16[128,1536]{1,0:T(8,128)(2,1)S(1)}, bf16[128,1536]{1,0:T(8,128)(2,1)S(1)}, u32[]{:S(2)}, u32[]{:S(2)}) collective-permute-start(bf16[128,1536]{1,0:T(8,128)(2,1)S(1)} %get-tuple-element.87.b0), channel_id=1, source_target_pairs={{0,24},{8,16},{16,8},{24,0},{1,25},{9,17},{17,9},{25,1},{2,26},{10... | collective-permute-start | bytes 1179656 | tf_op jit(solution)/shard_map/ppermute | solution.py:368
  12.0 17.9 %collective-permute-start.4 = (bf16[128,1536]{1,0:T(8,128)(2,1)S(1)}, bf16[128,1536]{1,0:T(8,128)(2,1)S(1)}, u32[]{:S(2)}, u32[]{:S(2)}) collective-permute-start(bf16[128,1536]{1,0:T(8,128)(2,1)S(1)} %get-tuple-element.87.b0), channel_id=1, source_target_pairs={{0,16},{8,24},{16,0},{24,8},{1,17},{9,25},{17,1},{25,9},{2,18},{10... | collective-permute-start | bytes 1179656 | tf_op jit(solution)/shard_map/ppermute | solution.py:368
  12.4 18.7 %collective-permute-start.3 = (bf16[128,1536]{1,0:T(8,128)(2,1)S(1)}, bf16[128,1536]{1,0:T(8,128)(2,1)S(1)}, u32[]{:S(2)}, u32[]{:S(2)}) collective-permute-start(bf16[128,1536]{1,0:T(8,128)(2,1)S(1)} %get-tuple-element.87.b0), channel_id=1, source_target_pairs={{0,8},{8,0},{16,24},{24,16},{1,9},{9,1},{17,25},{25,17},{2,10},{10... | collective-permute-start | bytes 1179656 | tf_op jit(solution)/shard_map/ppermute | solution.py:368
  12.7 33.4 %collective-permute-start.2 = (bf16[128,1536]{1,0:T(8,128)(2,1)S(1)}, bf16[128,1536]{1,0:T(8,128)(2,1)}, u32[]{:S(2)}, u32[]{:S(2)}) collective-permute-start(bf16[128,1536]{1,0:T(8,128)(2,1)S(1)} %get-tuple-element.88.b0), channel_id=1, source_target_pairs={{0,24},{8,16},{16,8},{24,0},{1,25},{9,17},{17,9},{25,1},{2,26},{10... | collective-permute-start | bytes 1179656 | tf_op jit(solution)/shard_map/ppermute | solution.py:368
  15.3 32.2 %collective-permute-start.1 = (bf16[128,1536]{1,0:T(8,128)(2,1)S(1)}, bf16[128,1536]{1,0:T(8,128)(2,1)}, u32[]{:S(2)}, u32[]{:S(2)}) collective-permute-start(bf16[128,1536]{1,0:T(8,128)(2,1)S(1)} %get-tuple-element.88.b0), channel_id=1, source_target_pairs={{0,16},{8,24},{16,0},{24,8},{1,17},{9,25},{17,1},{25,9},{2,18},{10... | collective-permute-start | bytes 1179656 | tf_op jit(solution)/shard_map/ppermute | solution.py:368
  29.2 0.8 copy-start.7
  29.9 17.6 %collective-permute-start = (bf16[128,1536]{1,0:T(8,128)(2,1)S(1)}, bf16[128,1536]{1,0:T(8,128)(2,1)}, u32[]{:S(2)}, u32[]{:S(2)}) collective-permute-start(bf16[128,1536]{1,0:T(8,128)(2,1)S(1)} %get-tuple-element.88.b0), channel_id=1, source_target_pairs={{0,8},{8,0},{16,24},{24,16},{1,9},{9,1},{17,25},{25,17},{2,10},{10... | collective-permute-start | bytes 1179656 | tf_op jit(solution)/shard_map/ppermute | solution.py:368
  29.9 1.2 copy-start.8
  29.9 26.0 %collective-permute-start.9 = (bf16[256,1536]{1,0:T(8,128)(2,1)}, bf16[256,1536]{1,0:T(8,128)(2,1)}, u32[]{:S(2)}, u32[]{:S(2)}) collective-permute-start(bf16[256,1536]{1,0:T(8,128)(2,1)} %refs_3_.1), channel_id=1, source_target_pairs={{0,1},{1,0},{2,3},{3,2},{4,5},{5,4},{6,7},{7,6},{8,9},{9,8},{10,11... | collective-permute-start | bytes 2359304 | tf_op jit(solution)/shard_map/ppermute | solution.py:368
  31.1 0.8 copy-start.9
  41.9 5.6 %collective-permute-start.6 = (bf16[128,1024]{1,0:T(8,128)(2,1)}, bf16[128,1024]{1,0:T(8,128)(2,1)}, u32[]{:S(2)}, u32[]{:S(2)}) collective-permute-start(bf16[128,1024]{1,0:T(8,128)(2,1)} %get-tuple-element.50), channel_id=1, source_target_pairs={{0,32},{32,0},{1,33},{33,1},{2,34},{34,2},{3,35},{35,3},{4,36},{36... | collective-permute-start | bytes 786440 | tf_op jit(solution)/shard_map/ppermute | solution.py:368
  46.1 2.9 %collective-permute-start.7 = (bf16[128,1024]{1,0:T(8,128)(2,1)}, bf16[128,1024]{1,0:T(8,128)(2,1)}, u32[]{:S(2)}, u32[]{:S(2)}) collective-permute-start(bf16[128,1024]{1,0:T(8,128)(2,1)} %get-tuple-element.51), channel_id=1, source_target_pairs={{0,32},{32,0},{1,33},{33,1},{2,34},{34,2},{3,35},{35,3},{4,36},{36... | collective-permute-start | bytes 786440 | tf_op jit(solution)/shard_map/ppermute | solution.py:368
  47.5 1.9 collective-permute-start.8
  47.5 7.8 %copy-start.14 = (bf16[128,3072]{1,0:T(8,128)(2,1)S(1)}, bf16[128,3072]{1,0:T(8,128)(2,1)}, u32[]{:S(2)}) copy-start(bf16[128,3072]{1,0:T(8,128)(2,1)} %get-tuple-element.60) | copy-start | bytes 2359300
  52.6 20.6 %collective-permute-start.16 = (bf16[128,3072]{1,0:T(8,128)(2,1)}, bf16[128,3072]{1,0:T(8,128)(2,1)}, u32[]{:S(2)}, u32[]{:S(2)}) collective-permute-start(bf16[128,3072]{1,0:T(8,128)(2,1)} %add.13.refs_1_.refs_3_), channel_id=1, source_target_pairs={{0,64},{64,0},{1,65},{65,1},{2,66},{66,2},{3,67},{67,3},{4,68},{68... | collective-permute-start | bytes 2359304 | tf_op jit(solution)/shard_map/ppermute | solution.py:368
  55.3 17.8 %collective-permute-start.15 = (bf16[128,3072]{1,0:T(8,128)(2,1)S(1)}, bf16[128,3072]{1,0:T(8,128)(2,1)}, u32[]{:S(2)}, u32[]{:S(2)}) collective-permute-start(bf16[128,3072]{1,0:T(8,128)(2,1)S(1)} %copy-done.14), channel_id=1, source_target_pairs={{0,32},{32,0},{1,33},{33,1},{2,34},{34,2},{3,35},{35,3},{4,36},{36... | collective-permute-start | bytes 2359304 | tf_op jit(solution)/shard_map/ppermute | solution.py:368
  65.9 2.0 collective-permute-start.11
  66.0 2.2 %collective-permute-start.12 = (bf16[128,1024]{1,0:T(8,128)(2,1)}, bf16[128,1024]{1,0:T(8,128)(2,1)}, u32[]{:S(2)}, u32[]{:S(2)}) collective-permute-start(bf16[128,1024]{1,0:T(8,128)(2,1)} %get-tuple-element.57), channel_id=1, source_target_pairs={{0,32},{32,0},{1,33},{33,1},{2,34},{34,2},{3,35},{35,3},{4,36},{36... | collective-permute-start | bytes 786440 | tf_op jit(solution)/shard_map/ppermute | solution.py:368
  66.5 2.1 collective-permute-start.13
  67.2 105.5 %reduce-scatter.2.cloned.1.call-start = ((), (), s32[]{:S(2)}) async-start(), calls=%async_computation.3 | async-start | bytes 1966080 | tf_op jit(solution)/shard_map/reduce_scatter | solution.py:410
  67.8 12.6 %collective-permute-start.10 = (bf16[128,3072]{1,0:T(8,128)(2,1)}, bf16[128,3072]{1,0:T(8,128)(2,1)}, u32[]{:S(2)}, u32[]{:S(2)}) collective-permute-start(bf16[128,3072]{1,0:T(8,128)(2,1)} %get-tuple-element.54), channel_id=1, source_target_pairs={{0,32},{32,0},{1,33},{33,1},{2,34},{34,2},{3,35},{35,3},{4,36},{36... | collective-permute-start | bytes 2359304 | tf_op jit(solution)/shard_map/ppermute | solution.py:368
  71.8 20.8 %collective-permute-start.14 = (bf16[128,3072]{1,0:T(8,128)(2,1)}, bf16[128,3072]{1,0:T(8,128)(2,1)}, u32[]{:S(2)}, u32[]{:S(2)}) collective-permute-start(bf16[128,3072]{1,0:T(8,128)(2,1)} %add.14.refs_1_), channel_id=1, source_target_pairs={{0,64},{64,0},{1,65},{65,1},{2,66},{66,2},{3,67},{67,3},{4,68},{68... | collective-permute-start | bytes 2359304 | tf_op jit(solution)/shard_map/ppermute | solution.py:368
  77.7 31.8 %collective-permute-start.17 = (bf16[128,3072]{1,0:T(8,128)(2,1)}, bf16[128,3072]{1,0:T(8,128)(2,1)S(1)}, u32[]{:S(2)}, u32[]{:S(2)}) collective-permute-start(bf16[128,3072]{1,0:T(8,128)(2,1)} %get-tuple-element.65.refs_0_), channel_id=1, source_target_pairs={{0,64},{64,0},{1,65},{65,1},{2,66},{66,2},{3,67},{67,3},{4,68},{68... | collective-permute-start | bytes 2359304 | tf_op jit(solution)/shard_map/ppermute | solution.py:368
  109.4 0.9 copy-start.1
  110.3 4.2 %collective-permute-start.18 = (bf16[128,3072]{1,0:T(8,128)(2,1)}, bf16[128,3072]{1,0:T(8,128)(2,1)S(1)}, u32[]{:S(2)}, u32[]{:S(2)}) collective-permute-start(bf16[128,3072]{1,0:T(8,128)(2,1)} %get-tuple-element.68.refs_7_.refs_1_), channel_id=1, source_target_pairs={{0,32},{32,0},{1,33},{33,1},{2,34},{34,2},{3,35},{35,3},{4,36},{36... | collective-permute-start | bytes 2359304 | tf_op jit(solution)/shard_map/ppermute | solution.py:368
  111.2 3.8 %collective-permute-start.20 = (bf16[128,3072]{1,0:T(8,128)(2,1)}, bf16[128,3072]{1,0:T(8,128)(2,1)}, u32[]{:S(2)}, u32[]{:S(2)}) collective-permute-start(bf16[128,3072]{1,0:T(8,128)(2,1)} %get-tuple-element.71.refs_1_.refs_3_), channel_id=1, source_target_pairs={{0,32},{32,0},{1,33},{33,1},{2,34},{34,2},{3,35},{35,3},{4,36},{36... | collective-permute-start | bytes 2359304 | tf_op jit(solution)/shard_map/ppermute | solution.py:368
  111.2 5.3 %collective-permute-start.21 = (bf16[128,3072]{1,0:T(8,128)(2,1)}, bf16[128,3072]{1,0:T(8,128)(2,1)}, u32[]{:S(2)}, u32[]{:S(2)}) collective-permute-start(bf16[128,3072]{1,0:T(8,128)(2,1)} %get-tuple-element.72.refs_3_.refs_5_), channel_id=1, source_target_pairs={{0,32},{32,0},{1,33},{33,1},{2,34},{34,2},{3,35},{35,3},{4,36},{36... | collective-permute-start | bytes 2359304 | tf_op jit(solution)/shard_map/ppermute | solution.py:368
  111.8 15.1 %collective-permute-start.24 = (bf16[256,512]{1,0:T(8,128)(2,1)}, bf16[256,512]{1,0:T(8,128)(2,1)}, u32[]{:S(2)}, u32[]{:S(2)}) collective-permute-start(bf16[256,512]{1,0:T(8,128)(2,1)} %get-tuple-element.67.refs_3_), channel_id=1, source_target_pairs={{0,65},{1,64},{64,1},{65,0},{2,67},{3,66},{66,3},{67,2},{4,69},{5,... | collective-permute-start | bytes 786440 | tf_op jit(solution)/shard_map/ppermute | solution.py:395
  112.6 14.0 %collective-permute-start.22 = (bf16[128,1024]{1,0:T(8,128)(2,1)}, bf16[128,1024]{1,0:T(8,128)(2,1)}, u32[]{:S(2)}, u32[]{:S(2)}) collective-permute-start(bf16[128,1024]{1,0:T(8,128)(2,1)} %get-tuple-element.73), channel_id=1, source_target_pairs={{0,64},{64,0},{1,65},{65,1},{2,66},{66,2},{3,67},{67,3},{4,68},{68... | collective-permute-start | bytes 786440 | tf_op jit(solution)/shard_map/ppermute | solution.py:368
  114.5 2.1 copy-start
  114.5 12.7 %collective-permute-start.23 = (bf16[256,512]{1,0:T(8,128)(2,1)}, bf16[256,512]{1,0:T(8,128)(2,1)}, u32[]{:S(2)}, u32[]{:S(2)}) collective-permute-start(bf16[256,512]{1,0:T(8,128)(2,1)} %get-tuple-element.67.refs_3_), channel_id=1, source_target_pairs={{0,1},{1,0},{2,3},{3,2},{4,5},{5,4},{6,7},{7,6},{8,9},{9,8},{10,11... | collective-permute-start | bytes 786440 | tf_op jit(solution)/shard_map/ppermute | solution.py:368
  115.0 25.4 %collective-permute-start.19 = (bf16[128,2048]{1,0:T(8,128)(2,1)}, bf16[128,2048]{1,0:T(8,128)(2,1)}, u32[]{:S(2)}, u32[]{:S(2)}) collective-permute-start(bf16[128,2048]{1,0:T(8,128)(2,1)} %get-tuple-element.69), channel_id=1, source_target_pairs={{0,64},{64,0},{1,65},{65,1},{2,66},{66,2},{3,67},{67,3},{4,68},{68... | collective-permute-start | bytes 1572872 | tf_op jit(solution)/shard_map/ppermute | solution.py:368
  127.1 3.2 %collective-permute-start.26 = (bf16[256,512]{1,0:T(8,128)(2,1)}, bf16[256,512]{1,0:T(8,128)(2,1)S(1)}, u32[]{:S(2)}, u32[]{:S(2)}) collective-permute-start(bf16[256,512]{1,0:T(8,128)(2,1)} %get-tuple-element.75.refs_11_), channel_id=1, source_target_pairs={{0,32},{32,0},{1,33},{33,1},{2,34},{34,2},{3,35},{35,3},{4,36},{36... | collective-permute-start | bytes 786440 | tf_op jit(solution)/shard_map/ppermute | solution.py:368
  128.9 1.7 collective-permute-start.27
  129.0 2.1 collective-permute-start.25
  130.3 0.8 copy-start.12
  130.7 0.7 copy-start.13
  131.1 0.7 copy-start.6
  140.5 2.2 %collective-permute-start.28 = (bf16[128,2048]{1,0:T(8,128)(2,1)}, bf16[128,2048]{1,0:T(8,128)(2,1)S(1)}, u32[]{:S(2)}, u32[]{:S(2)}) collective-permute-start(bf16[128,2048]{1,0:T(8,128)(2,1)} %after.11.refs_3_.refs_9_), channel_id=1, source_target_pairs={{0,32},{32,0},{1,33},{33,1},{2,34},{34,2},{3,35},{35,3},{4,36},{36... | collective-permute-start | bytes 1572872 | tf_op jit(solution)/shard_map/ppermute | solution.py:368
  140.9 17.2 %collective-permute-start.30 = (bf16[256,1024]{1,0:T(8,128)(2,1)}, bf16[256,1024]{1,0:T(8,128)(2,1)}, u32[]{:S(2)}, u32[]{:S(2)}) collective-permute-start(bf16[256,1024]{1,0:T(8,128)(2,1)} %get-tuple-element.77), channel_id=1, source_target_pairs={{0,65},{1,64},{64,1},{65,0},{2,67},{3,66},{66,3},{67,2},{4,69},{5,... | collective-permute-start | bytes 1572872 | tf_op jit(solution)/shard_map/ppermute | solution.py:395
  141.9 16.2 %collective-permute-start.29 = (bf16[256,1024]{1,0:T(8,128)(2,1)}, bf16[256,1024]{1,0:T(8,128)(2,1)}, u32[]{:S(2)}, u32[]{:S(2)}) collective-permute-start(bf16[256,1024]{1,0:T(8,128)(2,1)} %get-tuple-element.77), channel_id=1, source_target_pairs={{0,1},{1,0},{2,3},{3,2},{4,5},{5,4},{6,7},{7,6},{8,9},{9,8},{10,11... | collective-permute-start | bytes 1572872 | tf_op jit(solution)/shard_map/ppermute | solution.py:368
  142.7 0.8 copy-start.2
  153.4 42.0 %all-to-all-start = ((bf16[4,256,1536]{2,1,0:T(8,128)(2,1)}), bf16[4,256,1536]{2,1,0:T(8,128)(2,1)}, u32[]{:S(2)}, u32[]{:S(2)}) async-start(bf16[4,256,1536]{2,1,0:T(8,128)(2,1)} %input_part.3.refs_2_), calls=%async_computation | async-start | bytes 6291456 | tf_op jit(solution)/shard_map/all_to_all | solution.py:417
  158.1 2.2 %collective-permute-start.31 = (bf16[256,1024]{1,0:T(8,128)(2,1)}, bf16[256,1024]{1,0:T(8,128)(2,1)S(1)}, u32[]{:S(2)}, u32[]{:S(2)}) collective-permute-start(bf16[256,1024]{1,0:T(8,128)(2,1)} %get-tuple-element.78.refs_11_), channel_id=1, source_target_pairs={{0,32},{32,0},{1,33},{33,1},{2,34},{34,2},{3,35},{35,3},{4,36},{36... | collective-permute-start | bytes 1572872 | tf_op jit(solution)/shard_map/ppermute | solution.py:368
  158.6 2.6 %collective-permute-start.32 = (bf16[256,1024]{1,0:T(8,128)(2,1)}, bf16[256,1024]{1,0:T(8,128)(2,1)}, u32[]{:S(2)}, u32[]{:S(2)}) collective-permute-start(bf16[256,1024]{1,0:T(8,128)(2,1)} %get-tuple-element.79.refs_13_), channel_id=1, source_target_pairs={{0,32},{32,0},{1,33},{33,1},{2,34},{34,2},{3,35},{35,3},{4,36},{36... | collective-permute-start | bytes 1572872 | tf_op jit(solution)/shard_map/ppermute | solution.py:368
  160.3 0.9 copy-start.3
  168.9 14.6 %collective-permute-start.33 = (bf16[768,256]{1,0:T(8,128)(2,1)}, bf16[768,256]{1,0:T(8,128)(2,1)S(1)}, u32[]{:S(2)}, u32[]{:S(2)}) collective-permute-start(bf16[768,256]{1,0:T(8,128)(2,1)} %get-tuple-element.84), channel_id=1, source_target_pairs={{0,6},{2,4},{4,2},{6,0},{1,7},{3,5},{5,3},{7,1},{8,14},{10,12},{12... | collective-permute-start | bytes 1179656 | tf_op jit(solution)/shard_map/ppermute | solution.py:368
  172.6 10.9 %collective-permute-start.34 = (bf16[768,256]{1,0:T(8,128)(2,1)}, bf16[768,256]{1,0:T(8,128)(2,1)S(1)}, u32[]{:S(2)}, u32[]{:S(2)}) collective-permute-start(bf16[768,256]{1,0:T(8,128)(2,1)} %get-tuple-element.80.refs_15_), channel_id=1, source_target_pairs={{0,2},{2,0},{4,6},{6,4},{1,3},{3,1},{5,7},{7,5},{8,10},{10,8},{12,... | collective-permute-start | bytes 1179656 | tf_op jit(solution)/shard_map/ppermute | solution.py:368
  183.5 0.7 copy-start.10
  183.5 0.9 copy-start.11
  186.7 18.6 %collective-permute-start.35 = (bf16[1536,256]{1,0:T(8,128)(2,1)}, bf16[1536,256]{1,0:T(8,128)(2,1)}, u32[]{:S(2)}, u32[]{:S(2)}) collective-permute-start(bf16[1536,256]{1,0:T(8,128)(2,1)} %get-tuple-element.85), channel_id=1, source_target_pairs={{0,2},{2,0},{4,6},{6,4},{1,3},{3,1},{5,7},{7,5},{8,10},{10,8},{12,... | collective-permute-start | bytes 2359304 | tf_op jit(solution)/shard_map/ppermute | solution.py:368
  188.1 19.3 %collective-permute-start.36 = (bf16[1536,256]{1,0:T(8,128)(2,1)}, bf16[1536,256]{1,0:T(8,128)(2,1)}, u32[]{:S(2)}, u32[]{:S(2)}) collective-permute-start(bf16[1536,256]{1,0:T(8,128)(2,1)} %get-tuple-element.86), channel_id=1, source_target_pairs={{0,6},{2,4},{4,2},{6,0},{1,7},{3,5},{5,3},{7,1},{8,14},{10,12},{12... | collective-permute-start | bytes 2359304 | tf_op jit(solution)/shard_map/ppermute | solution.py:368
Sparse Core Ops, SparseCore 0:
  67.3 39.5 all-gather.1
  142.0 27.4 reduce-scatter.1

commit v6 on v5

--- a/solution.py
+++ b/solution.py
@@ -151,29 +151,31 @@
     )(xl, own, core, far, cot, *earlier, *wait)
 
 
-def weight_kernel(size, masks, ids_ref, tk_ref, tx_ref, *refs):
-    first, second, other = refs[:4], refs[4:8], refs[8:12]
-    outs, pg = refs[-(1 + count_outs(masks)):-1], refs[-1]
-    shares = masks or range(4)
+def weight_kernel(size, masks, halves, ids_ref, tk_ref, tx_ref, *refs):
+    count = max(1, len(masks))
+    groups = [refs[12 * n:12 * (n + 1)] for n in range(count)]
+    outs, pg = refs[-(1 + count * (1 + halves)):-1], refs[-1]
 
     @pl.when(pl.program_id(0) == 0)
     def _():
-        xl, r, z = ids_ref[0], ids_ref[1], ids_ref[2]
-        for n, share in enumerate(shares):
-            to = jnp.bitwise_xor(z, share) if masks else share
+        xl, r = ids_ref[0], ids_ref[1]
+        for n in range(len(masks) or 4):
             cols = slice(n * size, (n + 1) * size)
-            own = pl.ds(pl.multiple_of((2 * to + xl) * size, size), size)
-            near = pl.ds(pl.multiple_of(to * size, size), size)
+            own = near = slice(None)
+            if not masks:
+                own = pl.ds(pl.multiple_of((2 * n + xl) * size, size), size)
+                near = cols
+            group = groups[n if masks else 0]
             for k in range(4):
-                for part, grads in enumerate((first, second)):
+                for part in range(2):
                     row = (4 * part + k) * H
-                    pg[row:row + H, cols] = grads[k][:, own]
+                    pg[row:row + H, cols] = group[4 * part + k][:, own]
                 slot = pl.multiple_of(4 * S + jnp.bitwise_xor(r, k) * S, S)
-                pg[pl.ds(slot, S), cols] = other[k][:, near]
+                pg[pl.ds(slot, S), cols] = group[8 + k][:, near]
 
     tokens = jnp.concatenate([tk_ref[...], tx_ref[...]], axis=0)
     total = lax.dot_general(tokens, pg[...], (((0,), (0,)), ((), ())), preferred_element_type=f32).astype(bf16)
-    if len(shares) == 1:
+    if halves:
         for n, out_ref in enumerate(outs):
 
             @pl.when(pl.program_id(0) == n)
@@ -181,7 +183,7 @@
                 out_ref[...] = total
 
     else:
-        for n in range(len(shares)):
+        for n in range(len(masks) or 4):
             piece = total[:, n * size:(n + 1) * size]
             if masks:
                 outs[n][...] = piece
@@ -189,16 +191,24 @@
                 outs[0][n] = piece
 
 
-def count_outs(masks):
-    return max(2, len(masks)) if masks else 1
-
-
-def weight_part(ids, tk, tx, first, second, other, chunk, masks, wait):
+def weight_part(ids, tk, tx, first, second, other, chunk, masks, halves, wait):
     w = width(chunk)
     size = CHUNKS[chunk][1] * LANE
     rows = K // 2 if len(masks) == 1 else 512
-    at = lambda array: place(chunk) // w if array.shape[1] == F else 0
-    if len(masks) == 1:
+    specs = []
+    for m in masks:
+        for array in (*first, *second):
+            at = place(chunk) // size if array.shape[1] == F else 0
+            specs.append(
+                pl.BlockSpec((H, size), lambda i, x, at=at, m=m: (0, at + 2 * jnp.bitwise_xor(x[2], m) + x[0]))
+            )
+        specs += [pl.BlockSpec((S, size), lambda i, x, m=m: (0, jnp.bitwise_xor(x[2], m)))] * 4
+    if not masks:
+        for array in (*first, *second):
+            at = place(chunk) // w if array.shape[1] == F else 0
+            specs.append(pl.BlockSpec((H, w), lambda i, x, at=at: (0, at)))
+        specs += [pl.BlockSpec((S, w // 2), lambda i, x: (0, 0))] * 4
+    if halves:
         out_specs = [pl.BlockSpec((rows, size), lambda i, x: (0, 0))] * 2
         out_shape = [jax.ShapeDtypeStruct((rows, size), bf16)] * 2
     elif masks:
@@ -210,21 +220,18 @@
     grid_spec = pltpu.PrefetchScalarGridSpec(
         num_scalar_prefetch=1,
         grid=(K // rows,),
-        in_specs=[pl.BlockSpec((4 * S, rows), lambda i, x: (0, i))] * 2
-        + [pl.BlockSpec((H, w), lambda i, x, at=at(array): (0, at)) for array in (*first, *second)]
-        + [pl.BlockSpec((S, w // 2), lambda i, x: (0, 0))] * 4
-        + [ANY] * len(wait),
+        in_specs=[pl.BlockSpec((4 * S, rows), lambda i, x: (0, i))] * 2 + specs + [ANY] * len(wait),
         out_specs=out_specs,
         scratch_shapes=[pltpu.VMEM((8 * S, size * (len(masks) or 4)), bf16)],
     )
     return pl.pallas_call(
-        lambda *refs: weight_kernel(size, masks, *refs),
+        lambda *refs: weight_kernel(size, masks, halves, *refs),
         grid_spec=grid_spec,
         out_shape=out_shape,
         compiler_params=PARAMS,
         cost_estimate=cost(TK),
         name="weight_part",
-    )(ids, tk, tx, *first, *second, *other, *wait)
+    )(ids, tk, tx, *([*first, *second, *other] * max(1, len(masks))), *wait)
 
 
 def relay_kernel(a_ref, b_ref, last_ref, first_ref, a_out, b_out):
@@ -303,7 +310,7 @@
 
 
 def join(first, pieces, wait):
-    rows = 512
+    rows = 768
     block = lambda size: pl.BlockSpec((rows, size), lambda i: (i, 0))
     sizes = [first.shape[1], pieces[0].shape[1]]
     return pl.pallas_call(
@@ -321,17 +328,15 @@
 def add_kernel(a_ref, *refs):
     out_ref = refs[-1]
     for n in range(F // TILE):
-
-        @pl.when(pl.program_id(0) == n)
-        def _():
-            out_ref[...] = (a_ref[...].astype(f32) + refs[n][...].astype(f32)).astype(bf16)
+        at = slice(n * TILE, (n + 1) * TILE)
+        out_ref[:, at] = (a_ref[:, at].astype(f32) + refs[n][...].astype(f32)).astype(bf16)
 
 
 def add(a, pieces, wait):
-    block = pl.BlockSpec((H, TILE), lambda i: (0, i))
+    block = pl.BlockSpec((H, F), lambda i: (0, 0))
     return pl.pallas_call(
         add_kernel,
-        grid=(F // TILE,),
+        grid=(1,),
         in_specs=[block] + [pl.BlockSpec((H, TILE), lambda i: (0, 0))] * len(pieces) + [ANY],
         out_specs=block,
         out_shape=jax.ShapeDtypeStruct(a.shape, bf16),
@@ -402,17 +407,18 @@
     dx = input_part(ids, [[value] for value in first], weight, 0, (), (second_core, tx))
     far[0], near[0], cross[0] = pairs([far[0], near[0], cross[0]], dx)
     own = [second, second_core]
-    dw0 = weight_part(ids, tk, tx, first, [*own, *far[0]], [*near[0], *cross[0]], 0, (), ())
+    dw0 = weight_part(ids, tk, tx, first, [*own, *far[0]], [*near[0], *cross[0]], 0, (), False, ())
     (far[1],) = pairs([far[1]], dw0)
     blocks = [[value] for value in own] + [[far[chunk][c] for chunk in LAID] for c in range(2)]
     dx = input_part(ids, blocks, weight, 1, (dx,), ())
     near[1], cross[1] = pairs([near[1], cross[1]], dx, T4)
     dw0 = lax.psum_scatter(dw0, "z", scatter_dimension=0, tiled=True)[0]
     last = [first, [*own, *far[1]], [*near[1], *cross[1]], 1]
-    top, bottom = weight_part(ids, tk, tx, *last, (2,), ())
+    top, bottom = weight_part(ids, tk, tx, *last, (2,), True, ())
     to_right, to_left = swap(top, "z", 1), swap(bottom, "z", 3)
-    mine, one, three = weight_part(ids, tk, tx, *last, (0, 1, 3), (top, dw0))
+    one, three = weight_part(ids, tk, tx, *last, (1, 3), False, (top, dw0))
     one, three = relay(one, three, to_left, to_right)
+    (mine,) = weight_part(ids, tk, tx, *last, (0,), False, (one,))
 
     (dx,) = after([lax.all_to_all(dx, "y", 0, 0, tiled=True)], total, T5)
     input_grad = fold(dx)

time: 220 us -> 214 us (0.973)
  waiting for transfers between devices: 65.5 us -> 60.5 us
    ppermute x35, waiting for transfers between devices: 58 us -> 50.8 us  [swap(): return lax.ppermute(value, axis, [(i, i ^ mask) for i in range(n)])]
    pallas_call x5 -> x6, Pallas kernels: 33.6 us -> 33.8 us  [the longest x4 28.9 us: weight_part(): pl.pallas_call(lambda *refs: weight_kernel(size, masks, halves, *refs), g...]
  transfers between devices with their start and end apart: 40 -> 40, of which waited for: 22 -> 22; matrix products, arithmetic and copies ran while one was open for 0% -> 0% of each run, Pallas kernels for 40% -> 41%
where the time goes in v6:
time: 214 us; the launch traced here: 212 us
  Pallas kernels  90.8 us (42%)
  waiting for transfers between devices  60.5 us (28%)
  starting transfers between devices  40.3 us (19%)
  between operations  14.2 us (7%)
  local copies, waits for them, and re-layouts  5.84 us (3%)
    ppermute x35, waiting for transfers between devices, swap(): return lax.ppermute(value, axis, [(i, i ^ mask) for i in range(n)])  50.8 us
    ppermute x35, starting transfers between devices, swap(): return lax.ppermute(value, axis, [(i, i ^ mask) for i in range(n)])  33.7 us
    pallas_call x4, Pallas kernels, weight_part(): pl.pallas_call(lambda *refs: weight_kernel(size, masks, halves, *refs), g...  28.9 us
    pallas_call x2, Pallas kernels, input_part(): pl.pallas_call(lambda *refs: input_kernel(counts, *refs), grid_spec=grid_...  20.1 us
    pallas_call x2, Pallas kernels, block_partials(): pl.pallas_call(partial_kernel, grid_spec=grid_spec, out_shape=[jax.ShapeD...  19.9 us
    all_to_all x1, waiting for transfers between devices, shards(): dx, = after([lax.all_to_all(dx, 'y', 0, 0, tiled=True)], total, T5)  9.47 us
    pallas_call x2, Pallas kernels, gelu_pair(): pl.pallas_call(lambda *refs: gelu_kernel(part, *refs), grid_spec=grid_spe...  9.2 us
    pallas_call x2, Pallas kernels, add(): pl.pallas_call(add_kernel, grid=(1,), in_specs=[block] + [pl.BlockSpec((H...  4.9 us
  transfers between devices with their start and end apart: 40, of which 22 were waited for; matrix products, arithmetic and copies ran while one was open for 0% of the time, Pallas kernels for 41%

profile of v6, /device:TPU:1, one launch (start us, length us, event | category | flops | bytes accessed | tf_op | source)
XLA Modules:
  0.0 212.3 jit_solution(11095737928607604094)
XLA Ops:
  7.2 1.2 fusion
  8.4 3.6 %collective-permute-start.5 = (bf16[128,1536]{1,0:T(8,128)(2,1)S(1)}, bf16[128,1536]{1,0:T(8,128)(2,1)S(1)}, u32[]{:S(2)}, u32[]{:S(2)}) collective-permute-start(bf16[128,1536]{1,0:T(8,128)(2,1)S(1)} %get-tuple-element.85.b0), channel_id=1, source_target_pairs={{0,24},{8,16},{16,8},{24,0},{1,25},{9,17},{17,9},{25,1},{2,26},{10... | collective-permute-start | bytes 1179656 | tf_op jit(solution)/shard_map/ppermute | solution.py:373
  12.7 2.6 %collective-permute-start.2 = (bf16[128,1536]{1,0:T(8,128)(2,1)S(1)}, bf16[128,1536]{1,0:T(8,128)(2,1)}, u32[]{:S(2)}, u32[]{:S(2)}) collective-permute-start(bf16[128,1536]{1,0:T(8,128)(2,1)S(1)} %get-tuple-element.86.b0), channel_id=1, source_target_pairs={{0,24},{8,16},{16,8},{24,0},{1,25},{9,17},{17,9},{25,1},{2,26},{10... | collective-permute-start | bytes 1179656 | tf_op jit(solution)/shard_map/ppermute | solution.py:373
  15.6 13.5 %collective-permute-done.5.b3 = bf16[128,1536]{1,0:T(8,128)(2,1)S(1)} collective-permute-done((bf16[128,1536]{1,0:T(8,128)(2,1)S(1)}, bf16[128,1536]{1,0:T(8,128)(2,1)S(1)}, u32[]{:S(2)}, u32[]{:S(2)}) %collective-permute-start.5) | collective-permute-done | bytes 393248 | tf_op jit(solution)/shard_map/ppermute | solution.py:373
  29.2 0.8 copy-done.7
  29.9 1.2 collective-permute-start.9
  31.1 0.8 copy-done.9
  31.9 10.0 %block_partials.2 = (bf16[128,3072]{1,0:T(8,128)(2,1)}, bf16[128,3072]{1,0:T(8,128)(2,1)}, bf16[128,3072]{1,0:T(8,128)(2,1)}, bf16[128,1024]{1,0:T(8,128)(2,1)},...) custom-call(s32[1]{0:T(128)} %bitcast.3.q_ref, bf16[128,1536]{1,0:T(8,128)(2,1)} %copy-done.4, ...), custom_call_target="tpu_custom_call" | custom-call | flops 11500000 | bytes 36000 | tf_op jit(solution)/shard_map/block_partials/pallas_call | solution.py:88
  41.9 3.2 %collective-permute-start.6 = (bf16[128,1024]{1,0:T(8,128)(2,1)}, bf16[128,1024]{1,0:T(8,128)(2,1)}, u32[]{:S(2)}, u32[]{:S(2)}) collective-permute-start(bf16[128,1024]{1,0:T(8,128)(2,1)} %get-tuple-element.49), channel_id=1, source_target_pairs={{0,32},{32,0},{1,33},{33,1},{2,34},{34,2},{3,35},{35,3},{4,36},{36... | collective-permute-start | bytes 786440 | tf_op jit(solution)/shard_map/ppermute | solution.py:373
  45.1 1.1 collective-permute-done.2.refs_2_
  46.1 1.4 collective-permute-start.7
  47.5 1.5 collective-permute-done.7.refs_1_
  49.0 0.4 collective-permute-done.8.refs_2_
  49.4 2.5 %add.13.refs_1_.refs_3_ = bf16[128,3072]{1,0:T(8,128)(2,1)} custom-call(bf16[128,3072]{1,0:T(8,128)(2,1)} %get-tuple-element.48.a_ref, bf16[128,1024]{1,0:T(8,128)(2,1)} %collective-permute-done.6.refs_0_, bf16[128,1024]{1,0:T(8,128)(2,1)} %collective-permute-done.7.refs_1_, bf16[128,1024]{1,0:T(8,128)(2,1)} %collective-permute-done.8.refs_2_, ...), custom_call_target="tpu_custom_call" | custom-call | flops 1150000000 | bytes 3600000 | tf_op jit(solution)/shard_map/add/pallas_call | solution.py:337
  51.9 2.7 %collective-permute-start.16 = (bf16[128,3072]{1,0:T(8,128)(2,1)}, bf16[128,3072]{1,0:T(8,128)(2,1)}, u32[]{:S(2)}, u32[]{:S(2)}) collective-permute-start(bf16[128,3072]{1,0:T(8,128)(2,1)} %add.13.refs_1_.refs_3_), channel_id=1, source_target_pairs={{0,64},{64,0},{1,65},{65,1},{2,66},{66,2},{3,67},{67,3},{4,68},{68... | collective-permute-start | bytes 2359304 | tf_op jit(solution)/shard_map/ppermute | solution.py:373
  54.6 0.7 collective-permute-start.15
  55.3 9.9 %block_partials.3 = (bf16[128,3072]{1,0:T(8,128)(2,1)}, bf16[128,3072]{1,0:T(8,128)(2,1)}, bf16[128,3072]{1,0:T(8,128)(2,1)}, bf16[128,1024]{1,0:T(8,128)(2,1)},...) custom-call(s32[1]{0:T(128)} %bitcast.3.q_ref, ...), custom_call_target="tpu_custom_call", output_to_operand_aliasing={{6}: (6, {})} | custom-call | flops 11500000 | bytes 36000 | tf_op jit(solution)/shard_map/block_partials/pallas_call | solution.py:88
  65.3 0.5 collective-permute-start.12
  65.9 0.6 pad_add_fusion.refs_0_
  66.5 0.6 collective-permute-done.11.refs_0_
  67.5 0.4 collective-permute-done.13.refs_2_
  67.9 2.4 %add.14.refs_1_ = bf16[128,3072]{1,0:T(8,128)(2,1)} custom-call(bf16[128,3072]{1,0:T(8,128)(2,1)} %get-tuple-element.54.a_ref, bf16[128,1024]{1,0:T(8,128)(2,1)} %collective-permute-done.11.refs_0_, bf16[128,1024]{1,0:T(8,128)(2,1)} %collective-permute-done.12.refs_1_, bf16[128,1024]{1,0:T(8,128)(2,1)} %collective-permute-done.13.refs_2_, ...), custom_call_target="tpu_custom_call" | custom-call | flops 1150000000 | bytes 3600000 | tf_op jit(solution)/shard_map/add/pallas_call | solution.py:337
  70.5 1.9 collective-permute-done.16.refs_0_
  72.4 4.5 %gelu_pair.2 = (bf16[256,3072]{1,0:T(8,128)(2,1)}, bf16[256,512]{1,0:T(8,128)(2,1)}, bf16[256,1024]{1,0:T(8,128)(2,1)}, bf16[128,3072]{1,0:T(8,128)(2,1)}) custom-call(s32[3]{0:T(128)} %pad_add_fusion.refs_0_, bf16[128,3072]{1,0:T(8,128)(2,1)} %get-tuple-element.58.refs_1_, bf16[128,3072]{1,0:T(8,128)(2,1)} %collective-permute-done.15.refs_2_, ...), custom_call_target="tpu_custom_call" | custom-call | flops 34500001792 | bytes 108000000 | tf_op jit(solution)/shard_map/gelu_pair/pallas_call | solution.py:141
  77.0 2.7 %collective-permute-start.17 = (bf16[128,3072]{1,0:T(8,128)(2,1)}, bf16[128,3072]{1,0:T(8,128)(2,1)S(1)}, u32[]{:S(2)}, u32[]{:S(2)}) collective-permute-start(bf16[128,3072]{1,0:T(8,128)(2,1)} %get-tuple-element.64.refs_0_), channel_id=1, source_target_pairs={{0,64},{64,0},{1,65},{65,1},{2,66},{66,2},{3,67},{67,3},{4,68},{68... | collective-permute-start | bytes 2359304 | tf_op jit(solution)/shard_map/ppermute | solution.py:373
  79.7 11.4 %collective-permute-done.14.refs_3_ = bf16[128,3072]{1,0:T(8,128)(2,1)} collective-permute-done((bf16[128,3072]{1,0:T(8,128)(2,1)}, bf16[128,3072]{1,0:T(8,128)(2,1)}, u32[]{:S(2)}, u32[]{:S(2)}) %collective-permute-start.14) | collective-permute-done | bytes 786464 | tf_op jit(solution)/shard_map/ppermute | solution.py:373
  91.1 4.7 %gelu_pair.3 = (bf16[256,3072]{1,0:T(8,128)(2,1)}, bf16[256,512]{1,0:T(8,128)(2,1)}, bf16[256,1024]{1,0:T(8,128)(2,1)}, bf16[128,3072]{1,0:T(8,128)(2,1)}, bf16[...) custom-call(s32[3]{0:T(128)} %pad_add_fusion.refs_0_, ...), custom_call_target="tpu_custom_call", output_to_operand_aliasing={{0}: (5, {}), {1}: (6, {}), {2}: (7, {})} | custom-call | flops 34500001792 | bytes 108000000 | tf_op jit(solution)/shard_map/gelu_pair/pallas_call | solution.py:141
  95.8 12.1 %collective-permute-done.17.refs_1_ = bf16[128,3072]{1,0:T(8,128)(2,1)S(1)} collective-permute-done((bf16[128,3072]{1,0:T(8,128)(2,1)}, bf16[128,3072]{1,0:T(8,128)(2,1)S(1)}, u32[]{:S(2)}, u32[]{:S(2)}) %collective-permute-start.17) | collective-permute-done | bytes 786464 | tf_op jit(solution)/shard_map/ppermute | solution.py:373
  107.9 0.9 copy-done.1
  108.8 1.0 collective-permute-start.18
  109.7 0.5 collective-permute-start.21
  110.2 0.9 collective-permute-start.24
  111.1 1.2 collective-permute-start.22
  112.3 0.6 collective-permute-done.18.refs_6_.refs_8_.refs_2_.refs_20_
  112.9 0.6 collective-permute-start.23
  113.5 1.5 collective-permute-start.19
  115.0 10.1 %input_part.2.refs_3_.refs_8_ = bf16[4,256,1536]{2,1,0:T(8,128)(2,1)} custom-call(s32[3]{0:T(128)} %pad_add_fusion.refs_0_, bf16[128,3072]{1,0:T(8,128)(2,1)} %get-tuple-element.70.refs_1_.refs_3_.refs_15_, bf16[128,3072]{1,0:T(8,128)(2,1)} %collective-permute-done.20.refs_2_.refs_4_.refs_16_, bf16[128,3072]{1,0:T(8,128)(2,1)} %get-tuple-element.71.refs_3_.refs_5_.refs_17_, ...), custom_call_target="tpu_custom_call" | custom-call | flops 575000000 | bytes 1800000 | tf_op jit(solution)/shard_map/input_part/pallas_call | solution.py:292
  125.6 1.8 collective-permute-start.26
  127.4 0.5 collective-permute-start.25
  127.9 0.9 collective-permute-done.26.refs_12_
  129.2 0.4 collective-permute-done.25.refs_10_.refs_6_
  129.9 0.4 copy-done.6
  130.2 8.7 %weight_part.4.refs_1_ = bf16[4,1536,128]{2,1,0:T(8,128)(2,1)} custom-call(s32[3]{0:T(128)} %pad_add_fusion.refs_0_, bf16[1024,1536]{1,0:T(8,128)(2,1)} %get-tuple-element.69.refs_1_, bf16[1024,1536]{1,0:T(8,128)(2,1)} %all-gather.2.cloned.1.call-done.refs_7_.refs_2_, bf16[128,3072]{1,0:T(8,128)(2,1)} %get-tuple-element.70.refs_1_.refs_3_.refs_15_, ...), custom_call_target="tpu_custom_call" | custom-call | flops 575000000 | bytes 1800000 | tf_op jit(solution)/shard_map/weight_part/pallas_call | solution.py:227
  138.9 0.5 collective-permute-start.28
  139.4 1.0 collective-permute-start.30
  140.4 0.8 collective-permute-done.28.refs_5_.refs_10_.refs_22_
  141.1 0.8 copy-done.2
  141.9 10.0 %input_part.3.refs_2_ = bf16[4,256,1536]{2,1,0:T(8,128)(2,1)} custom-call(s32[3]{0:T(128)} %pad_add_fusion.refs_0_, bf16[128,3072]{1,0:T(8,128)(2,1)} %get-tuple-element.67.refs_7_.refs_1_.refs_19_, bf16[128,3072]{1,0:T(8,128)(2,1)} %copy-done, bf16[128,2048]{1,0:T(8,128)(2,1)} %after.11.refs_3_.refs_9_.refs_21_, ...), custom_call_target="tpu_custom_call", output_to_operand_aliasing={{}: (8, {})} | custom-call | flops 575000000 | bytes 1800000 | tf_op jit(solution)/shard_map/input_part/pallas_call | solution.py:292
  151.9 4.6 %all-to-all-start = ((bf16[4,256,1536]{2,1,0:T(8,128)(2,1)}), bf16[4,256,1536]{2,1,0:T(8,128)(2,1)}, u32[]{:S(2)}, u32[]{:S(2)}) async-start(bf16[4,256,1536]{2,1,0:T(8,128)(2,1)} %input_part.3.refs_2_), calls=%async_computation | async-start | bytes 6291456 | tf_op jit(solution)/shard_map/all_to_all | solution.py:423
  156.6 0.5 collective-permute-start.31
  157.2 1.6 collective-permute-done.31.refs_12_.refs_24_
  158.8 0.9 collective-permute-done.32.refs_14_.refs_26_
  159.7 6.1 %weight_part.5 = (bf16[768,256]{1,0:T(8,128)(2,1)}, bf16[768,256]{1,0:T(8,128)(2,1)}) custom-call(s32[3]{0:T(128)} %pad_add_fusion.refs_0_, bf16[1024,1536]{1,0:T(8,128)(2,1)} %get-tuple-element.69.refs_1_, bf16[1024,1536]{1,0:T(8,128)(2,1)} %all-gather.2.cloned.1.call-done.refs_7_.refs_2_, bf16[128,3072]{1,0:T(8,128)(2,1)} %get-tuple-element.70.refs_1_.refs_3_.refs_15_, ...), custom_call_target="tpu_custom_call" | custom-call | flops 575000000 | bytes 1800000 | tf_op jit(solution)/shard_map/weight_part/pallas_call | solution.py:227
  165.9 3.7 %collective-permute-start.33 = (bf16[768,256]{1,0:T(8,128)(2,1)}, bf16[768,256]{1,0:T(8,128)(2,1)S(1)}, u32[]{:S(2)}, u32[]{:S(2)}) collective-permute-start(bf16[768,256]{1,0:T(8,128)(2,1)} %get-tuple-element.82), channel_id=1, source_target_pairs={{0,6},{2,4},{4,2},{6,0},{1,7},{3,5},{5,3},{7,1},{8,14},{10,12},{12... | collective-permute-start | bytes 1179656 | tf_op jit(solution)/shard_map/ppermute | solution.py:373
  169.6 8.3 %weight_part.6 = (bf16[1536,256]{1,0:T(8,128)(2,1)}, bf16[1536,256]{1,0:T(8,128)(2,1)}) custom-call(s32[3]{0:T(128)} %pad_add_fusion.refs_0_, bf16[1024,1536]{1,0:T(8,128)(2,1)} %get-tuple-element.69.refs_1_, bf16[1024,1536]{1,0:T(8,128)(2,1)} %all-gather.2.cloned.1.call-done.refs_7_.refs_2_, bf16[128,3072]{1,0:T(8,128)(2,1)} %get-tuple-element.70.refs_1_.refs_3_.refs_15_, ...), custom_call_target="tpu_custom_call" | custom-call | flops 575000000 | bytes 1800000 | tf_op jit(solution)/shard_map/weight_part/pallas_call | solution.py:227
  177.9 1.2 collective-permute-done.33.last_ref
  179.0 0.8 collective-permute-done.34.first_ref
  179.9 0.7 copy-done.11
  180.6 2.2 %relay.1 = (bf16[1536,256]{1,0:T(8,128)(2,1)}, bf16[1536,256]{1,0:T(8,128)(2,1)}) custom-call(bf16[1536,256]{1,0:T(8,128)(2,1)} %get-tuple-element.80.a_ref, bf16[1536,256]{1,0:T(8,128)(2,1)} %get-tuple-element.81.b_ref, bf16[768,256]{1,0:T(8,128)(2,1)} %copy-done.10, bf16[768,256]{1,0:T(8,128)(2,1)} %copy-done.11), custom_call_target="tpu_custom_call", output_to_operand_aliasing={{0}: (0, {}), {1}: (1, {})} | custom-call | flops 575000000 | bytes 1800000 | tf_op jit(solution)/shard_map/relay/pallas_call | solution.py:246
  182.8 1.7 collective-permute-start.36
  184.5 9.5 %all-to-all-done.refs_0_ = bf16[4,256,1536]{2,1,0:T(8,128)(2,1)} async-done(((bf16[4,256,1536]{2,1,0:T(8,128)(2,1)}), bf16[4,256,1536]{2,1,0:T(8,128)(2,1)}, u32[]{:S(2)}, u32[]{:S(2)}) %all-to-all-start) | async-done | bytes 3145760 | tf_op jit(solution)/shard_map/all_to_all | solution.py:423
  194.0 2.8 %fold.1.refs_4_ = bf16[256,1536]{1,0:T(8,128)(2,1)} custom-call(bf16[4,256,1536]{2,1,0:T(8,128)(2,1)} %after.12.in_ref), custom_call_target="tpu_custom_call" | custom-call | flops 575000000 | bytes 1800000 | tf_op jit(solution)/shard_map/fold/pallas_call | solution.py:359
  196.8 5.8 %weight_part.7.refs_1_ = bf16[1536,256]{1,0:T(8,128)(2,1)} custom-call(s32[3]{0:T(128)} %pad_add_fusion.refs_0_, bf16[1024,1536]{1,0:T(8,128)(2,1)} %get-tuple-element.69.refs_1_, bf16[1024,1536]{1,0:T(8,128)(2,1)} %all-gather.2.cloned.1.call-done.refs_7_.refs_2_, bf16[128,3072]{1,0:T(8,128)(2,1)} %get-tuple-element.70.refs_1_.refs_3_.refs_15_, ...), custom_call_target="tpu_custom_call" | custom-call | flops 575000000 | bytes 1800000 | tf_op jit(solution)/shard_map/weight_part/pallas_call | solution.py:227
  202.7 2.8 %join.1 = bf16[1536,384]{1,0:T(8,128)(2,1)} custom-call(bf16[1536,128]{1,0:T(8,128)(2,1)} %bitcast.6, bf16[1536,256]{1,0:T(8,128)(2,1)} %weight_part.7.refs_1_, bf16[1536,256]{1,0:T(8,128)(2,1)} %collective-permute-done.35.refs_2_, bf16[1536,256]{1,0:T(8,128)(2,1)} %collective-permute-done.36.refs_3_, bf16[256,1536]{1,0:T(8,128)(2,1)} %fold.1.refs_4_), custom_call_target="tpu_custom_call" | custom-call | flops 575000000 | bytes 1800000 | tf_op jit(solution)/shard_map/join/pallas_call | solution.py:316
  (72 shorter events, 3.4 us)
Async XLA Ops:
  7.2 107.8 %all-gather.2.cloned.1.call-start = ((), (), s32[]{:S(2)}) async-start(), calls=%async_computation.2 | async-start | bytes 3932160 | tf_op jit(solution)/shard_map/all_gather | solution.py:383
  8.4 23.5 %copy-start.4 = (bf16[128,1536]{1,0:T(8,128)(2,1)}, bf16[128,1536]{1,0:T(8,128)(2,1)S(1)}, u32[]{:S(2)}) copy-start(bf16[128,1536]{1,0:T(8,128)(2,1)S(1)} %get-tuple-element.85.b0) | copy-start | bytes 1179652
  8.4 33.5 %copy-start.5 = (bf16[128,1536]{1,0:T(8,128)(2,1)}, bf16[128,1536]{1,0:T(8,128)(2,1)S(1)}, u32[]{:S(2)}) copy-start(bf16[128,1536]{1,0:T(8,128)(2,1)S(1)} %get-tuple-element.86.b0) | copy-start | bytes 1179652
  8.4 20.8 %collective-permute-start.5 = (bf16[128,1536]{1,0:T(8,128)(2,1)S(1)}, bf16[128,1536]{1,0:T(8,128)(2,1)S(1)}, u32[]{:S(2)}, u32[]{:S(2)}) collective-permute-start(bf16[128,1536]{1,0:T(8,128)(2,1)S(1)} %get-tuple-element.85.b0), channel_id=1, source_target_pairs={{0,24},{8,16},{16,8},{24,0},{1,25},{9,17},{17,9},{25,1},{2,26},{10... | collective-permute-start | bytes 1179656 | tf_op jit(solution)/shard_map/ppermute | solution.py:373
  12.0 17.9 %collective-permute-start.4 = (bf16[128,1536]{1,0:T(8,128)(2,1)S(1)}, bf16[128,1536]{1,0:T(8,128)(2,1)S(1)}, u32[]{:S(2)}, u32[]{:S(2)}) collective-permute-start(bf16[128,1536]{1,0:T(8,128)(2,1)S(1)} %get-tuple-element.85.b0), channel_id=1, source_target_pairs={{0,16},{8,24},{16,0},{24,8},{1,17},{9,25},{17,1},{25,9},{2,18},{10... | collective-permute-start | bytes 1179656 | tf_op jit(solution)/shard_map/ppermute | solution.py:373
  12.4 18.7 %collective-permute-start.3 = (bf16[128,1536]{1,0:T(8,128)(2,1)S(1)}, bf16[128,1536]{1,0:T(8,128)(2,1)S(1)}, u32[]{:S(2)}, u32[]{:S(2)}) collective-permute-start(bf16[128,1536]{1,0:T(8,128)(2,1)S(1)} %get-tuple-element.85.b0), channel_id=1, source_target_pairs={{0,8},{8,0},{16,24},{24,16},{1,9},{9,1},{17,25},{25,17},{2,10},{10... | collective-permute-start | bytes 1179656 | tf_op jit(solution)/shard_map/ppermute | solution.py:373
  12.7 33.4 %collective-permute-start.2 = (bf16[128,1536]{1,0:T(8,128)(2,1)S(1)}, bf16[128,1536]{1,0:T(8,128)(2,1)}, u32[]{:S(2)}, u32[]{:S(2)}) collective-permute-start(bf16[128,1536]{1,0:T(8,128)(2,1)S(1)} %get-tuple-element.86.b0), channel_id=1, source_target_pairs={{0,24},{8,16},{16,8},{24,0},{1,25},{9,17},{17,9},{25,1},{2,26},{10... | collective-permute-start | bytes 1179656 | tf_op jit(solution)/shard_map/ppermute | solution.py:373
  15.3 32.2 %collective-permute-start.1 = (bf16[128,1536]{1,0:T(8,128)(2,1)S(1)}, bf16[128,1536]{1,0:T(8,128)(2,1)}, u32[]{:S(2)}, u32[]{:S(2)}) collective-permute-start(bf16[128,1536]{1,0:T(8,128)(2,1)S(1)} %get-tuple-element.86.b0), channel_id=1, source_target_pairs={{0,16},{8,24},{16,0},{24,8},{1,17},{9,25},{17,1},{25,9},{2,18},{10... | collective-permute-start | bytes 1179656 | tf_op jit(solution)/shard_map/ppermute | solution.py:373
  29.2 0.8 copy-start.7
  29.9 17.6 %collective-permute-start = (bf16[128,1536]{1,0:T(8,128)(2,1)S(1)}, bf16[128,1536]{1,0:T(8,128)(2,1)}, u32[]{:S(2)}, u32[]{:S(2)}) collective-permute-start(bf16[128,1536]{1,0:T(8,128)(2,1)S(1)} %get-tuple-element.86.b0), channel_id=1, source_target_pairs={{0,8},{8,0},{16,24},{24,16},{1,9},{9,1},{17,25},{25,17},{2,10},{10... | collective-permute-start | bytes 1179656 | tf_op jit(solution)/shard_map/ppermute | solution.py:373
  29.9 1.2 copy-start.8
  29.9 25.3 %collective-permute-start.9 = (bf16[256,1536]{1,0:T(8,128)(2,1)}, bf16[256,1536]{1,0:T(8,128)(2,1)}, u32[]{:S(2)}, u32[]{:S(2)}) collective-permute-start(bf16[256,1536]{1,0:T(8,128)(2,1)} %refs_3_.1), channel_id=1, source_target_pairs={{0,1},{1,0},{2,3},{3,2},{4,5},{5,4},{6,7},{7,6},{8,9},{9,8},{10,11... | collective-permute-start | bytes 2359304 | tf_op jit(solution)/shard_map/ppermute | solution.py:373
  31.1 0.8 copy-start.9
  41.9 5.7 %collective-permute-start.6 = (bf16[128,1024]{1,0:T(8,128)(2,1)}, bf16[128,1024]{1,0:T(8,128)(2,1)}, u32[]{:S(2)}, u32[]{:S(2)}) collective-permute-start(bf16[128,1024]{1,0:T(8,128)(2,1)} %get-tuple-element.49), channel_id=1, source_target_pairs={{0,32},{32,0},{1,33},{33,1},{2,34},{34,2},{3,35},{35,3},{4,36},{36... | collective-permute-start | bytes 786440 | tf_op jit(solution)/shard_map/ppermute | solution.py:373
  46.1 2.9 %collective-permute-start.7 = (bf16[128,1024]{1,0:T(8,128)(2,1)}, bf16[128,1024]{1,0:T(8,128)(2,1)}, u32[]{:S(2)}, u32[]{:S(2)}) collective-permute-start(bf16[128,1024]{1,0:T(8,128)(2,1)} %get-tuple-element.50), channel_id=1, source_target_pairs={{0,32},{32,0},{1,33},{33,1},{2,34},{34,2},{3,35},{35,3},{4,36},{36... | collective-permute-start | bytes 786440 | tf_op jit(solution)/shard_map/ppermute | solution.py:373
  47.5 1.9 collective-permute-start.8
  47.5 7.1 %copy-start.14 = (bf16[128,3072]{1,0:T(8,128)(2,1)S(1)}, bf16[128,3072]{1,0:T(8,128)(2,1)}, u32[]{:S(2)}) copy-start(bf16[128,3072]{1,0:T(8,128)(2,1)} %get-tuple-element.59) | copy-start | bytes 2359300
  51.9 20.6 %collective-permute-start.16 = (bf16[128,3072]{1,0:T(8,128)(2,1)}, bf16[128,3072]{1,0:T(8,128)(2,1)}, u32[]{:S(2)}, u32[]{:S(2)}) collective-permute-start(bf16[128,3072]{1,0:T(8,128)(2,1)} %add.13.refs_1_.refs_3_), channel_id=1, source_target_pairs={{0,64},{64,0},{1,65},{65,1},{2,66},{66,2},{3,67},{67,3},{4,68},{68... | collective-permute-start | bytes 2359304 | tf_op jit(solution)/shard_map/ppermute | solution.py:373
  54.6 17.8 %collective-permute-start.15 = (bf16[128,3072]{1,0:T(8,128)(2,1)S(1)}, bf16[128,3072]{1,0:T(8,128)(2,1)}, u32[]{:S(2)}, u32[]{:S(2)}) collective-permute-start(bf16[128,3072]{1,0:T(8,128)(2,1)S(1)} %copy-done.14), channel_id=1, source_target_pairs={{0,32},{32,0},{1,33},{33,1},{2,34},{34,2},{3,35},{35,3},{4,36},{36... | collective-permute-start | bytes 2359304 | tf_op jit(solution)/shard_map/ppermute | solution.py:373
  65.2 2.0 collective-permute-start.11
  65.3 2.2 %collective-permute-start.12 = (bf16[128,1024]{1,0:T(8,128)(2,1)}, bf16[128,1024]{1,0:T(8,128)(2,1)}, u32[]{:S(2)}, u32[]{:S(2)}) collective-permute-start(bf16[128,1024]{1,0:T(8,128)(2,1)} %get-tuple-element.56), channel_id=1, source_target_pairs={{0,32},{32,0},{1,33},{33,1},{2,34},{34,2},{3,35},{35,3},{4,36},{36... | collective-permute-start | bytes 786440 | tf_op jit(solution)/shard_map/ppermute | solution.py:373
  65.8 2.1 collective-permute-start.13
  66.4 103.1 %reduce-scatter.2.cloned.1.call-start = ((), (), s32[]{:S(2)}) async-start(), calls=%async_computation.3 | async-start | bytes 1966080 | tf_op jit(solution)/shard_map/reduce_scatter | solution.py:415
  67.1 12.6 %collective-permute-start.10 = (bf16[128,3072]{1,0:T(8,128)(2,1)}, bf16[128,3072]{1,0:T(8,128)(2,1)}, u32[]{:S(2)}, u32[]{:S(2)}) collective-permute-start(bf16[128,3072]{1,0:T(8,128)(2,1)} %get-tuple-element.53), channel_id=1, source_target_pairs={{0,32},{32,0},{1,33},{33,1},{2,34},{34,2},{3,35},{35,3},{4,36},{36... | collective-permute-start | bytes 2359304 | tf_op jit(solution)/shard_map/ppermute | solution.py:373
  70.3 20.8 %collective-permute-start.14 = (bf16[128,3072]{1,0:T(8,128)(2,1)}, bf16[128,3072]{1,0:T(8,128)(2,1)}, u32[]{:S(2)}, u32[]{:S(2)}) collective-permute-start(bf16[128,3072]{1,0:T(8,128)(2,1)} %add.14.refs_1_), channel_id=1, source_target_pairs={{0,64},{64,0},{1,65},{65,1},{2,66},{66,2},{3,67},{67,3},{4,68},{68... | collective-permute-start | bytes 2359304 | tf_op jit(solution)/shard_map/ppermute | solution.py:373
  77.0 30.9 %collective-permute-start.17 = (bf16[128,3072]{1,0:T(8,128)(2,1)}, bf16[128,3072]{1,0:T(8,128)(2,1)S(1)}, u32[]{:S(2)}, u32[]{:S(2)}) collective-permute-start(bf16[128,3072]{1,0:T(8,128)(2,1)} %get-tuple-element.64.refs_0_), channel_id=1, source_target_pairs={{0,64},{64,0},{1,65},{65,1},{2,66},{66,2},{3,67},{67,3},{4,68},{68... | collective-permute-start | bytes 2359304 | tf_op jit(solution)/shard_map/ppermute | solution.py:373
  107.9 0.9 copy-start.1
  108.8 4.2 %collective-permute-start.18 = (bf16[128,3072]{1,0:T(8,128)(2,1)}, bf16[128,3072]{1,0:T(8,128)(2,1)S(1)}, u32[]{:S(2)}, u32[]{:S(2)}) collective-permute-start(bf16[128,3072]{1,0:T(8,128)(2,1)} %get-tuple-element.67.refs_7_.refs_1_.refs_19_), channel_id=1, source_target_pairs={{0,32},{32,0},{1,33},{33,1},{2,34},{34,2},{3,35},{35,3},{4,36},{36... | collective-permute-start | bytes 2359304 | tf_op jit(solution)/shard_map/ppermute | solution.py:373
  109.7 3.8 %collective-permute-start.20 = (bf16[128,3072]{1,0:T(8,128)(2,1)}, bf16[128,3072]{1,0:T(8,128)(2,1)}, u32[]{:S(2)}, u32[]{:S(2)}) collective-permute-start(bf16[128,3072]{1,0:T(8,128)(2,1)} %get-tuple-element.70.refs_1_.refs_3_.refs_15_), channel_id=1, source_target_pairs={{0,32},{32,0},{1,33},{33,1},{2,34},{34,2},{3,35},{35,3},{4,36},{36... | collective-permute-start | bytes 2359304 | tf_op jit(solution)/shard_map/ppermute | solution.py:373
  109.7 5.3 %collective-permute-start.21 = (bf16[128,3072]{1,0:T(8,128)(2,1)}, bf16[128,3072]{1,0:T(8,128)(2,1)}, u32[]{:S(2)}, u32[]{:S(2)}) collective-permute-start(bf16[128,3072]{1,0:T(8,128)(2,1)} %get-tuple-element.71.refs_3_.refs_5_.refs_17_), channel_id=1, source_target_pairs={{0,32},{32,0},{1,33},{33,1},{2,34},{34,2},{3,35},{35,3},{4,36},{36... | collective-permute-start | bytes 2359304 | tf_op jit(solution)/shard_map/ppermute | solution.py:373
  110.2 15.1 %collective-permute-start.24 = (bf16[256,512]{1,0:T(8,128)(2,1)}, bf16[256,512]{1,0:T(8,128)(2,1)}, u32[]{:S(2)}, u32[]{:S(2)}) collective-permute-start(bf16[256,512]{1,0:T(8,128)(2,1)} %get-tuple-element.66.refs_3_), channel_id=1, source_target_pairs={{0,65},{1,64},{64,1},{65,0},{2,67},{3,66},{66,3},{67,2},{4,69},{5,... | collective-permute-start | bytes 786440 | tf_op jit(solution)/shard_map/ppermute | solution.py:400
  111.1 14.0 %collective-permute-start.22 = (bf16[128,1024]{1,0:T(8,128)(2,1)}, bf16[128,1024]{1,0:T(8,128)(2,1)}, u32[]{:S(2)}, u32[]{:S(2)}) collective-permute-start(bf16[128,1024]{1,0:T(8,128)(2,1)} %get-tuple-element.72), channel_id=1, source_target_pairs={{0,64},{64,0},{1,65},{65,1},{2,66},{66,2},{3,67},{67,3},{4,68},{68... | collective-permute-start | bytes 786440 | tf_op jit(solution)/shard_map/ppermute | solution.py:373
  112.9 2.1 copy-start
  112.9 12.7 %collective-permute-start.23 = (bf16[256,512]{1,0:T(8,128)(2,1)}, bf16[256,512]{1,0:T(8,128)(2,1)}, u32[]{:S(2)}, u32[]{:S(2)}) collective-permute-start(bf16[256,512]{1,0:T(8,128)(2,1)} %get-tuple-element.66.refs_3_), channel_id=1, source_target_pairs={{0,1},{1,0},{2,3},{3,2},{4,5},{5,4},{6,7},{7,6},{8,9},{9,8},{10,11... | collective-permute-start | bytes 786440 | tf_op jit(solution)/shard_map/ppermute | solution.py:373
  113.5 25.4 %collective-permute-start.19 = (bf16[128,2048]{1,0:T(8,128)(2,1)}, bf16[128,2048]{1,0:T(8,128)(2,1)}, u32[]{:S(2)}, u32[]{:S(2)}) collective-permute-start(bf16[128,2048]{1,0:T(8,128)(2,1)} %get-tuple-element.68), channel_id=1, source_target_pairs={{0,64},{64,0},{1,65},{65,1},{2,66},{66,2},{3,67},{67,3},{4,68},{68... | collective-permute-start | bytes 1572872 | tf_op jit(solution)/shard_map/ppermute | solution.py:373
  125.6 3.2 %collective-permute-start.26 = (bf16[256,512]{1,0:T(8,128)(2,1)}, bf16[256,512]{1,0:T(8,128)(2,1)S(1)}, u32[]{:S(2)}, u32[]{:S(2)}) collective-permute-start(bf16[256,512]{1,0:T(8,128)(2,1)} %get-tuple-element.74.refs_11_), channel_id=1, source_target_pairs={{0,32},{32,0},{1,33},{33,1},{2,34},{34,2},{3,35},{35,3},{4,36},{36... | collective-permute-start | bytes 786440 | tf_op jit(solution)/shard_map/ppermute | solution.py:373
  127.4 1.7 collective-permute-start.27
  127.4 2.1 collective-permute-start.25
  128.8 0.8 copy-start.12
  129.2 0.7 copy-start.13
  129.5 0.7 copy-start.6
  138.9 2.2 %collective-permute-start.28 = (bf16[128,2048]{1,0:T(8,128)(2,1)}, bf16[128,2048]{1,0:T(8,128)(2,1)S(1)}, u32[]{:S(2)}, u32[]{:S(2)}) collective-permute-start(bf16[128,2048]{1,0:T(8,128)(2,1)} %after.11.refs_3_.refs_9_.refs_21_), channel_id=1, source_target_pairs={{0,32},{32,0},{1,33},{33,1},{2,34},{34,2},{3,35},{35,3},{4,36},{36... | collective-permute-start | bytes 1572872 | tf_op jit(solution)/shard_map/ppermute | solution.py:373
  139.4 17.2 %collective-permute-start.30 = (bf16[256,1024]{1,0:T(8,128)(2,1)}, bf16[256,1024]{1,0:T(8,128)(2,1)}, u32[]{:S(2)}, u32[]{:S(2)}) collective-permute-start(bf16[256,1024]{1,0:T(8,128)(2,1)} %get-tuple-element.76), channel_id=1, source_target_pairs={{0,65},{1,64},{64,1},{65,0},{2,67},{3,66},{66,3},{67,2},{4,69},{5,... | collective-permute-start | bytes 1572872 | tf_op jit(solution)/shard_map/ppermute | solution.py:400
  140.3 16.3 %collective-permute-start.29 = (bf16[256,1024]{1,0:T(8,128)(2,1)}, bf16[256,1024]{1,0:T(8,128)(2,1)}, u32[]{:S(2)}, u32[]{:S(2)}) collective-permute-start(bf16[256,1024]{1,0:T(8,128)(2,1)} %get-tuple-element.76), channel_id=1, source_target_pairs={{0,1},{1,0},{2,3},{3,2},{4,5},{5,4},{6,7},{7,6},{8,9},{9,8},{10,11... | collective-permute-start | bytes 1572872 | tf_op jit(solution)/shard_map/ppermute | solution.py:373
  141.1 0.8 copy-start.2
  151.9 42.0 %all-to-all-start = ((bf16[4,256,1536]{2,1,0:T(8,128)(2,1)}), bf16[4,256,1536]{2,1,0:T(8,128)(2,1)}, u32[]{:S(2)}, u32[]{:S(2)}) async-start(bf16[4,256,1536]{2,1,0:T(8,128)(2,1)} %input_part.3.refs_2_), calls=%async_computation | async-start | bytes 6291456 | tf_op jit(solution)/shard_map/all_to_all | solution.py:423
  156.6 2.2 %collective-permute-start.31 = (bf16[256,1024]{1,0:T(8,128)(2,1)}, bf16[256,1024]{1,0:T(8,128)(2,1)S(1)}, u32[]{:S(2)}, u32[]{:S(2)}) collective-permute-start(bf16[256,1024]{1,0:T(8,128)(2,1)} %get-tuple-element.77.refs_11_.refs_23_), channel_id=1, source_target_pairs={{0,32},{32,0},{1,33},{33,1},{2,34},{34,2},{3,35},{35,3},{4,36},{36... | collective-permute-start | bytes 1572872 | tf_op jit(solution)/shard_map/ppermute | solution.py:373
  157.1 2.6 %collective-permute-start.32 = (bf16[256,1024]{1,0:T(8,128)(2,1)}, bf16[256,1024]{1,0:T(8,128)(2,1)}, u32[]{:S(2)}, u32[]{:S(2)}) collective-permute-start(bf16[256,1024]{1,0:T(8,128)(2,1)} %get-tuple-element.78.refs_13_.refs_25_), channel_id=1, source_target_pairs={{0,32},{32,0},{1,33},{33,1},{2,34},{34,2},{3,35},{35,3},{4,36},{36... | collective-permute-start | bytes 1572872 | tf_op jit(solution)/shard_map/ppermute | solution.py:373
  158.8 0.9 copy-start.3
  165.9 13.2 %collective-permute-start.33 = (bf16[768,256]{1,0:T(8,128)(2,1)}, bf16[768,256]{1,0:T(8,128)(2,1)S(1)}, u32[]{:S(2)}, u32[]{:S(2)}) collective-permute-start(bf16[768,256]{1,0:T(8,128)(2,1)} %get-tuple-element.82), channel_id=1, source_target_pairs={{0,6},{2,4},{4,2},{6,0},{1,7},{3,5},{5,3},{7,1},{8,14},{10,12},{12... | collective-permute-start | bytes 1179656 | tf_op jit(solution)/shard_map/ppermute | solution.py:373
  169.6 10.3 %collective-permute-start.34 = (bf16[768,256]{1,0:T(8,128)(2,1)}, bf16[768,256]{1,0:T(8,128)(2,1)S(1)}, u32[]{:S(2)}, u32[]{:S(2)}) collective-permute-start(bf16[768,256]{1,0:T(8,128)(2,1)} %get-tuple-element.79.refs_27_), channel_id=1, source_target_pairs={{0,2},{2,0},{4,6},{6,4},{1,3},{3,1},{5,7},{7,5},{8,10},{10,8},{12,... | collective-permute-start | bytes 1179656 | tf_op jit(solution)/shard_map/ppermute | solution.py:373
  179.0 0.8 copy-start.10
  179.8 0.7 copy-start.11
  182.8 19.8 %collective-permute-start.36 = (bf16[1536,256]{1,0:T(8,128)(2,1)}, bf16[1536,256]{1,0:T(8,128)(2,1)}, u32[]{:S(2)}, u32[]{:S(2)}) collective-permute-start(bf16[1536,256]{1,0:T(8,128)(2,1)} %get-tuple-element.84), channel_id=1, source_target_pairs={{0,6},{2,4},{4,2},{6,0},{1,7},{3,5},{5,3},{7,1},{8,14},{10,12},{12... | collective-permute-start | bytes 2359304 | tf_op jit(solution)/shard_map/ppermute | solution.py:373
  184.5 18.2 %collective-permute-start.35 = (bf16[1536,256]{1,0:T(8,128)(2,1)}, bf16[1536,256]{1,0:T(8,128)(2,1)}, u32[]{:S(2)}, u32[]{:S(2)}) collective-permute-start(bf16[1536,256]{1,0:T(8,128)(2,1)} %get-tuple-element.83.refs_15_), channel_id=1, source_target_pairs={{0,2},{2,0},{4,6},{6,4},{1,3},{3,1},{5,7},{7,5},{8,10},{10,8},{12,... | collective-permute-start | bytes 2359304 | tf_op jit(solution)/shard_map/ppermute | solution.py:373
Sparse Core Ops, SparseCore 0:
  66.6 39.5 all-gather.1
  140.5 27.4 reduce-scatter.1

commit v7 on v6

--- a/solution.py
+++ b/solution.py
@@ -23,7 +23,7 @@
 MIB = 1 << 20
 TF, TG, TK, TE, T3, T4, T5 = 0.01, 30, 0.5, 300, 2, 300, 300
 ANY = pl.BlockSpec(memory_space=pl.ANY)
-PARAMS = pltpu.CompilerParams(vmem_limit_bytes=63 * MIB)
+PARAMS = pltpu.CompilerParams(vmem_limit_bytes=64 * MIB)
 
 
 def cost(micros):

time: 214 us -> 212 us (level)
  local copies, waits for them, and re-layouts: 5.84 us -> 3.53 us
    unnamed x30 -> x8, local copies, waits for them, and re-layouts: 4.67 us -> 1.6 us
  transfers between devices with their start and end apart: 40 -> 40, of which waited for: 22 -> 21; matrix products, arithmetic and copies ran while one was open for 0% -> 0% of each run, Pallas kernels for 41% -> 42%
where the time goes in v7:
time: 212 us; the launch traced here: 211 us
  Pallas kernels  90.8 us (43%)
  waiting for transfers between devices  61 us (29%)
  starting transfers between devices  40.8 us (19%)
  between operations  14.2 us (7%)
  local copies, waits for them, and re-layouts  3.53 us (2%)
    ppermute x35, waiting for transfers between devices, swap(): return lax.ppermute(value, axis, [(i, i ^ mask) for i in range(n)])  49.9 us
    ppermute x35, starting transfers between devices, swap(): return lax.ppermute(value, axis, [(i, i ^ mask) for i in range(n)])  33.7 us
    pallas_call x4, Pallas kernels, weight_part(): pl.pallas_call(lambda *refs: weight_kernel(size, masks, halves, *refs), g...  28.9 us
    pallas_call x2, Pallas kernels, input_part(): pl.pallas_call(lambda *refs: input_kernel(counts, *refs), grid_spec=grid_...  20 us
    pallas_call x2, Pallas kernels, block_partials(): pl.pallas_call(partial_kernel, grid_spec=grid_spec, out_shape=[jax.ShapeD...  19.9 us
    all_to_all x1, waiting for transfers between devices, shards(): dx, = after([lax.all_to_all(dx, 'y', 0, 0, tiled=True)], total, T5)  10.3 us
    pallas_call x2, Pallas kernels, gelu_pair(): pl.pallas_call(lambda *refs: gelu_kernel(part, *refs), grid_spec=grid_spe...  9.19 us
    pallas_call x2, Pallas kernels, add(): pl.pallas_call(add_kernel, grid=(1,), in_specs=[block] + [pl.BlockSpec((H...  4.91 us
  transfers between devices with their start and end apart: 40, of which 21 were waited for; matrix products, arithmetic and copies ran while one was open for 0% of the time, Pallas kernels for 42%

profile of v7, /device:TPU:1, one launch (start us, length us, event | category | flops | bytes accessed | tf_op | source)
XLA Modules:
  0.0 211.0 jit_solution(3286969384803234131)
XLA Ops:
  7.2 1.9 fusion
  9.1 3.6 %collective-permute-start.5 = (bf16[128,1536]{1,0:T(8,128)(2,1)S(1)}, bf16[128,1536]{1,0:T(8,128)(2,1)S(1)}, u32[]{:S(2)}, u32[]{:S(2)}) collective-permute-start(bf16[128,1536]{1,0:T(8,128)(2,1)S(1)} %get-tuple-element.85.b0), channel_id=1, source_target_pairs={{0,24},{8,16},{16,8},{24,0},{1,25},{9,17},{17,9},{25,1},{2,26},{10... | collective-permute-start | bytes 1179656 | tf_op jit(solution)/shard_map/ppermute | solution.py:373
  12.7 0.3 collective-permute-start.4
  13.3 2.7 %collective-permute-start.2 = (bf16[128,1536]{1,0:T(8,128)(2,1)}, bf16[128,1536]{1,0:T(8,128)(2,1)}, u32[]{:S(2)}, u32[]{:S(2)}) collective-permute-start(bf16[128,1536]{1,0:T(8,128)(2,1)} %get-tuple-element.86.b0), channel_id=1, source_target_pairs={{0,24},{8,16},{16,8},{24,0},{1,25},{9,17},{17,9},{25,1},{2,26},{10... | collective-permute-start | bytes 1179656 | tf_op jit(solution)/shard_map/ppermute | solution.py:373
  16.0 0.3 collective-permute-start.1
  16.3 13.5 %collective-permute-done.5.b3 = bf16[128,1536]{1,0:T(8,128)(2,1)S(1)} collective-permute-done((bf16[128,1536]{1,0:T(8,128)(2,1)S(1)}, bf16[128,1536]{1,0:T(8,128)(2,1)S(1)}, u32[]{:S(2)}, u32[]{:S(2)}) %collective-permute-start.5) | collective-permute-done | bytes 393248 | tf_op jit(solution)/shard_map/ppermute | solution.py:373
  29.8 0.8 copy-done.1
  30.6 1.2 collective-permute-start.9
  31.9 0.8 copy-done.3
  32.6 9.9 %block_partials.2 = (bf16[128,3072]{1,0:T(8,128)(2,1)}, bf16[128,3072]{1,0:T(8,128)(2,1)}, bf16[128,3072]{1,0:T(8,128)(2,1)}, bf16[128,1024]{1,0:T(8,128)(2,1)},...) custom-call(s32[1]{0:T(128)} %bitcast.3.q_ref, bf16[128,1536]{1,0:T(8,128)(2,1)} %copy-done, ...), custom_call_target="tpu_custom_call" | custom-call | flops 11500000 | bytes 36000 | tf_op jit(solution)/shard_map/block_partials/pallas_call | solution.py:88
  42.6 3.2 %collective-permute-start.6 = (bf16[128,1024]{1,0:T(8,128)(2,1)}, bf16[128,1024]{1,0:T(8,128)(2,1)}, u32[]{:S(2)}, u32[]{:S(2)}) collective-permute-start(bf16[128,1024]{1,0:T(8,128)(2,1)} %get-tuple-element.49), channel_id=1, source_target_pairs={{0,32},{32,0},{1,33},{33,1},{2,34},{34,2},{3,35},{35,3},{4,36},{36... | collective-permute-start | bytes 786440 | tf_op jit(solution)/shard_map/ppermute | solution.py:373
  45.8 1.0 collective-permute-done.2.refs_2_
  46.8 1.4 collective-permute-start.7
  48.2 1.5 collective-permute-done.7.refs_1_
  49.7 0.4 collective-permute-done.8.refs_2_
  50.0 2.4 %add.13.refs_1_.refs_3_ = bf16[128,3072]{1,0:T(8,128)(2,1)} custom-call(bf16[128,3072]{1,0:T(8,128)(2,1)} %get-tuple-element.48.a_ref, bf16[128,1024]{1,0:T(8,128)(2,1)} %collective-permute-done.6.refs_0_, bf16[128,1024]{1,0:T(8,128)(2,1)} %collective-permute-done.7.refs_1_, bf16[128,1024]{1,0:T(8,128)(2,1)} %collective-permute-done.8.refs_2_, ...), custom_call_target="tpu_custom_call" | custom-call | flops 1150000000 | bytes 3600000 | tf_op jit(solution)/shard_map/add/pallas_call | solution.py:337
  52.5 2.7 %collective-permute-start.16 = (bf16[128,3072]{1,0:T(8,128)(2,1)}, bf16[128,3072]{1,0:T(8,128)(2,1)}, u32[]{:S(2)}, u32[]{:S(2)}) collective-permute-start(bf16[128,3072]{1,0:T(8,128)(2,1)} %add.13.refs_1_.refs_3_), channel_id=1, source_target_pairs={{0,64},{64,0},{1,65},{65,1},{2,66},{66,2},{3,67},{67,3},{4,68},{68... | collective-permute-start | bytes 2359304 | tf_op jit(solution)/shard_map/ppermute | solution.py:373
  55.2 0.7 collective-permute-start.15
  55.8 10.0 %block_partials.3 = (bf16[128,3072]{1,0:T(8,128)(2,1)}, bf16[128,3072]{1,0:T(8,128)(2,1)}, bf16[128,3072]{1,0:T(8,128)(2,1)}, bf16[128,1024]{1,0:T(8,128)(2,1)},...) custom-call(s32[1]{0:T(128)} %bitcast.3.q_ref, ...), custom_call_target="tpu_custom_call", output_to_operand_aliasing={{6}: (6, {})} | custom-call | flops 11500000 | bytes 36000 | tf_op jit(solution)/shard_map/block_partials/pallas_call | solution.py:88
  65.9 0.5 collective-permute-start.12
  66.5 0.6 pad_add_fusion.refs_0_
  67.2 0.5 collective-permute-done.11.refs_0_
  68.1 0.4 collective-permute-done.13.refs_2_
  68.5 2.5 %add.14.refs_1_ = bf16[128,3072]{1,0:T(8,128)(2,1)} custom-call(bf16[128,3072]{1,0:T(8,128)(2,1)} %get-tuple-element.54.a_ref, bf16[128,1024]{1,0:T(8,128)(2,1)} %collective-permute-done.11.refs_0_, bf16[128,1024]{1,0:T(8,128)(2,1)} %collective-permute-done.12.refs_1_, bf16[128,1024]{1,0:T(8,128)(2,1)} %collective-permute-done.13.refs_2_, ...), custom_call_target="tpu_custom_call" | custom-call | flops 1150000000 | bytes 3600000 | tf_op jit(solution)/shard_map/add/pallas_call | solution.py:337
  71.2 1.8 collective-permute-done.16.refs_0_
  73.0 4.5 %gelu_pair.2 = (bf16[256,3072]{1,0:T(8,128)(2,1)}, bf16[256,512]{1,0:T(8,128)(2,1)}, bf16[256,1024]{1,0:T(8,128)(2,1)}, bf16[128,3072]{1,0:T(8,128)(2,1)}) custom-call(s32[3]{0:T(128)} %pad_add_fusion.refs_0_, bf16[128,3072]{1,0:T(8,128)(2,1)} %get-tuple-element.58.refs_1_, bf16[128,3072]{1,0:T(8,128)(2,1)} %collective-permute-done.15.refs_2_, ...), custom_call_target="tpu_custom_call" | custom-call | flops 34500001792 | bytes 108000000 | tf_op jit(solution)/shard_map/gelu_pair/pallas_call | solution.py:141
  77.5 2.7 %collective-permute-start.17 = (bf16[128,3072]{1,0:T(8,128)(2,1)}, bf16[128,3072]{1,0:T(8,128)(2,1)}, u32[]{:S(2)}, u32[]{:S(2)}) collective-permute-start(bf16[128,3072]{1,0:T(8,128)(2,1)} %get-tuple-element.64.refs_0_), channel_id=1, source_target_pairs={{0,64},{64,0},{1,65},{65,1},{2,66},{66,2},{3,67},{67,3},{4,68},{68... | collective-permute-start | bytes 2359304 | tf_op jit(solution)/shard_map/ppermute | solution.py:373
  80.3 11.5 %collective-permute-done.14.refs_3_ = bf16[128,3072]{1,0:T(8,128)(2,1)} collective-permute-done((bf16[128,3072]{1,0:T(8,128)(2,1)}, bf16[128,3072]{1,0:T(8,128)(2,1)}, u32[]{:S(2)}, u32[]{:S(2)}) %collective-permute-start.14) | collective-permute-done | bytes 786464 | tf_op jit(solution)/shard_map/ppermute | solution.py:373
  91.8 4.7 %gelu_pair.3 = (bf16[256,3072]{1,0:T(8,128)(2,1)}, bf16[256,512]{1,0:T(8,128)(2,1)}, bf16[256,1024]{1,0:T(8,128)(2,1)}, bf16[128,3072]{1,0:T(8,128)(2,1)}, bf16[...) custom-call(s32[3]{0:T(128)} %pad_add_fusion.refs_0_, ...), custom_call_target="tpu_custom_call", output_to_operand_aliasing={{0}: (5, {}), {1}: (6, {}), {2}: (7, {})} | custom-call | flops 34500001792 | bytes 108000000 | tf_op jit(solution)/shard_map/gelu_pair/pallas_call | solution.py:141
  96.5 12.2 %collective-permute-done.17.refs_1_ = bf16[128,3072]{1,0:T(8,128)(2,1)} collective-permute-done((bf16[128,3072]{1,0:T(8,128)(2,1)}, bf16[128,3072]{1,0:T(8,128)(2,1)}, u32[]{:S(2)}, u32[]{:S(2)}) %collective-permute-start.17) | collective-permute-done | bytes 786464 | tf_op jit(solution)/shard_map/ppermute | solution.py:373
  108.7 1.0 collective-permute-start.18
  109.7 0.5 collective-permute-start.21
  110.2 0.9 collective-permute-start.24
  111.0 1.2 collective-permute-start.22
  112.3 1.2 collective-permute-start.23
  113.4 1.0 collective-permute-start.19
  114.5 10.0 %input_part.2.refs_3_.refs_8_ = bf16[4,256,1536]{2,1,0:T(8,128)(2,1)} custom-call(s32[3]{0:T(128)} %pad_add_fusion.refs_0_, bf16[128,3072]{1,0:T(8,128)(2,1)} %get-tuple-element.70.refs_1_.refs_3_.refs_15_, bf16[128,3072]{1,0:T(8,128)(2,1)} %collective-permute-done.20.refs_2_.refs_4_.refs_16_, bf16[128,3072]{1,0:T(8,128)(2,1)} %get-tuple-element.71.refs_3_.refs_5_.refs_17_, ...), custom_call_target="tpu_custom_call" | custom-call | flops 575000000 | bytes 1800000 | tf_op jit(solution)/shard_map/input_part/pallas_call | solution.py:292
  124.5 0.7 collective-permute-done.24.refs_2_
  125.2 0.3 collective-permute-done.23.refs_1_
  125.5 1.8 collective-permute-start.26
  127.4 0.5 collective-permute-start.25
  127.9 1.0 collective-permute-done.26.refs_12_
  128.9 0.4 collective-permute-done.27.refs_14_
  129.2 0.4 collective-permute-done.25.refs_10_.refs_6_
  129.6 8.7 %weight_part.4.refs_1_ = bf16[4,1536,128]{2,1,0:T(8,128)(2,1)} custom-call(s32[3]{0:T(128)} %pad_add_fusion.refs_0_, bf16[1024,1536]{1,0:T(8,128)(2,1)} %get-tuple-element.69.refs_1_, bf16[1024,1536]{1,0:T(8,128)(2,1)} %all-gather.2.cloned.1.call-done.refs_7_.refs_2_, bf16[128,3072]{1,0:T(8,128)(2,1)} %get-tuple-element.70.refs_1_.refs_3_.refs_15_, ...), custom_call_target="tpu_custom_call" | custom-call | flops 575000000 | bytes 1800000 | tf_op jit(solution)/shard_map/weight_part/pallas_call | solution.py:227
  138.3 0.5 collective-permute-start.28
  138.7 1.5 collective-permute-start.30
  140.3 0.3 collective-permute-done.28.refs_5_.refs_10_.refs_22_
  140.6 10.0 %input_part.3.refs_2_ = bf16[4,256,1536]{2,1,0:T(8,128)(2,1)} custom-call(s32[3]{0:T(128)} %pad_add_fusion.refs_0_, bf16[128,3072]{1,0:T(8,128)(2,1)} %get-tuple-element.67.refs_7_.refs_1_.refs_19_, bf16[128,3072]{1,0:T(8,128)(2,1)} %collective-permute-done.18.refs_6_.refs_8_.refs_2_.refs_20_, ...), custom_call_target="tpu_custom_call", output_to_operand_aliasing={{}: (8, {})} | custom-call | flops 575000000 | bytes 1800000 | tf_op jit(solution)/shard_map/input_part/pallas_call | solution.py:292
  150.6 4.6 %all-to-all-start = ((bf16[4,256,1536]{2,1,0:T(8,128)(2,1)}), bf16[4,256,1536]{2,1,0:T(8,128)(2,1)}, u32[]{:S(2)}, u32[]{:S(2)}) async-start(bf16[4,256,1536]{2,1,0:T(8,128)(2,1)} %input_part.3.refs_2_), calls=%async_computation | async-start | bytes 6291456 | tf_op jit(solution)/shard_map/all_to_all | solution.py:423
  155.3 0.4 collective-permute-start.31
  155.9 1.7 collective-permute-done.31.refs_12_.refs_24_
  157.6 0.7 collective-permute-done.32.refs_14_.refs_26_
  158.4 6.1 %weight_part.5 = (bf16[768,256]{1,0:T(8,128)(2,1)}, bf16[768,256]{1,0:T(8,128)(2,1)}) custom-call(s32[3]{0:T(128)} %pad_add_fusion.refs_0_, bf16[1024,1536]{1,0:T(8,128)(2,1)} %get-tuple-element.69.refs_1_, bf16[1024,1536]{1,0:T(8,128)(2,1)} %all-gather.2.cloned.1.call-done.refs_7_.refs_2_, bf16[128,3072]{1,0:T(8,128)(2,1)} %get-tuple-element.70.refs_1_.refs_3_.refs_15_, ...), custom_call_target="tpu_custom_call" | custom-call | flops 575000000 | bytes 1800000 | tf_op jit(solution)/shard_map/weight_part/pallas_call | solution.py:227
  164.5 3.8 %collective-permute-start.33 = (bf16[768,256]{1,0:T(8,128)(2,1)}, bf16[768,256]{1,0:T(8,128)(2,1)}, u32[]{:S(2)}, u32[]{:S(2)}) collective-permute-start(bf16[768,256]{1,0:T(8,128)(2,1)} %get-tuple-element.82), channel_id=1, source_target_pairs={{0,6},{2,4},{4,2},{6,0},{1,7},{3,5},{5,3},{7,1},{8,14},{10,12},{12... | collective-permute-start | bytes 1179656 | tf_op jit(solution)/shard_map/ppermute | solution.py:373
  168.2 8.3 %weight_part.6 = (bf16[1536,256]{1,0:T(8,128)(2,1)}, bf16[1536,256]{1,0:T(8,128)(2,1)}) custom-call(s32[3]{0:T(128)} %pad_add_fusion.refs_0_, bf16[1024,1536]{1,0:T(8,128)(2,1)} %get-tuple-element.69.refs_1_, bf16[1024,1536]{1,0:T(8,128)(2,1)} %all-gather.2.cloned.1.call-done.refs_7_.refs_2_, bf16[128,3072]{1,0:T(8,128)(2,1)} %get-tuple-element.70.refs_1_.refs_3_.refs_15_, ...), custom_call_target="tpu_custom_call" | custom-call | flops 575000000 | bytes 1800000 | tf_op jit(solution)/shard_map/weight_part/pallas_call | solution.py:227
  176.5 1.2 collective-permute-done.33.last_ref
  177.7 0.8 collective-permute-done.34.first_ref
  178.5 2.3 %relay.1 = (bf16[1536,256]{1,0:T(8,128)(2,1)}, bf16[1536,256]{1,0:T(8,128)(2,1)}) custom-call(bf16[1536,256]{1,0:T(8,128)(2,1)} %get-tuple-element.80.a_ref, bf16[1536,256]{1,0:T(8,128)(2,1)} %get-tuple-element.81.b_ref, bf16[768,256]{1,0:T(8,128)(2,1)} %collective-permute-done.33.last_ref, ...), custom_call_target="tpu_custom_call", output_to_operand_aliasing={{0}: (0, {}), {1}: (1, {})} | custom-call | flops 575000000 | bytes 1800000 | tf_op jit(solution)/shard_map/relay/pallas_call | solution.py:246
  180.8 1.5 collective-permute-start.36
  182.4 10.3 %all-to-all-done.refs_0_ = bf16[4,256,1536]{2,1,0:T(8,128)(2,1)} async-done(((bf16[4,256,1536]{2,1,0:T(8,128)(2,1)}), bf16[4,256,1536]{2,1,0:T(8,128)(2,1)}, u32[]{:S(2)}, u32[]{:S(2)}) %all-to-all-start) | async-done | bytes 3145760 | tf_op jit(solution)/shard_map/all_to_all | solution.py:423
  192.6 2.8 %fold.1.refs_4_ = bf16[256,1536]{1,0:T(8,128)(2,1)} custom-call(bf16[4,256,1536]{2,1,0:T(8,128)(2,1)} %after.12.in_ref), custom_call_target="tpu_custom_call" | custom-call | flops 575000000 | bytes 1800000 | tf_op jit(solution)/shard_map/fold/pallas_call | solution.py:359
  195.5 5.9 %weight_part.7.refs_1_ = bf16[1536,256]{1,0:T(8,128)(2,1)} custom-call(s32[3]{0:T(128)} %pad_add_fusion.refs_0_, bf16[1024,1536]{1,0:T(8,128)(2,1)} %get-tuple-element.69.refs_1_, bf16[1024,1536]{1,0:T(8,128)(2,1)} %all-gather.2.cloned.1.call-done.refs_7_.refs_2_, bf16[128,3072]{1,0:T(8,128)(2,1)} %get-tuple-element.70.refs_1_.refs_3_.refs_15_, ...), custom_call_target="tpu_custom_call" | custom-call | flops 575000000 | bytes 1800000 | tf_op jit(solution)/shard_map/weight_part/pallas_call | solution.py:227
  201.4 2.8 %join.1 = bf16[1536,384]{1,0:T(8,128)(2,1)} custom-call(bf16[1536,128]{1,0:T(8,128)(2,1)} %bitcast.6, bf16[1536,256]{1,0:T(8,128)(2,1)} %weight_part.7.refs_1_, bf16[1536,256]{1,0:T(8,128)(2,1)} %collective-permute-done.35.refs_2_, bf16[1536,256]{1,0:T(8,128)(2,1)} %collective-permute-done.36.refs_3_, bf16[256,1536]{1,0:T(8,128)(2,1)} %fold.1.refs_4_), custom_call_target="tpu_custom_call" | custom-call | flops 575000000 | bytes 1800000 | tf_op jit(solution)/shard_map/join/pallas_call | solution.py:316
  (50 shorter events, 1.4 us)
Async XLA Ops:
  7.2 107.3 %all-gather.2.cloned.1.call-start = ((), (), s32[]{:S(2)}) async-start(), calls=%async_computation.2 | async-start | bytes 3932160 | tf_op jit(solution)/shard_map/all_gather | solution.py:383
  9.1 3.9 %copy-start = (bf16[128,1536]{1,0:T(8,128)(2,1)}, bf16[128,1536]{1,0:T(8,128)(2,1)S(1)}, u32[]{:S(2)}) copy-start(bf16[128,1536]{1,0:T(8,128)(2,1)S(1)} %get-tuple-element.85.b0) | copy-start | bytes 1179652
  9.1 20.7 %collective-permute-start.5 = (bf16[128,1536]{1,0:T(8,128)(2,1)S(1)}, bf16[128,1536]{1,0:T(8,128)(2,1)S(1)}, u32[]{:S(2)}, u32[]{:S(2)}) collective-permute-start(bf16[128,1536]{1,0:T(8,128)(2,1)S(1)} %get-tuple-element.85.b0), channel_id=1, source_target_pairs={{0,24},{8,16},{16,8},{24,0},{1,25},{9,17},{17,9},{25,1},{2,26},{10... | collective-permute-start | bytes 1179656 | tf_op jit(solution)/shard_map/ppermute | solution.py:373
  12.7 17.9 %collective-permute-start.4 = (bf16[128,1536]{1,0:T(8,128)(2,1)S(1)}, bf16[128,1536]{1,0:T(8,128)(2,1)S(1)}, u32[]{:S(2)}, u32[]{:S(2)}) collective-permute-start(bf16[128,1536]{1,0:T(8,128)(2,1)S(1)} %get-tuple-element.85.b0), channel_id=1, source_target_pairs={{0,16},{8,24},{16,0},{24,8},{1,17},{9,25},{17,1},{25,9},{2,18},{10... | collective-permute-start | bytes 1179656 | tf_op jit(solution)/shard_map/ppermute | solution.py:373
  13.1 18.8 %collective-permute-start.3 = (bf16[128,1536]{1,0:T(8,128)(2,1)S(1)}, bf16[128,1536]{1,0:T(8,128)(2,1)S(1)}, u32[]{:S(2)}, u32[]{:S(2)}) collective-permute-start(bf16[128,1536]{1,0:T(8,128)(2,1)S(1)} %get-tuple-element.85.b0), channel_id=1, source_target_pairs={{0,8},{8,0},{16,24},{24,16},{1,9},{9,1},{17,25},{25,17},{2,10},{10... | collective-permute-start | bytes 1179656 | tf_op jit(solution)/shard_map/ppermute | solution.py:373
  13.3 33.5 %collective-permute-start.2 = (bf16[128,1536]{1,0:T(8,128)(2,1)}, bf16[128,1536]{1,0:T(8,128)(2,1)}, u32[]{:S(2)}, u32[]{:S(2)}) collective-permute-start(bf16[128,1536]{1,0:T(8,128)(2,1)} %get-tuple-element.86.b0), channel_id=1, source_target_pairs={{0,24},{8,16},{16,8},{24,0},{1,25},{9,17},{17,9},{25,1},{2,26},{10... | collective-permute-start | bytes 1179656 | tf_op jit(solution)/shard_map/ppermute | solution.py:373
  16.0 32.2 %collective-permute-start.1 = (bf16[128,1536]{1,0:T(8,128)(2,1)}, bf16[128,1536]{1,0:T(8,128)(2,1)}, u32[]{:S(2)}, u32[]{:S(2)}) collective-permute-start(bf16[128,1536]{1,0:T(8,128)(2,1)} %get-tuple-element.86.b0), channel_id=1, source_target_pairs={{0,16},{8,24},{16,0},{24,8},{1,17},{9,25},{17,1},{25,9},{2,18},{10... | collective-permute-start | bytes 1179656 | tf_op jit(solution)/shard_map/ppermute | solution.py:373
  29.8 0.8 copy-start.1
  30.6 17.6 %collective-permute-start = (bf16[128,1536]{1,0:T(8,128)(2,1)}, bf16[128,1536]{1,0:T(8,128)(2,1)}, u32[]{:S(2)}, u32[]{:S(2)}) collective-permute-start(bf16[128,1536]{1,0:T(8,128)(2,1)} %get-tuple-element.86.b0), channel_id=1, source_target_pairs={{0,8},{8,0},{16,24},{24,16},{1,9},{9,1},{17,25},{25,17},{2,10},{10... | collective-permute-start | bytes 1179656 | tf_op jit(solution)/shard_map/ppermute | solution.py:373
  30.6 1.2 copy-start.2
  30.6 25.2 %collective-permute-start.9 = (bf16[256,1536]{1,0:T(8,128)(2,1)}, bf16[256,1536]{1,0:T(8,128)(2,1)}, u32[]{:S(2)}, u32[]{:S(2)}) collective-permute-start(bf16[256,1536]{1,0:T(8,128)(2,1)} %refs_3_.1), channel_id=1, source_target_pairs={{0,1},{1,0},{2,3},{3,2},{4,5},{5,4},{6,7},{7,6},{8,9},{9,8},{10,11... | collective-permute-start | bytes 2359304 | tf_op jit(solution)/shard_map/ppermute | solution.py:373
  31.9 0.8 copy-start.3
  42.6 5.6 %collective-permute-start.6 = (bf16[128,1024]{1,0:T(8,128)(2,1)}, bf16[128,1024]{1,0:T(8,128)(2,1)}, u32[]{:S(2)}, u32[]{:S(2)}) collective-permute-start(bf16[128,1024]{1,0:T(8,128)(2,1)} %get-tuple-element.49), channel_id=1, source_target_pairs={{0,32},{32,0},{1,33},{33,1},{2,34},{34,2},{3,35},{35,3},{4,36},{36... | collective-permute-start | bytes 786440 | tf_op jit(solution)/shard_map/ppermute | solution.py:373
  46.8 2.9 %collective-permute-start.7 = (bf16[128,1024]{1,0:T(8,128)(2,1)}, bf16[128,1024]{1,0:T(8,128)(2,1)}, u32[]{:S(2)}, u32[]{:S(2)}) collective-permute-start(bf16[128,1024]{1,0:T(8,128)(2,1)} %get-tuple-element.50), channel_id=1, source_target_pairs={{0,32},{32,0},{1,33},{33,1},{2,34},{34,2},{3,35},{35,3},{4,36},{36... | collective-permute-start | bytes 786440 | tf_op jit(solution)/shard_map/ppermute | solution.py:373
  48.2 1.9 collective-permute-start.8
  52.5 20.6 %collective-permute-start.16 = (bf16[128,3072]{1,0:T(8,128)(2,1)}, bf16[128,3072]{1,0:T(8,128)(2,1)}, u32[]{:S(2)}, u32[]{:S(2)}) collective-permute-start(bf16[128,3072]{1,0:T(8,128)(2,1)} %add.13.refs_1_.refs_3_), channel_id=1, source_target_pairs={{0,64},{64,0},{1,65},{65,1},{2,66},{66,2},{3,67},{67,3},{4,68},{68... | collective-permute-start | bytes 2359304 | tf_op jit(solution)/shard_map/ppermute | solution.py:373
  55.2 17.8 %collective-permute-start.15 = (bf16[128,3072]{1,0:T(8,128)(2,1)}, bf16[128,3072]{1,0:T(8,128)(2,1)}, u32[]{:S(2)}, u32[]{:S(2)}) collective-permute-start(bf16[128,3072]{1,0:T(8,128)(2,1)} %get-tuple-element.59), channel_id=1, source_target_pairs={{0,32},{32,0},{1,33},{33,1},{2,34},{34,2},{3,35},{35,3},{4,36},{36... | collective-permute-start | bytes 2359304 | tf_op jit(solution)/shard_map/ppermute | solution.py:373
  65.8 2.0 collective-permute-start.11
  65.9 2.2 %collective-permute-start.12 = (bf16[128,1024]{1,0:T(8,128)(2,1)}, bf16[128,1024]{1,0:T(8,128)(2,1)}, u32[]{:S(2)}, u32[]{:S(2)}) collective-permute-start(bf16[128,1024]{1,0:T(8,128)(2,1)} %get-tuple-element.56), channel_id=1, source_target_pairs={{0,32},{32,0},{1,33},{33,1},{2,34},{34,2},{3,35},{35,3},{4,36},{36... | collective-permute-start | bytes 786440 | tf_op jit(solution)/shard_map/ppermute | solution.py:373
  66.4 2.1 %collective-permute-start.13 = (bf16[128,1024]{1,0:T(8,128)(2,1)}, bf16[128,1024]{1,0:T(8,128)(2,1)}, u32[]{:S(2)}, u32[]{:S(2)}) collective-permute-start(bf16[128,1024]{1,0:T(8,128)(2,1)} %get-tuple-element.57), channel_id=1, source_target_pairs={{0,32},{32,0},{1,33},{33,1},{2,34},{34,2},{3,35},{35,3},{4,36},{36... | collective-permute-start | bytes 786440 | tf_op jit(solution)/shard_map/ppermute | solution.py:373
  67.2 101.1 %reduce-scatter.2.cloned.1.call-start = ((), (), s32[]{:S(2)}) async-start(), calls=%async_computation.3 | async-start | bytes 1966080 | tf_op jit(solution)/shard_map/reduce_scatter | solution.py:415
  67.8 12.5 %collective-permute-start.10 = (bf16[128,3072]{1,0:T(8,128)(2,1)}, bf16[128,3072]{1,0:T(8,128)(2,1)}, u32[]{:S(2)}, u32[]{:S(2)}) collective-permute-start(bf16[128,3072]{1,0:T(8,128)(2,1)} %get-tuple-element.53), channel_id=1, source_target_pairs={{0,32},{32,0},{1,33},{33,1},{2,34},{34,2},{3,35},{35,3},{4,36},{36... | collective-permute-start | bytes 2359304 | tf_op jit(solution)/shard_map/ppermute | solution.py:373
  71.0 20.8 %collective-permute-start.14 = (bf16[128,3072]{1,0:T(8,128)(2,1)}, bf16[128,3072]{1,0:T(8,128)(2,1)}, u32[]{:S(2)}, u32[]{:S(2)}) collective-permute-start(bf16[128,3072]{1,0:T(8,128)(2,1)} %add.14.refs_1_), channel_id=1, source_target_pairs={{0,64},{64,0},{1,65},{65,1},{2,66},{66,2},{3,67},{67,3},{4,68},{68... | collective-permute-start | bytes 2359304 | tf_op jit(solution)/shard_map/ppermute | solution.py:373
  77.5 31.1 %collective-permute-start.17 = (bf16[128,3072]{1,0:T(8,128)(2,1)}, bf16[128,3072]{1,0:T(8,128)(2,1)}, u32[]{:S(2)}, u32[]{:S(2)}) collective-permute-start(bf16[128,3072]{1,0:T(8,128)(2,1)} %get-tuple-element.64.refs_0_), channel_id=1, source_target_pairs={{0,64},{64,0},{1,65},{65,1},{2,66},{66,2},{3,67},{67,3},{4,68},{68... | collective-permute-start | bytes 2359304 | tf_op jit(solution)/shard_map/ppermute | solution.py:373
  108.7 3.6 %collective-permute-start.18 = (bf16[128,3072]{1,0:T(8,128)(2,1)}, bf16[128,3072]{1,0:T(8,128)(2,1)}, u32[]{:S(2)}, u32[]{:S(2)}) collective-permute-start(bf16[128,3072]{1,0:T(8,128)(2,1)} %get-tuple-element.67.refs_7_.refs_1_.refs_19_), channel_id=1, source_target_pairs={{0,32},{32,0},{1,33},{33,1},{2,34},{34,2},{3,35},{35,3},{4,36},{36... | collective-permute-start | bytes 2359304 | tf_op jit(solution)/shard_map/ppermute | solution.py:373
  109.7 3.8 %collective-permute-start.20 = (bf16[128,3072]{1,0:T(8,128)(2,1)}, bf16[128,3072]{1,0:T(8,128)(2,1)}, u32[]{:S(2)}, u32[]{:S(2)}) collective-permute-start(bf16[128,3072]{1,0:T(8,128)(2,1)} %get-tuple-element.70.refs_1_.refs_3_.refs_15_), channel_id=1, source_target_pairs={{0,32},{32,0},{1,33},{33,1},{2,34},{34,2},{3,35},{35,3},{4,36},{36... | collective-permute-start | bytes 2359304 | tf_op jit(solution)/shard_map/ppermute | solution.py:373
  109.7 4.8 %collective-permute-start.21 = (bf16[128,3072]{1,0:T(8,128)(2,1)}, bf16[128,3072]{1,0:T(8,128)(2,1)}, u32[]{:S(2)}, u32[]{:S(2)}) collective-permute-start(bf16[128,3072]{1,0:T(8,128)(2,1)} %get-tuple-element.71.refs_3_.refs_5_.refs_17_), channel_id=1, source_target_pairs={{0,32},{32,0},{1,33},{33,1},{2,34},{34,2},{3,35},{35,3},{4,36},{36... | collective-permute-start | bytes 2359304 | tf_op jit(solution)/shard_map/ppermute | solution.py:373
  110.2 15.1 %collective-permute-start.24 = (bf16[256,512]{1,0:T(8,128)(2,1)}, bf16[256,512]{1,0:T(8,128)(2,1)}, u32[]{:S(2)}, u32[]{:S(2)}) collective-permute-start(bf16[256,512]{1,0:T(8,128)(2,1)} %get-tuple-element.66.refs_3_), channel_id=1, source_target_pairs={{0,65},{1,64},{64,1},{65,0},{2,67},{3,66},{66,3},{67,2},{4,69},{5,... | collective-permute-start | bytes 786440 | tf_op jit(solution)/shard_map/ppermute | solution.py:400
  111.0 13.5 %collective-permute-start.22 = (bf16[128,1024]{1,0:T(8,128)(2,1)}, bf16[128,1024]{1,0:T(8,128)(2,1)}, u32[]{:S(2)}, u32[]{:S(2)}) collective-permute-start(bf16[128,1024]{1,0:T(8,128)(2,1)} %get-tuple-element.72), channel_id=1, source_target_pairs={{0,64},{64,0},{1,65},{65,1},{2,66},{66,2},{3,67},{67,3},{4,68},{68... | collective-permute-start | bytes 786440 | tf_op jit(solution)/shard_map/ppermute | solution.py:373
  112.3 13.3 %collective-permute-start.23 = (bf16[256,512]{1,0:T(8,128)(2,1)}, bf16[256,512]{1,0:T(8,128)(2,1)}, u32[]{:S(2)}, u32[]{:S(2)}) collective-permute-start(bf16[256,512]{1,0:T(8,128)(2,1)} %get-tuple-element.66.refs_3_), channel_id=1, source_target_pairs={{0,1},{1,0},{2,3},{3,2},{4,5},{5,4},{6,7},{7,6},{8,9},{9,8},{10,11... | collective-permute-start | bytes 786440 | tf_op jit(solution)/shard_map/ppermute | solution.py:373
  113.4 24.8 %collective-permute-start.19 = (bf16[128,2048]{1,0:T(8,128)(2,1)}, bf16[128,2048]{1,0:T(8,128)(2,1)}, u32[]{:S(2)}, u32[]{:S(2)}) collective-permute-start(bf16[128,2048]{1,0:T(8,128)(2,1)} %get-tuple-element.68), channel_id=1, source_target_pairs={{0,64},{64,0},{1,65},{65,1},{2,66},{66,2},{3,67},{67,3},{4,68},{68... | collective-permute-start | bytes 1572872 | tf_op jit(solution)/shard_map/ppermute | solution.py:373
  125.5 3.3 %collective-permute-start.26 = (bf16[256,512]{1,0:T(8,128)(2,1)}, bf16[256,512]{1,0:T(8,128)(2,1)}, u32[]{:S(2)}, u32[]{:S(2)}) collective-permute-start(bf16[256,512]{1,0:T(8,128)(2,1)} %get-tuple-element.74.refs_11_), channel_id=1, source_target_pairs={{0,32},{32,0},{1,33},{33,1},{2,34},{34,2},{3,35},{35,3},{4,36},{36... | collective-permute-start | bytes 786440 | tf_op jit(solution)/shard_map/ppermute | solution.py:373
  127.4 1.9 collective-permute-start.27
  127.4 2.3 %collective-permute-start.25 = (bf16[128,1024]{1,0:T(8,128)(2,1)}, bf16[128,1024]{1,0:T(8,128)(2,1)}, u32[]{:S(2)}, u32[]{:S(2)}) collective-permute-start(bf16[128,1024]{1,0:T(8,128)(2,1)} %get-tuple-element.73.refs_9_.refs_4_), channel_id=1, source_target_pairs={{0,32},{32,0},{1,33},{33,1},{2,34},{34,2},{3,35},{35,3},{4,36},{36... | collective-permute-start | bytes 786440 | tf_op jit(solution)/shard_map/ppermute | solution.py:373
  138.3 2.3 %collective-permute-start.28 = (bf16[128,2048]{1,0:T(8,128)(2,1)}, bf16[128,2048]{1,0:T(8,128)(2,1)}, u32[]{:S(2)}, u32[]{:S(2)}) collective-permute-start(bf16[128,2048]{1,0:T(8,128)(2,1)} %after.11.refs_3_.refs_9_.refs_21_), channel_id=1, source_target_pairs={{0,32},{32,0},{1,33},{33,1},{2,34},{34,2},{3,35},{35,3},{4,36},{36... | collective-permute-start | bytes 1572872 | tf_op jit(solution)/shard_map/ppermute | solution.py:373
  138.7 16.5 %collective-permute-start.30 = (bf16[256,1024]{1,0:T(8,128)(2,1)}, bf16[256,1024]{1,0:T(8,128)(2,1)}, u32[]{:S(2)}, u32[]{:S(2)}) collective-permute-start(bf16[256,1024]{1,0:T(8,128)(2,1)} %get-tuple-element.76), channel_id=1, source_target_pairs={{0,65},{1,64},{64,1},{65,0},{2,67},{3,66},{66,3},{67,2},{4,69},{5,... | collective-permute-start | bytes 1572872 | tf_op jit(solution)/shard_map/ppermute | solution.py:400
  140.3 15.0 %collective-permute-start.29 = (bf16[256,1024]{1,0:T(8,128)(2,1)}, bf16[256,1024]{1,0:T(8,128)(2,1)}, u32[]{:S(2)}, u32[]{:S(2)}) collective-permute-start(bf16[256,1024]{1,0:T(8,128)(2,1)} %get-tuple-element.76), channel_id=1, source_target_pairs={{0,1},{1,0},{2,3},{3,2},{4,5},{5,4},{6,7},{7,6},{8,9},{9,8},{10,11... | collective-permute-start | bytes 1572872 | tf_op jit(solution)/shard_map/ppermute | solution.py:373
  150.6 42.0 %all-to-all-start = ((bf16[4,256,1536]{2,1,0:T(8,128)(2,1)}), bf16[4,256,1536]{2,1,0:T(8,128)(2,1)}, u32[]{:S(2)}, u32[]{:S(2)}) async-start(bf16[4,256,1536]{2,1,0:T(8,128)(2,1)} %input_part.3.refs_2_), calls=%async_computation | async-start | bytes 6291456 | tf_op jit(solution)/shard_map/all_to_all | solution.py:423
  155.3 2.3 %collective-permute-start.31 = (bf16[256,1024]{1,0:T(8,128)(2,1)}, bf16[256,1024]{1,0:T(8,128)(2,1)}, u32[]{:S(2)}, u32[]{:S(2)}) collective-permute-start(bf16[256,1024]{1,0:T(8,128)(2,1)} %get-tuple-element.77.refs_11_.refs_23_), channel_id=1, source_target_pairs={{0,32},{32,0},{1,33},{33,1},{2,34},{34,2},{3,35},{35,3},{4,36},{36... | collective-permute-start | bytes 1572872 | tf_op jit(solution)/shard_map/ppermute | solution.py:373
  155.7 2.6 %collective-permute-start.32 = (bf16[256,1024]{1,0:T(8,128)(2,1)}, bf16[256,1024]{1,0:T(8,128)(2,1)}, u32[]{:S(2)}, u32[]{:S(2)}) collective-permute-start(bf16[256,1024]{1,0:T(8,128)(2,1)} %get-tuple-element.78.refs_13_.refs_25_), channel_id=1, source_target_pairs={{0,32},{32,0},{1,33},{33,1},{2,34},{34,2},{3,35},{35,3},{4,36},{36... | collective-permute-start | bytes 1572872 | tf_op jit(solution)/shard_map/ppermute | solution.py:373
  164.5 13.3 %collective-permute-start.33 = (bf16[768,256]{1,0:T(8,128)(2,1)}, bf16[768,256]{1,0:T(8,128)(2,1)}, u32[]{:S(2)}, u32[]{:S(2)}) collective-permute-start(bf16[768,256]{1,0:T(8,128)(2,1)} %get-tuple-element.82), channel_id=1, source_target_pairs={{0,6},{2,4},{4,2},{6,0},{1,7},{3,5},{5,3},{7,1},{8,14},{10,12},{12... | collective-permute-start | bytes 1179656 | tf_op jit(solution)/shard_map/ppermute | solution.py:373
  168.2 10.3 %collective-permute-start.34 = (bf16[768,256]{1,0:T(8,128)(2,1)}, bf16[768,256]{1,0:T(8,128)(2,1)}, u32[]{:S(2)}, u32[]{:S(2)}) collective-permute-start(bf16[768,256]{1,0:T(8,128)(2,1)} %get-tuple-element.79.refs_27_), channel_id=1, source_target_pairs={{0,2},{2,0},{4,6},{6,4},{1,3},{3,1},{5,7},{7,5},{8,10},{10,8},{12,... | collective-permute-start | bytes 1179656 | tf_op jit(solution)/shard_map/ppermute | solution.py:373
  180.8 20.5 %collective-permute-start.36 = (bf16[1536,256]{1,0:T(8,128)(2,1)}, bf16[1536,256]{1,0:T(8,128)(2,1)}, u32[]{:S(2)}, u32[]{:S(2)}) collective-permute-start(bf16[1536,256]{1,0:T(8,128)(2,1)} %get-tuple-element.84), channel_id=1, source_target_pairs={{0,6},{2,4},{4,2},{6,0},{1,7},{3,5},{5,3},{7,1},{8,14},{10,12},{12... | collective-permute-start | bytes 2359304 | tf_op jit(solution)/shard_map/ppermute | solution.py:373
  182.4 19.0 %collective-permute-start.35 = (bf16[1536,256]{1,0:T(8,128)(2,1)}, bf16[1536,256]{1,0:T(8,128)(2,1)}, u32[]{:S(2)}, u32[]{:S(2)}) collective-permute-start(bf16[1536,256]{1,0:T(8,128)(2,1)} %get-tuple-element.83.refs_15_), channel_id=1, source_target_pairs={{0,2},{2,0},{4,6},{6,4},{1,3},{3,1},{5,7},{7,5},{8,10},{10,8},{12,... | collective-permute-start | bytes 2359304 | tf_op jit(solution)/shard_map/ppermute | solution.py:373
Sparse Core Ops, SparseCore 0:
  67.3 39.5 all-gather.1
  140.4 26.8 reduce-scatter.1

commit v8 on v7

--- a/solution.py
+++ b/solution.py
@@ -194,7 +194,7 @@
 def weight_part(ids, tk, tx, first, second, other, chunk, masks, halves, wait):
     w = width(chunk)
     size = CHUNKS[chunk][1] * LANE
-    rows = K // 2 if len(masks) == 1 else 512
+    rows = K // 2
     specs = []
     for m in masks:
         for array in (*first, *second):

time: 212 us -> 212 us (level)
  no operation moved by 1% of the time
where the time goes in v8:
time: 212 us; the launch traced here: 211 us
  Pallas kernels  90.6 us (43%)
  waiting for transfers between devices  60.8 us (29%)
  starting transfers between devices  41 us (19%)
  between operations  14.2 us (7%)
  local copies, waits for them, and re-layouts  3.53 us (2%)
    ppermute x35, waiting for transfers between devices, swap(): return lax.ppermute(value, axis, [(i, i ^ mask) for i in range(n)])  49.8 us
    ppermute x35, starting transfers between devices, swap(): return lax.ppermute(value, axis, [(i, i ^ mask) for i in range(n)])  33.7 us
    pallas_call x4, Pallas kernels, weight_part(): pl.pallas_call(lambda *refs: weight_kernel(size, masks, halves, *refs), g...  28.7 us
    pallas_call x2, Pallas kernels, input_part(): pl.pallas_call(lambda *refs: input_kernel(counts, *refs), grid_spec=grid_...  20 us
    pallas_call x2, Pallas kernels, block_partials(): pl.pallas_call(partial_kernel, grid_spec=grid_spec, out_shape=[jax.ShapeD...  19.9 us
    all_to_all x1, waiting for transfers between devices, shards(): dx, = after([lax.all_to_all(dx, 'y', 0, 0, tiled=True)], total, T5)  10.3 us
    pallas_call x2, Pallas kernels, gelu_pair(): pl.pallas_call(lambda *refs: gelu_kernel(part, *refs), grid_spec=grid_spe...  9.19 us
    pallas_call x2, Pallas kernels, add(): pl.pallas_call(add_kernel, grid=(1,), in_specs=[block] + [pl.BlockSpec((H...  4.91 us
  transfers between devices with their start and end apart: 40, of which 21 were waited for; matrix products, arithmetic and copies ran while one was open for 0% of the time, Pallas kernels for 42%

profile of v8, /device:TPU:1, one launch (start us, length us, event | category | flops | bytes accessed | tf_op | source)
XLA Modules:
  0.0 210.7 jit_solution(1995790207980670520)
XLA Ops:
  7.2 1.9 fusion
  9.1 3.6 %collective-permute-start.5 = (bf16[128,1536]{1,0:T(8,128)(2,1)S(1)}, bf16[128,1536]{1,0:T(8,128)(2,1)S(1)}, u32[]{:S(2)}, u32[]{:S(2)}) collective-permute-start(bf16[128,1536]{1,0:T(8,128)(2,1)S(1)} %get-tuple-element.85.b0), channel_id=1, source_target_pairs={{0,24},{8,16},{16,8},{24,0},{1,25},{9,17},{17,9},{25,1},{2,26},{10... | collective-permute-start | bytes 1179656 | tf_op jit(solution)/shard_map/ppermute | solution.py:373
  12.7 0.3 collective-permute-start.4
  13.3 2.7 %collective-permute-start.2 = (bf16[128,1536]{1,0:T(8,128)(2,1)}, bf16[128,1536]{1,0:T(8,128)(2,1)}, u32[]{:S(2)}, u32[]{:S(2)}) collective-permute-start(bf16[128,1536]{1,0:T(8,128)(2,1)} %get-tuple-element.86.b0), channel_id=1, source_target_pairs={{0,24},{8,16},{16,8},{24,0},{1,25},{9,17},{17,9},{25,1},{2,26},{10... | collective-permute-start | bytes 1179656 | tf_op jit(solution)/shard_map/ppermute | solution.py:373
  16.0 0.3 collective-permute-start.1
  16.3 13.5 %collective-permute-done.5.b3 = bf16[128,1536]{1,0:T(8,128)(2,1)S(1)} collective-permute-done((bf16[128,1536]{1,0:T(8,128)(2,1)S(1)}, bf16[128,1536]{1,0:T(8,128)(2,1)S(1)}, u32[]{:S(2)}, u32[]{:S(2)}) %collective-permute-start.5) | collective-permute-done | bytes 393248 | tf_op jit(solution)/shard_map/ppermute | solution.py:373
  29.8 0.8 copy-done.1
  30.6 1.2 collective-permute-start.9
  31.9 0.8 copy-done.3
  32.6 9.9 %block_partials.2 = (bf16[128,3072]{1,0:T(8,128)(2,1)}, bf16[128,3072]{1,0:T(8,128)(2,1)}, bf16[128,3072]{1,0:T(8,128)(2,1)}, bf16[128,1024]{1,0:T(8,128)(2,1)},...) custom-call(s32[1]{0:T(128)} %bitcast.3.q_ref, bf16[128,1536]{1,0:T(8,128)(2,1)} %copy-done, ...), custom_call_target="tpu_custom_call" | custom-call | flops 11500000 | bytes 36000 | tf_op jit(solution)/shard_map/block_partials/pallas_call | solution.py:88
  42.6 3.2 %collective-permute-start.6 = (bf16[128,1024]{1,0:T(8,128)(2,1)}, bf16[128,1024]{1,0:T(8,128)(2,1)}, u32[]{:S(2)}, u32[]{:S(2)}) collective-permute-start(bf16[128,1024]{1,0:T(8,128)(2,1)} %get-tuple-element.49), channel_id=1, source_target_pairs={{0,32},{32,0},{1,33},{33,1},{2,34},{34,2},{3,35},{35,3},{4,36},{36... | collective-permute-start | bytes 786440 | tf_op jit(solution)/shard_map/ppermute | solution.py:373
  45.8 1.0 collective-permute-done.2.refs_2_
  46.8 1.4 collective-permute-start.7
  48.2 1.5 collective-permute-done.7.refs_1_
  49.7 0.4 collective-permute-done.8.refs_2_
  50.0 2.4 %add.13.refs_1_.refs_3_ = bf16[128,3072]{1,0:T(8,128)(2,1)} custom-call(bf16[128,3072]{1,0:T(8,128)(2,1)} %get-tuple-element.48.a_ref, bf16[128,1024]{1,0:T(8,128)(2,1)} %collective-permute-done.6.refs_0_, bf16[128,1024]{1,0:T(8,128)(2,1)} %collective-permute-done.7.refs_1_, bf16[128,1024]{1,0:T(8,128)(2,1)} %collective-permute-done.8.refs_2_, ...), custom_call_target="tpu_custom_call" | custom-call | flops 1150000000 | bytes 3600000 | tf_op jit(solution)/shard_map/add/pallas_call | solution.py:337
  52.5 2.7 %collective-permute-start.16 = (bf16[128,3072]{1,0:T(8,128)(2,1)}, bf16[128,3072]{1,0:T(8,128)(2,1)}, u32[]{:S(2)}, u32[]{:S(2)}) collective-permute-start(bf16[128,3072]{1,0:T(8,128)(2,1)} %add.13.refs_1_.refs_3_), channel_id=1, source_target_pairs={{0,64},{64,0},{1,65},{65,1},{2,66},{66,2},{3,67},{67,3},{4,68},{68... | collective-permute-start | bytes 2359304 | tf_op jit(solution)/shard_map/ppermute | solution.py:373
  55.2 0.7 collective-permute-start.15
  55.8 10.0 %block_partials.3 = (bf16[128,3072]{1,0:T(8,128)(2,1)}, bf16[128,3072]{1,0:T(8,128)(2,1)}, bf16[128,3072]{1,0:T(8,128)(2,1)}, bf16[128,1024]{1,0:T(8,128)(2,1)},...) custom-call(s32[1]{0:T(128)} %bitcast.3.q_ref, ...), custom_call_target="tpu_custom_call", output_to_operand_aliasing={{6}: (6, {})} | custom-call | flops 11500000 | bytes 36000 | tf_op jit(solution)/shard_map/block_partials/pallas_call | solution.py:88
  65.9 0.5 collective-permute-start.12
  66.5 0.6 pad_add_fusion.refs_0_
  67.2 0.5 collective-permute-done.11.refs_0_
  67.9 0.2 collective-permute-done.12.refs_1_
  68.1 0.4 collective-permute-done.13.refs_2_
  68.5 2.5 %add.14.refs_1_ = bf16[128,3072]{1,0:T(8,128)(2,1)} custom-call(bf16[128,3072]{1,0:T(8,128)(2,1)} %get-tuple-element.54.a_ref, bf16[128,1024]{1,0:T(8,128)(2,1)} %collective-permute-done.11.refs_0_, bf16[128,1024]{1,0:T(8,128)(2,1)} %collective-permute-done.12.refs_1_, bf16[128,1024]{1,0:T(8,128)(2,1)} %collective-permute-done.13.refs_2_, ...), custom_call_target="tpu_custom_call" | custom-call | flops 1150000000 | bytes 3600000 | tf_op jit(solution)/shard_map/add/pallas_call | solution.py:337
  71.2 1.8 collective-permute-done.16.refs_0_
  73.0 4.5 %gelu_pair.2 = (bf16[256,3072]{1,0:T(8,128)(2,1)}, bf16[256,512]{1,0:T(8,128)(2,1)}, bf16[256,1024]{1,0:T(8,128)(2,1)}, bf16[128,3072]{1,0:T(8,128)(2,1)}) custom-call(s32[3]{0:T(128)} %pad_add_fusion.refs_0_, bf16[128,3072]{1,0:T(8,128)(2,1)} %get-tuple-element.58.refs_1_, bf16[128,3072]{1,0:T(8,128)(2,1)} %collective-permute-done.15.refs_2_, ...), custom_call_target="tpu_custom_call" | custom-call | flops 34500001792 | bytes 108000000 | tf_op jit(solution)/shard_map/gelu_pair/pallas_call | solution.py:141
  77.5 2.7 %collective-permute-start.17 = (bf16[128,3072]{1,0:T(8,128)(2,1)}, bf16[128,3072]{1,0:T(8,128)(2,1)}, u32[]{:S(2)}, u32[]{:S(2)}) collective-permute-start(bf16[128,3072]{1,0:T(8,128)(2,1)} %get-tuple-element.64.refs_0_), channel_id=1, source_target_pairs={{0,64},{64,0},{1,65},{65,1},{2,66},{66,2},{3,67},{67,3},{4,68},{68... | collective-permute-start | bytes 2359304 | tf_op jit(solution)/shard_map/ppermute | solution.py:373
  80.3 11.5 %collective-permute-done.14.refs_3_ = bf16[128,3072]{1,0:T(8,128)(2,1)} collective-permute-done((bf16[128,3072]{1,0:T(8,128)(2,1)}, bf16[128,3072]{1,0:T(8,128)(2,1)}, u32[]{:S(2)}, u32[]{:S(2)}) %collective-permute-start.14) | collective-permute-done | bytes 786464 | tf_op jit(solution)/shard_map/ppermute | solution.py:373
  91.8 4.7 %gelu_pair.3 = (bf16[256,3072]{1,0:T(8,128)(2,1)}, bf16[256,512]{1,0:T(8,128)(2,1)}, bf16[256,1024]{1,0:T(8,128)(2,1)}, bf16[128,3072]{1,0:T(8,128)(2,1)}, bf16[...) custom-call(s32[3]{0:T(128)} %pad_add_fusion.refs_0_, ...), custom_call_target="tpu_custom_call", output_to_operand_aliasing={{0}: (5, {}), {1}: (6, {}), {2}: (7, {})} | custom-call | flops 34500001792 | bytes 108000000 | tf_op jit(solution)/shard_map/gelu_pair/pallas_call | solution.py:141
  96.5 12.2 %collective-permute-done.17.refs_1_ = bf16[128,3072]{1,0:T(8,128)(2,1)} collective-permute-done((bf16[128,3072]{1,0:T(8,128)(2,1)}, bf16[128,3072]{1,0:T(8,128)(2,1)}, u32[]{:S(2)}, u32[]{:S(2)}) %collective-permute-start.17) | collective-permute-done | bytes 786464 | tf_op jit(solution)/shard_map/ppermute | solution.py:373
  108.7 1.0 collective-permute-start.18
  109.7 0.5 collective-permute-start.21
  110.2 0.9 collective-permute-start.24
  111.0 1.2 collective-permute-start.22
  112.3 1.2 collective-permute-start.23
  113.4 1.0 collective-permute-start.19
  114.5 10.0 %input_part.2.refs_3_.refs_8_ = bf16[4,256,1536]{2,1,0:T(8,128)(2,1)} custom-call(s32[3]{0:T(128)} %pad_add_fusion.refs_0_, bf16[128,3072]{1,0:T(8,128)(2,1)} %get-tuple-element.70.refs_1_.refs_3_.refs_15_, bf16[128,3072]{1,0:T(8,128)(2,1)} %collective-permute-done.20.refs_2_.refs_4_.refs_16_, bf16[128,3072]{1,0:T(8,128)(2,1)} %get-tuple-element.71.refs_3_.refs_5_.refs_17_, ...), custom_call_target="tpu_custom_call" | custom-call | flops 575000000 | bytes 1800000 | tf_op jit(solution)/shard_map/input_part/pallas_call | solution.py:292
  124.5 0.7 collective-permute-done.24.refs_2_
  125.2 0.3 collective-permute-done.23.refs_1_
  125.5 1.8 collective-permute-start.26
  127.4 0.5 collective-permute-start.25
  127.9 1.0 collective-permute-done.26.refs_12_
  128.9 0.4 collective-permute-done.27.refs_14_
  129.2 0.4 collective-permute-done.25.refs_10_.refs_6_
  129.6 8.4 %weight_part.4.refs_1_ = bf16[4,1536,128]{2,1,0:T(8,128)(2,1)} custom-call(s32[3]{0:T(128)} %pad_add_fusion.refs_0_, bf16[1024,1536]{1,0:T(8,128)(2,1)} %get-tuple-element.69.refs_1_, bf16[1024,1536]{1,0:T(8,128)(2,1)} %all-gather.2.cloned.1.call-done.refs_7_.refs_2_, bf16[128,3072]{1,0:T(8,128)(2,1)} %get-tuple-element.70.refs_1_.refs_3_.refs_15_, ...), custom_call_target="tpu_custom_call" | custom-call | flops 575000000 | bytes 1800000 | tf_op jit(solution)/shard_map/weight_part/pallas_call | solution.py:227
  138.1 0.5 collective-permute-start.28
  138.5 1.8 collective-permute-start.30
  140.4 10.0 %input_part.3.refs_2_ = bf16[4,256,1536]{2,1,0:T(8,128)(2,1)} custom-call(s32[3]{0:T(128)} %pad_add_fusion.refs_0_, bf16[128,3072]{1,0:T(8,128)(2,1)} %get-tuple-element.67.refs_7_.refs_1_.refs_19_, bf16[128,3072]{1,0:T(8,128)(2,1)} %collective-permute-done.18.refs_6_.refs_8_.refs_2_.refs_20_, ...), custom_call_target="tpu_custom_call", output_to_operand_aliasing={{}: (8, {})} | custom-call | flops 575000000 | bytes 1800000 | tf_op jit(solution)/shard_map/input_part/pallas_call | solution.py:292
  150.4 4.6 %all-to-all-start = ((bf16[4,256,1536]{2,1,0:T(8,128)(2,1)}), bf16[4,256,1536]{2,1,0:T(8,128)(2,1)}, u32[]{:S(2)}, u32[]{:S(2)}) async-start(bf16[4,256,1536]{2,1,0:T(8,128)(2,1)} %input_part.3.refs_2_), calls=%async_computation | async-start | bytes 6291456 | tf_op jit(solution)/shard_map/all_to_all | solution.py:423
  155.1 0.5 collective-permute-start.31
  155.6 1.7 collective-permute-done.31.refs_12_.refs_24_
  157.4 0.7 collective-permute-done.32.refs_14_.refs_26_
  158.1 6.1 %weight_part.5 = (bf16[768,256]{1,0:T(8,128)(2,1)}, bf16[768,256]{1,0:T(8,128)(2,1)}) custom-call(s32[3]{0:T(128)} %pad_add_fusion.refs_0_, bf16[1024,1536]{1,0:T(8,128)(2,1)} %get-tuple-element.69.refs_1_, bf16[1024,1536]{1,0:T(8,128)(2,1)} %all-gather.2.cloned.1.call-done.refs_7_.refs_2_, bf16[128,3072]{1,0:T(8,128)(2,1)} %get-tuple-element.70.refs_1_.refs_3_.refs_15_, ...), custom_call_target="tpu_custom_call" | custom-call | flops 575000000 | bytes 1800000 | tf_op jit(solution)/shard_map/weight_part/pallas_call | solution.py:227
  164.2 3.7 %collective-permute-start.33 = (bf16[768,256]{1,0:T(8,128)(2,1)}, bf16[768,256]{1,0:T(8,128)(2,1)}, u32[]{:S(2)}, u32[]{:S(2)}) collective-permute-start(bf16[768,256]{1,0:T(8,128)(2,1)} %get-tuple-element.82), channel_id=1, source_target_pairs={{0,6},{2,4},{4,2},{6,0},{1,7},{3,5},{5,3},{7,1},{8,14},{10,12},{12... | collective-permute-start | bytes 1179656 | tf_op jit(solution)/shard_map/ppermute | solution.py:373
  168.0 8.2 %weight_part.6 = (bf16[1536,256]{1,0:T(8,128)(2,1)}, bf16[1536,256]{1,0:T(8,128)(2,1)}) custom-call(s32[3]{0:T(128)} %pad_add_fusion.refs_0_, bf16[1024,1536]{1,0:T(8,128)(2,1)} %get-tuple-element.69.refs_1_, bf16[1024,1536]{1,0:T(8,128)(2,1)} %all-gather.2.cloned.1.call-done.refs_7_.refs_2_, bf16[128,3072]{1,0:T(8,128)(2,1)} %get-tuple-element.70.refs_1_.refs_3_.refs_15_, ...), custom_call_target="tpu_custom_call" | custom-call | flops 575000000 | bytes 1800000 | tf_op jit(solution)/shard_map/weight_part/pallas_call | solution.py:227
  176.2 1.2 collective-permute-done.33.last_ref
  177.5 0.8 collective-permute-done.34.first_ref
  178.3 2.3 %relay.1 = (bf16[1536,256]{1,0:T(8,128)(2,1)}, bf16[1536,256]{1,0:T(8,128)(2,1)}) custom-call(bf16[1536,256]{1,0:T(8,128)(2,1)} %get-tuple-element.80.a_ref, bf16[1536,256]{1,0:T(8,128)(2,1)} %get-tuple-element.81.b_ref, bf16[768,256]{1,0:T(8,128)(2,1)} %collective-permute-done.33.last_ref, ...), custom_call_target="tpu_custom_call", output_to_operand_aliasing={{0}: (0, {}), {1}: (1, {})} | custom-call | flops 575000000 | bytes 1800000 | tf_op jit(solution)/shard_map/relay/pallas_call | solution.py:246
  180.6 1.5 collective-permute-start.36
  182.1 10.3 %all-to-all-done.refs_0_ = bf16[4,256,1536]{2,1,0:T(8,128)(2,1)} async-done(((bf16[4,256,1536]{2,1,0:T(8,128)(2,1)}), bf16[4,256,1536]{2,1,0:T(8,128)(2,1)}, u32[]{:S(2)}, u32[]{:S(2)}) %all-to-all-start) | async-done | bytes 3145760 | tf_op jit(solution)/shard_map/all_to_all | solution.py:423
  192.4 2.8 %fold.1.refs_4_ = bf16[256,1536]{1,0:T(8,128)(2,1)} custom-call(bf16[4,256,1536]{2,1,0:T(8,128)(2,1)} %after.12.in_ref), custom_call_target="tpu_custom_call" | custom-call | flops 575000000 | bytes 1800000 | tf_op jit(solution)/shard_map/fold/pallas_call | solution.py:359
  195.2 5.9 %weight_part.7.refs_1_ = bf16[1536,256]{1,0:T(8,128)(2,1)} custom-call(s32[3]{0:T(128)} %pad_add_fusion.refs_0_, bf16[1024,1536]{1,0:T(8,128)(2,1)} %get-tuple-element.69.refs_1_, bf16[1024,1536]{1,0:T(8,128)(2,1)} %all-gather.2.cloned.1.call-done.refs_7_.refs_2_, bf16[128,3072]{1,0:T(8,128)(2,1)} %get-tuple-element.70.refs_1_.refs_3_.refs_15_, ...), custom_call_target="tpu_custom_call" | custom-call | flops 575000000 | bytes 1800000 | tf_op jit(solution)/shard_map/weight_part/pallas_call | solution.py:227
  201.1 2.8 %join.1 = bf16[1536,384]{1,0:T(8,128)(2,1)} custom-call(bf16[1536,128]{1,0:T(8,128)(2,1)} %bitcast.6, bf16[1536,256]{1,0:T(8,128)(2,1)} %weight_part.7.refs_1_, bf16[1536,256]{1,0:T(8,128)(2,1)} %collective-permute-done.35.refs_2_, bf16[1536,256]{1,0:T(8,128)(2,1)} %collective-permute-done.36.refs_3_, bf16[256,1536]{1,0:T(8,128)(2,1)} %fold.1.refs_4_), custom_call_target="tpu_custom_call" | custom-call | flops 575000000 | bytes 1800000 | tf_op jit(solution)/shard_map/join/pallas_call | solution.py:316
  (50 shorter events, 1.2 us)
Async XLA Ops:
  7.2 107.3 %all-gather.2.cloned.1.call-start = ((), (), s32[]{:S(2)}) async-start(), calls=%async_computation.2 | async-start | bytes 3932160 | tf_op jit(solution)/shard_map/all_gather | solution.py:383
  9.1 3.9 %copy-start = (bf16[128,1536]{1,0:T(8,128)(2,1)}, bf16[128,1536]{1,0:T(8,128)(2,1)S(1)}, u32[]{:S(2)}) copy-start(bf16[128,1536]{1,0:T(8,128)(2,1)S(1)} %get-tuple-element.85.b0) | copy-start | bytes 1179652
  9.1 20.7 %collective-permute-start.5 = (bf16[128,1536]{1,0:T(8,128)(2,1)S(1)}, bf16[128,1536]{1,0:T(8,128)(2,1)S(1)}, u32[]{:S(2)}, u32[]{:S(2)}) collective-permute-start(bf16[128,1536]{1,0:T(8,128)(2,1)S(1)} %get-tuple-element.85.b0), channel_id=1, source_target_pairs={{0,24},{8,16},{16,8},{24,0},{1,25},{9,17},{17,9},{25,1},{2,26},{10... | collective-permute-start | bytes 1179656 | tf_op jit(solution)/shard_map/ppermute | solution.py:373
  12.7 17.9 %collective-permute-start.4 = (bf16[128,1536]{1,0:T(8,128)(2,1)S(1)}, bf16[128,1536]{1,0:T(8,128)(2,1)S(1)}, u32[]{:S(2)}, u32[]{:S(2)}) collective-permute-start(bf16[128,1536]{1,0:T(8,128)(2,1)S(1)} %get-tuple-element.85.b0), channel_id=1, source_target_pairs={{0,16},{8,24},{16,0},{24,8},{1,17},{9,25},{17,1},{25,9},{2,18},{10... | collective-permute-start | bytes 1179656 | tf_op jit(solution)/shard_map/ppermute | solution.py:373
  13.1 18.8 %collective-permute-start.3 = (bf16[128,1536]{1,0:T(8,128)(2,1)S(1)}, bf16[128,1536]{1,0:T(8,128)(2,1)S(1)}, u32[]{:S(2)}, u32[]{:S(2)}) collective-permute-start(bf16[128,1536]{1,0:T(8,128)(2,1)S(1)} %get-tuple-element.85.b0), channel_id=1, source_target_pairs={{0,8},{8,0},{16,24},{24,16},{1,9},{9,1},{17,25},{25,17},{2,10},{10... | collective-permute-start | bytes 1179656 | tf_op jit(solution)/shard_map/ppermute | solution.py:373
  13.3 33.5 %collective-permute-start.2 = (bf16[128,1536]{1,0:T(8,128)(2,1)}, bf16[128,1536]{1,0:T(8,128)(2,1)}, u32[]{:S(2)}, u32[]{:S(2)}) collective-permute-start(bf16[128,1536]{1,0:T(8,128)(2,1)} %get-tuple-element.86.b0), channel_id=1, source_target_pairs={{0,24},{8,16},{16,8},{24,0},{1,25},{9,17},{17,9},{25,1},{2,26},{10... | collective-permute-start | bytes 1179656 | tf_op jit(solution)/shard_map/ppermute | solution.py:373
  16.0 32.2 %collective-permute-start.1 = (bf16[128,1536]{1,0:T(8,128)(2,1)}, bf16[128,1536]{1,0:T(8,128)(2,1)}, u32[]{:S(2)}, u32[]{:S(2)}) collective-permute-start(bf16[128,1536]{1,0:T(8,128)(2,1)} %get-tuple-element.86.b0), channel_id=1, source_target_pairs={{0,16},{8,24},{16,0},{24,8},{1,17},{9,25},{17,1},{25,9},{2,18},{10... | collective-permute-start | bytes 1179656 | tf_op jit(solution)/shard_map/ppermute | solution.py:373
  29.8 0.8 copy-start.1
  30.6 17.6 %collective-permute-start = (bf16[128,1536]{1,0:T(8,128)(2,1)}, bf16[128,1536]{1,0:T(8,128)(2,1)}, u32[]{:S(2)}, u32[]{:S(2)}) collective-permute-start(bf16[128,1536]{1,0:T(8,128)(2,1)} %get-tuple-element.86.b0), channel_id=1, source_target_pairs={{0,8},{8,0},{16,24},{24,16},{1,9},{9,1},{17,25},{25,17},{2,10},{10... | collective-permute-start | bytes 1179656 | tf_op jit(solution)/shard_map/ppermute | solution.py:373
  30.6 1.2 copy-start.2
  30.6 25.2 %collective-permute-start.9 = (bf16[256,1536]{1,0:T(8,128)(2,1)}, bf16[256,1536]{1,0:T(8,128)(2,1)}, u32[]{:S(2)}, u32[]{:S(2)}) collective-permute-start(bf16[256,1536]{1,0:T(8,128)(2,1)} %refs_3_.1), channel_id=1, source_target_pairs={{0,1},{1,0},{2,3},{3,2},{4,5},{5,4},{6,7},{7,6},{8,9},{9,8},{10,11... | collective-permute-start | bytes 2359304 | tf_op jit(solution)/shard_map/ppermute | solution.py:373
  31.9 0.8 copy-start.3
  42.6 5.6 %collective-permute-start.6 = (bf16[128,1024]{1,0:T(8,128)(2,1)}, bf16[128,1024]{1,0:T(8,128)(2,1)}, u32[]{:S(2)}, u32[]{:S(2)}) collective-permute-start(bf16[128,1024]{1,0:T(8,128)(2,1)} %get-tuple-element.49), channel_id=1, source_target_pairs={{0,32},{32,0},{1,33},{33,1},{2,34},{34,2},{3,35},{35,3},{4,36},{36... | collective-permute-start | bytes 786440 | tf_op jit(solution)/shard_map/ppermute | solution.py:373
  46.8 2.9 %collective-permute-start.7 = (bf16[128,1024]{1,0:T(8,128)(2,1)}, bf16[128,1024]{1,0:T(8,128)(2,1)}, u32[]{:S(2)}, u32[]{:S(2)}) collective-permute-start(bf16[128,1024]{1,0:T(8,128)(2,1)} %get-tuple-element.50), channel_id=1, source_target_pairs={{0,32},{32,0},{1,33},{33,1},{2,34},{34,2},{3,35},{35,3},{4,36},{36... | collective-permute-start | bytes 786440 | tf_op jit(solution)/shard_map/ppermute | solution.py:373
  48.2 1.9 collective-permute-start.8
  52.5 20.6 %collective-permute-start.16 = (bf16[128,3072]{1,0:T(8,128)(2,1)}, bf16[128,3072]{1,0:T(8,128)(2,1)}, u32[]{:S(2)}, u32[]{:S(2)}) collective-permute-start(bf16[128,3072]{1,0:T(8,128)(2,1)} %add.13.refs_1_.refs_3_), channel_id=1, source_target_pairs={{0,64},{64,0},{1,65},{65,1},{2,66},{66,2},{3,67},{67,3},{4,68},{68... | collective-permute-start | bytes 2359304 | tf_op jit(solution)/shard_map/ppermute | solution.py:373
  55.2 17.8 %collective-permute-start.15 = (bf16[128,3072]{1,0:T(8,128)(2,1)}, bf16[128,3072]{1,0:T(8,128)(2,1)}, u32[]{:S(2)}, u32[]{:S(2)}) collective-permute-start(bf16[128,3072]{1,0:T(8,128)(2,1)} %get-tuple-element.59), channel_id=1, source_target_pairs={{0,32},{32,0},{1,33},{33,1},{2,34},{34,2},{3,35},{35,3},{4,36},{36... | collective-permute-start | bytes 2359304 | tf_op jit(solution)/shard_map/ppermute | solution.py:373
  65.8 2.0 collective-permute-start.11
  65.9 2.2 %collective-permute-start.12 = (bf16[128,1024]{1,0:T(8,128)(2,1)}, bf16[128,1024]{1,0:T(8,128)(2,1)}, u32[]{:S(2)}, u32[]{:S(2)}) collective-permute-start(bf16[128,1024]{1,0:T(8,128)(2,1)} %get-tuple-element.56), channel_id=1, source_target_pairs={{0,32},{32,0},{1,33},{33,1},{2,34},{34,2},{3,35},{35,3},{4,36},{36... | collective-permute-start | bytes 786440 | tf_op jit(solution)/shard_map/ppermute | solution.py:373
  66.4 2.1 %collective-permute-start.13 = (bf16[128,1024]{1,0:T(8,128)(2,1)}, bf16[128,1024]{1,0:T(8,128)(2,1)}, u32[]{:S(2)}, u32[]{:S(2)}) collective-permute-start(bf16[128,1024]{1,0:T(8,128)(2,1)} %get-tuple-element.57), channel_id=1, source_target_pairs={{0,32},{32,0},{1,33},{33,1},{2,34},{34,2},{3,35},{35,3},{4,36},{36... | collective-permute-start | bytes 786440 | tf_op jit(solution)/shard_map/ppermute | solution.py:373
  67.2 100.8 %reduce-scatter.2.cloned.1.call-start = ((), (), s32[]{:S(2)}) async-start(), calls=%async_computation.3 | async-start | bytes 1966080 | tf_op jit(solution)/shard_map/reduce_scatter | solution.py:415
  67.8 12.5 %collective-permute-start.10 = (bf16[128,3072]{1,0:T(8,128)(2,1)}, bf16[128,3072]{1,0:T(8,128)(2,1)}, u32[]{:S(2)}, u32[]{:S(2)}) collective-permute-start(bf16[128,3072]{1,0:T(8,128)(2,1)} %get-tuple-element.53), channel_id=1, source_target_pairs={{0,32},{32,0},{1,33},{33,1},{2,34},{34,2},{3,35},{35,3},{4,36},{36... | collective-permute-start | bytes 2359304 | tf_op jit(solution)/shard_map/ppermute | solution.py:373
  71.0 20.8 %collective-permute-start.14 = (bf16[128,3072]{1,0:T(8,128)(2,1)}, bf16[128,3072]{1,0:T(8,128)(2,1)}, u32[]{:S(2)}, u32[]{:S(2)}) collective-permute-start(bf16[128,3072]{1,0:T(8,128)(2,1)} %add.14.refs_1_), channel_id=1, source_target_pairs={{0,64},{64,0},{1,65},{65,1},{2,66},{66,2},{3,67},{67,3},{4,68},{68... | collective-permute-start | bytes 2359304 | tf_op jit(solution)/shard_map/ppermute | solution.py:373
  77.5 31.1 %collective-permute-start.17 = (bf16[128,3072]{1,0:T(8,128)(2,1)}, bf16[128,3072]{1,0:T(8,128)(2,1)}, u32[]{:S(2)}, u32[]{:S(2)}) collective-permute-start(bf16[128,3072]{1,0:T(8,128)(2,1)} %get-tuple-element.64.refs_0_), channel_id=1, source_target_pairs={{0,64},{64,0},{1,65},{65,1},{2,66},{66,2},{3,67},{67,3},{4,68},{68... | collective-permute-start | bytes 2359304 | tf_op jit(solution)/shard_map/ppermute | solution.py:373
  108.7 3.6 %collective-permute-start.18 = (bf16[128,3072]{1,0:T(8,128)(2,1)}, bf16[128,3072]{1,0:T(8,128)(2,1)}, u32[]{:S(2)}, u32[]{:S(2)}) collective-permute-start(bf16[128,3072]{1,0:T(8,128)(2,1)} %get-tuple-element.67.refs_7_.refs_1_.refs_19_), channel_id=1, source_target_pairs={{0,32},{32,0},{1,33},{33,1},{2,34},{34,2},{3,35},{35,3},{4,36},{36... | collective-permute-start | bytes 2359304 | tf_op jit(solution)/shard_map/ppermute | solution.py:373
  109.7 3.8 %collective-permute-start.20 = (bf16[128,3072]{1,0:T(8,128)(2,1)}, bf16[128,3072]{1,0:T(8,128)(2,1)}, u32[]{:S(2)}, u32[]{:S(2)}) collective-permute-start(bf16[128,3072]{1,0:T(8,128)(2,1)} %get-tuple-element.70.refs_1_.refs_3_.refs_15_), channel_id=1, source_target_pairs={{0,32},{32,0},{1,33},{33,1},{2,34},{34,2},{3,35},{35,3},{4,36},{36... | collective-permute-start | bytes 2359304 | tf_op jit(solution)/shard_map/ppermute | solution.py:373
  109.7 4.8 %collective-permute-start.21 = (bf16[128,3072]{1,0:T(8,128)(2,1)}, bf16[128,3072]{1,0:T(8,128)(2,1)}, u32[]{:S(2)}, u32[]{:S(2)}) collective-permute-start(bf16[128,3072]{1,0:T(8,128)(2,1)} %get-tuple-element.71.refs_3_.refs_5_.refs_17_), channel_id=1, source_target_pairs={{0,32},{32,0},{1,33},{33,1},{2,34},{34,2},{3,35},{35,3},{4,36},{36... | collective-permute-start | bytes 2359304 | tf_op jit(solution)/shard_map/ppermute | solution.py:373
  110.2 15.1 %collective-permute-start.24 = (bf16[256,512]{1,0:T(8,128)(2,1)}, bf16[256,512]{1,0:T(8,128)(2,1)}, u32[]{:S(2)}, u32[]{:S(2)}) collective-permute-start(bf16[256,512]{1,0:T(8,128)(2,1)} %get-tuple-element.66.refs_3_), channel_id=1, source_target_pairs={{0,65},{1,64},{64,1},{65,0},{2,67},{3,66},{66,3},{67,2},{4,69},{5,... | collective-permute-start | bytes 786440 | tf_op jit(solution)/shard_map/ppermute | solution.py:400
  111.0 13.5 %collective-permute-start.22 = (bf16[128,1024]{1,0:T(8,128)(2,1)}, bf16[128,1024]{1,0:T(8,128)(2,1)}, u32[]{:S(2)}, u32[]{:S(2)}) collective-permute-start(bf16[128,1024]{1,0:T(8,128)(2,1)} %get-tuple-element.72), channel_id=1, source_target_pairs={{0,64},{64,0},{1,65},{65,1},{2,66},{66,2},{3,67},{67,3},{4,68},{68... | collective-permute-start | bytes 786440 | tf_op jit(solution)/shard_map/ppermute | solution.py:373
  112.3 13.3 %collective-permute-start.23 = (bf16[256,512]{1,0:T(8,128)(2,1)}, bf16[256,512]{1,0:T(8,128)(2,1)}, u32[]{:S(2)}, u32[]{:S(2)}) collective-permute-start(bf16[256,512]{1,0:T(8,128)(2,1)} %get-tuple-element.66.refs_3_), channel_id=1, source_target_pairs={{0,1},{1,0},{2,3},{3,2},{4,5},{5,4},{6,7},{7,6},{8,9},{9,8},{10,11... | collective-permute-start | bytes 786440 | tf_op jit(solution)/shard_map/ppermute | solution.py:373
  113.4 24.6 %collective-permute-start.19 = (bf16[128,2048]{1,0:T(8,128)(2,1)}, bf16[128,2048]{1,0:T(8,128)(2,1)}, u32[]{:S(2)}, u32[]{:S(2)}) collective-permute-start(bf16[128,2048]{1,0:T(8,128)(2,1)} %get-tuple-element.68), channel_id=1, source_target_pairs={{0,64},{64,0},{1,65},{65,1},{2,66},{66,2},{3,67},{67,3},{4,68},{68... | collective-permute-start | bytes 1572872 | tf_op jit(solution)/shard_map/ppermute | solution.py:373
  125.5 3.3 %collective-permute-start.26 = (bf16[256,512]{1,0:T(8,128)(2,1)}, bf16[256,512]{1,0:T(8,128)(2,1)}, u32[]{:S(2)}, u32[]{:S(2)}) collective-permute-start(bf16[256,512]{1,0:T(8,128)(2,1)} %get-tuple-element.74.refs_11_), channel_id=1, source_target_pairs={{0,32},{32,0},{1,33},{33,1},{2,34},{34,2},{3,35},{35,3},{4,36},{36... | collective-permute-start | bytes 786440 | tf_op jit(solution)/shard_map/ppermute | solution.py:373
  127.4 1.9 collective-permute-start.27
  127.4 2.3 %collective-permute-start.25 = (bf16[128,1024]{1,0:T(8,128)(2,1)}, bf16[128,1024]{1,0:T(8,128)(2,1)}, u32[]{:S(2)}, u32[]{:S(2)}) collective-permute-start(bf16[128,1024]{1,0:T(8,128)(2,1)} %get-tuple-element.73.refs_9_.refs_4_), channel_id=1, source_target_pairs={{0,32},{32,0},{1,33},{33,1},{2,34},{34,2},{3,35},{35,3},{4,36},{36... | collective-permute-start | bytes 786440 | tf_op jit(solution)/shard_map/ppermute | solution.py:373
  138.1 2.3 %collective-permute-start.28 = (bf16[128,2048]{1,0:T(8,128)(2,1)}, bf16[128,2048]{1,0:T(8,128)(2,1)}, u32[]{:S(2)}, u32[]{:S(2)}) collective-permute-start(bf16[128,2048]{1,0:T(8,128)(2,1)} %after.11.refs_3_.refs_9_.refs_21_), channel_id=1, source_target_pairs={{0,32},{32,0},{1,33},{33,1},{2,34},{34,2},{3,35},{35,3},{4,36},{36... | collective-permute-start | bytes 1572872 | tf_op jit(solution)/shard_map/ppermute | solution.py:373
  138.5 16.5 %collective-permute-start.30 = (bf16[256,1024]{1,0:T(8,128)(2,1)}, bf16[256,1024]{1,0:T(8,128)(2,1)}, u32[]{:S(2)}, u32[]{:S(2)}) collective-permute-start(bf16[256,1024]{1,0:T(8,128)(2,1)} %get-tuple-element.76), channel_id=1, source_target_pairs={{0,65},{1,64},{64,1},{65,0},{2,67},{3,66},{66,3},{67,2},{4,69},{5,... | collective-permute-start | bytes 1572872 | tf_op jit(solution)/shard_map/ppermute | solution.py:400
  140.3 14.8 %collective-permute-start.29 = (bf16[256,1024]{1,0:T(8,128)(2,1)}, bf16[256,1024]{1,0:T(8,128)(2,1)}, u32[]{:S(2)}, u32[]{:S(2)}) collective-permute-start(bf16[256,1024]{1,0:T(8,128)(2,1)} %get-tuple-element.76), channel_id=1, source_target_pairs={{0,1},{1,0},{2,3},{3,2},{4,5},{5,4},{6,7},{7,6},{8,9},{9,8},{10,11... | collective-permute-start | bytes 1572872 | tf_op jit(solution)/shard_map/ppermute | solution.py:373
  150.4 42.0 %all-to-all-start = ((bf16[4,256,1536]{2,1,0:T(8,128)(2,1)}), bf16[4,256,1536]{2,1,0:T(8,128)(2,1)}, u32[]{:S(2)}, u32[]{:S(2)}) async-start(bf16[4,256,1536]{2,1,0:T(8,128)(2,1)} %input_part.3.refs_2_), calls=%async_computation | async-start | bytes 6291456 | tf_op jit(solution)/shard_map/all_to_all | solution.py:423
  155.1 2.3 %collective-permute-start.31 = (bf16[256,1024]{1,0:T(8,128)(2,1)}, bf16[256,1024]{1,0:T(8,128)(2,1)}, u32[]{:S(2)}, u32[]{:S(2)}) collective-permute-start(bf16[256,1024]{1,0:T(8,128)(2,1)} %get-tuple-element.77.refs_11_.refs_23_), channel_id=1, source_target_pairs={{0,32},{32,0},{1,33},{33,1},{2,34},{34,2},{3,35},{35,3},{4,36},{36... | collective-permute-start | bytes 1572872 | tf_op jit(solution)/shard_map/ppermute | solution.py:373
  155.5 2.6 %collective-permute-start.32 = (bf16[256,1024]{1,0:T(8,128)(2,1)}, bf16[256,1024]{1,0:T(8,128)(2,1)}, u32[]{:S(2)}, u32[]{:S(2)}) collective-permute-start(bf16[256,1024]{1,0:T(8,128)(2,1)} %get-tuple-element.78.refs_13_.refs_25_), channel_id=1, source_target_pairs={{0,32},{32,0},{1,33},{33,1},{2,34},{34,2},{3,35},{35,3},{4,36},{36... | collective-permute-start | bytes 1572872 | tf_op jit(solution)/shard_map/ppermute | solution.py:373
  164.2 13.3 %collective-permute-start.33 = (bf16[768,256]{1,0:T(8,128)(2,1)}, bf16[768,256]{1,0:T(8,128)(2,1)}, u32[]{:S(2)}, u32[]{:S(2)}) collective-permute-start(bf16[768,256]{1,0:T(8,128)(2,1)} %get-tuple-element.82), channel_id=1, source_target_pairs={{0,6},{2,4},{4,2},{6,0},{1,7},{3,5},{5,3},{7,1},{8,14},{10,12},{12... | collective-permute-start | bytes 1179656 | tf_op jit(solution)/shard_map/ppermute | solution.py:373
  168.0 10.3 %collective-permute-start.34 = (bf16[768,256]{1,0:T(8,128)(2,1)}, bf16[768,256]{1,0:T(8,128)(2,1)}, u32[]{:S(2)}, u32[]{:S(2)}) collective-permute-start(bf16[768,256]{1,0:T(8,128)(2,1)} %get-tuple-element.79.refs_27_), channel_id=1, source_target_pairs={{0,2},{2,0},{4,6},{6,4},{1,3},{3,1},{5,7},{7,5},{8,10},{10,8},{12,... | collective-permute-start | bytes 1179656 | tf_op jit(solution)/shard_map/ppermute | solution.py:373
  180.6 20.5 %collective-permute-start.36 = (bf16[1536,256]{1,0:T(8,128)(2,1)}, bf16[1536,256]{1,0:T(8,128)(2,1)}, u32[]{:S(2)}, u32[]{:S(2)}) collective-permute-start(bf16[1536,256]{1,0:T(8,128)(2,1)} %get-tuple-element.84), channel_id=1, source_target_pairs={{0,6},{2,4},{4,2},{6,0},{1,7},{3,5},{5,3},{7,1},{8,14},{10,12},{12... | collective-permute-start | bytes 2359304 | tf_op jit(solution)/shard_map/ppermute | solution.py:373
  182.1 19.0 %collective-permute-start.35 = (bf16[1536,256]{1,0:T(8,128)(2,1)}, bf16[1536,256]{1,0:T(8,128)(2,1)}, u32[]{:S(2)}, u32[]{:S(2)}) collective-permute-start(bf16[1536,256]{1,0:T(8,128)(2,1)} %get-tuple-element.83.refs_15_), channel_id=1, source_target_pairs={{0,2},{2,0},{4,6},{6,4},{1,3},{3,1},{5,7},{7,5},{8,10},{10,8},{12,... | collective-permute-start | bytes 2359304 | tf_op jit(solution)/shard_map/ppermute | solution.py:373
Sparse Core Ops, SparseCore 0:
  67.3 39.5 all-gather.1
  140.4 26.6 reduce-scatter.1
